TPU v7x, 32 devices: a whole 2x2x4 slice. The times are simulated.
32 devices in a mesh: row: 8 (over z, y), col: 4 (over x, core).
Axes of the slice: x: 2, y: 2, z: 4, core: 2. Of those that a mesh axis runs over, the one named last changes fastest.
Arguments:
- adjoint_source: float32 [96, 64, 2, 128], P('row', 'col'), may hold values from -6 to 6
- saved_currents: float32 [96, 64, 2, 128], P('row', 'col'), may hold values from -6 to 6
- lag_blocks: float32 [7, 7, 2, 128, 128], replicated, may hold values from -0.01875 to 0.01875
- element_inverse: float32 [2, 128, 128], replicated, may hold values from -0.088388348 to 1.0883883
Outputs:
- adjoint: float32 [96, 64, 2, 128], P('row', 'col')
- lag_grad: float32 [7, 7, 2, 128, 128], P(None, None, None, 'row')
All inputs are finite; a program needn't handle non-finite values.
Results may differ from a plain program's by a relative error of at most 0.0001.
Values sent between devices are 32-bit elements; how exact they have to be, the bound alone decides.
No kernel may reach another device: no remote copies, remote signals or barrier semaphores. Data moves between devices by JAX's collectives and lax.ppermute only.
A program may use at most 128 MiB of HBM per device.

v0:
```python
import functools
import math

import jax
import jax.numpy as jnp
from jax import lax
from jax.experimental import pallas as pl
from jax.experimental.pallas import tpu as pltpu
from jax.sharding import PartitionSpec as P

SWEEPS = 2
VMEM_LIMIT = 56 * 1024 * 1024

f32 = jnp.float32
bf16 = jnp.bfloat16


def split(value):
    high = value.astype(bf16)
    return high, (value - high.astype(f32)).astype(bf16)


def dot(left, right):
    return jnp.dot(left, right, preferred_element_type=f32)


def dot3(left, right):
    (left_high, left_low), (right_high, right_low) = left, right
    return dot(left_high, right_high) + dot(left_low, right_high) + dot(left_high, right_low)


def round_up(count, unit):
    return (count + unit - 1) // unit * unit


def store_block(ref, index, real, imag):
    width = real.shape[0]
    low, high = slice(0, width), slice(width, 2 * width)
    ref[index + (low, low)] = real
    ref[index + (low, high)] = -imag
    ref[index + (high, low)] = imag
    ref[index + (high, high)] = real


def weights_kernel(blocks_ref, high_ref, low_ref):
    span, _, width, _ = blocks_ref.shape[1:]
    for b in range(span):
        real_high, real_low = split(blocks_ref[0, b, 0])
        imag_high, imag_low = split(blocks_ref[0, b, 1])
        store_block(high_ref, (0, b), real_high, imag_high)
        store_block(low_ref, (0, b), real_low, imag_low)


def prepare_weights(lag_blocks):
    span, _, parts, width, _ = lag_blocks.shape
    shape = jax.ShapeDtypeStruct((span, span, parts * width, parts * width), bf16)
    spec = pl.BlockSpec((1,) + shape.shape[1:], lambda a: (a, 0, 0, 0))
    size = lag_blocks.size * 4
    return pl.pallas_call(
        weights_kernel,
        grid=(span,),
        in_specs=[pl.BlockSpec((1,) + lag_blocks.shape[1:], lambda a: (a, 0, 0, 0, 0))],
        out_specs=[spec, spec],
        out_shape=[shape, shape],
        cost_estimate=pl.CostEstimate(flops=0, bytes_accessed=3 * size, transcendentals=0),
        compiler_params=pltpu.CompilerParams(vmem_limit_bytes=VMEM_LIMIT),
        name="weights",
    )(lag_blocks)


def inside(rows, cols, pitch, margin, tile_rows, tile_cols):
    at = lax.broadcasted_iota(jnp.int32, (rows * pitch, 1), 0)
    i = at // pitch
    j = at - i * pitch
    row = i + (lax.axis_index("row") * tile_rows - margin)
    col = j + (lax.axis_index("col") * tile_cols - margin)
    row_ok = (row >= 0) & (row < tile_rows * lax.axis_size("row"))
    col_ok = (col >= 0) & (col < tile_cols * lax.axis_size("col"))
    return row_ok & col_ok & (j < cols)


def sweeps_kernel(
    sizes,
    source_ref,
    inverse_ref,
    high_hbm,
    low_hbm,
    adjoint_ref,
    *rest,
):
    rows, cols, span, peers, pitch, wide = sizes
    sends = rest[:peers]
    (first, second, x1_high, x1_low, x2_high, x2_low, acc, turned, w_high, w_low, e_high, e_low, sems) = rest[peers:]
    reach = span // 2
    mid_rows, mid_cols = rows + 2 * reach, cols + 2 * reach
    full_rows = rows + 4 * reach
    lanes = source_ref.shape[-1]
    width = lanes // 2

    def weight_copies(a):
        return (
            pltpu.make_async_copy(high_hbm.at[a], w_high.at[a], sems.at[0, a]),
            pltpu.make_async_copy(low_hbm.at[a], w_low.at[a], sems.at[1, a]),
        )

    for a in range(span):
        for copy in weight_copies(a):
            copy.start()

    real_high, real_low = split(inverse_ref[0])
    imag_high, imag_low = split(inverse_ref[1])
    store_block(e_high, (), real_high, imag_high)
    store_block(e_low, (), real_low, imag_low)

    def invert(value):
        return dot3(split(value), (e_high[...], e_low[...]))

    step_rows = 4

    @pl.loop(0, full_rows // step_rows)
    def _(s):
        at = pl.ds(s * step_rows, step_rows)
        piece = source_ref[at].reshape(step_rows * wide, lanes)
        first[at] = invert(piece).reshape(step_rows, wide, lanes)

    first[full_rows] = jnp.zeros((wide, lanes), f32)

    @pl.loop(0, full_rows // 2)
    def _(s):
        for odd in range(2):
            for b in range(span):
                value = first[pl.ds(2 * s + odd, 2), pl.ds(b, pitch), :]
                high, low = split(value.reshape(2 * pitch, lanes))
                to = pl.ds(pl.multiple_of(s * 2 * pitch, 2 * pitch), 2 * pitch)
                x1_high[odd, to, b * lanes : (b + 1) * lanes] = high
                x1_low[odd, to, b * lanes : (b + 1) * lanes] = low

    acc[...] = jnp.zeros_like(acc)

    @pl.loop(0, span)
    def _(a):
        for copy in weight_copies(a):
            copy.wait()
        odd = a % 2
        at = pl.ds(pl.multiple_of((a // 2) * 2 * pitch, 2 * pitch), mid_rows * pitch)
        high = x1_high[odd, at, :]
        low = x1_low[odd, at, :]
        weight_high = w_high[a].reshape(span * lanes, lanes)
        weight_low = w_low[a].reshape(span * lanes, lanes)
        acc[...] += dot(high, weight_high) + dot(low, weight_high) + dot(high, weight_low)

    step_rows = 3

    mask = inside(mid_rows, mid_cols, pitch, reach, rows, cols)
    for s in range(mid_rows // step_rows):
        at = pl.ds(s * step_rows + reach, step_rows)
        flat = slice(s * step_rows * pitch, (s + 1) * step_rows * pitch)
        centre = first[at, pl.ds(reach, pitch), :].reshape(step_rows * pitch, lanes)
        source = source_ref[at, pl.ds(reach, pitch), :].reshape(step_rows * pitch, lanes)
        value = centre + invert(source - centre - acc[flat, :])
        value = jnp.where(mask[flat], value, 0.0)
        second[s * step_rows : (s + 1) * step_rows] = value.reshape(step_rows, pitch, lanes)

    @pl.loop(0, mid_rows)
    def _(i):
        for b in range(span):
            high, low = split(second[i, pl.ds(b, cols), :])
            to = pl.ds(pl.multiple_of(i * cols, cols), cols)
            x2_high[to, b * lanes : (b + 1) * lanes] = high
            x2_low[to, b * lanes : (b + 1) * lanes] = low

    own = rows * cols
    acc[:own] = jnp.zeros((own, lanes), f32)

    @pl.loop(0, span)
    def _(a):
        at = pl.ds(pl.multiple_of(a * cols, cols), own)
        high = x2_high[at, :]
        low = x2_low[at, :]
        weight_high = w_high[a].reshape(span * lanes, lanes)
        weight_low = w_low[a].reshape(span * lanes, lanes)
        acc[:own] += dot(high, weight_high) + dot(low, weight_high) + dot(high, weight_low)

    centre = second[reach : reach + rows, pl.ds(reach, cols), :].reshape(own, lanes)
    source = source_ref[2 * reach : 2 * reach + rows, pl.ds(2 * reach, cols), :].reshape(own, lanes)
    value = centre + invert(source - centre - acc[:own])
    adjoint_ref[...] = value.reshape(adjoint_ref.shape)
    turned[...] = value.T

    share = width // peers
    me = lax.axis_index("row")
    for k in range(peers):
        peer = lax.rem(me + k, peers)
        for part in range(2):
            at = pl.multiple_of(part * width + peer * share, share)
            sends[k][part * share : (part + 1) * share, :] = turned[pl.ds(at, share), :]


def run_sweeps(source, inverse, high, low, rows, cols, peers):
    span = high.shape[0]
    reach = span // 2
    lanes = source.shape[-1]
    wide = source.shape[1]
    pitch = round_up(cols + 2 * reach, 8)
    full_rows, mid_rows = rows + 4 * reach, rows + 2 * reach
    share = lanes // 2 // peers
    sizes = (rows, cols, span, peers, pitch, wide)
    vmem = pl.BlockSpec(memory_space=pltpu.VMEM)
    hbm = pl.BlockSpec(memory_space=pl.ANY)
    send = jax.ShapeDtypeStruct((2 * share, rows * cols), f32)
    flops = 6 * span * span * lanes * lanes * (mid_rows * pitch + rows * cols)
    out = pl.pallas_call(
        functools.partial(sweeps_kernel, sizes),
        in_specs=[vmem, vmem, hbm, hbm],
        out_specs=[vmem] * (1 + peers),
        out_shape=[jax.ShapeDtypeStruct((rows, cols, lanes), f32)] + [send] * peers,
        scratch_shapes=[
            pltpu.VMEM((full_rows + 1, wide, lanes), f32),
            pltpu.VMEM((mid_rows, pitch, lanes), f32),
            pltpu.VMEM((2, full_rows * pitch, span * lanes), bf16),
            pltpu.VMEM((2, full_rows * pitch, span * lanes), bf16),
            pltpu.VMEM((mid_rows * cols, span * lanes), bf16),
            pltpu.VMEM((mid_rows * cols, span * lanes), bf16),
            pltpu.VMEM((mid_rows * pitch, lanes), f32),
            pltpu.VMEM((lanes, rows * cols), f32),
            pltpu.VMEM(high.shape, bf16),
            pltpu.VMEM(high.shape, bf16),
            pltpu.VMEM((lanes, lanes), bf16),
            pltpu.VMEM((lanes, lanes), bf16),
            pltpu.SemaphoreType.DMA((2, span)),
        ],
        cost_estimate=pl.CostEstimate(
            flops=flops, bytes_accessed=4 * high.size, transcendentals=0
        ),
        compiler_params=pltpu.CompilerParams(vmem_limit_bytes=VMEM_LIMIT),
        name="sweeps",
    )(source, inverse, high, low)
    return out[0], out[1:]


def correlate_kernel(sizes, factor, *refs):
    rows, cols, span, peers = sizes
    shares = refs[:peers]
    currents = refs[peers : 2 * peers]
    mine_ref, other_ref = refs[2 * peers : 2 * peers + 2]
    placed, flat, l_high, l_low, s_high, s_low = refs[2 * peers + 2 :]
    reach = span // 2
    own = rows * cols
    double = shares[0].shape[0]
    share = double // 2
    width = currents[0].shape[-1]
    lanes = 2 * width
    side = round_up(reach * cols, 128)
    me = lax.axis_index("row")

    twin = me + 1 - 2 * lax.rem(me, 2)
    for k in range(peers):
        placed[lax.rem(me - k + peers, peers)] = shares[k][...]
        tile = lax.rem((twin if k % 2 else me) - k + k % 2 + peers, peers)

        @pl.loop(0, rows)
        def _(i):
            to = pl.ds(pl.multiple_of(tile * own + i * cols, cols), cols)
            for b in range(span):
                for h in range(2):
                    value = currents[k][h, i, pl.ds(span - 1 - b, cols), :]
                    high, low = split(value)
                    at = b * lanes + h * width
                    s_high[to, at : at + width] = high
                    s_low[to, at : at + width] = low

    total = peers * own
    flat[:, :side] = jnp.zeros((double, side), f32)
    flat[:, side + total :] = jnp.zeros((double, side), f32)
    for tile in range(peers):
        flat[:, side + tile * own : side + (tile + 1) * own] = placed[tile]
    for a in range(span):
        start = side + (a - reach) * cols
        high, low = split(flat[:, start : start + total])
        l_high[a * double : (a + 1) * double, :] = high
        l_low[a * double : (a + 1) * double, :] = low

    half = share // 2
    upper = lax.axis_index("col") % 2 == 1
    for b in range(span):
        at = slice(b * lanes, (b + 1) * lanes)
        product = dot3((l_high[...], l_low[...]), (s_high[:, at], s_low[:, at])) * factor
        for a in range(span):
            top = product[a * double : a * double + share]
            bottom = product[a * double + share : (a + 1) * double]
            real = top[:, :width] + bottom[:, width:]
            imag = bottom[:, :width] - top[:, width:]
            for c, value in enumerate((real, imag)):
                mine_ref[a, b, c] = jnp.where(upper, value[half:], value[:half])
                other_ref[a, b, c] = jnp.where(upper, value[:half], value[half:])


def correlate(shares, currents, rows, cols, span, factor):
    peers = len(shares)
    reach = span // 2
    double, own = shares[0].shape
    share = double // 2
    width = currents[0].shape[-1]
    total = peers * own
    side = round_up(reach * cols, 128)
    vmem = pl.BlockSpec(memory_space=pltpu.VMEM)
    out = jax.ShapeDtypeStruct((span, span, 2, share // 2, width), f32)
    return pl.pallas_call(
        functools.partial(correlate_kernel, (rows, cols, span, peers), factor),
        in_specs=[vmem] * (2 * peers),
        out_specs=[vmem, vmem],
        out_shape=[out, out],
        scratch_shapes=[
            pltpu.VMEM((peers, double, own), f32),
            pltpu.VMEM((double, total + 2 * side), f32),
            pltpu.VMEM((span * double, total), bf16),
            pltpu.VMEM((span * double, total), bf16),
            pltpu.VMEM((total, span * 2 * width), bf16),
            pltpu.VMEM((total, span * 2 * width), bf16),
        ],
        cost_estimate=pl.CostEstimate(
            flops=6 * span * double * total * span * 2 * width,
            bytes_accessed=4 * (2 * out.size + peers * currents[0].size),
            transcendentals=0,
        ),
        compiler_params=pltpu.CompilerParams(vmem_limit_bytes=VMEM_LIMIT),
        name="correlate",
    )(*shares, *currents)


def swap(value, axis, first):
    pairs = []
    for low in range(first, lax.axis_size(axis) - 1, 2):
        pairs += [(low, low + 1), (low + 1, low)]
    if not pairs:
        return jnp.zeros_like(value)
    return lax.ppermute(value, axis, pairs)


def shifted(value, axis, shift):
    peers = lax.axis_size(axis)
    if shift % peers == 0:
        return value
    return lax.ppermute(value, axis, [(i, (i + shift) % peers) for i in range(peers)])


def edges(initial, last, axis):
    even = lax.axis_index(axis) % 2 == 0
    inner = swap(jnp.where(even, last, initial), axis, 0)
    outer = swap(jnp.where(even, initial, last), axis, 1)
    return jnp.where(even, outer, inner), jnp.where(even, inner, outer)


def on_device(adjoint_source, saved_currents, lag_blocks, element_inverse):
    rows, cols, parts, width = adjoint_source.shape
    span = lag_blocks.shape[0]
    reach = span // 2
    halo = SWEEPS * reach
    lanes = parts * width
    peers = lax.axis_size("row")
    source = adjoint_source.reshape(rows, cols, lanes)
    saved = saved_currents.reshape(rows, cols, lanes)

    high, low = prepare_weights(lag_blocks)

    initial = jnp.concatenate([source[:, :halo], saved[:, :reach]], axis=1)
    last = jnp.concatenate([source[:, cols - halo :], saved[:, cols - reach :]], axis=1)
    before, after = edges(initial, last, "col")
    wide = round_up(cols + 2 * halo, 8)
    filler = jnp.zeros((rows, wide - cols - 2 * halo, lanes), f32)
    source = jnp.concatenate([before[:, :halo], source, after[:, :halo], filler], axis=1)
    saved = jnp.concatenate([before[:, halo:], saved, after[:, halo:]], axis=1)
    before, after = edges(source[:halo], source[rows - halo :], "row")
    source = jnp.concatenate([before, source, after], axis=0)

    saved = jnp.pad(saved, ((0, 0), (0, round_up(cols + 2 * reach, 8) - cols - 2 * reach), (0, 0)))
    saved = saved.reshape(rows, -1, parts, width).transpose(2, 0, 1, 3)
    currents = [None] * peers
    for k in range(0, peers, 2):
        piece = shifted(saved, "row", k)
        twin = swap(piece, "row", 0)
        currents[k] = piece
        currents[k + 1] = twin

    adjoint, sends = run_sweeps(source, element_inverse, high, low, rows, cols, peers)
    shares = [shifted(send, "row", k) for k, send in enumerate(sends)]

    elements = rows * peers * cols * lax.axis_size("col")
    factor = -1.0 / math.sqrt(elements)
    mine, other = correlate(shares, currents, rows, cols, span, factor)
    mine = mine + swap(other, "col", 0)
    total = mine
    for k in range(2, lax.axis_size("col"), 2):
        total = total + shifted(mine, "col", k)
    twin = swap(total, "col", 0)
    even = lax.axis_index("col") % 2 == 0
    lag_grad = jnp.concatenate(
        [jnp.where(even, total, twin), jnp.where(even, twin, total)], axis=3
    )
    return (adjoint.reshape(adjoint_source.shape), lag_grad)


def solution(mesh):
    return jax.shard_map(
        on_device,
        mesh=mesh,
        in_specs=(P("row", "col", None, None), P("row", "col", None, None), P(), P()),
        out_specs=(P("row", "col", None, None), P(None, None, None, "row", None)),
        check_vma=False,
    )
```

profile of v0, /device:TPU:0, one launch (start us, length us, event | category | flops | bytes accessed | tf_op | source)
XLA Modules:
  0.0 141.2 jit_solution(12914741044666447033)
XLA Ops:
  0.6 1.1 reshape.16
  1.8 1.1 reshape.17
  2.9 0.1 fusion.2
  2.9 0.7 collective-permute-start
  3.6 4.4 %collective-permute-start.1 = (f32[12,9,256]{2,1,0:T(8,128)S(1)}, f32[12,9,256]{2,1,0:T(8,128)S(1)}, u32[]{:S(2)}, u32[]{:S(2)}) collective-permute-start(f32[12,9,256]{2,1,0:T(8,128)S(1)} %get-tuple-element.37), channel_id=1, source_target_pairs={{0,1},{1,0},{2,3},{3,2},{4,5},{5,4},{6,7},{7,6},{8,9},{9,8},{10,11... | collective-permute-start | bytes 331784 | tf_op jit(solution)/shard_map/ppermute | solution.py:337
  8.0 0.0 collective-permute-done
  8.0 1.1 collective-permute-done.1
  9.1 0.1 pad_maximum_fusion.2
  9.2 0.7 collective-permute-start.2
  9.9 4.3 %collective-permute-start.3 = (f32[6,32,256]{2,1,0:T(8,128)S(1)}, f32[6,32,256]{2,1,0:T(8,128)S(1)}, u32[]{:S(2)}, u32[]{:S(2)}) collective-permute-start(f32[6,32,256]{2,1,0:T(8,128)S(1)} %get-tuple-element.33), channel_id=1, source_target_pairs={{0,4},{4,0},{8,12},{12,8},{16,20},{20,16},{24,28},{28,24},{1,5},{5... | collective-permute-start | bytes 589832 | tf_op jit(solution)/shard_map/ppermute | solution.py:337
  14.3 9.2 %weights.1 = (bf16[7,7,256,256]{3,2,1,0:T(8,128)(2,1)}, bf16[7,7,256,256]{3,2,1,0:T(8,128)(2,1)}) custom-call(f32[7,7,2,128,128]{4,3,2,1,0:T(8,128)} %blocks_ref.1), custom_call_target="tpu_custom_call" | custom-call | bytes 19267584 | tf_op jit(solution)/shard_map/weights/pallas_call | solution.py:59
  23.5 0.1 bitcast_bitcast_fusion.refs_8_
  23.6 0.0 copy-start
  23.6 1.6 %collective-permute-start.12 = (f32[2,12,24,128]{3,2,1,0:T(8,128)S(1)}, f32[2,12,24,128]{3,2,1,0:T(8,128)S(1)}, u32[]{:S(2)}, u32[]{:S(2)}) collective-permute-start(f32[2,12,24,128]{3,2,1,0:T(8,128)S(1)} %bitcast_bitcast_fusion.refs_8_), channel_id=1, source_target_pairs={{0,8},{4,12},{8,16},{12,20},{16,24},{20,28},{24,0},{28,4},{1,9},{5... | collective-permute-start | bytes 884744 | tf_op jit(solution)/shard_map/ppermute | solution.py:344
  25.2 1.1 collective-permute-start.14
  26.3 2.8 %collective-permute-start.16 = (f32[2,12,24,128]{3,2,1,0:T(8,128)S(1)}, f32[2,12,24,128]{3,2,1,0:T(8,128)S(1)}, u32[]{:S(2)}, u32[]{:S(2)}) collective-permute-start(f32[2,12,24,128]{3,2,1,0:T(8,128)S(1)} %bitcast_bitcast_fusion.refs_8_), channel_id=1, source_target_pairs={{0,24},{4,28},{8,0},{12,4},{16,8},{20,12},{24,16},{28,20},{1,25},{... | collective-permute-start | bytes 884744 | tf_op jit(solution)/shard_map/ppermute | solution.py:344
  29.1 0.0 collective-permute-done.2
  29.1 0.4 collective-permute-start.11
  29.5 0.0 collective-permute-done.3
  29.6 1.0 pad_maximum_fusion.1.source_ref
  30.5 4.3 %collective-permute-done.12.refs_10_ = f32[2,12,24,128]{3,2,1,0:T(8,128)S(1)} collective-permute-done((f32[2,12,24,128]{3,2,1,0:T(8,128)S(1)}, f32[2,12,24,128]{3,2,1,0:T(8,128)S(1)}, u32[]{:S(2)}, u32[]{:S(2)}) %collective-permute-start.12) | collective-permute-done | bytes 294944 | tf_op jit(solution)/shard_map/ppermute | solution.py:344
  34.9 0.0 collective-permute-start.13
  34.9 13.1 %collective-permute-done.14.refs_12_ = f32[2,12,24,128]{3,2,1,0:T(8,128)S(1)} collective-permute-done((f32[2,12,24,128]{3,2,1,0:T(8,128)S(1)}, f32[2,12,24,128]{3,2,1,0:T(8,128)S(1)}, u32[]{:S(2)}, u32[]{:S(2)}) %collective-permute-start.14) | collective-permute-done | bytes 294944 | tf_op jit(solution)/shard_map/ppermute | solution.py:344
  47.9 0.2 collective-permute-start.15
  48.1 0.0 collective-permute-done.16.refs_14_
  48.1 1.9 %collective-permute-start.17 = (f32[2,12,24,128]{3,2,1,0:T(8,128)S(1)}, f32[2,12,24,128]{3,2,1,0:T(8,128)S(1)}, u32[]{:S(2)}, u32[]{:S(2)}) collective-permute-start(f32[2,12,24,128]{3,2,1,0:T(8,128)S(1)} %collective-permute-done.16.refs_14_), channel_id=1, source_target_pairs={{0,4},{4,0},{8,12},{12,8},{16,20},{20,16},{24,28},{28,24},{1,5},{5... | collective-permute-start | bytes 884744 | tf_op jit(solution)/shard_map/ppermute | solution.py:337
  50.0 21.2 %sweeps.1 = (f32[12,16,256]{2,1,0:T(8,128)}, f32[32,192]{1,0:T(8,128)}, f32[32,192]{1,0:T(8,128)}, f32[32,192]{1,0:T(8,128)}, f32[32,192]{1,0:T(8,128)}, /*index...) custom-call(f32[24,32,256]{2,1,0:T(8,128)} %pad_maximum_fusion.1.source_ref, ...), custom_call_target="tpu_custom_call" | custom-call | flops 12022972416 | bytes 12845056 | tf_op jit(solution)/shard_map/sweeps/pallas_call | solution.py:212
  71.2 0.0 copy-done
  71.2 7.3 %collective-permute-start.10 = (f32[32,192]{1,0:T(8,128)}, f32[32,192]{1,0:T(8,128)S(1)}, u32[]{:S(2)}, u32[]{:S(2)}) collective-permute-start(f32[32,192]{1,0:T(8,128)} %get-tuple-element.25), channel_id=1, source_target_pairs={{0,28},{4,0},{8,4},{12,8},{16,12},{20,16},{24,20},{28,24},{1,29},{... | collective-permute-start | bytes 73736 | tf_op jit(solution)/shard_map/ppermute | solution.py:344
  78.5 1.9 %collective-permute-done.10.refs_7_ = f32[32,192]{1,0:T(8,128)S(1)} collective-permute-done((f32[32,192]{1,0:T(8,128)}, f32[32,192]{1,0:T(8,128)S(1)}, u32[]{:S(2)}, u32[]{:S(2)}) %collective-permute-start.10) | collective-permute-done | bytes 24608 | tf_op jit(solution)/shard_map/ppermute | solution.py:344
  80.4 0.0 collective-permute-start.4
  80.4 7.0 %collective-permute-done.4.refs_1_ = f32[32,192]{1,0:T(8,128)S(1)} collective-permute-done((f32[32,192]{1,0:T(8,128)}, f32[32,192]{1,0:T(8,128)S(1)}, u32[]{:S(2)}, u32[]{:S(2)}) %collective-permute-start.4) | collective-permute-done | bytes 24608 | tf_op jit(solution)/shard_map/ppermute | solution.py:344
  87.4 0.0 collective-permute-start.5
  87.4 6.2 %collective-permute-done.5.refs_2_ = f32[32,192]{1,0:T(8,128)S(1)} collective-permute-done((f32[32,192]{1,0:T(8,128)}, f32[32,192]{1,0:T(8,128)S(1)}, u32[]{:S(2)}, u32[]{:S(2)}) %collective-permute-start.5) | collective-permute-done | bytes 24608 | tf_op jit(solution)/shard_map/ppermute | solution.py:344
  93.6 0.0 collective-permute-start.6
  93.6 5.9 %collective-permute-done.6.refs_3_ = f32[32,192]{1,0:T(8,128)S(1)} collective-permute-done((f32[32,192]{1,0:T(8,128)}, f32[32,192]{1,0:T(8,128)S(1)}, u32[]{:S(2)}, u32[]{:S(2)}) %collective-permute-start.6) | collective-permute-done | bytes 24608 | tf_op jit(solution)/shard_map/ppermute | solution.py:344
  99.5 0.0 collective-permute-start.7
  99.5 5.1 %collective-permute-done.7.refs_4_ = f32[32,192]{1,0:T(8,128)S(1)} collective-permute-done((f32[32,192]{1,0:T(8,128)}, f32[32,192]{1,0:T(8,128)S(1)}, u32[]{:S(2)}, u32[]{:S(2)}) %collective-permute-start.7) | collective-permute-done | bytes 24608 | tf_op jit(solution)/shard_map/ppermute | solution.py:344
  104.7 0.0 collective-permute-start.8
  104.7 5.0 %collective-permute-done.8.refs_5_ = f32[32,192]{1,0:T(8,128)S(1)} collective-permute-done((f32[32,192]{1,0:T(8,128)}, f32[32,192]{1,0:T(8,128)S(1)}, u32[]{:S(2)}, u32[]{:S(2)}) %collective-permute-start.8) | collective-permute-done | bytes 24608 | tf_op jit(solution)/shard_map/ppermute | solution.py:344
  109.7 1.5 %collective-permute-start.9 = (f32[32,192]{1,0:T(8,128)}, f32[32,192]{1,0:T(8,128)S(1)}, u32[]{:S(2)}, u32[]{:S(2)}) collective-permute-start(f32[32,192]{1,0:T(8,128)} %get-tuple-element.24), channel_id=1, source_target_pairs={{0,24},{4,28},{8,0},{12,4},{16,8},{20,12},{24,16},{28,20},{1,25},{... | collective-permute-start | bytes 73736 | tf_op jit(solution)/shard_map/ppermute | solution.py:344
  111.2 2.7 %collective-permute-done.9.refs_6_ = f32[32,192]{1,0:T(8,128)S(1)} collective-permute-done((f32[32,192]{1,0:T(8,128)}, f32[32,192]{1,0:T(8,128)S(1)}, u32[]{:S(2)}, u32[]{:S(2)}) %collective-permute-start.9) | collective-permute-done | bytes 24608 | tf_op jit(solution)/shard_map/ppermute | solution.py:344
  113.8 0.0 collective-permute-done.11.refs_9_
  113.8 0.0 collective-permute-done.13.refs_11_
  113.8 0.0 copy-start.6
  113.8 0.0 collective-permute-done.15.refs_13_
  113.9 0.0 collective-permute-done.17.refs_15_
  114.0 0.5 copy-done.15
  114.4 0.1 copy-done.5
  114.6 0.1 copy-done.6
  114.7 0.1 copy-done.7
  114.8 0.1 copy-done.8
  114.9 9.0 %correlate.1 = (f32[7,7,2,8,128]{4,3,2,1,0:T(8,128)}, f32[7,7,2,8,128]{4,3,2,1,0:T(8,128)}) custom-call(f32[32,192]{1,0:T(8,128)} %get-tuple-element.18.refs_0_, f32[32,192]{1,0:T(8,128)} %copy-done.10, f32[32,192]{1,0:T(8,128)} %copy-done.11, f32[32,192]{1,0:T(8,128)} %copy-done.12, f32[32,192]{1,0:T(8,128)} %copy-done.13, f32[32,192]{1,0:T(8,128)} %copy-done.14, ...), custom_call_target="tpu_custom_call" | custom-call | flops 3699376128 | bytes 3162112 | tf_op jit(solution)/shard_map/correlate/pallas_call | solution.py:308
  123.9 0.0 collective-permute-start.18
  123.9 1.9 %collective-permute-done.18 = f32[7,7,2,8,128]{4,3,2,1,0:T(8,128)S(1)} collective-permute-done((f32[7,7,2,8,128]{4,3,2,1,0:T(8,128)}, f32[7,7,2,8,128]{4,3,2,1,0:T(8,128)S(1)}, u32[]{:S(2)}, u32[]{:S(2)}) %collective-permute-start.18) | collective-permute-done | bytes 401440 | tf_op jit(solution)/shard_map/ppermute | solution.py:337
  125.8 1.1 add.18
  126.9 0.1 collective-permute-start.19
  127.0 11.3 %collective-permute-done.19 = f32[7,7,2,8,128]{4,3,2,1,0:T(8,128)S(1)} collective-permute-done((f32[7,7,2,8,128]{4,3,2,1,0:T(8,128)S(1)}, f32[7,7,2,8,128]{4,3,2,1,0:T(8,128)S(1)}, u32[]{:S(2)}, u32[]{:S(2)}) %collective-permute-start.19) | collective-permute-done | bytes 401440 | tf_op jit(solution)/shard_map/ppermute | solution.py:344
  138.3 0.1 add.19
  138.3 0.1 collective-permute-start.20
  138.4 0.8 reshape.18
  139.2 0.9 collective-permute-done.20
  140.1 0.1 broadcast_select_fusion.1
  140.2 1.0 pad_maximum_fusion
  (34 shorter events, 0.2 us)
Async XLA Ops:
  2.9 5.0 %collective-permute-start = (f32[12,9,256]{2,1,0:T(8,128)S(1)}, f32[12,9,256]{2,1,0:T(8,128)S(1)}, u32[]{:S(2)}, u32[]{:S(2)}) collective-permute-start(f32[12,9,256]{2,1,0:T(8,128)S(1)} %get-tuple-element.36), channel_id=1, source_target_pairs={{1,2},{2,1},{5,6},{6,5},{9,10},{10,9},{13,14},{14,13},{17,18},{18,... | collective-permute-start | bytes 331784 | tf_op jit(solution)/shard_map/ppermute | solution.py:337
  3.6 5.4 %collective-permute-start.1 = (f32[12,9,256]{2,1,0:T(8,128)S(1)}, f32[12,9,256]{2,1,0:T(8,128)S(1)}, u32[]{:S(2)}, u32[]{:S(2)}) collective-permute-start(f32[12,9,256]{2,1,0:T(8,128)S(1)} %get-tuple-element.37), channel_id=1, source_target_pairs={{0,1},{1,0},{2,3},{3,2},{4,5},{5,4},{6,7},{7,6},{8,9},{9,8},{10,11... | collective-permute-start | bytes 331784 | tf_op jit(solution)/shard_map/ppermute | solution.py:337
  9.2 19.9 %collective-permute-start.2 = (f32[6,32,256]{2,1,0:T(8,128)S(1)}, f32[6,32,256]{2,1,0:T(8,128)S(1)}, u32[]{:S(2)}, u32[]{:S(2)}) collective-permute-start(f32[6,32,256]{2,1,0:T(8,128)S(1)} %get-tuple-element.32), channel_id=1, source_target_pairs={{4,8},{8,4},{12,16},{16,12},{20,24},{24,20},{5,9},{9,5},{13,17},{1... | collective-permute-start | bytes 589832 | tf_op jit(solution)/shard_map/ppermute | solution.py:337
  9.9 19.6 %collective-permute-start.3 = (f32[6,32,256]{2,1,0:T(8,128)S(1)}, f32[6,32,256]{2,1,0:T(8,128)S(1)}, u32[]{:S(2)}, u32[]{:S(2)}) collective-permute-start(f32[6,32,256]{2,1,0:T(8,128)S(1)} %get-tuple-element.33), channel_id=1, source_target_pairs={{0,4},{4,0},{8,12},{12,8},{16,20},{20,16},{24,28},{28,24},{1,5},{5... | collective-permute-start | bytes 589832 | tf_op jit(solution)/shard_map/ppermute | solution.py:337
  23.6 47.6 %copy-start = (f32[2,12,24,128]{3,2,1,0:T(8,128)}, f32[2,12,24,128]{3,2,1,0:T(8,128)S(1)}, u32[]{:S(2)}) copy-start(f32[2,12,24,128]{3,2,1,0:T(8,128)S(1)} %bitcast_bitcast_fusion.refs_8_) | copy-start | bytes 884740
  23.6 11.3 %collective-permute-start.12 = (f32[2,12,24,128]{3,2,1,0:T(8,128)S(1)}, f32[2,12,24,128]{3,2,1,0:T(8,128)S(1)}, u32[]{:S(2)}, u32[]{:S(2)}) collective-permute-start(f32[2,12,24,128]{3,2,1,0:T(8,128)S(1)} %bitcast_bitcast_fusion.refs_8_), channel_id=1, source_target_pairs={{0,8},{4,12},{8,16},{12,20},{16,24},{20,28},{24,0},{28,4},{1,9},{5... | collective-permute-start | bytes 884744 | tf_op jit(solution)/shard_map/ppermute | solution.py:344
  25.2 22.7 %collective-permute-start.14 = (f32[2,12,24,128]{3,2,1,0:T(8,128)S(1)}, f32[2,12,24,128]{3,2,1,0:T(8,128)S(1)}, u32[]{:S(2)}, u32[]{:S(2)}) collective-permute-start(f32[2,12,24,128]{3,2,1,0:T(8,128)S(1)} %bitcast_bitcast_fusion.refs_8_), channel_id=1, source_target_pairs={{0,16},{4,20},{8,24},{12,28},{16,0},{20,4},{24,8},{28,12},{1,17},{... | collective-permute-start | bytes 884744 | tf_op jit(solution)/shard_map/ppermute | solution.py:344
  26.3 21.8 %collective-permute-start.16 = (f32[2,12,24,128]{3,2,1,0:T(8,128)S(1)}, f32[2,12,24,128]{3,2,1,0:T(8,128)S(1)}, u32[]{:S(2)}, u32[]{:S(2)}) collective-permute-start(f32[2,12,24,128]{3,2,1,0:T(8,128)S(1)} %bitcast_bitcast_fusion.refs_8_), channel_id=1, source_target_pairs={{0,24},{4,28},{8,0},{12,4},{16,8},{20,12},{24,16},{28,20},{1,25},{... | collective-permute-start | bytes 884744 | tf_op jit(solution)/shard_map/ppermute | solution.py:344
  29.1 84.7 %collective-permute-start.11 = (f32[2,12,24,128]{3,2,1,0:T(8,128)S(1)}, f32[2,12,24,128]{3,2,1,0:T(8,128)S(1)}, u32[]{:S(2)}, u32[]{:S(2)}) collective-permute-start(f32[2,12,24,128]{3,2,1,0:T(8,128)S(1)} %bitcast_bitcast_fusion.refs_8_), channel_id=1, source_target_pairs={{0,4},{4,0},{8,12},{12,8},{16,20},{20,16},{24,28},{28,24},{1,5},{5... | collective-permute-start | bytes 884744 | tf_op jit(solution)/shard_map/ppermute | solution.py:337
  34.9 36.3 %copy-start.2 = (f32[2,12,24,128]{3,2,1,0:T(8,128)}, f32[2,12,24,128]{3,2,1,0:T(8,128)S(1)}, u32[]{:S(2)}) copy-start(f32[2,12,24,128]{3,2,1,0:T(8,128)S(1)} %collective-permute-done.12.refs_10_) | copy-start | bytes 884740
  34.9 79.0 %collective-permute-start.13 = (f32[2,12,24,128]{3,2,1,0:T(8,128)S(1)}, f32[2,12,24,128]{3,2,1,0:T(8,128)S(1)}, u32[]{:S(2)}, u32[]{:S(2)}) collective-permute-start(f32[2,12,24,128]{3,2,1,0:T(8,128)S(1)} %collective-permute-done.12.refs_10_), channel_id=1, source_target_pairs={{0,4},{4,0},{8,12},{12,8},{16,20},{20,16},{24,28},{28,24},{1,5},{5... | collective-permute-start | bytes 884744 | tf_op jit(solution)/shard_map/ppermute | solution.py:337
  47.9 23.3 %copy-start.3 = (f32[2,12,24,128]{3,2,1,0:T(8,128)}, f32[2,12,24,128]{3,2,1,0:T(8,128)S(1)}, u32[]{:S(2)}) copy-start(f32[2,12,24,128]{3,2,1,0:T(8,128)S(1)} %collective-permute-done.14.refs_12_) | copy-start | bytes 884740
  47.9 65.9 %collective-permute-start.15 = (f32[2,12,24,128]{3,2,1,0:T(8,128)S(1)}, f32[2,12,24,128]{3,2,1,0:T(8,128)S(1)}, u32[]{:S(2)}, u32[]{:S(2)}) collective-permute-start(f32[2,12,24,128]{3,2,1,0:T(8,128)S(1)} %collective-permute-done.14.refs_12_), channel_id=1, source_target_pairs={{0,4},{4,0},{8,12},{12,8},{16,20},{20,16},{24,28},{28,24},{1,5},{5... | collective-permute-start | bytes 884744 | tf_op jit(solution)/shard_map/ppermute | solution.py:337
  48.1 23.1 %copy-start.4 = (f32[2,12,24,128]{3,2,1,0:T(8,128)}, f32[2,12,24,128]{3,2,1,0:T(8,128)S(1)}, u32[]{:S(2)}) copy-start(f32[2,12,24,128]{3,2,1,0:T(8,128)S(1)} %collective-permute-done.16.refs_14_) | copy-start | bytes 884740
  48.1 65.7 %collective-permute-start.17 = (f32[2,12,24,128]{3,2,1,0:T(8,128)S(1)}, f32[2,12,24,128]{3,2,1,0:T(8,128)S(1)}, u32[]{:S(2)}, u32[]{:S(2)}) collective-permute-start(f32[2,12,24,128]{3,2,1,0:T(8,128)S(1)} %collective-permute-done.16.refs_14_), channel_id=1, source_target_pairs={{0,4},{4,0},{8,12},{12,8},{16,20},{20,16},{24,28},{28,24},{1,5},{5... | collective-permute-start | bytes 884744 | tf_op jit(solution)/shard_map/ppermute | solution.py:337
  71.2 9.2 %collective-permute-start.10 = (f32[32,192]{1,0:T(8,128)}, f32[32,192]{1,0:T(8,128)S(1)}, u32[]{:S(2)}, u32[]{:S(2)}) collective-permute-start(f32[32,192]{1,0:T(8,128)} %get-tuple-element.25), channel_id=1, source_target_pairs={{0,28},{4,0},{8,4},{12,8},{16,12},{20,16},{24,20},{28,24},{1,29},{... | collective-permute-start | bytes 73736 | tf_op jit(solution)/shard_map/ppermute | solution.py:344
  80.4 33.5 %copy-start.9 = (f32[32,192]{1,0:T(8,128)}, f32[32,192]{1,0:T(8,128)S(1)}, u32[]{:S(2)}) copy-start(f32[32,192]{1,0:T(8,128)S(1)} %collective-permute-done.10.refs_7_) | copy-start | bytes 73732
  80.4 7.0 %collective-permute-start.4 = (f32[32,192]{1,0:T(8,128)}, f32[32,192]{1,0:T(8,128)S(1)}, u32[]{:S(2)}, u32[]{:S(2)}) collective-permute-start(f32[32,192]{1,0:T(8,128)} %get-tuple-element.19), channel_id=1, source_target_pairs={{0,4},{4,8},{8,12},{12,16},{16,20},{20,24},{24,28},{28,0},{1,5},{5... | collective-permute-start | bytes 73736 | tf_op jit(solution)/shard_map/ppermute | solution.py:344
  87.4 26.5 %copy-start.10 = (f32[32,192]{1,0:T(8,128)}, f32[32,192]{1,0:T(8,128)S(1)}, u32[]{:S(2)}) copy-start(f32[32,192]{1,0:T(8,128)S(1)} %collective-permute-done.4.refs_1_) | copy-start | bytes 73732
  87.4 6.2 %collective-permute-start.5 = (f32[32,192]{1,0:T(8,128)}, f32[32,192]{1,0:T(8,128)S(1)}, u32[]{:S(2)}, u32[]{:S(2)}) collective-permute-start(f32[32,192]{1,0:T(8,128)} %get-tuple-element.20), channel_id=1, source_target_pairs={{0,8},{4,12},{8,16},{12,20},{16,24},{20,28},{24,0},{28,4},{1,9},{5... | collective-permute-start | bytes 73736 | tf_op jit(solution)/shard_map/ppermute | solution.py:344
  93.6 20.3 %copy-start.11 = (f32[32,192]{1,0:T(8,128)}, f32[32,192]{1,0:T(8,128)S(1)}, u32[]{:S(2)}) copy-start(f32[32,192]{1,0:T(8,128)S(1)} %collective-permute-done.5.refs_2_) | copy-start | bytes 73732
  93.6 5.9 %collective-permute-start.6 = (f32[32,192]{1,0:T(8,128)}, f32[32,192]{1,0:T(8,128)S(1)}, u32[]{:S(2)}, u32[]{:S(2)}) collective-permute-start(f32[32,192]{1,0:T(8,128)} %get-tuple-element.21), channel_id=1, source_target_pairs={{0,12},{4,16},{8,20},{12,24},{16,28},{20,0},{24,4},{28,8},{1,13},{... | collective-permute-start | bytes 73736 | tf_op jit(solution)/shard_map/ppermute | solution.py:344
  99.5 14.4 %copy-start.12 = (f32[32,192]{1,0:T(8,128)}, f32[32,192]{1,0:T(8,128)S(1)}, u32[]{:S(2)}) copy-start(f32[32,192]{1,0:T(8,128)S(1)} %collective-permute-done.6.refs_3_) | copy-start | bytes 73732
  99.5 5.1 %collective-permute-start.7 = (f32[32,192]{1,0:T(8,128)}, f32[32,192]{1,0:T(8,128)S(1)}, u32[]{:S(2)}, u32[]{:S(2)}) collective-permute-start(f32[32,192]{1,0:T(8,128)} %get-tuple-element.22), channel_id=1, source_target_pairs={{0,16},{4,20},{8,24},{12,28},{16,0},{20,4},{24,8},{28,12},{1,17},{... | collective-permute-start | bytes 73736 | tf_op jit(solution)/shard_map/ppermute | solution.py:344
  104.7 9.3 %copy-start.13 = (f32[32,192]{1,0:T(8,128)}, f32[32,192]{1,0:T(8,128)S(1)}, u32[]{:S(2)}) copy-start(f32[32,192]{1,0:T(8,128)S(1)} %collective-permute-done.7.refs_4_) | copy-start | bytes 73732
  104.7 5.0 %collective-permute-start.8 = (f32[32,192]{1,0:T(8,128)}, f32[32,192]{1,0:T(8,128)S(1)}, u32[]{:S(2)}, u32[]{:S(2)}) collective-permute-start(f32[32,192]{1,0:T(8,128)} %get-tuple-element.23), channel_id=1, source_target_pairs={{0,20},{4,24},{8,28},{12,0},{16,4},{20,8},{24,12},{28,16},{1,21},{... | collective-permute-start | bytes 73736 | tf_op jit(solution)/shard_map/ppermute | solution.py:344
  109.7 4.2 %copy-start.14 = (f32[32,192]{1,0:T(8,128)}, f32[32,192]{1,0:T(8,128)S(1)}, u32[]{:S(2)}) copy-start(f32[32,192]{1,0:T(8,128)S(1)} %collective-permute-done.8.refs_5_) | copy-start | bytes 73732
  109.7 4.1 %collective-permute-start.9 = (f32[32,192]{1,0:T(8,128)}, f32[32,192]{1,0:T(8,128)S(1)}, u32[]{:S(2)}, u32[]{:S(2)}) collective-permute-start(f32[32,192]{1,0:T(8,128)} %get-tuple-element.24), channel_id=1, source_target_pairs={{0,24},{4,28},{8,0},{12,4},{16,8},{20,12},{24,16},{28,20},{1,25},{... | collective-permute-start | bytes 73736 | tf_op jit(solution)/shard_map/ppermute | solution.py:344
  113.8 0.6 copy-start.15
  113.8 0.7 copy-start.5
  113.8 0.8 copy-start.6
  113.9 1.0 copy-start.7
  113.9 1.0 copy-start.8
  114.9 23.5 %copy-start.1 = (f32[12,16,256]{2,1,0:T(8,128)S(1)}, f32[12,16,256]{2,1,0:T(8,128)}, u32[]{:S(2)}) copy-start(f32[12,16,256]{2,1,0:T(8,128)} %get-tuple-element.17) | copy-start | bytes 589828
  123.9 1.9 %collective-permute-start.18 = (f32[7,7,2,8,128]{4,3,2,1,0:T(8,128)}, f32[7,7,2,8,128]{4,3,2,1,0:T(8,128)S(1)}, u32[]{:S(2)}, u32[]{:S(2)}) collective-permute-start(f32[7,7,2,8,128]{4,3,2,1,0:T(8,128)} %get-tuple-element.27), channel_id=1, source_target_pairs={{0,1},{1,0},{2,3},{3,2},{4,5},{5,4},{6,7},{7,6},{8,9},{9,8},{10,11... | collective-permute-start | bytes 1204232 | tf_op jit(solution)/shard_map/ppermute | solution.py:337
  126.9 11.4 %collective-permute-start.19 = (f32[7,7,2,8,128]{4,3,2,1,0:T(8,128)S(1)}, f32[7,7,2,8,128]{4,3,2,1,0:T(8,128)S(1)}, u32[]{:S(2)}, u32[]{:S(2)}) collective-permute-start(f32[7,7,2,8,128]{4,3,2,1,0:T(8,128)S(1)} %add.18), channel_id=1, source_target_pairs={{0,2},{1,3},{2,0},{3,1},{4,6},{5,7},{6,4},{7,5},{8,10},{9,11},{10,... | collective-permute-start | bytes 1204232 | tf_op jit(solution)/shard_map/ppermute | solution.py:344
  138.3 1.8 %collective-permute-start.20 = (f32[7,7,2,8,128]{4,3,2,1,0:T(8,128)S(1)}, f32[7,7,2,8,128]{4,3,2,1,0:T(8,128)S(1)}, u32[]{:S(2)}, u32[]{:S(2)}) collective-permute-start(f32[7,7,2,8,128]{4,3,2,1,0:T(8,128)S(1)} %add.19), channel_id=1, source_target_pairs={{0,1},{1,0},{2,3},{3,2},{4,5},{5,4},{6,7},{7,6},{8,9},{9,8},{10,11... | collective-permute-start | bytes 1204232 | tf_op jit(solution)/shard_map/ppermute | solution.py:337
where the time goes:
time: 142 us; the launch traced here: 141 us
  waiting for transfers between devices  66.5 us (47%)
  Pallas kernels  39.4 us (28%)
  starting transfers between devices  26.9 us (19%)
  local copies, waits for them, and re-layouts  4.02 us (3%)
  other arithmetic  3.4 us (2%)
    ppermute x11, waiting for transfers between devices, shifted(): lax.ppermute(value, axis, [(i, (i + shift) % peers) for i in range(peers)])  62.6 us
    pallas_call x1, Pallas kernels, run_sweeps(): pl.pallas_call(functools.partial(sweeps_kernel, sizes), in_specs=[vmem, v...  21.2 us
    ppermute x11, starting transfers between devices, shifted(): lax.ppermute(value, axis, [(i, (i + shift) % peers) for i in range(peers)])  14.4 us
    ppermute x10, starting transfers between devices, swap(): return lax.ppermute(value, axis, pairs)  12.5 us
    pallas_call x1, Pallas kernels, prepare_weights(): pl.pallas_call(weights_kernel, grid=(span,), in_specs=[pl.BlockSpec((1,)...  9.18 us
    pallas_call x1, Pallas kernels, correlate(): pl.pallas_call(functools.partial(correlate_kernel, (rows, cols, span, pee...  8.98 us
    ppermute x10, waiting for transfers between devices, swap(): return lax.ppermute(value, axis, pairs)  3.96 us
  transfers between devices with their start and end apart: 21, of which 13 were waited for; matrix products, arithmetic and copies ran while one was open for 1% of the time, Pallas kernels for 22%

commit v1 on v0

v1 whole, which is shorter than its diff:
```python
import functools
import math

import jax
import jax.numpy as jnp
from jax import lax
from jax.experimental import pallas as pl
from jax.experimental.pallas import tpu as pltpu
from jax.sharding import PartitionSpec as P

SWEEPS = 2
VMEM_LIMIT = 56 * 1024 * 1024

f32 = jnp.float32
bf16 = jnp.bfloat16


def split(value):
    high = value.astype(bf16)
    return high, (value - high.astype(f32)).astype(bf16)


def dot(left, right):
    return jnp.dot(left, right, preferred_element_type=f32)


def dot3(left, right):
    (left_high, left_low), (right_high, right_low) = left, right
    return dot(left_high, right_high) + dot(left_low, right_high) + dot(left_high, right_low)


def round_up(count, unit):
    return (count + unit - 1) // unit * unit


def store_block(ref, index, real, imag):
    width = real.shape[0]
    low, high = slice(0, width), slice(width, 2 * width)
    ref[index + (low, low)] = real
    ref[index + (low, high)] = -imag
    ref[index + (high, low)] = imag
    ref[index + (high, high)] = real


def inside(first_row, rows, cols, pitch, margin, tile_rows, tile_cols):
    at = lax.broadcasted_iota(jnp.int32, (rows * pitch, 1), 0)
    i = at // pitch
    j = at - i * pitch
    row = i + (first_row + lax.axis_index("row") * tile_rows - margin)
    col = j + (lax.axis_index("col") * tile_cols - margin)
    row_ok = (row >= 0) & (row < tile_rows * lax.axis_size("row"))
    col_ok = (col >= 0) & (col < tile_cols * lax.axis_size("col"))
    return row_ok & col_ok & (j < cols)


def sweeps_kernel(
    sizes,
    source_ref,
    inverse_ref,
    blocks_hbm,
    adjoint_ref,
    *rest,
):
    rows, cols, span, peers, pitch, wide = sizes
    sends = rest[:peers]
    (first, second, x1_high, x1_low, x2_high, x2_low, acc, turned, raw, w_high, w_low, e_high, e_low, sems) = rest[peers:]
    reach = span // 2
    mid_rows, mid_cols = rows + 2 * reach, cols + 2 * reach
    full_rows = rows + 4 * reach
    lanes = source_ref.shape[-1]
    width = lanes // 2

    def block_copy(a):
        return pltpu.make_async_copy(blocks_hbm.at[a], raw.at[a], sems.at[a])

    for a in range(span):
        block_copy(a).start()

    def prepare(a):
        @pl.loop(0, span)
        def _(b):
            real_high, real_low = split(raw[a, b, 0])
            imag_high, imag_low = split(raw[a, b, 1])
            store_block(w_high, (a, b), real_high, imag_high)
            store_block(w_low, (a, b), real_low, imag_low)

    def products(a, high, low):
        weight_high = w_high[a].reshape(span * lanes, lanes)
        weight_low = w_low[a].reshape(span * lanes, lanes)
        return dot(high, weight_high) + dot(low, weight_high) + dot(high, weight_low)

    real_high, real_low = split(inverse_ref[0])
    imag_high, imag_low = split(inverse_ref[1])
    store_block(e_high, (), real_high, imag_high)
    store_block(e_low, (), real_low, imag_low)

    def invert(value):
        return dot3(split(value), (e_high[...], e_low[...]))

    step_rows = 4

    @pl.loop(0, full_rows // step_rows)
    def _(s):
        at = pl.ds(s * step_rows, step_rows)
        piece = source_ref[at].reshape(step_rows * wide, lanes)
        first[at] = invert(piece).reshape(step_rows, wide, lanes)

    first[full_rows] = jnp.zeros((wide, lanes), f32)

    @pl.loop(0, full_rows // 2)
    def _(s):
        for odd in range(2):
            for b in range(span):
                value = first[pl.ds(2 * s + odd, 2), pl.ds(b, pitch), :]
                high, low = split(value.reshape(2 * pitch, lanes))
                to = pl.ds(pl.multiple_of(s * 2 * pitch, 2 * pitch), 2 * pitch)
                x1_high[odd, to, b * lanes : (b + 1) * lanes] = high
                x1_low[odd, to, b * lanes : (b + 1) * lanes] = low

    acc[...] = jnp.zeros_like(acc)

    @pl.loop(0, span)
    def _(a):
        block_copy(a).wait()
        prepare(a)
        at = pl.ds(pl.multiple_of((a // 2) * 2 * pitch, 2 * pitch), mid_rows * pitch)
        acc[...] += products(a, x1_high[a % 2, at, :], x1_low[a % 2, at, :])

    step_rows = 3

    @pl.loop(0, mid_rows // step_rows)
    def _(s):
        at = pl.ds(s * step_rows + reach, step_rows)
        count = step_rows * pitch
        flat = pl.ds(pl.multiple_of(s * count, 8), count)
        centre = first[at, pl.ds(reach, pitch), :].reshape(count, lanes)
        source = source_ref[at, pl.ds(reach, pitch), :].reshape(count, lanes)
        value = centre + invert(source - centre - acc[flat, :])
        mask = inside(s * step_rows, step_rows, mid_cols, pitch, reach, rows, cols)
        value = jnp.where(mask, value, 0.0)
        second[pl.ds(s * step_rows, step_rows)] = value.reshape(step_rows, pitch, lanes)

    @pl.loop(0, mid_rows)
    def _(i):
        for b in range(span):
            high, low = split(second[i, pl.ds(b, cols), :])
            to = pl.ds(pl.multiple_of(i * cols, cols), cols)
            x2_high[to, b * lanes : (b + 1) * lanes] = high
            x2_low[to, b * lanes : (b + 1) * lanes] = low

    own = rows * cols
    acc[:own] = jnp.zeros((own, lanes), f32)

    @pl.loop(0, span)
    def _(a):
        at = pl.ds(pl.multiple_of(a * cols, cols), own)
        acc[:own] += products(a, x2_high[at, :], x2_low[at, :])

    centre = second[reach : reach + rows, pl.ds(reach, cols), :].reshape(own, lanes)
    source = source_ref[2 * reach : 2 * reach + rows, pl.ds(2 * reach, cols), :].reshape(own, lanes)
    value = centre + invert(source - centre - acc[:own])
    adjoint_ref[...] = value.reshape(adjoint_ref.shape)
    turned[...] = value.T

    share = width // peers
    me = lax.axis_index("row")
    for k in range(peers):
        peer = lax.rem(me + k, peers)
        for part in range(2):
            at = pl.multiple_of(part * width + peer * share, share)
            sends[k][part * share : (part + 1) * share, :] = turned[pl.ds(at, share), :]


def run_sweeps(source, inverse, lag_blocks, rows, cols, peers):
    span = lag_blocks.shape[0]
    reach = span // 2
    lanes = source.shape[-1]
    wide = source.shape[1]
    pitch = round_up(cols + 2 * reach, 8)
    full_rows, mid_rows = rows + 4 * reach, rows + 2 * reach
    share = lanes // 2 // peers
    sizes = (rows, cols, span, peers, pitch, wide)
    vmem = pl.BlockSpec(memory_space=pltpu.VMEM)
    hbm = pl.BlockSpec(memory_space=pl.ANY)
    send = jax.ShapeDtypeStruct((2 * share, rows * cols), f32)
    flops = 6 * span * span * lanes * lanes * (mid_rows * pitch + rows * cols)
    out = pl.pallas_call(
        functools.partial(sweeps_kernel, sizes),
        in_specs=[vmem, vmem, hbm],
        out_specs=[vmem] * (1 + peers),
        out_shape=[jax.ShapeDtypeStruct((rows, cols, lanes), f32)] + [send] * peers,
        scratch_shapes=[
            pltpu.VMEM((full_rows + 1, wide, lanes), f32),
            pltpu.VMEM((mid_rows, pitch, lanes), f32),
            pltpu.VMEM((2, full_rows * pitch, span * lanes), bf16),
            pltpu.VMEM((2, full_rows * pitch, span * lanes), bf16),
            pltpu.VMEM((mid_rows * cols, span * lanes), bf16),
            pltpu.VMEM((mid_rows * cols, span * lanes), bf16),
            pltpu.VMEM((mid_rows * pitch, lanes), f32),
            pltpu.VMEM((lanes, rows * cols), f32),
            pltpu.VMEM(lag_blocks.shape, f32),
            pltpu.VMEM((span, span, lanes, lanes), bf16),
            pltpu.VMEM((span, span, lanes, lanes), bf16),
            pltpu.VMEM((lanes, lanes), bf16),
            pltpu.VMEM((lanes, lanes), bf16),
            pltpu.SemaphoreType.DMA((span,)),
        ],
        cost_estimate=pl.CostEstimate(
            flops=flops, bytes_accessed=4 * lag_blocks.size, transcendentals=0
        ),
        compiler_params=pltpu.CompilerParams(vmem_limit_bytes=VMEM_LIMIT),
        name="sweeps",
    )(source, inverse, lag_blocks)
    return out[0], out[1:]


def correlate_kernel(sizes, factor, *refs):
    rows, cols, span, peers = sizes
    shares = refs[:peers]
    piece_refs = refs[peers : peers + peers // 2]
    own_twin_ref, twins_ref = refs[peers + peers // 2 : peers + peers // 2 + 2]
    refs = refs[peers + peers // 2 + 2 :]
    mine_ref, other_ref = refs[:2]
    placed, flat, l_high, l_low, stage, s_high, s_low, sems = refs[2:]
    reach = span // 2
    own = rows * cols
    double = shares[0].shape[0]
    share = double // 2
    width = stage.shape[-1]
    me = lax.axis_index("row")
    even = me - lax.rem(me, 2)
    odd = 1 - lax.rem(me, 2)

    copies = []
    for k in range(peers // 2):
        base = lax.rem(even - 2 * k + peers, peers)
        twin = own_twin_ref if k == 0 else twins_ref.at[k - 1]
        copies.append(pltpu.make_async_copy(piece_refs[k], stage.at[base + 1 - odd], sems.at[0, k]))
        copies.append(pltpu.make_async_copy(twin, stage.at[base + odd], sems.at[1, k]))
    for copy in copies:
        copy.start()

    for k in range(peers):
        placed[lax.rem(me - k + peers, peers)] = shares[k][...]
    total = peers * own
    side = round_up(reach * cols, 128)
    flat[:, :side] = jnp.zeros((double, side), f32)
    flat[:, side + total :] = jnp.zeros((double, side), f32)
    for tile in range(peers):
        flat[:, side + tile * own : side + (tile + 1) * own] = placed[tile]

    @pl.loop(0, 2)
    def _(part):
        rows_at = pl.ds(pl.multiple_of(part * share, 8), share)
        for a in range(span):
            start = side + (a - reach) * cols
            high, low = split(flat[rows_at, start : start + total])
            l_high[a, part] = high
            l_low[a, part] = low

    for copy in copies:
        copy.wait()

    @pl.loop(0, peers)
    def _(tile):
        @pl.loop(0, rows)
        def _(i):
            to = pl.ds(pl.multiple_of(tile * own + i * cols, cols), cols)
            for b in range(span):
                for h in range(2):
                    high, low = split(stage[tile, h, i, pl.ds(span - 1 - b, cols), :])
                    s_high[b, to, h * width : (h + 1) * width] = high
                    s_low[b, to, h * width : (h + 1) * width] = low

    half = share // 2
    upper = lax.axis_index("col") % 2 == 1

    @pl.loop(0, span)
    def _(b):
        left = tuple(ref[...].reshape(span * double, total) for ref in (l_high, l_low))
        product = dot3(left, (s_high[b], s_low[b])) * factor
        for a in range(span):
            top = product[a * double : a * double + share]
            bottom = product[a * double + share : (a + 1) * double]
            real = top[:, :width] + bottom[:, width:]
            imag = bottom[:, :width] - top[:, width:]
            for c, value in enumerate((real, imag)):
                mine_ref[a, b, c] = jnp.where(upper, value[half:], value[:half])
                other_ref[a, b, c] = jnp.where(upper, value[:half], value[half:])


def correlate(shares, pieces, own_twin, twins, rows, cols, span, factor):
    peers = len(shares)
    reach = span // 2
    double, own = shares[0].shape
    share = double // 2
    width = own_twin.shape[-1]
    total = peers * own
    side = round_up(reach * cols, 128)
    vmem = pl.BlockSpec(memory_space=pltpu.VMEM)
    hbm = pl.BlockSpec(memory_space=pl.ANY)
    out = jax.ShapeDtypeStruct((span, span, 2, share // 2, width), f32)
    return pl.pallas_call(
        functools.partial(correlate_kernel, (rows, cols, span, peers), factor),
        in_specs=[vmem] * peers + [hbm] * (peers // 2 + 2),
        out_specs=[vmem, vmem],
        out_shape=[out, out],
        scratch_shapes=[
            pltpu.VMEM((peers, double, own), f32),
            pltpu.VMEM((double, total + 2 * side), f32),
            pltpu.VMEM((span, 2, share, total), bf16),
            pltpu.VMEM((span, 2, share, total), bf16),
            pltpu.VMEM((peers,) + own_twin.shape, f32),
            pltpu.VMEM((span, total, 2 * width), bf16),
            pltpu.VMEM((span, total, 2 * width), bf16),
            pltpu.SemaphoreType.DMA((2, peers // 2)),
        ],
        cost_estimate=pl.CostEstimate(
            flops=6 * span * double * total * span * 2 * width,
            bytes_accessed=4 * (2 * out.size + peers * own_twin.size),
            transcendentals=0,
        ),
        compiler_params=pltpu.CompilerParams(vmem_limit_bytes=VMEM_LIMIT),
        name="correlate",
    )(*shares, *pieces, own_twin, twins)


def swap(value, axis, first):
    pairs = []
    for low in range(first, lax.axis_size(axis) - 1, 2):
        pairs += [(low, low + 1), (low + 1, low)]
    if not pairs:
        return jnp.zeros_like(value)
    return lax.ppermute(value, axis, pairs)


def shifted(value, axis, shift):
    peers = lax.axis_size(axis)
    if shift % peers == 0:
        return value
    return lax.ppermute(value, axis, [(i, (i + shift) % peers) for i in range(peers)])


def edges(initial, last, axis):
    even = lax.axis_index(axis) % 2 == 0
    inner = swap(jnp.where(even, last, initial), axis, 0)
    outer = swap(jnp.where(even, initial, last), axis, 1)
    return jnp.where(even, outer, inner), jnp.where(even, inner, outer)


def on_device(adjoint_source, saved_currents, lag_blocks, element_inverse):
    rows, cols, parts, width = adjoint_source.shape
    span = lag_blocks.shape[0]
    reach = span // 2
    halo = SWEEPS * reach
    lanes = parts * width
    peers = lax.axis_size("row")
    source = adjoint_source.reshape(rows, cols, lanes)
    saved = saved_currents.reshape(rows, cols, lanes)

    initial = jnp.concatenate([source[:, :halo], saved[:, :reach]], axis=1)
    last = jnp.concatenate([source[:, cols - halo :], saved[:, cols - reach :]], axis=1)
    before, after = edges(initial, last, "col")
    wide = round_up(cols + 2 * halo, 8)
    filler = jnp.zeros((rows, wide - cols - 2 * halo, lanes), f32)
    source = jnp.concatenate([before[:, :halo], source, after[:, :halo], filler], axis=1)
    saved = jnp.concatenate([before[:, halo:], saved, after[:, halo:]], axis=1)
    before, after = edges(source[:halo], source[rows - halo :], "row")
    source = jnp.concatenate([before, source, after], axis=0)

    saved = jnp.pad(saved, ((0, 0), (0, round_up(cols + 2 * reach, 8) - cols - 2 * reach), (0, 0)))
    saved = saved.reshape(rows, -1, parts, width).transpose(2, 0, 1, 3)
    pieces = [shifted(saved, "row", k) for k in range(0, peers, 2)]
    own_twin = swap(saved, "row", 0)

    adjoint, sends = run_sweeps(source, element_inverse, lag_blocks, rows, cols, peers)
    twins, sends = lax.optimization_barrier((jnp.stack(pieces[1:]), sends))
    twins = swap(twins, "row", 0)
    shares = [shifted(send, "row", k) for k, send in enumerate(sends)]

    elements = rows * peers * cols * lax.axis_size("col")
    factor = -1.0 / math.sqrt(elements)
    mine, other = correlate(shares, pieces, own_twin, twins, rows, cols, span, factor)
    mine = mine + swap(other, "col", 0)
    total = mine
    for k in range(2, lax.axis_size("col"), 2):
        total = total + shifted(mine, "col", k)
    twin = swap(total, "col", 0)
    even = lax.axis_index("col") % 2 == 0
    lag_grad = jnp.concatenate(
        [jnp.where(even, total, twin), jnp.where(even, twin, total)], axis=3
    )
    return (adjoint.reshape(adjoint_source.shape), lag_grad)


def solution(mesh):
    return jax.shard_map(
        on_device,
        mesh=mesh,
        in_specs=(P("row", "col", None, None), P("row", "col", None, None), P(), P()),
        out_specs=(P("row", "col", None, None), P(None, None, None, "row", None)),
        check_vma=False,
    )
```

time: 142 us -> 119 us (0.84)
  waiting for transfers between devices: 66.5 us -> 42.9 us
  starting transfers between devices: 26.9 us -> 32.2 us
  Pallas kernels: 39.4 us -> 34.4 us
    ppermute x11, waiting for transfers between devices: 62.6 us -> 15.5 us  [shifted(): lax.ppermute(value, axis, [(i, (i + shift) % peers) for i in range(peers)])]
    ppermute x10 -> x8, waiting for transfers between devices: 3.96 us -> 27.5 us  [swap(): return lax.ppermute(value, axis, pairs)]
    pallas_call x1 -> x0, Pallas kernels: 9.18 us -> none  [prepare_weights(): pl.pallas_call(weights_kernel, grid=(span,), in_specs=[pl.BlockSpec((1,)...]
    ppermute x11, starting transfers between devices: 14.4 us -> 19.3 us  [shifted(): lax.ppermute(value, axis, [(i, (i + shift) % peers) for i in range(peers)])]
    pallas_call x1, Pallas kernels: 21.2 us -> 23.6 us  [run_sweeps(): pl.pallas_call(functools.partial(sweeps_kernel, sizes), in_specs=[vmem, v...]
    pallas_call x1, Pallas kernels: 8.98 us -> 10.8 us  [correlate(): pl.pallas_call(functools.partial(correlate_kernel, (rows, cols, span, pee...]
    ppermute x10 -> x8, starting transfers between devices: 12.5 us -> 12.8 us  [swap(): return lax.ppermute(value, axis, pairs)]
  transfers between devices with their start and end apart: 21 -> 19, of which waited for: 13 -> 8; matrix products, arithmetic and copies ran while one was open for 1% -> 2% of each run, Pallas kernels for 22% -> 20%
where the time goes in v1:
time: 119 us; the launch traced here: 118 us
  waiting for transfers between devices  42.9 us (36%)
  Pallas kernels  34.4 us (29%)
  starting transfers between devices  32.2 us (27%)
  local copies, waits for them, and re-layouts  4.5 us (4%)
  other arithmetic  3.46 us (3%)
    ppermute x8, waiting for transfers between devices, swap(): return lax.ppermute(value, axis, pairs)  27.5 us
    pallas_call x1, Pallas kernels, run_sweeps(): pl.pallas_call(functools.partial(sweeps_kernel, sizes), in_specs=[vmem, v...  23.6 us
    ppermute x11, starting transfers between devices, shifted(): lax.ppermute(value, axis, [(i, (i + shift) % peers) for i in range(peers)])  19.3 us
    ppermute x11, waiting for transfers between devices, shifted(): lax.ppermute(value, axis, [(i, (i + shift) % peers) for i in range(peers)])  15.5 us
    ppermute x8, starting transfers between devices, swap(): return lax.ppermute(value, axis, pairs)  12.8 us
    pallas_call x1, Pallas kernels, correlate(): pl.pallas_call(functools.partial(correlate_kernel, (rows, cols, span, pee...  10.8 us
  transfers between devices with their start and end apart: 19, of which 8 were waited for; matrix products, arithmetic and copies ran while one was open for 2% of the time, Pallas kernels for 20%

profile of v1, /device:TPU:0, one launch (start us, length us, event | category | flops | bytes accessed | tf_op | source)
XLA Modules:
  0.0 118.5 jit_solution(17222278135390940182)
XLA Ops:
  0.6 1.1 reshape.16
  1.8 1.1 reshape.17
  2.9 0.1 fusion.2
  2.9 0.7 collective-permute-start
  3.6 4.4 %collective-permute-start.1 = (f32[12,9,256]{2,1,0:T(8,128)S(1)}, f32[12,9,256]{2,1,0:T(8,128)S(1)}, u32[]{:S(2)}, u32[]{:S(2)}) collective-permute-start(f32[12,9,256]{2,1,0:T(8,128)S(1)} %get-tuple-element.51), channel_id=1, source_target_pairs={{0,1},{1,0},{2,3},{3,2},{4,5},{5,4},{6,7},{7,6},{8,9},{9,8},{10,11... | collective-permute-start | bytes 331784 | tf_op jit(solution)/shard_map/ppermute | solution.py:334
  8.0 0.0 collective-permute-done
  8.0 1.1 collective-permute-done.1
  9.1 0.1 pad_maximum_fusion.3
  9.2 0.7 collective-permute-start.2
  9.9 4.3 %collective-permute-start.3 = (f32[6,32,256]{2,1,0:T(8,128)S(1)}, f32[6,32,256]{2,1,0:T(8,128)S(1)}, u32[]{:S(2)}, u32[]{:S(2)}) collective-permute-start(f32[6,32,256]{2,1,0:T(8,128)S(1)} %get-tuple-element.47), channel_id=1, source_target_pairs={{0,4},{4,0},{8,12},{12,8},{16,20},{20,16},{24,28},{28,24},{1,5},{5... | collective-permute-start | bytes 589832 | tf_op jit(solution)/shard_map/ppermute | solution.py:334
  14.3 0.1 bitcast_bitcast_fusion.refs_8_
  14.4 1.6 %collective-permute-start.4 = (f32[2,12,24,128]{3,2,1,0:T(8,128)S(1)}, f32[2,12,24,128]{3,2,1,0:T(8,128)S(1)}, u32[]{:S(2)}, u32[]{:S(2)}) collective-permute-start(f32[2,12,24,128]{3,2,1,0:T(8,128)S(1)} %bitcast_bitcast_fusion.refs_8_), channel_id=1, source_target_pairs={{0,8},{4,12},{8,16},{12,20},{16,24},{20,28},{24,0},{28,4},{1,9},{5... | collective-permute-start | bytes 884744 | tf_op jit(solution)/shard_map/ppermute | solution.py:341
  16.0 1.1 collective-permute-start.5
  17.1 2.8 %collective-permute-start.6 = (f32[2,12,24,128]{3,2,1,0:T(8,128)S(1)}, f32[2,12,24,128]{3,2,1,0:T(8,128)S(1)}, u32[]{:S(2)}, u32[]{:S(2)}) collective-permute-start(f32[2,12,24,128]{3,2,1,0:T(8,128)S(1)} %bitcast_bitcast_fusion.refs_8_), channel_id=1, source_target_pairs={{0,24},{4,28},{8,0},{12,4},{16,8},{20,12},{24,16},{28,20},{1,25},{... | collective-permute-start | bytes 884744 | tf_op jit(solution)/shard_map/ppermute | solution.py:341
  19.9 0.0 collective-permute-done.2
  20.0 3.0 %collective-permute-done.3 = f32[6,32,256]{2,1,0:T(8,128)S(1)} collective-permute-done((f32[6,32,256]{2,1,0:T(8,128)S(1)}, f32[6,32,256]{2,1,0:T(8,128)S(1)}, u32[]{:S(2)}, u32[]{:S(2)}) %collective-permute-start.3) | collective-permute-done | bytes 196640 | tf_op jit(solution)/shard_map/ppermute | solution.py:334
  23.0 1.0 pad_maximum_fusion.2.source_ref
  24.0 23.6 %sweeps.1 = (f32[12,16,256]{2,1,0:T(8,128)}, f32[32,192]{1,0:T(8,128)}, f32[32,192]{1,0:T(8,128)}, f32[32,192]{1,0:T(8,128)}, f32[32,192]{1,0:T(8,128)}, /*index...) custom-call(f32[24,32,256]{2,1,0:T(8,128)} %pad_maximum_fusion.2.source_ref, ...), custom_call_target="tpu_custom_call" | custom-call | flops 12022972416 | bytes 6422528 | tf_op jit(solution)/shard_map/sweeps/pallas_call | solution.py:187
  47.6 0.0 collective-permute-done.4.refs_9_
  47.6 0.0 collective-permute-done.5.refs_10_
  47.7 0.0 collective-permute-done.6.refs_11_
  47.7 0.0 copy-start.2
  47.7 0.1 pad_maximum_fusion
  47.7 0.0 copy-start.4
  47.8 2.5 %collective-permute-start.15 = (f32[3,2,12,24,128]{4,3,2,1,0:T(8,128)S(1)}, f32[3,2,12,24,128]{4,3,2,1,0:T(8,128)S(1)}, u32[]{:S(2)}, u32[]{:S(2)}) collective-permute-start(f32[3,2,12,24,128]{4,3,2,1,0:T(8,128)S(1)} %pad_maximum_fusion), channel_id=1, source_target_pairs={{0,4},{4,0},{8,12},{12,8},{16,20},{20,16},{24,28},{28,24},{1,5},{5... | collective-permute-start | bytes 2654216 | tf_op jit(solution)/shard_map/ppermute | solution.py:334
  50.3 0.1 collective-permute-start.14
  50.4 3.0 %collective-permute-start.10 = (f32[32,192]{1,0:T(8,128)}, f32[32,192]{1,0:T(8,128)S(1)}, u32[]{:S(2)}, u32[]{:S(2)}) collective-permute-start(f32[32,192]{1,0:T(8,128)} %get-tuple-element.35), channel_id=1, source_target_pairs={{0,16},{4,20},{8,24},{12,28},{16,0},{20,4},{24,8},{28,12},{1,17},{... | collective-permute-start | bytes 73736 | tf_op jit(solution)/shard_map/ppermute | solution.py:341
  53.4 1.3 %collective-permute-start.11 = (f32[32,192]{1,0:T(8,128)}, f32[32,192]{1,0:T(8,128)S(1)}, u32[]{:S(2)}, u32[]{:S(2)}) collective-permute-start(f32[32,192]{1,0:T(8,128)} %get-tuple-element.36), channel_id=1, source_target_pairs={{0,20},{4,24},{8,28},{12,0},{16,4},{20,8},{24,12},{28,16},{1,21},{... | collective-permute-start | bytes 73736 | tf_op jit(solution)/shard_map/ppermute | solution.py:341
  54.7 2.2 %collective-permute-start.12 = (f32[32,192]{1,0:T(8,128)}, f32[32,192]{1,0:T(8,128)S(1)}, u32[]{:S(2)}, u32[]{:S(2)}) collective-permute-start(f32[32,192]{1,0:T(8,128)} %get-tuple-element.37), channel_id=1, source_target_pairs={{0,24},{4,28},{8,0},{12,4},{16,8},{20,12},{24,16},{28,20},{1,25},{... | collective-permute-start | bytes 73736 | tf_op jit(solution)/shard_map/ppermute | solution.py:341
  56.9 20.5 %collective-permute-done.14.refs_12_ = f32[2,12,24,128]{3,2,1,0:T(8,128)S(1)} collective-permute-done((f32[2,12,24,128]{3,2,1,0:T(8,128)S(1)}, f32[2,12,24,128]{3,2,1,0:T(8,128)S(1)}, u32[]{:S(2)}, u32[]{:S(2)}) %collective-permute-start.14) | collective-permute-done | bytes 294944 | tf_op jit(solution)/shard_map/ppermute | solution.py:334
  77.4 3.5 %collective-permute-start.13 = (f32[32,192]{1,0:T(8,128)}, f32[32,192]{1,0:T(8,128)S(1)}, u32[]{:S(2)}, u32[]{:S(2)}) collective-permute-start(f32[32,192]{1,0:T(8,128)} %get-tuple-element.38), channel_id=1, source_target_pairs={{0,28},{4,0},{8,4},{12,8},{16,12},{20,16},{24,20},{28,24},{1,29},{... | collective-permute-start | bytes 73736 | tf_op jit(solution)/shard_map/ppermute | solution.py:341
  80.9 0.0 collective-permute-done.10.refs_4_
  80.9 0.0 collective-permute-start.7
  80.9 0.0 collective-permute-done.11.refs_5_
  80.9 0.2 collective-permute-start.8
  81.1 0.0 collective-permute-done.12.refs_6_
  81.1 3.5 %collective-permute-start.9 = (f32[32,192]{1,0:T(8,128)}, f32[32,192]{1,0:T(8,128)S(1)}, u32[]{:S(2)}, u32[]{:S(2)}) collective-permute-start(f32[32,192]{1,0:T(8,128)} %get-tuple-element.34), channel_id=1, source_target_pairs={{0,12},{4,16},{8,20},{12,24},{16,28},{20,0},{24,4},{28,8},{1,13},{... | collective-permute-start | bytes 73736 | tf_op jit(solution)/shard_map/ppermute | solution.py:341
  84.6 0.0 collective-permute-done.13.refs_7_
  84.6 3.1 %collective-permute-done.7.refs_1_ = f32[32,192]{1,0:T(8,128)S(1)} collective-permute-done((f32[32,192]{1,0:T(8,128)}, f32[32,192]{1,0:T(8,128)S(1)}, u32[]{:S(2)}, u32[]{:S(2)}) %collective-permute-start.7) | collective-permute-done | bytes 24608 | tf_op jit(solution)/shard_map/ppermute | solution.py:341
  87.7 0.0 collective-permute-done.8.refs_2_
  87.7 1.0 collective-permute-done.9.refs_3_
  88.8 0.0 collective-permute-done.15.refs_13_
  88.8 0.0 copy-done.1
  88.8 0.0 copy-done.2
  88.8 0.0 copy-done.6
  88.8 0.0 copy-done.7
  88.8 0.0 copy-done.8
  88.8 0.0 copy-done.9
  88.8 0.0 copy-done.10
  88.9 0.0 copy-done.11
  88.9 0.5 copy-done.13
  89.4 0.9 copy-done.5
  90.3 10.8 %correlate.1 = (f32[7,7,2,8,128]{4,3,2,1,0:T(8,128)}, f32[7,7,2,8,128]{4,3,2,1,0:T(8,128)}) custom-call(f32[32,192]{1,0:T(8,128)} %get-tuple-element.31.refs_0_, f32[32,192]{1,0:T(8,128)} %copy-done.11, f32[32,192]{1,0:T(8,128)} %copy-done.12, f32[32,192]{1,0:T(8,128)} %copy-done.13, f32[32,192]{1,0:T(8,128)} %copy-done.7, f32[32,192]{1,0:T(8,128)} %copy-done.8, ...), custom_call_target="tpu_custom_call" | custom-call | flops 3699376128 | bytes 3162112 | tf_op jit(solution)/shard_map/correlate/pallas_call | solution.py:303
  101.1 0.1 collective-permute-start.16
  101.2 1.9 %collective-permute-done.16 = f32[7,7,2,8,128]{4,3,2,1,0:T(8,128)S(1)} collective-permute-done((f32[7,7,2,8,128]{4,3,2,1,0:T(8,128)}, f32[7,7,2,8,128]{4,3,2,1,0:T(8,128)S(1)}, u32[]{:S(2)}, u32[]{:S(2)}) %collective-permute-start.16) | collective-permute-done | bytes 401440 | tf_op jit(solution)/shard_map/ppermute | solution.py:334
  103.1 1.1 add.18
  104.2 0.1 collective-permute-start.17
  104.2 11.3 %collective-permute-done.17 = f32[7,7,2,8,128]{4,3,2,1,0:T(8,128)S(1)} collective-permute-done((f32[7,7,2,8,128]{4,3,2,1,0:T(8,128)S(1)}, f32[7,7,2,8,128]{4,3,2,1,0:T(8,128)S(1)}, u32[]{:S(2)}, u32[]{:S(2)}) %collective-permute-start.17) | collective-permute-done | bytes 401440 | tf_op jit(solution)/shard_map/ppermute | solution.py:341
  115.6 0.1 add.19
  115.6 0.1 collective-permute-start.18
  115.7 0.8 reshape.18
  116.5 0.9 collective-permute-done.18
  117.4 0.1 broadcast_select_fusion.1
  117.5 1.0 pad_maximum_fusion.1
  (26 shorter events, 0.2 us)
Async XLA Ops:
  2.9 5.0 %collective-permute-start = (f32[12,9,256]{2,1,0:T(8,128)S(1)}, f32[12,9,256]{2,1,0:T(8,128)S(1)}, u32[]{:S(2)}, u32[]{:S(2)}) collective-permute-start(f32[12,9,256]{2,1,0:T(8,128)S(1)} %get-tuple-element.50), channel_id=1, source_target_pairs={{1,2},{2,1},{5,6},{6,5},{9,10},{10,9},{13,14},{14,13},{17,18},{18,... | collective-permute-start | bytes 331784 | tf_op jit(solution)/shard_map/ppermute | solution.py:334
  3.6 5.4 %collective-permute-start.1 = (f32[12,9,256]{2,1,0:T(8,128)S(1)}, f32[12,9,256]{2,1,0:T(8,128)S(1)}, u32[]{:S(2)}, u32[]{:S(2)}) collective-permute-start(f32[12,9,256]{2,1,0:T(8,128)S(1)} %get-tuple-element.51), channel_id=1, source_target_pairs={{0,1},{1,0},{2,3},{3,2},{4,5},{5,4},{6,7},{7,6},{8,9},{9,8},{10,11... | collective-permute-start | bytes 331784 | tf_op jit(solution)/shard_map/ppermute | solution.py:334
  9.2 10.7 %collective-permute-start.2 = (f32[6,32,256]{2,1,0:T(8,128)S(1)}, f32[6,32,256]{2,1,0:T(8,128)S(1)}, u32[]{:S(2)}, u32[]{:S(2)}) collective-permute-start(f32[6,32,256]{2,1,0:T(8,128)S(1)} %get-tuple-element.46), channel_id=1, source_target_pairs={{4,8},{8,4},{12,16},{16,12},{20,24},{24,20},{5,9},{9,5},{13,17},{1... | collective-permute-start | bytes 589832 | tf_op jit(solution)/shard_map/ppermute | solution.py:334
  9.9 13.0 %collective-permute-start.3 = (f32[6,32,256]{2,1,0:T(8,128)S(1)}, f32[6,32,256]{2,1,0:T(8,128)S(1)}, u32[]{:S(2)}, u32[]{:S(2)}) collective-permute-start(f32[6,32,256]{2,1,0:T(8,128)S(1)} %get-tuple-element.47), channel_id=1, source_target_pairs={{0,4},{4,0},{8,12},{12,8},{16,20},{20,16},{24,28},{28,24},{1,5},{5... | collective-permute-start | bytes 589832 | tf_op jit(solution)/shard_map/ppermute | solution.py:334
  14.4 35.9 %copy-start.3 = (f32[2,12,24,128]{3,2,1,0:T(8,128)}, f32[2,12,24,128]{3,2,1,0:T(8,128)S(1)}, u32[]{:S(2)}) copy-start(f32[2,12,24,128]{3,2,1,0:T(8,128)S(1)} %bitcast_bitcast_fusion.refs_8_) | copy-start | bytes 884740
  14.4 33.2 %collective-permute-start.4 = (f32[2,12,24,128]{3,2,1,0:T(8,128)S(1)}, f32[2,12,24,128]{3,2,1,0:T(8,128)S(1)}, u32[]{:S(2)}, u32[]{:S(2)}) collective-permute-start(f32[2,12,24,128]{3,2,1,0:T(8,128)S(1)} %bitcast_bitcast_fusion.refs_8_), channel_id=1, source_target_pairs={{0,8},{4,12},{8,16},{12,20},{16,24},{20,28},{24,0},{28,4},{1,9},{5... | collective-permute-start | bytes 884744 | tf_op jit(solution)/shard_map/ppermute | solution.py:341
  16.0 31.6 %collective-permute-start.5 = (f32[2,12,24,128]{3,2,1,0:T(8,128)S(1)}, f32[2,12,24,128]{3,2,1,0:T(8,128)S(1)}, u32[]{:S(2)}, u32[]{:S(2)}) collective-permute-start(f32[2,12,24,128]{3,2,1,0:T(8,128)S(1)} %bitcast_bitcast_fusion.refs_8_), channel_id=1, source_target_pairs={{0,16},{4,20},{8,24},{12,28},{16,0},{20,4},{24,8},{28,12},{1,17},{... | collective-permute-start | bytes 884744 | tf_op jit(solution)/shard_map/ppermute | solution.py:341
  17.1 30.6 %collective-permute-start.6 = (f32[2,12,24,128]{3,2,1,0:T(8,128)S(1)}, f32[2,12,24,128]{3,2,1,0:T(8,128)S(1)}, u32[]{:S(2)}, u32[]{:S(2)}) collective-permute-start(f32[2,12,24,128]{3,2,1,0:T(8,128)S(1)} %bitcast_bitcast_fusion.refs_8_), channel_id=1, source_target_pairs={{0,24},{4,28},{8,0},{12,4},{16,8},{20,12},{24,16},{28,20},{1,25},{... | collective-permute-start | bytes 884744 | tf_op jit(solution)/shard_map/ppermute | solution.py:341
  47.6 41.2 %copy-start = (f32[2,12,24,128]{3,2,1,0:T(8,128)}, f32[2,12,24,128]{3,2,1,0:T(8,128)S(1)}, u32[]{:S(2)}) copy-start(f32[2,12,24,128]{3,2,1,0:T(8,128)S(1)} %collective-permute-done.4.refs_9_) | copy-start | bytes 884740
  47.6 41.1 %copy-start.1 = (f32[2,12,24,128]{3,2,1,0:T(8,128)}, f32[2,12,24,128]{3,2,1,0:T(8,128)S(1)}, u32[]{:S(2)}) copy-start(f32[2,12,24,128]{3,2,1,0:T(8,128)S(1)} %collective-permute-done.5.refs_10_) | copy-start | bytes 884740
  47.7 41.1 %copy-start.2 = (f32[2,12,24,128]{3,2,1,0:T(8,128)}, f32[2,12,24,128]{3,2,1,0:T(8,128)S(1)}, u32[]{:S(2)}) copy-start(f32[2,12,24,128]{3,2,1,0:T(8,128)S(1)} %collective-permute-done.6.refs_11_) | copy-start | bytes 884740
  47.7 68.0 %copy-start.4 = (f32[12,16,256]{2,1,0:T(8,128)S(1)}, f32[12,16,256]{2,1,0:T(8,128)}, u32[]{:S(2)}) copy-start(f32[12,16,256]{2,1,0:T(8,128)} %get-tuple-element.22) | copy-start | bytes 589828
  47.8 41.0 %collective-permute-start.15 = (f32[3,2,12,24,128]{4,3,2,1,0:T(8,128)S(1)}, f32[3,2,12,24,128]{4,3,2,1,0:T(8,128)S(1)}, u32[]{:S(2)}, u32[]{:S(2)}) collective-permute-start(f32[3,2,12,24,128]{4,3,2,1,0:T(8,128)S(1)} %pad_maximum_fusion), channel_id=1, source_target_pairs={{0,4},{4,0},{8,12},{12,8},{16,20},{20,16},{24,28},{28,24},{1,5},{5... | collective-permute-start | bytes 2654216 | tf_op jit(solution)/shard_map/ppermute | solution.py:334
  50.3 27.0 %collective-permute-start.14 = (f32[2,12,24,128]{3,2,1,0:T(8,128)S(1)}, f32[2,12,24,128]{3,2,1,0:T(8,128)S(1)}, u32[]{:S(2)}, u32[]{:S(2)}) collective-permute-start(f32[2,12,24,128]{3,2,1,0:T(8,128)S(1)} %bitcast_bitcast_fusion.refs_8_), channel_id=1, source_target_pairs={{0,4},{4,0},{8,12},{12,8},{16,20},{20,16},{24,28},{28,24},{1,5},{5... | collective-permute-start | bytes 884744 | tf_op jit(solution)/shard_map/ppermute | solution.py:334
  50.4 30.5 %collective-permute-start.10 = (f32[32,192]{1,0:T(8,128)}, f32[32,192]{1,0:T(8,128)S(1)}, u32[]{:S(2)}, u32[]{:S(2)}) collective-permute-start(f32[32,192]{1,0:T(8,128)} %get-tuple-element.35), channel_id=1, source_target_pairs={{0,16},{4,20},{8,24},{12,28},{16,0},{20,4},{24,8},{28,12},{1,17},{... | collective-permute-start | bytes 73736 | tf_op jit(solution)/shard_map/ppermute | solution.py:341
  53.4 27.5 %collective-permute-start.11 = (f32[32,192]{1,0:T(8,128)}, f32[32,192]{1,0:T(8,128)S(1)}, u32[]{:S(2)}, u32[]{:S(2)}) collective-permute-start(f32[32,192]{1,0:T(8,128)} %get-tuple-element.36), channel_id=1, source_target_pairs={{0,20},{4,24},{8,28},{12,0},{16,4},{20,8},{24,12},{28,16},{1,21},{... | collective-permute-start | bytes 73736 | tf_op jit(solution)/shard_map/ppermute | solution.py:341
  54.7 26.4 %collective-permute-start.12 = (f32[32,192]{1,0:T(8,128)}, f32[32,192]{1,0:T(8,128)S(1)}, u32[]{:S(2)}, u32[]{:S(2)}) collective-permute-start(f32[32,192]{1,0:T(8,128)} %get-tuple-element.37), channel_id=1, source_target_pairs={{0,24},{4,28},{8,0},{12,4},{16,8},{20,12},{24,16},{28,20},{1,25},{... | collective-permute-start | bytes 73736 | tf_op jit(solution)/shard_map/ppermute | solution.py:341
  77.4 11.5 %copy-start.6 = (f32[2,12,24,128]{3,2,1,0:T(8,128)}, f32[2,12,24,128]{3,2,1,0:T(8,128)S(1)}, u32[]{:S(2)}) copy-start(f32[2,12,24,128]{3,2,1,0:T(8,128)S(1)} %collective-permute-done.14.refs_12_) | copy-start | bytes 884740
  77.4 7.3 %collective-permute-start.13 = (f32[32,192]{1,0:T(8,128)}, f32[32,192]{1,0:T(8,128)S(1)}, u32[]{:S(2)}, u32[]{:S(2)}) collective-permute-start(f32[32,192]{1,0:T(8,128)} %get-tuple-element.38), channel_id=1, source_target_pairs={{0,28},{4,0},{8,4},{12,8},{16,12},{20,16},{24,20},{28,24},{1,29},{... | collective-permute-start | bytes 73736 | tf_op jit(solution)/shard_map/ppermute | solution.py:341
  80.9 7.9 %copy-start.7 = (f32[32,192]{1,0:T(8,128)}, f32[32,192]{1,0:T(8,128)S(1)}, u32[]{:S(2)}) copy-start(f32[32,192]{1,0:T(8,128)S(1)} %collective-permute-done.10.refs_4_) | copy-start | bytes 73732
  80.9 6.8 %collective-permute-start.7 = (f32[32,192]{1,0:T(8,128)}, f32[32,192]{1,0:T(8,128)S(1)}, u32[]{:S(2)}, u32[]{:S(2)}) collective-permute-start(f32[32,192]{1,0:T(8,128)} %get-tuple-element.32), channel_id=1, source_target_pairs={{0,4},{4,8},{8,12},{12,16},{16,20},{20,24},{24,28},{28,0},{1,5},{5... | collective-permute-start | bytes 73736 | tf_op jit(solution)/shard_map/ppermute | solution.py:341
  80.9 7.9 %copy-start.8 = (f32[32,192]{1,0:T(8,128)}, f32[32,192]{1,0:T(8,128)S(1)}, u32[]{:S(2)}) copy-start(f32[32,192]{1,0:T(8,128)S(1)} %collective-permute-done.11.refs_5_) | copy-start | bytes 73732
  80.9 6.8 %collective-permute-start.8 = (f32[32,192]{1,0:T(8,128)}, f32[32,192]{1,0:T(8,128)S(1)}, u32[]{:S(2)}, u32[]{:S(2)}) collective-permute-start(f32[32,192]{1,0:T(8,128)} %get-tuple-element.33), channel_id=1, source_target_pairs={{0,8},{4,12},{8,16},{12,20},{16,24},{20,28},{24,0},{28,4},{1,9},{5... | collective-permute-start | bytes 73736 | tf_op jit(solution)/shard_map/ppermute | solution.py:341
  81.1 7.7 %copy-start.9 = (f32[32,192]{1,0:T(8,128)}, f32[32,192]{1,0:T(8,128)S(1)}, u32[]{:S(2)}) copy-start(f32[32,192]{1,0:T(8,128)S(1)} %collective-permute-done.12.refs_6_) | copy-start | bytes 73732
  81.1 7.7 %collective-permute-start.9 = (f32[32,192]{1,0:T(8,128)}, f32[32,192]{1,0:T(8,128)S(1)}, u32[]{:S(2)}, u32[]{:S(2)}) collective-permute-start(f32[32,192]{1,0:T(8,128)} %get-tuple-element.34), channel_id=1, source_target_pairs={{0,12},{4,16},{8,20},{12,24},{16,28},{20,0},{24,4},{28,8},{1,13},{... | collective-permute-start | bytes 73736 | tf_op jit(solution)/shard_map/ppermute | solution.py:341
  84.6 4.2 %copy-start.10 = (f32[32,192]{1,0:T(8,128)}, f32[32,192]{1,0:T(8,128)S(1)}, u32[]{:S(2)}) copy-start(f32[32,192]{1,0:T(8,128)S(1)} %collective-permute-done.13.refs_7_) | copy-start | bytes 73732
  87.7 1.1 copy-start.11
  87.7 1.1 copy-start.12
  88.8 0.6 copy-start.13
  89.4 0.9 copy-start.5
  101.1 2.0 %collective-permute-start.16 = (f32[7,7,2,8,128]{4,3,2,1,0:T(8,128)}, f32[7,7,2,8,128]{4,3,2,1,0:T(8,128)S(1)}, u32[]{:S(2)}, u32[]{:S(2)}) collective-permute-start(f32[7,7,2,8,128]{4,3,2,1,0:T(8,128)} %get-tuple-element.41), channel_id=1, source_target_pairs={{0,1},{1,0},{2,3},{3,2},{4,5},{5,4},{6,7},{7,6},{8,9},{9,8},{10,11... | collective-permute-start | bytes 1204232 | tf_op jit(solution)/shard_map/ppermute | solution.py:334
  104.2 11.4 %collective-permute-start.17 = (f32[7,7,2,8,128]{4,3,2,1,0:T(8,128)S(1)}, f32[7,7,2,8,128]{4,3,2,1,0:T(8,128)S(1)}, u32[]{:S(2)}, u32[]{:S(2)}) collective-permute-start(f32[7,7,2,8,128]{4,3,2,1,0:T(8,128)S(1)} %add.18), channel_id=1, source_target_pairs={{0,2},{1,3},{2,0},{3,1},{4,6},{5,7},{6,4},{7,5},{8,10},{9,11},{10,... | collective-permute-start | bytes 1204232 | tf_op jit(solution)/shard_map/ppermute | solution.py:341
  115.6 1.8 %collective-permute-start.18 = (f32[7,7,2,8,128]{4,3,2,1,0:T(8,128)S(1)}, f32[7,7,2,8,128]{4,3,2,1,0:T(8,128)S(1)}, u32[]{:S(2)}, u32[]{:S(2)}) collective-permute-start(f32[7,7,2,8,128]{4,3,2,1,0:T(8,128)S(1)} %add.19), channel_id=1, source_target_pairs={{0,1},{1,0},{2,3},{3,2},{4,5},{5,4},{6,7},{7,6},{8,9},{9,8},{10,11... | collective-permute-start | bytes 1204232 | tf_op jit(solution)/shard_map/ppermute | solution.py:334

commit v2 on v1

--- a/solution.py
+++ b/solution.py
@@ -62,8 +62,8 @@
     *rest,
 ):
     rows, cols, span, peers, pitch, wide = sizes
-    sends = rest[:peers]
-    (first, second, x1_high, x1_low, x2_high, x2_low, acc, turned, raw, w_high, w_low, e_high, e_low, sems) = rest[peers:]
+    sends = rest[: peers // 2]
+    (first, second, x1_high, x1_low, x2_high, x2_low, acc, turned, raw, w_high, w_low, e_high, e_low, sems) = rest[peers // 2 :]
     reach = span // 2
     mid_rows, mid_cols = rows + 2 * reach, cols + 2 * reach
     full_rows = rows + 4 * reach
@@ -164,11 +164,13 @@
 
     share = width // peers
     me = lax.axis_index("row")
-    for k in range(peers):
-        peer = lax.rem(me + k, peers)
-        for part in range(2):
-            at = pl.multiple_of(part * width + peer * share, share)
-            sends[k][part * share : (part + 1) * share, :] = turned[pl.ds(at, share), :]
+    twin = me + 1 - 2 * lax.rem(me, 2)
+    for k in range(peers // 2):
+        for n, target in enumerate((me, twin)):
+            peer = lax.rem(target + 2 * k, peers)
+            for part in range(2):
+                at = pl.multiple_of(part * width + peer * share, share)
+                sends[k][n, part * share : (part + 1) * share, :] = turned[pl.ds(at, share), :]
 
 
 def run_sweeps(source, inverse, lag_blocks, rows, cols, peers):
@@ -182,13 +184,13 @@
     sizes = (rows, cols, span, peers, pitch, wide)
     vmem = pl.BlockSpec(memory_space=pltpu.VMEM)
     hbm = pl.BlockSpec(memory_space=pl.ANY)
-    send = jax.ShapeDtypeStruct((2 * share, rows * cols), f32)
+    send = jax.ShapeDtypeStruct((2, 2 * share, rows * cols), f32)
     flops = 6 * span * span * lanes * lanes * (mid_rows * pitch + rows * cols)
     out = pl.pallas_call(
         functools.partial(sweeps_kernel, sizes),
         in_specs=[vmem, vmem, hbm],
-        out_specs=[vmem] * (1 + peers),
-        out_shape=[jax.ShapeDtypeStruct((rows, cols, lanes), f32)] + [send] * peers,
+        out_specs=[vmem] * (1 + peers // 2),
+        out_shape=[jax.ShapeDtypeStruct((rows, cols, lanes), f32)] + [send] * (peers // 2),
         scratch_shapes=[
             pltpu.VMEM((full_rows + 1, wide, lanes), f32),
             pltpu.VMEM((mid_rows, pitch, lanes), f32),
@@ -216,32 +218,31 @@
 
 def correlate_kernel(sizes, factor, *refs):
     rows, cols, span, peers = sizes
-    shares = refs[:peers]
-    piece_refs = refs[peers : peers + peers // 2]
-    own_twin_ref, twins_ref = refs[peers + peers // 2 : peers + peers // 2 + 2]
-    refs = refs[peers + peers // 2 + 2 :]
-    mine_ref, other_ref = refs[:2]
-    placed, flat, l_high, l_low, stage, s_high, s_low, sems = refs[2:]
+    half_peers = peers // 2
+    shares, piece_refs = refs[:half_peers], refs[half_peers:peers]
+    twin_shares_ref, own_twin_ref, twins_ref, mine_ref, other_ref = refs[peers : peers + 5]
+    placed, flat, l_high, l_low, stage, s_high, s_low, sems = refs[peers + 5 :]
     reach = span // 2
     own = rows * cols
-    double = shares[0].shape[0]
+    double = shares[0].shape[1]
     share = double // 2
     width = stage.shape[-1]
     me = lax.axis_index("row")
     even = me - lax.rem(me, 2)
     odd = 1 - lax.rem(me, 2)
 
-    copies = []
-    for k in range(peers // 2):
+    def tiles(k):
         base = lax.rem(even - 2 * k + peers, peers)
+        return base + 1 - odd, base + odd
+
+    for k in range(half_peers):
         twin = own_twin_ref if k == 0 else twins_ref.at[k - 1]
-        copies.append(pltpu.make_async_copy(piece_refs[k], stage.at[base + 1 - odd], sems.at[0, k]))
-        copies.append(pltpu.make_async_copy(twin, stage.at[base + odd], sems.at[1, k]))
-    for copy in copies:
-        copy.start()
-
-    for k in range(peers):
-        placed[lax.rem(me - k + peers, peers)] = shares[k][...]
+        for n, (source, tile) in enumerate(zip((piece_refs[k], twin), tiles(k))):
+            pltpu.make_async_copy(source, stage.at[tile], sems.at[n, k]).start()
+        first, second = tiles(k)
+        placed[first] = shares[k][0]
+        placed[second] = twin_shares_ref[k]
+
     total = peers * own
     side = round_up(reach * cols, 128)
     flat[:, :side] = jnp.zeros((double, side), f32)
@@ -258,11 +259,13 @@
             l_high[a, part] = high
             l_low[a, part] = low
 
-    for copy in copies:
-        copy.wait()
-
     @pl.loop(0, peers)
-    def _(tile):
+    def _(at):
+        n, k = lax.rem(at, 2), at // 2
+        first, second = tiles(k)
+        tile = jnp.where(n == 0, first, second)
+        pltpu.make_async_copy(own_twin_ref, stage.at[tile], sems.at[n, k]).wait()
+
         @pl.loop(0, rows)
         def _(i):
             to = pl.ds(pl.multiple_of(tile * own + i * cols, cols), cols)
@@ -289,10 +292,10 @@
                 other_ref[a, b, c] = jnp.where(upper, value[:half], value[half:])
 
 
-def correlate(shares, pieces, own_twin, twins, rows, cols, span, factor):
-    peers = len(shares)
+def correlate(shares, twin_shares, pieces, own_twin, twins, rows, cols, span, factor):
+    peers = 2 * len(shares)
     reach = span // 2
-    double, own = shares[0].shape
+    double, own = twin_shares.shape[1:]
     share = double // 2
     width = own_twin.shape[-1]
     total = peers * own
@@ -302,7 +305,7 @@
     out = jax.ShapeDtypeStruct((span, span, 2, share // 2, width), f32)
     return pl.pallas_call(
         functools.partial(correlate_kernel, (rows, cols, span, peers), factor),
-        in_specs=[vmem] * peers + [hbm] * (peers // 2 + 2),
+        in_specs=[vmem] * (peers // 2) + [hbm] * (peers // 2) + [vmem, hbm, hbm],
         out_specs=[vmem, vmem],
         out_shape=[out, out],
         scratch_shapes=[
@@ -322,7 +325,7 @@
         ),
         compiler_params=pltpu.CompilerParams(vmem_limit_bytes=VMEM_LIMIT),
         name="correlate",
-    )(*shares, *pieces, own_twin, twins)
+    )(*shares, *pieces, twin_shares, own_twin, twins)
 
 
 def swap(value, axis, first):
@@ -355,32 +358,34 @@
     halo = SWEEPS * reach
     lanes = parts * width
     peers = lax.axis_size("row")
-    source = adjoint_source.reshape(rows, cols, lanes)
-    saved = saved_currents.reshape(rows, cols, lanes)
-
-    initial = jnp.concatenate([source[:, :halo], saved[:, :reach]], axis=1)
-    last = jnp.concatenate([source[:, cols - halo :], saved[:, cols - reach :]], axis=1)
+
+    initial = jnp.concatenate([adjoint_source[:, :halo], saved_currents[:, :reach]], axis=1)
+    last = jnp.concatenate(
+        [adjoint_source[:, cols - halo :], saved_currents[:, cols - reach :]], axis=1
+    )
     before, after = edges(initial, last, "col")
-    wide = round_up(cols + 2 * halo, 8)
-    filler = jnp.zeros((rows, wide - cols - 2 * halo, lanes), f32)
-    source = jnp.concatenate([before[:, :halo], source, after[:, :halo], filler], axis=1)
-    saved = jnp.concatenate([before[:, halo:], saved, after[:, halo:]], axis=1)
+    source = jnp.concatenate([before[:, :halo], adjoint_source, after[:, :halo]], axis=1)
+    source = source.reshape(rows, cols + 2 * halo, lanes)
+    saved = jnp.concatenate([before[:, halo:], saved_currents, after[:, halo:]], axis=1)
     before, after = edges(source[:halo], source[rows - halo :], "row")
     source = jnp.concatenate([before, source, after], axis=0)
-
-    saved = jnp.pad(saved, ((0, 0), (0, round_up(cols + 2 * reach, 8) - cols - 2 * reach), (0, 0)))
-    saved = saved.reshape(rows, -1, parts, width).transpose(2, 0, 1, 3)
+    wide = round_up(cols + 2 * halo, 8)
+    source = jnp.pad(source, ((0, 0), (0, wide - cols - 2 * halo), (0, 0)))
+
+    pitch = round_up(cols + 2 * reach, 8)
+    saved = jnp.pad(saved.transpose(2, 0, 1, 3), ((0, 0), (0, 0), (0, pitch - cols - 2 * reach), (0, 0)))
     pieces = [shifted(saved, "row", k) for k in range(0, peers, 2)]
     own_twin = swap(saved, "row", 0)
 
     adjoint, sends = run_sweeps(source, element_inverse, lag_blocks, rows, cols, peers)
-    twins, sends = lax.optimization_barrier((jnp.stack(pieces[1:]), sends))
+    twins, own_twin, sends = lax.optimization_barrier((jnp.stack(pieces[1:]), own_twin, sends))
     twins = swap(twins, "row", 0)
-    shares = [shifted(send, "row", k) for k, send in enumerate(sends)]
+    shares = [shifted(send, "row", 2 * k) for k, send in enumerate(sends)]
+    twin_shares = swap(jnp.stack([received[1] for received in shares]), "row", 0)
 
     elements = rows * peers * cols * lax.axis_size("col")
     factor = -1.0 / math.sqrt(elements)
-    mine, other = correlate(shares, pieces, own_twin, twins, rows, cols, span, factor)
+    mine, other = correlate(shares, twin_shares, pieces, own_twin, twins, rows, cols, span, factor)
     mine = mine + swap(other, "col", 0)
     total = mine
     for k in range(2, lax.axis_size("col"), 2):

time: 119 us -> 104 us (0.87)
  waiting for transfers between devices: 42.9 us -> 33.2 us
  starting transfers between devices: 32.2 us -> 25.1 us
  local copies, waits for them, and re-layouts: 4.5 us -> 6.72 us
    ppermute x8 -> x9, waiting for transfers between devices: 27.5 us -> 19.1 us  [swap(): return lax.ppermute(value, axis, pairs)]
    ppermute x11 -> x7, starting transfers between devices: 19.3 us -> 11.2 us  [shifted(): lax.ppermute(value, axis, [(i, (i + shift) % peers) for i in range(peers)])]
    unnamed x28 -> x27, local copies, waits for them, and re-layouts: 1.46 us -> 3.53 us
    reshape x2 -> x1, local copies, waits for them, and re-layouts: 2.17 us -> 0.28 us  [on_device(): source = source.reshape(rows, cols + 2 * halo, lanes)]
    slice x4 -> x8, local copies, waits for them, and re-layouts: 0.07 us -> 1.76 us  [the longest x1 0.94 us: on_device(): adjoint_source[:, :halo]]
    ppermute x11 -> x7, waiting for transfers between devices: 15.5 us -> 14.1 us  [shifted(): lax.ppermute(value, axis, [(i, (i + shift) % peers) for i in range(peers)])]
    ppermute x8 -> x9, starting transfers between devices: 12.8 us -> 14 us  [swap(): return lax.ppermute(value, axis, pairs)]
  transfers between devices with their start and end apart: 19 -> 16, of which waited for: 8 -> 8; matrix products, arithmetic and copies ran while one was open for 2% -> 3% of each run, Pallas kernels for 20% -> 23%
where the time goes in v2:
time: 104 us
  Pallas kernels  34 us (33%)
  waiting for transfers between devices  33.2 us (32%)
  starting transfers between devices  25.1 us (24%)
  local copies, waits for them, and re-layouts  6.72 us (6%)
  other arithmetic  3.48 us (3%)
  between operations  1.04 us (1%)
    pallas_call x1, Pallas kernels, run_sweeps(): pl.pallas_call(functools.partial(sweeps_kernel, sizes), in_specs=[vmem, v...  23.6 us
    ppermute x9, waiting for transfers between devices, swap(): return lax.ppermute(value, axis, pairs)  19.1 us
    ppermute x7, waiting for transfers between devices, shifted(): lax.ppermute(value, axis, [(i, (i + shift) % peers) for i in range(peers)])  14.1 us
    ppermute x9, starting transfers between devices, swap(): return lax.ppermute(value, axis, pairs)  14 us
    ppermute x7, starting transfers between devices, shifted(): lax.ppermute(value, axis, [(i, (i + shift) % peers) for i in range(peers)])  11.2 us
    pallas_call x1, Pallas kernels, correlate(): pl.pallas_call(functools.partial(correlate_kernel, (rows, cols, span, pee...  10.4 us
    unnamed x27, local copies, waits for them, and re-layouts  3.53 us
  transfers between devices with their start and end apart: 16, of which 8 were waited for; matrix products, arithmetic and copies ran while one was open for 3% of the time, Pallas kernels for 23%

profile of v2, /device:TPU:0, one launch (start us, length us, event | category | flops | bytes accessed | tf_op | source)
XLA Modules:
  0.0 103.6 jit_solution(1052399425134574192)
XLA Ops:
  0.6 0.9 copy.7
  1.6 0.9 fusion.2
  2.6 0.1 fusion
  2.7 0.7 collective-permute-start
  3.4 4.4 %collective-permute-start.1 = (f32[12,9,2,128]{3,1,0,2:T(8,128)S(1)}, f32[12,9,2,128]{3,1,0,2:T(8,128)S(1)}, u32[]{:S(2)}, u32[]{:S(2)}) collective-permute-start(f32[12,9,2,128]{3,1,0,2:T(8,128)S(1)} %get-tuple-element.36), channel_id=1, source_target_pairs={{0,1},{1,0},{2,3},{3,2},{4,5},{5,4},{6,7},{7,6},{8,9},{9,8},{10,11... | collective-permute-start | bytes 331784 | tf_op jit(solution)/shard_map/ppermute | solution.py:337
  7.7 0.0 collective-permute-done
  7.7 1.1 %collective-permute-done.1 = f32[12,9,2,128]{3,1,0,2:T(8,128)S(1)} collective-permute-done((f32[12,9,2,128]{3,1,0,2:T(8,128)S(1)}, f32[12,9,2,128]{3,1,0,2:T(8,128)S(1)}, u32[]{:S(2)}, u32[]{:S(2)}) %collective-permute-start.1) | collective-permute-done | bytes 110624 | tf_op jit(solution)/shard_map/ppermute | solution.py:337
  8.8 0.1 copy_dynamic-update-slice_fusion.1
  8.9 1.0 constant_dynamic-update-slice_fusion
  9.9 0.1 copy_dynamic-update-slice_fusion
  10.0 0.1 broadcast_select_fusion.3
  10.1 0.1 select_n.83
  10.2 0.7 collective-permute-start.2
  10.9 0.1 select_n.85
  11.1 4.3 %collective-permute-start.3 = (f32[6,28,256]{2,1,0:T(8,128)S(1)}, f32[6,28,256]{2,1,0:T(8,128)S(1)}, u32[]{:S(2)}, u32[]{:S(2)}) collective-permute-start(f32[6,28,256]{2,1,0:T(8,128)S(1)} %select_n.85), channel_id=1, source_target_pairs={{0,4},{4,0},{8,12},{12,8},{16,20},{20,16},{24,28},{28,24},{1,5},{5... | collective-permute-start | bytes 516104 | tf_op jit(solution)/shard_map/ppermute | solution.py:337
  15.5 0.0 copy-start.3
  15.5 1.6 %collective-permute-start.4 = (f32[2,12,24,128]{3,2,1,0:T(8,128)S(1)}, f32[2,12,24,128]{3,2,1,0:T(8,128)S(1)}, u32[]{:S(2)}, u32[]{:S(2)}) collective-permute-start(f32[2,12,24,128]{3,2,1,0:T(8,128)S(1)} %pad.9.refs_4_), channel_id=1, source_target_pairs={{0,8},{4,12},{8,16},{12,20},{16,24},{20,28},{24,0},{28,4},{1,9},{5... | collective-permute-start | bytes 884744 | tf_op jit(solution)/shard_map/ppermute | solution.py:344
  17.2 1.1 %collective-permute-start.5 = (f32[2,12,24,128]{3,2,1,0:T(8,128)S(1)}, f32[2,12,24,128]{3,2,1,0:T(8,128)S(1)}, u32[]{:S(2)}, u32[]{:S(2)}) collective-permute-start(f32[2,12,24,128]{3,2,1,0:T(8,128)S(1)} %pad.9.refs_4_), channel_id=1, source_target_pairs={{0,16},{4,20},{8,24},{12,28},{16,0},{20,4},{24,8},{28,12},{1,17},{... | collective-permute-start | bytes 884744 | tf_op jit(solution)/shard_map/ppermute | solution.py:344
  18.2 2.8 %collective-permute-start.6 = (f32[2,12,24,128]{3,2,1,0:T(8,128)S(1)}, f32[2,12,24,128]{3,2,1,0:T(8,128)S(1)}, u32[]{:S(2)}, u32[]{:S(2)}) collective-permute-start(f32[2,12,24,128]{3,2,1,0:T(8,128)S(1)} %pad.9.refs_4_), channel_id=1, source_target_pairs={{0,24},{4,28},{8,0},{12,4},{16,8},{20,12},{24,16},{28,20},{1,25},{... | collective-permute-start | bytes 884744 | tf_op jit(solution)/shard_map/ppermute | solution.py:344
  21.1 0.3 reshape.16
  21.4 0.0 collective-permute-done.2
  21.4 0.5 collective-permute-start.7
  21.8 2.1 %collective-permute-done.3 = f32[6,28,256]{2,1,0:T(8,128)S(1)} collective-permute-done((f32[6,28,256]{2,1,0:T(8,128)S(1)}, f32[6,28,256]{2,1,0:T(8,128)S(1)}, u32[]{:S(2)}, u32[]{:S(2)}) %collective-permute-start.3) | collective-permute-done | bytes 172064 | tf_op jit(solution)/shard_map/ppermute | solution.py:337
  24.0 1.0 select_maximum_fusion.source_ref
  25.0 23.6 %sweeps.1 = (f32[12,16,256]{2,1,0:T(8,128)}, f32[2,32,192]{2,1,0:T(8,128)}, f32[2,32,192]{2,1,0:T(8,128)}, f32[2,32,192]{2,1,0:T(8,128)}, f32[2,32,192]{2,1,0:T(8,128)}) custom-call(f32[24,32,256]{2,1,0:T(8,128)} %select_maximum_fusion.source_ref, f32[2,128,128]{2,1,0:T(8,128)} %inverse_ref.1, f32[7,7,2,128,128]{4,3,2,1,0:T(8,128)} %blocks_hbm.1), custom_call_target="tpu_custom_call" | custom-call | flops 12022972416 | bytes 6422528 | tf_op jit(solution)/shard_map/sweeps/pallas_call | solution.py:189
  48.6 0.0 copy-done.3
  48.6 0.0 collective-permute-done.4.refs_5_
  48.6 0.0 collective-permute-done.5.refs_6_
  48.6 0.0 collective-permute-done.6.refs_7_
  48.7 0.1 pad_maximum_fusion
  48.7 0.0 collective-permute-done.7.refs_9_
  48.8 2.5 %collective-permute-start.12 = (f32[3,2,12,24,128]{4,3,2,1,0:T(8,128)S(1)}, f32[3,2,12,24,128]{4,3,2,1,0:T(8,128)S(1)}, u32[]{:S(2)}, u32[]{:S(2)}) collective-permute-start(f32[3,2,12,24,128]{4,3,2,1,0:T(8,128)S(1)} %pad_maximum_fusion), channel_id=1, source_target_pairs={{0,4},{4,0},{8,12},{12,8},{16,20},{20,16},{24,28},{28,24},{1,5},{5... | collective-permute-start | bytes 2654216 | tf_op jit(solution)/shard_map/ppermute | solution.py:337
  51.3 1.6 %collective-permute-start.8 = (f32[2,32,192]{2,1,0:T(8,128)}, f32[2,32,192]{2,1,0:T(8,128)S(1)}, u32[]{:S(2)}, u32[]{:S(2)}) collective-permute-start(f32[2,32,192]{2,1,0:T(8,128)} %get-tuple-element.21), channel_id=1, source_target_pairs={{0,8},{4,12},{8,16},{12,20},{16,24},{20,28},{24,0},{28,4},{1,9},{5... | collective-permute-start | bytes 147464 | tf_op jit(solution)/shard_map/ppermute | solution.py:344
  52.9 1.1 %collective-permute-start.9 = (f32[2,32,192]{2,1,0:T(8,128)}, f32[2,32,192]{2,1,0:T(8,128)S(1)}, u32[]{:S(2)}, u32[]{:S(2)}) collective-permute-start(f32[2,32,192]{2,1,0:T(8,128)} %get-tuple-element.22), channel_id=1, source_target_pairs={{0,16},{4,20},{8,24},{12,28},{16,0},{20,4},{24,8},{28,12},{1,17},{... | collective-permute-start | bytes 147464 | tf_op jit(solution)/shard_map/ppermute | solution.py:344
  54.0 2.8 %collective-permute-start.10 = (f32[2,32,192]{2,1,0:T(8,128)}, f32[2,32,192]{2,1,0:T(8,128)S(1)}, u32[]{:S(2)}, u32[]{:S(2)}) collective-permute-start(f32[2,32,192]{2,1,0:T(8,128)} %get-tuple-element.23), channel_id=1, source_target_pairs={{0,24},{4,28},{8,0},{12,4},{16,8},{20,12},{24,16},{28,20},{1,25},{... | collective-permute-start | bytes 147464 | tf_op jit(solution)/shard_map/ppermute | solution.py:344
  56.8 0.8 slice.54
  57.6 0.3 collective-permute-done.8.refs_1_
  57.9 2.5 %collective-permute-done.9.refs_2_ = f32[2,32,192]{2,1,0:T(8,128)S(1)} collective-permute-done((f32[2,32,192]{2,1,0:T(8,128)}, f32[2,32,192]{2,1,0:T(8,128)S(1)}, u32[]{:S(2)}, u32[]{:S(2)}) %collective-permute-start.9) | collective-permute-done | bytes 49184 | tf_op jit(solution)/shard_map/ppermute | solution.py:344
  60.4 0.0 collective-permute-done.10.refs_3_
  60.4 0.0 copy-start.4
  60.4 0.8 collective-permute-start.11
  61.2 13.0 %collective-permute-done.11.refs_8_ = f32[4,32,192]{2,1,0:T(8,128)S(1)} collective-permute-done((f32[4,32,192]{2,1,0:T(8,128)S(1)}, f32[4,32,192]{2,1,0:T(8,128)S(1)}, u32[]{:S(2)}, u32[]{:S(2)}) %collective-permute-start.11) | collective-permute-done | bytes 98336 | tf_op jit(solution)/shard_map/ppermute | solution.py:337
  74.2 0.0 collective-permute-done.12.refs_10_
  74.2 0.0 copy-done.1
  74.2 0.0 copy-done.2
  74.3 0.0 copy-done.9
  74.3 0.0 copy-done.5
  74.3 0.0 copy-done.6
  74.3 0.0 copy-done.7
  74.3 0.6 copy-done.10
  74.9 0.9 copy-done.8
  75.8 10.4 %correlate.1 = (f32[7,7,2,8,128]{4,3,2,1,0:T(8,128)}, f32[7,7,2,8,128]{4,3,2,1,0:T(8,128)}) custom-call(f32[2,32,192]{2,1,0:T(8,128)} %get-tuple-element.20.refs_0_, f32[2,32,192]{2,1,0:T(8,128)} %copy-done.5, f32[2,32,192]{2,1,0:T(8,128)} %copy-done.6, f32[2,32,192]{2,1,0:T(8,128)} %copy-done.7, f32[2,12,24,128]{3,2,1,0:T(8,128)} %copy-done.3, ...), custom_call_target="tpu_custom_call" | custom-call | flops 3699376128 | bytes 3162112 | tf_op jit(solution)/shard_map/correlate/pallas_call | solution.py:306
  86.2 0.1 collective-permute-start.13
  86.3 1.9 %collective-permute-done.13 = f32[7,7,2,8,128]{4,3,2,1,0:T(8,128)S(1)} collective-permute-done((f32[7,7,2,8,128]{4,3,2,1,0:T(8,128)}, f32[7,7,2,8,128]{4,3,2,1,0:T(8,128)S(1)}, u32[]{:S(2)}, u32[]{:S(2)}) %collective-permute-start.13) | collective-permute-done | bytes 401440 | tf_op jit(solution)/shard_map/ppermute | solution.py:337
  88.2 1.1 %add.20 = f32[7,7,2,8,128]{4,3,2,1,0:T(8,128)S(1)} add(f32[7,7,2,8,128]{4,3,2,1,0:T(8,128)} %get-tuple-element.26, f32[7,7,2,8,128]{4,3,2,1,0:T(8,128)S(1)} %collective-permute-done.13) | non-fusion elementwise | flops 100352 | bytes 1204224 | tf_op jit(solution)/shard_map/add | solution.py:389
  89.3 0.1 collective-permute-start.14
  89.3 11.3 %collective-permute-done.14 = f32[7,7,2,8,128]{4,3,2,1,0:T(8,128)S(1)} collective-permute-done((f32[7,7,2,8,128]{4,3,2,1,0:T(8,128)S(1)}, f32[7,7,2,8,128]{4,3,2,1,0:T(8,128)S(1)}, u32[]{:S(2)}, u32[]{:S(2)}) %collective-permute-start.14) | collective-permute-done | bytes 401440 | tf_op jit(solution)/shard_map/ppermute | solution.py:344
  100.7 0.1 add.21
  100.7 0.1 collective-permute-start.15
  100.8 0.0 copy-done.4
  100.8 0.8 reshape.17
  101.6 0.9 collective-permute-done.15
  102.5 0.1 broadcast_select_fusion.1
  102.6 1.0 pad_maximum_fusion.1
  (25 shorter events, 0.3 us)
Async XLA Ops:
  2.7 5.0 %collective-permute-start = (f32[12,9,2,128]{3,1,0,2:T(8,128)S(1)}, f32[12,9,2,128]{3,1,0,2:T(8,128)S(1)}, u32[]{:S(2)}, u32[]{:S(2)}) collective-permute-start(f32[12,9,2,128]{3,1,0,2:T(8,128)S(1)} %get-tuple-element.37), channel_id=1, source_target_pairs={{1,2},{2,1},{5,6},{6,5},{9,10},{10,9},{13,14},{14,13},{17,18},{18,... | collective-permute-start | bytes 331784 | tf_op jit(solution)/shard_map/ppermute | solution.py:337
  3.4 5.4 %collective-permute-start.1 = (f32[12,9,2,128]{3,1,0,2:T(8,128)S(1)}, f32[12,9,2,128]{3,1,0,2:T(8,128)S(1)}, u32[]{:S(2)}, u32[]{:S(2)}) collective-permute-start(f32[12,9,2,128]{3,1,0,2:T(8,128)S(1)} %get-tuple-element.36), channel_id=1, source_target_pairs={{0,1},{1,0},{2,3},{3,2},{4,5},{5,4},{6,7},{7,6},{8,9},{9,8},{10,11... | collective-permute-start | bytes 331784 | tf_op jit(solution)/shard_map/ppermute | solution.py:337
  10.2 11.2 %collective-permute-start.2 = (f32[6,28,256]{2,1,0:T(8,128)S(1)}, f32[6,28,256]{2,1,0:T(8,128)S(1)}, u32[]{:S(2)}, u32[]{:S(2)}) collective-permute-start(f32[6,28,256]{2,1,0:T(8,128)S(1)} %select_n.83), channel_id=1, source_target_pairs={{4,8},{8,4},{12,16},{16,12},{20,24},{24,20},{5,9},{9,5},{13,17},{1... | collective-permute-start | bytes 516104 | tf_op jit(solution)/shard_map/ppermute | solution.py:337
  11.1 12.9 %collective-permute-start.3 = (f32[6,28,256]{2,1,0:T(8,128)S(1)}, f32[6,28,256]{2,1,0:T(8,128)S(1)}, u32[]{:S(2)}, u32[]{:S(2)}) collective-permute-start(f32[6,28,256]{2,1,0:T(8,128)S(1)} %select_n.85), channel_id=1, source_target_pairs={{0,4},{4,0},{8,12},{12,8},{16,20},{20,16},{24,28},{28,24},{1,5},{5... | collective-permute-start | bytes 516104 | tf_op jit(solution)/shard_map/ppermute | solution.py:337
  15.5 33.1 %copy-start.3 = (f32[2,12,24,128]{3,2,1,0:T(8,128)}, f32[2,12,24,128]{3,2,1,0:T(8,128)S(1)}, u32[]{:S(2)}) copy-start(f32[2,12,24,128]{3,2,1,0:T(8,128)S(1)} %pad.9.refs_4_) | copy-start | bytes 884740
  15.5 33.1 %collective-permute-start.4 = (f32[2,12,24,128]{3,2,1,0:T(8,128)S(1)}, f32[2,12,24,128]{3,2,1,0:T(8,128)S(1)}, u32[]{:S(2)}, u32[]{:S(2)}) collective-permute-start(f32[2,12,24,128]{3,2,1,0:T(8,128)S(1)} %pad.9.refs_4_), channel_id=1, source_target_pairs={{0,8},{4,12},{8,16},{12,20},{16,24},{20,28},{24,0},{28,4},{1,9},{5... | collective-permute-start | bytes 884744 | tf_op jit(solution)/shard_map/ppermute | solution.py:344
  17.2 31.5 %collective-permute-start.5 = (f32[2,12,24,128]{3,2,1,0:T(8,128)S(1)}, f32[2,12,24,128]{3,2,1,0:T(8,128)S(1)}, u32[]{:S(2)}, u32[]{:S(2)}) collective-permute-start(f32[2,12,24,128]{3,2,1,0:T(8,128)S(1)} %pad.9.refs_4_), channel_id=1, source_target_pairs={{0,16},{4,20},{8,24},{12,28},{16,0},{20,4},{24,8},{28,12},{1,17},{... | collective-permute-start | bytes 884744 | tf_op jit(solution)/shard_map/ppermute | solution.py:344
  18.2 30.4 %collective-permute-start.6 = (f32[2,12,24,128]{3,2,1,0:T(8,128)S(1)}, f32[2,12,24,128]{3,2,1,0:T(8,128)S(1)}, u32[]{:S(2)}, u32[]{:S(2)}) collective-permute-start(f32[2,12,24,128]{3,2,1,0:T(8,128)S(1)} %pad.9.refs_4_), channel_id=1, source_target_pairs={{0,24},{4,28},{8,0},{12,4},{16,8},{20,12},{24,16},{28,20},{1,25},{... | collective-permute-start | bytes 884744 | tf_op jit(solution)/shard_map/ppermute | solution.py:344
  21.4 27.4 %collective-permute-start.7 = (f32[2,12,24,128]{3,2,1,0:T(8,128)S(1)}, f32[2,12,24,128]{3,2,1,0:T(8,128)S(1)}, u32[]{:S(2)}, u32[]{:S(2)}) collective-permute-start(f32[2,12,24,128]{3,2,1,0:T(8,128)S(1)} %pad.9.refs_4_), channel_id=1, source_target_pairs={{0,4},{4,0},{8,12},{12,8},{16,20},{20,16},{24,28},{28,24},{1,5},{5... | collective-permute-start | bytes 884744 | tf_op jit(solution)/shard_map/ppermute | solution.py:337
  48.6 25.6 %copy-start = (f32[2,12,24,128]{3,2,1,0:T(8,128)}, f32[2,12,24,128]{3,2,1,0:T(8,128)S(1)}, u32[]{:S(2)}) copy-start(f32[2,12,24,128]{3,2,1,0:T(8,128)S(1)} %collective-permute-done.4.refs_5_) | copy-start | bytes 884740
  48.6 25.6 %copy-start.1 = (f32[2,12,24,128]{3,2,1,0:T(8,128)}, f32[2,12,24,128]{3,2,1,0:T(8,128)S(1)}, u32[]{:S(2)}) copy-start(f32[2,12,24,128]{3,2,1,0:T(8,128)S(1)} %collective-permute-done.5.refs_6_) | copy-start | bytes 884740
  48.7 25.6 %copy-start.2 = (f32[2,12,24,128]{3,2,1,0:T(8,128)}, f32[2,12,24,128]{3,2,1,0:T(8,128)S(1)}, u32[]{:S(2)}) copy-start(f32[2,12,24,128]{3,2,1,0:T(8,128)S(1)} %collective-permute-done.6.refs_7_) | copy-start | bytes 884740
  48.7 25.5 %copy-start.9 = (f32[2,12,24,128]{3,2,1,0:T(8,128)}, f32[2,12,24,128]{3,2,1,0:T(8,128)S(1)}, u32[]{:S(2)}) copy-start(f32[2,12,24,128]{3,2,1,0:T(8,128)S(1)} %collective-permute-done.7.refs_9_) | copy-start | bytes 884740
  48.8 25.5 %collective-permute-start.12 = (f32[3,2,12,24,128]{4,3,2,1,0:T(8,128)S(1)}, f32[3,2,12,24,128]{4,3,2,1,0:T(8,128)S(1)}, u32[]{:S(2)}, u32[]{:S(2)}) collective-permute-start(f32[3,2,12,24,128]{4,3,2,1,0:T(8,128)S(1)} %pad_maximum_fusion), channel_id=1, source_target_pairs={{0,4},{4,0},{8,12},{12,8},{16,20},{20,16},{24,28},{28,24},{1,5},{5... | collective-permute-start | bytes 2654216 | tf_op jit(solution)/shard_map/ppermute | solution.py:337
  51.3 6.6 %collective-permute-start.8 = (f32[2,32,192]{2,1,0:T(8,128)}, f32[2,32,192]{2,1,0:T(8,128)S(1)}, u32[]{:S(2)}, u32[]{:S(2)}) collective-permute-start(f32[2,32,192]{2,1,0:T(8,128)} %get-tuple-element.21), channel_id=1, source_target_pairs={{0,8},{4,12},{8,16},{12,20},{16,24},{20,28},{24,0},{28,4},{1,9},{5... | collective-permute-start | bytes 147464 | tf_op jit(solution)/shard_map/ppermute | solution.py:344
  52.9 7.5 %collective-permute-start.9 = (f32[2,32,192]{2,1,0:T(8,128)}, f32[2,32,192]{2,1,0:T(8,128)S(1)}, u32[]{:S(2)}, u32[]{:S(2)}) collective-permute-start(f32[2,32,192]{2,1,0:T(8,128)} %get-tuple-element.22), channel_id=1, source_target_pairs={{0,16},{4,20},{8,24},{12,28},{16,0},{20,4},{24,8},{28,12},{1,17},{... | collective-permute-start | bytes 147464 | tf_op jit(solution)/shard_map/ppermute | solution.py:344
  54.0 6.4 %collective-permute-start.10 = (f32[2,32,192]{2,1,0:T(8,128)}, f32[2,32,192]{2,1,0:T(8,128)S(1)}, u32[]{:S(2)}, u32[]{:S(2)}) collective-permute-start(f32[2,32,192]{2,1,0:T(8,128)} %get-tuple-element.23), channel_id=1, source_target_pairs={{0,24},{4,28},{8,0},{12,4},{16,8},{20,12},{24,16},{28,20},{1,25},{... | collective-permute-start | bytes 147464 | tf_op jit(solution)/shard_map/ppermute | solution.py:344
  57.9 16.4 %copy-start.5 = (f32[2,32,192]{2,1,0:T(8,128)}, f32[2,32,192]{2,1,0:T(8,128)S(1)}, u32[]{:S(2)}) copy-start(f32[2,32,192]{2,1,0:T(8,128)S(1)} %collective-permute-done.8.refs_1_) | copy-start | bytes 147460
  60.4 13.9 %copy-start.6 = (f32[2,32,192]{2,1,0:T(8,128)}, f32[2,32,192]{2,1,0:T(8,128)S(1)}, u32[]{:S(2)}) copy-start(f32[2,32,192]{2,1,0:T(8,128)S(1)} %collective-permute-done.9.refs_2_) | copy-start | bytes 147460
  60.4 13.9 %copy-start.7 = (f32[2,32,192]{2,1,0:T(8,128)}, f32[2,32,192]{2,1,0:T(8,128)S(1)}, u32[]{:S(2)}) copy-start(f32[2,32,192]{2,1,0:T(8,128)S(1)} %collective-permute-done.10.refs_3_) | copy-start | bytes 147460
  60.4 40.4 %copy-start.4 = (f32[12,16,256]{2,1,0:T(8,128)S(1)}, f32[12,16,256]{2,1,0:T(8,128)}, u32[]{:S(2)}) copy-start(f32[12,16,256]{2,1,0:T(8,128)} %get-tuple-element.15) | copy-start | bytes 589828
  60.4 13.8 %collective-permute-start.11 = (f32[4,32,192]{2,1,0:T(8,128)S(1)}, f32[4,32,192]{2,1,0:T(8,128)S(1)}, u32[]{:S(2)}, u32[]{:S(2)}) collective-permute-start(f32[4,32,192]{2,1,0:T(8,128)S(1)} %pad_maximum_fusion.4), channel_id=1, source_target_pairs={{0,4},{4,0},{8,12},{12,8},{16,20},{20,16},{24,28},{28,24},{1,5},{5... | collective-permute-start | bytes 294920 | tf_op jit(solution)/shard_map/ppermute | solution.py:337
  74.2 0.7 copy-start.10
  74.9 0.9 copy-start.8
  86.2 2.0 %collective-permute-start.13 = (f32[7,7,2,8,128]{4,3,2,1,0:T(8,128)}, f32[7,7,2,8,128]{4,3,2,1,0:T(8,128)S(1)}, u32[]{:S(2)}, u32[]{:S(2)}) collective-permute-start(f32[7,7,2,8,128]{4,3,2,1,0:T(8,128)} %get-tuple-element.27), channel_id=1, source_target_pairs={{0,1},{1,0},{2,3},{3,2},{4,5},{5,4},{6,7},{7,6},{8,9},{9,8},{10,11... | collective-permute-start | bytes 1204232 | tf_op jit(solution)/shard_map/ppermute | solution.py:337
  89.3 11.4 %collective-permute-start.14 = (f32[7,7,2,8,128]{4,3,2,1,0:T(8,128)S(1)}, f32[7,7,2,8,128]{4,3,2,1,0:T(8,128)S(1)}, u32[]{:S(2)}, u32[]{:S(2)}) collective-permute-start(f32[7,7,2,8,128]{4,3,2,1,0:T(8,128)S(1)} %add.20), channel_id=1, source_target_pairs={{0,2},{1,3},{2,0},{3,1},{4,6},{5,7},{6,4},{7,5},{8,10},{9,11},{10,... | collective-permute-start | bytes 1204232 | tf_op jit(solution)/shard_map/ppermute | solution.py:344
  100.7 1.8 %collective-permute-start.15 = (f32[7,7,2,8,128]{4,3,2,1,0:T(8,128)S(1)}, f32[7,7,2,8,128]{4,3,2,1,0:T(8,128)S(1)}, u32[]{:S(2)}, u32[]{:S(2)}) collective-permute-start(f32[7,7,2,8,128]{4,3,2,1,0:T(8,128)S(1)} %add.21), channel_id=1, source_target_pairs={{0,1},{1,0},{2,3},{3,2},{4,5},{5,4},{6,7},{7,6},{8,9},{9,8},{10,11... | collective-permute-start | bytes 1204232 | tf_op jit(solution)/shard_map/ppermute | solution.py:337

commit v3 on v2

--- a/solution.py
+++ b/solution.py
@@ -9,7 +9,6 @@
 from jax.sharding import PartitionSpec as P
 
 SWEEPS = 2
-VMEM_LIMIT = 56 * 1024 * 1024
 
 f32 = jnp.float32
 bf16 = jnp.bfloat16
@@ -53,49 +52,64 @@
     return row_ok & col_ok & (j < cols)
 
 
-def sweeps_kernel(
+def store_inverse(inverse_ref, high_ref, low_ref):
+    real_high, real_low = split(inverse_ref[0])
+    imag_high, imag_low = split(inverse_ref[1])
+    store_block(high_ref, (), real_high, imag_high)
+    store_block(low_ref, (), real_low, imag_low)
+
+
+def products(high, low, weight_high, weight_low):
+    lanes = weight_high.shape[-1]
+    weight_high = weight_high.reshape(-1, lanes)
+    weight_low = weight_low.reshape(-1, lanes)
+    return dot(high, weight_high) + dot(low, weight_high) + dot(high, weight_low)
+
+
+def first_sweep_kernel(
     sizes,
     source_ref,
     inverse_ref,
     blocks_hbm,
-    adjoint_ref,
-    *rest,
+    second_ref,
+    own_source_ref,
+    high_hbm,
+    low_hbm,
+    first,
+    x_high,
+    x_low,
+    acc,
+    raw,
+    w_high,
+    w_low,
+    e_high,
+    e_low,
+    sems,
 ):
-    rows, cols, span, peers, pitch, wide = sizes
-    sends = rest[: peers // 2]
-    (first, second, x1_high, x1_low, x2_high, x2_low, acc, turned, raw, w_high, w_low, e_high, e_low, sems) = rest[peers // 2 :]
+    rows, cols, span, pitch, wide = sizes
     reach = span // 2
     mid_rows, mid_cols = rows + 2 * reach, cols + 2 * reach
     full_rows = rows + 4 * reach
     lanes = source_ref.shape[-1]
-    width = lanes // 2
 
     def block_copy(a):
-        return pltpu.make_async_copy(blocks_hbm.at[a], raw.at[a], sems.at[a])
+        return pltpu.make_async_copy(blocks_hbm.at[a], raw.at[a], sems.at[0, a])
+
+    def part_copies(a):
+        return (
+            pltpu.make_async_copy(w_high.at[a], high_hbm.at[a], sems.at[1, a]),
+            pltpu.make_async_copy(w_low.at[a], low_hbm.at[a], sems.at[2, a]),
+        )
 
     for a in range(span):
         block_copy(a).start()
 
-    def prepare(a):
-        @pl.loop(0, span)
-        def _(b):
-            real_high, real_low = split(raw[a, b, 0])
-            imag_high, imag_low = split(raw[a, b, 1])
-            store_block(w_high, (a, b), real_high, imag_high)
-            store_block(w_low, (a, b), real_low, imag_low)
-
-    def products(a, high, low):
-        weight_high = w_high[a].reshape(span * lanes, lanes)
-        weight_low = w_low[a].reshape(span * lanes, lanes)
-        return dot(high, weight_high) + dot(low, weight_high) + dot(high, weight_low)
-
-    real_high, real_low = split(inverse_ref[0])
-    imag_high, imag_low = split(inverse_ref[1])
-    store_block(e_high, (), real_high, imag_high)
-    store_block(e_low, (), real_low, imag_low)
+    store_inverse(inverse_ref, e_high, e_low)
 
     def invert(value):
         return dot3(split(value), (e_high[...], e_low[...]))
+
+    own_source_ref[...] = source_ref[2 * reach : 2 * reach + rows, pl.ds(2 * reach, cols), :]
 
     step_rows = 4
 
@@ -114,17 +128,26 @@
                 value = first[pl.ds(2 * s + odd, 2), pl.ds(b, pitch), :]
                 high, low = split(value.reshape(2 * pitch, lanes))
                 to = pl.ds(pl.multiple_of(s * 2 * pitch, 2 * pitch), 2 * pitch)
-                x1_high[odd, to, b * lanes : (b + 1) * lanes] = high
-                x1_low[odd, to, b * lanes : (b + 1) * lanes] = low
+                x_high[odd, to, b * lanes : (b + 1) * lanes] = high
+                x_low[odd, to, b * lanes : (b + 1) * lanes] = low
 
     acc[...] = jnp.zeros_like(acc)
 
     @pl.loop(0, span)
     def _(a):
         block_copy(a).wait()
-        prepare(a)
+
+        @pl.loop(0, span)
+        def _(b):
+            real_high, real_low = split(raw[a, b, 0])
+            imag_high, imag_low = split(raw[a, b, 1])
+            store_block(w_high, (a, b), real_high, imag_high)
+            store_block(w_low, (a, b), real_low, imag_low)
+
+        for copy in part_copies(a):
+            copy.start()
         at = pl.ds(pl.multiple_of((a // 2) * 2 * pitch, 2 * pitch), mid_rows * pitch)
-        acc[...] += products(a, x1_high[a % 2, at, :], x1_low[a % 2, at, :])
+        acc[...] += products(x_high[a % 2, at, :], x_low[a % 2, at, :], w_high[a], w_low[a])
 
     step_rows = 3
 
@@ -138,27 +161,107 @@
         value = centre + invert(source - centre - acc[flat, :])
         mask = inside(s * step_rows, step_rows, mid_cols, pitch, reach, rows, cols)
         value = jnp.where(mask, value, 0.0)
-        second[pl.ds(s * step_rows, step_rows)] = value.reshape(step_rows, pitch, lanes)
+        second_ref[pl.ds(s * step_rows, step_rows)] = value.reshape(step_rows, pitch, lanes)
+
+    @pl.loop(0, span)
+    def _(a):
+        for copy in part_copies(a):
+            copy.wait()
+
+
+def first_sweep(source, inverse, lag_blocks, rows, cols):
+    span = lag_blocks.shape[0]
+    reach = span // 2
+    lanes = source.shape[-1]
+    wide = source.shape[1]
+    pitch = round_up(cols + 2 * reach, 8)
+    full_rows, mid_rows = rows + 4 * reach, rows + 2 * reach
+    vmem = pl.BlockSpec(memory_space=pltpu.VMEM)
+    hbm = pl.BlockSpec(memory_space=pltpu.HBM)
+    weights = (span, span, lanes, lanes)
+    return pl.pallas_call(
+        functools.partial(first_sweep_kernel, (rows, cols, span, pitch, wide)),
+        in_specs=[vmem, vmem, hbm],
+        out_specs=[vmem, vmem, hbm, hbm],
+        out_shape=[
+            jax.ShapeDtypeStruct((mid_rows, pitch, lanes), f32),
+            jax.ShapeDtypeStruct((rows, cols, lanes), f32),
+            jax.ShapeDtypeStruct(weights, bf16),
+            jax.ShapeDtypeStruct(weights, bf16),
+        ],
+        scratch_shapes=[
+            pltpu.VMEM((full_rows + 1, wide, lanes), f32),
+            pltpu.VMEM((2, full_rows * pitch, span * lanes), bf16),
+            pltpu.VMEM((2, full_rows * pitch, span * lanes), bf16),
+            pltpu.VMEM((mid_rows * pitch, lanes), f32),
+            pltpu.VMEM(lag_blocks.shape, f32),
+            pltpu.VMEM(weights, bf16),
+            pltpu.VMEM(weights, bf16),
+            pltpu.VMEM((lanes, lanes), bf16),
+            pltpu.VMEM((lanes, lanes), bf16),
+            pltpu.SemaphoreType.DMA((3, span)),
+        ],
+        cost_estimate=pl.CostEstimate(
+            flops=6 * span * span * lanes * lanes * mid_rows * pitch,
+            bytes_accessed=12 * lag_blocks.size,
+            transcendentals=0,
+        ),
+        compiler_params=pltpu.CompilerParams(vmem_limit_bytes=40 * 1024 * 1024),
+        name="first_sweep",
+    )(source, inverse, lag_blocks)
+
+
+def second_sweep_kernel(
+    sizes,
+    second_ref,
+    source_ref,
+    inverse_ref,
+    high_hbm,
+    low_hbm,
+    adjoint_ref,
+    *rest,
+):
+    rows, cols, span, peers = sizes
+    sends = rest[: peers // 2]
+    x_high, x_low, acc, turned, w_high, w_low, e_high, e_low, sems = rest[peers // 2 :]
+    reach = span // 2
+    mid_rows = rows + 2 * reach
+    own = rows * cols
+    lanes = source_ref.shape[-1]
+    width = lanes // 2
+
+    def part_copies(a):
+        return (
+            pltpu.make_async_copy(high_hbm.at[a], w_high.at[a], sems.at[0, a]),
+            pltpu.make_async_copy(low_hbm.at[a], w_low.at[a], sems.at[1, a]),
+        )
+
+    for a in range(span):
+        for copy in part_copies(a):
+            copy.start()
+
+    store_inverse(inverse_ref, e_high, e_low)
 
     @pl.loop(0, mid_rows)
     def _(i):
         for b in range(span):
-            high, low = split(second[i, pl.ds(b, cols), :])
+            high, low = split(second_ref[i, pl.ds(b, cols), :])
             to = pl.ds(pl.multiple_of(i * cols, cols), cols)
-            x2_high[to, b * lanes : (b + 1) * lanes] = high
-            x2_low[to, b * lanes : (b + 1) * lanes] = low
-
-    own = rows * cols
-    acc[:own] = jnp.zeros((own, lanes), f32)
+            x_high[to, b * lanes : (b + 1) * lanes] = high
+            x_low[to, b * lanes : (b + 1) * lanes] = low
+
+    acc[...] = jnp.zeros_like(acc)
 
     @pl.loop(0, span)
     def _(a):
+        for copy in part_copies(a):
+            copy.wait()
         at = pl.ds(pl.multiple_of(a * cols, cols), own)
-        acc[:own] += products(a, x2_high[at, :], x2_low[at, :])
-
-    centre = second[reach : reach + rows, pl.ds(reach, cols), :].reshape(own, lanes)
-    source = source_ref[2 * reach : 2 * reach + rows, pl.ds(2 * reach, cols), :].reshape(own, lanes)
-    value = centre + invert(source - centre - acc[:own])
+        acc[...] += products(x_high[at, :], x_low[at, :], w_high[a], w_low[a])
+
+    centre = second_ref[reach : reach + rows, pl.ds(reach, cols), :].reshape(own, lanes)
+    source = source_ref[...].reshape(own, lanes)
+    value = centre + dot3(split(source - centre - acc[...]), (e_high[...], e_low[...]))
     adjoint_ref[...] = value.reshape(adjoint_ref.shape)
     turned[...] = value.T
 
@@ -173,46 +276,38 @@
                 sends[k][n, part * share : (part + 1) * share, :] = turned[pl.ds(at, share), :]
 
 
-def run_sweeps(source, inverse, lag_blocks, rows, cols, peers):
-    span = lag_blocks.shape[0]
-    reach = span // 2
-    lanes = source.shape[-1]
-    wide = source.shape[1]
-    pitch = round_up(cols + 2 * reach, 8)
-    full_rows, mid_rows = rows + 4 * reach, rows + 2 * reach
+def second_sweep(second, source, inverse, high, low, peers):
+    span = high.shape[0]
+    rows, cols, lanes = source.shape
+    mid_rows = second.shape[0]
     share = lanes // 2 // peers
-    sizes = (rows, cols, span, peers, pitch, wide)
     vmem = pl.BlockSpec(memory_space=pltpu.VMEM)
-    hbm = pl.BlockSpec(memory_space=pl.ANY)
+    hbm = pl.BlockSpec(memory_space=pltpu.HBM)
     send = jax.ShapeDtypeStruct((2, 2 * share, rows * cols), f32)
-    flops = 6 * span * span * lanes * lanes * (mid_rows * pitch + rows * cols)
     out = pl.pallas_call(
-        functools.partial(sweeps_kernel, sizes),
-        in_specs=[vmem, vmem, hbm],
+        functools.partial(second_sweep_kernel, (rows, cols, span, peers)),
+        in_specs=[vmem, vmem, vmem, hbm, hbm],
         out_specs=[vmem] * (1 + peers // 2),
         out_shape=[jax.ShapeDtypeStruct((rows, cols, lanes), f32)] + [send] * (peers // 2),
         scratch_shapes=[
-            pltpu.VMEM((full_rows + 1, wide, lanes), f32),
-            pltpu.VMEM((mid_rows, pitch, lanes), f32),
-            pltpu.VMEM((2, full_rows * pitch, span * lanes), bf16),
-            pltpu.VMEM((2, full_rows * pitch, span * lanes), bf16),
             pltpu.VMEM((mid_rows * cols, span * lanes), bf16),
             pltpu.VMEM((mid_rows * cols, span * lanes), bf16),
-            pltpu.VMEM((mid_rows * pitch, lanes), f32),
+            pltpu.VMEM((rows * cols, lanes), f32),
             pltpu.VMEM((lanes, rows * cols), f32),
-            pltpu.VMEM(lag_blocks.shape, f32),
-            pltpu.VMEM((span, span, lanes, lanes), bf16),
-            pltpu.VMEM((span, span, lanes, lanes), bf16),
+            pltpu.VMEM(high.shape, bf16),
+            pltpu.VMEM(high.shape, bf16),
             pltpu.VMEM((lanes, lanes), bf16),
             pltpu.VMEM((lanes, lanes), bf16),
-            pltpu.SemaphoreType.DMA((span,)),
+            pltpu.SemaphoreType.DMA((2, span)),
         ],
         cost_estimate=pl.CostEstimate(
-            flops=flops, bytes_accessed=4 * lag_blocks.size, transcendentals=0
+            flops=6 * span * span * lanes * lanes * rows * cols,
+            bytes_accessed=4 * high.size,
+            transcendentals=0,
         ),
-        compiler_params=pltpu.CompilerParams(vmem_limit_bytes=VMEM_LIMIT),
-        name="sweeps",
-    )(source, inverse, lag_blocks)
+        compiler_params=pltpu.CompilerParams(vmem_limit_bytes=28 * 1024 * 1024),
+        name="second_sweep",
+    )(second, source, inverse, high, low)
     return out[0], out[1:]
 
 
@@ -220,8 +315,9 @@
     rows, cols, span, peers = sizes
     half_peers = peers // 2
     shares, piece_refs = refs[:half_peers], refs[half_peers:peers]
-    twin_shares_ref, own_twin_ref, twins_ref, mine_ref, other_ref = refs[peers : peers + 5]
-    placed, flat, l_high, l_low, stage, s_high, s_low, sems = refs[peers + 5 :]
+    twin_shares_ref, own_twin_ref, early_ref, late_ref = refs[peers : peers + 4]
+    mine_ref, other_ref = refs[peers + 4 : peers + 6]
+    placed, flat, l_high, l_low, stage, s_high, s_low, sems = refs[peers + 6 :]
     reach = span // 2
     own = rows * cols
     double = shares[0].shape[1]
@@ -236,7 +332,10 @@
         return base + 1 - odd, base + odd
 
     for k in range(half_peers):
-        twin = own_twin_ref if k == 0 else twins_ref.at[k - 1]
+        if k == 0:
+            twin = own_twin_ref
+        else:
+            twin = late_ref if k == half_peers - 1 else early_ref.at[k - 1]
         for n, (source, tile) in enumerate(zip((piece_refs[k], twin), tiles(k))):
             pltpu.make_async_copy(source, stage.at[tile], sems.at[n, k]).start()
         first, second = tiles(k)
@@ -292,20 +391,21 @@
                 other_ref[a, b, c] = jnp.where(upper, value[:half], value[half:])
 
 
-def correlate(shares, twin_shares, pieces, own_twin, twins, rows, cols, span, factor):
+def correlate(shares, twin_shares, pieces, twins, rows, cols, span, factor):
     peers = 2 * len(shares)
     reach = span // 2
     double, own = twin_shares.shape[1:]
     share = double // 2
+    own_twin = twins[0]
     width = own_twin.shape[-1]
     total = peers * own
     side = round_up(reach * cols, 128)
     vmem = pl.BlockSpec(memory_space=pltpu.VMEM)
-    hbm = pl.BlockSpec(memory_space=pl.ANY)
+    hbm = pl.BlockSpec(memory_space=pltpu.HBM)
     out = jax.ShapeDtypeStruct((span, span, 2, share // 2, width), f32)
     return pl.pallas_call(
         functools.partial(correlate_kernel, (rows, cols, span, peers), factor),
-        in_specs=[vmem] * (peers // 2) + [hbm] * (peers // 2) + [vmem, hbm, hbm],
+        in_specs=[vmem] * (peers // 2) + [hbm] * (peers // 2) + [vmem, hbm, hbm, hbm],
         out_specs=[vmem, vmem],
         out_shape=[out, out],
         scratch_shapes=[
@@ -323,9 +423,9 @@
             bytes_accessed=4 * (2 * out.size + peers * own_twin.size),
             transcendentals=0,
         ),
-        compiler_params=pltpu.CompilerParams(vmem_limit_bytes=VMEM_LIMIT),
+        compiler_params=pltpu.CompilerParams(vmem_limit_bytes=28 * 1024 * 1024),
         name="correlate",
-    )(*shares, *pieces, twin_shares, own_twin, twins)
+    )(*shares, *pieces, twin_shares, *twins)
 
 
 def swap(value, axis, first):
@@ -377,15 +477,20 @@
     pieces = [shifted(saved, "row", k) for k in range(0, peers, 2)]
     own_twin = swap(saved, "row", 0)
 
-    adjoint, sends = run_sweeps(source, element_inverse, lag_blocks, rows, cols, peers)
-    twins, own_twin, sends = lax.optimization_barrier((jnp.stack(pieces[1:]), own_twin, sends))
-    twins = swap(twins, "row", 0)
+    second, own_source, high, low = first_sweep(source, element_inverse, lag_blocks, rows, cols)
+    second, own_twin, early = lax.optimization_barrier((second, own_twin, jnp.stack(pieces[1:-1])))
+    early_twins = swap(early, "row", 0)
+    adjoint, sends = second_sweep(second, own_source, element_inverse, high, low, peers)
+    late, sends = lax.optimization_barrier((pieces[-1], sends))
+    late_twin = swap(late, "row", 0)
     shares = [shifted(send, "row", 2 * k) for k, send in enumerate(sends)]
     twin_shares = swap(jnp.stack([received[1] for received in shares]), "row", 0)
 
     elements = rows * peers * cols * lax.axis_size("col")
     factor = -1.0 / math.sqrt(elements)
-    mine, other = correlate(shares, twin_shares, pieces, own_twin, twins, rows, cols, span, factor)
+    mine, other = correlate(
+        shares, twin_shares, pieces, (own_twin, early_twins, late_twin), rows, cols, span, factor
+    )
     mine = mine + swap(other, "col", 0)
     total = mine
     for k in range(2, lax.axis_size("col"), 2):

time: 104 us -> 101 us (0.971)
  waiting for transfers between devices: 33.2 us -> 21.1 us
  starting transfers between devices: 25.1 us -> 35.2 us
  Pallas kernels: 34 us -> 37 us
  local copies, waits for them, and re-layouts: 6.72 us -> 4.46 us
  other arithmetic: 3.48 us -> 1.59 us
    ppermute x9 -> x10, waiting for transfers between devices: 19.1 us -> 7.85 us  [swap(): return lax.ppermute(value, axis, pairs)]
    ppermute x7, starting transfers between devices: 11.2 us -> 18.7 us  [shifted(): lax.ppermute(value, axis, [(i, (i + shift) % peers) for i in range(peers)])]
    pallas_call x1 -> x2, Pallas kernels: 23.6 us -> 28.4 us  [the longest x1 18.9 us: first_sweep(): pl.pallas_call(functools.partial(first_sweep_kernel, (rows, cols, span, p...]
    ppermute x9 -> x10, starting transfers between devices: 14 us -> 16.5 us  [swap(): return lax.ppermute(value, axis, pairs)]
    pallas_call x1, Pallas kernels: 10.4 us -> 8.62 us  [correlate(): pl.pallas_call(functools.partial(correlate_kernel, (rows, cols, span, pee...]
    unnamed x27 -> x7, local copies, waits for them, and re-layouts: 3.53 us -> 2.02 us
  transfers between devices with their start and end apart: 16 -> 17, of which waited for: 8 -> 9; matrix products, arithmetic and copies ran while one was open for 3% -> 1% of each run, Pallas kernels for 23% -> 28%
where the time goes in v3:
time: 101 us; the launch traced here: 100 us
  Pallas kernels  37 us (37%)
  starting transfers between devices  35.2 us (35%)
  waiting for transfers between devices  21.1 us (21%)
  local copies, waits for them, and re-layouts  4.46 us (4%)
  other arithmetic  1.59 us (2%)
    pallas_call x1, Pallas kernels, first_sweep(): pl.pallas_call(functools.partial(first_sweep_kernel, (rows, cols, span, p...  18.9 us
    ppermute x7, starting transfers between devices, shifted(): lax.ppermute(value, axis, [(i, (i + shift) % peers) for i in range(peers)])  18.7 us
    ppermute x10, starting transfers between devices, swap(): return lax.ppermute(value, axis, pairs)  16.5 us
    ppermute x7, waiting for transfers between devices, shifted(): lax.ppermute(value, axis, [(i, (i + shift) % peers) for i in range(peers)])  13.3 us
    pallas_call x1, Pallas kernels, second_sweep(): pl.pallas_call(functools.partial(second_sweep_kernel, (rows, cols, span,...  9.5 us
    pallas_call x1, Pallas kernels, correlate(): pl.pallas_call(functools.partial(correlate_kernel, (rows, cols, span, pee...  8.62 us
    ppermute x10, waiting for transfers between devices, swap(): return lax.ppermute(value, axis, pairs)  7.85 us
    unnamed x7, local copies, waits for them, and re-layouts  2.02 us
  transfers between devices with their start and end apart: 17, of which 9 were waited for; matrix products, arithmetic and copies ran while one was open for 1% of the time, Pallas kernels for 28%

profile of v3, /device:TPU:0, one launch (start us, length us, event | category | flops | bytes accessed | tf_op | source)
XLA Modules:
  0.0 100.3 jit_solution(698303550711983286)
XLA Ops:
  0.6 0.0 copy-start
  0.7 1.0 copy.7
  1.7 0.9 fusion.2
  2.6 0.1 fusion
  2.7 0.7 collective-permute-start
  3.4 4.4 %collective-permute-start.1 = (f32[12,9,2,128]{3,1,0,2:T(8,128)S(1)}, f32[12,9,2,128]{3,1,0,2:T(8,128)S(1)}, u32[]{:S(2)}, u32[]{:S(2)}) collective-permute-start(f32[12,9,2,128]{3,1,0,2:T(8,128)S(1)} %get-tuple-element.48), channel_id=1, source_target_pairs={{0,1},{1,0},{2,3},{3,2},{4,5},{5,4},{6,7},{7,6},{8,9},{9,8},{10,11... | collective-permute-start | bytes 331784 | tf_op jit(solution)/shard_map/ppermute | solution.py:437
  7.8 0.0 collective-permute-done
  7.8 1.1 %collective-permute-done.1 = f32[12,9,2,128]{3,1,0,2:T(8,128)S(1)} collective-permute-done((f32[12,9,2,128]{3,1,0,2:T(8,128)S(1)}, f32[12,9,2,128]{3,1,0,2:T(8,128)S(1)}, u32[]{:S(2)}, u32[]{:S(2)}) %collective-permute-start.1) | collective-permute-done | bytes 110624 | tf_op jit(solution)/shard_map/ppermute | solution.py:437
  8.9 0.1 copy_dynamic-update-slice_fusion.1
  8.9 1.0 constant_dynamic-update-slice_fusion
  9.9 0.1 copy_dynamic-update-slice_fusion
  10.0 0.1 broadcast_select_fusion.3
  10.1 0.1 select_n.83
  10.3 0.7 collective-permute-start.2
  11.0 0.1 select_n.85
  11.1 4.3 %collective-permute-start.3 = (f32[6,28,256]{2,1,0:T(8,128)S(1)}, f32[6,28,256]{2,1,0:T(8,128)S(1)}, u32[]{:S(2)}, u32[]{:S(2)}) collective-permute-start(f32[6,28,256]{2,1,0:T(8,128)S(1)} %select_n.85), channel_id=1, source_target_pairs={{0,4},{4,0},{8,12},{12,8},{16,20},{20,16},{24,28},{28,24},{1,5},{5... | collective-permute-start | bytes 516104 | tf_op jit(solution)/shard_map/ppermute | solution.py:437
  15.4 0.3 reshape.16
  15.8 1.6 %collective-permute-start.5 = (f32[2,12,24,128]{3,2,1,0:T(8,128)S(1)}, f32[2,12,24,128]{3,2,1,0:T(8,128)S(1)}, u32[]{:S(2)}, u32[]{:S(2)}) collective-permute-start(f32[2,12,24,128]{3,2,1,0:T(8,128)S(1)} %pad.9.refs_4_), channel_id=1, source_target_pairs={{0,8},{4,12},{8,16},{12,20},{16,24},{20,28},{24,0},{28,4},{1,9},{5... | collective-permute-start | bytes 884744 | tf_op jit(solution)/shard_map/ppermute | solution.py:444
  17.5 1.1 %collective-permute-start.6 = (f32[2,12,24,128]{3,2,1,0:T(8,128)S(1)}, f32[2,12,24,128]{3,2,1,0:T(8,128)S(1)}, u32[]{:S(2)}, u32[]{:S(2)}) collective-permute-start(f32[2,12,24,128]{3,2,1,0:T(8,128)S(1)} %pad.9.refs_4_), channel_id=1, source_target_pairs={{0,16},{4,20},{8,24},{12,28},{16,0},{20,4},{24,8},{28,12},{1,17},{... | collective-permute-start | bytes 884744 | tf_op jit(solution)/shard_map/ppermute | solution.py:444
  18.6 1.9 %collective-permute-start.4 = (f32[2,12,24,128]{3,2,1,0:T(8,128)S(1)}, f32[2,12,24,128]{3,2,1,0:T(8,128)S(1)}, u32[]{:S(2)}, u32[]{:S(2)}) collective-permute-start(f32[2,12,24,128]{3,2,1,0:T(8,128)S(1)} %pad.9.refs_4_), channel_id=1, source_target_pairs={{0,4},{4,0},{8,12},{12,8},{16,20},{20,16},{24,28},{28,24},{1,5},{5... | collective-permute-start | bytes 884744 | tf_op jit(solution)/shard_map/ppermute | solution.py:437
  20.5 0.0 collective-permute-done.2
  20.5 2.8 %collective-permute-start.7 = (f32[2,12,24,128]{3,2,1,0:T(8,128)S(1)}, f32[2,12,24,128]{3,2,1,0:T(8,128)S(1)}, u32[]{:S(2)}, u32[]{:S(2)}) collective-permute-start(f32[2,12,24,128]{3,2,1,0:T(8,128)S(1)} %pad.9.refs_4_), channel_id=1, source_target_pairs={{0,24},{4,28},{8,0},{12,4},{16,8},{20,12},{24,16},{28,20},{1,25},{... | collective-permute-start | bytes 884744 | tf_op jit(solution)/shard_map/ppermute | solution.py:444
  23.3 0.7 collective-permute-done.3
  24.0 0.1 select_maximum_fusion.source_ref
  24.1 0.0 copy-done
  24.1 18.9 %first_sweep.1 = (f32[18,24,256]{2,1,0:T(8,128)S(1)}, f32[12,16,256]{2,1,0:T(8,128)S(1)}, bf16[7,7,256,256]{3,2,1,0:T(8,128)(2,1)S(1)}, bf16[7,7,256,256]{3,2,1,0:T(8,128)(2,1)S(1)}) custom-call(f32[24,32,256]{2,1,0:T(8,128)S(1)} %select_maximum_fusion.source_ref, f32[2,128,128]{2,1,0:T(8,128)S(1)} %copy-done, f32[7,7,2,128,128]{4,3,2,1,0:T(8,128)} %blocks_hbm.1), custom_call_target="tpu_custom_call" | custom-call | flops 8323596288 | bytes 19267584 | tf_op jit(solution)/shard_map/first_sweep/pallas_call | solution.py:182
  43.0 0.0 collective-permute-done.5.refs_5_
  43.0 0.0 collective-permute-done.6.refs_6_
  43.1 0.0 collective-permute-done.4.refs_9_
  43.1 2.5 %collective-permute-start.12 = (f32[2,2,12,24,128]{4,3,2,1,0:T(8,128)S(1)}, f32[2,2,12,24,128]{4,3,2,1,0:T(8,128)S(1)}, u32[]{:S(2)}, u32[]{:S(2)}) collective-permute-start(f32[2,2,12,24,128]{4,3,2,1,0:T(8,128)S(1)} %pad_maximum_fusion.1), channel_id=1, source_target_pairs={{0,4},{4,0},{8,12},{12,8},{16,20},{20,16},{24,28},{28,24},{1,5},{5... | collective-permute-start | bytes 1769480 | tf_op jit(solution)/shard_map/ppermute | solution.py:437
  45.7 9.5 %second_sweep.1 = (f32[12,16,256]{2,1,0:T(8,128)S(1)}, f32[2,32,192]{2,1,0:T(8,128)S(1)}, f32[2,32,192]{2,1,0:T(8,128)S(1)}, f32[2,32,192]{2,1,0:T(8,128)S(1)}, f32[2,32,192]{2,1,0:T(8,128)S(1)}) custom-call(f32[18,24,256]{2,1,0:T(8,128)S(1)} %get-tuple-element.22.second_ref, f32[12,16,256]{2,1,0:T(8,128)S(1)} %get-tuple-element.23.source_ref, ...), custom_call_target="tpu_custom_call" | custom-call | flops 3699376128 | bytes 12845056 | tf_op jit(solution)/shard_map/second_sweep/pallas_call | solution.py:287
  55.2 0.0 collective-permute-done.7.refs_7_
  55.2 0.1 collective-permute-start.13
  55.3 2.1 %collective-permute-start.8 = (f32[2,32,192]{2,1,0:T(8,128)S(1)}, f32[2,32,192]{2,1,0:T(8,128)S(1)}, u32[]{:S(2)}, u32[]{:S(2)}) collective-permute-start(f32[2,32,192]{2,1,0:T(8,128)S(1)} %get-tuple-element.32), channel_id=1, source_target_pairs={{0,8},{4,12},{8,16},{12,20},{16,24},{20,28},{24,0},{28,4},{1,9},{5... | collective-permute-start | bytes 147464 | tf_op jit(solution)/shard_map/ppermute | solution.py:444
  57.3 2.6 %collective-permute-start.9 = (f32[2,32,192]{2,1,0:T(8,128)S(1)}, f32[2,32,192]{2,1,0:T(8,128)S(1)}, u32[]{:S(2)}, u32[]{:S(2)}) collective-permute-start(f32[2,32,192]{2,1,0:T(8,128)S(1)} %get-tuple-element.33), channel_id=1, source_target_pairs={{0,16},{4,20},{8,24},{12,28},{16,0},{20,4},{24,8},{28,12},{1,17},{... | collective-permute-start | bytes 147464 | tf_op jit(solution)/shard_map/ppermute | solution.py:444
  59.9 1.3 %collective-permute-start.10 = (f32[2,32,192]{2,1,0:T(8,128)S(1)}, f32[2,32,192]{2,1,0:T(8,128)S(1)}, u32[]{:S(2)}, u32[]{:S(2)}) collective-permute-start(f32[2,32,192]{2,1,0:T(8,128)S(1)} %get-tuple-element.34), channel_id=1, source_target_pairs={{0,24},{4,28},{8,0},{12,4},{16,8},{20,12},{24,16},{28,20},{1,25},{... | collective-permute-start | bytes 147464 | tf_op jit(solution)/shard_map/ppermute | solution.py:444
  61.3 1.1 %collective-permute-done.8.refs_1_ = f32[2,32,192]{2,1,0:T(8,128)S(1)} collective-permute-done((f32[2,32,192]{2,1,0:T(8,128)S(1)}, f32[2,32,192]{2,1,0:T(8,128)S(1)}, u32[]{:S(2)}, u32[]{:S(2)}) %collective-permute-start.8) | collective-permute-done | bytes 49184 | tf_op jit(solution)/shard_map/ppermute | solution.py:444
  62.3 2.4 %collective-permute-done.9.refs_2_ = f32[2,32,192]{2,1,0:T(8,128)S(1)} collective-permute-done((f32[2,32,192]{2,1,0:T(8,128)S(1)}, f32[2,32,192]{2,1,0:T(8,128)S(1)}, u32[]{:S(2)}, u32[]{:S(2)}) %collective-permute-start.9) | collective-permute-done | bytes 49184 | tf_op jit(solution)/shard_map/ppermute | solution.py:444
  64.7 0.2 collective-permute-done.10.refs_3_
  65.0 1.8 %collective-permute-start.11 = (f32[4,32,192]{2,1,0:T(8,128)S(1)}, f32[4,32,192]{2,1,0:T(8,128)S(1)}, u32[]{:S(2)}, u32[]{:S(2)}) collective-permute-start(f32[4,32,192]{2,1,0:T(8,128)S(1)} %pad_maximum_fusion.4), channel_id=1, source_target_pairs={{0,4},{4,0},{8,12},{12,8},{16,20},{20,16},{24,28},{28,24},{1,5},{5... | collective-permute-start | bytes 294920 | tf_op jit(solution)/shard_map/ppermute | solution.py:437
  66.7 3.4 %collective-permute-done.11.refs_8_ = f32[4,32,192]{2,1,0:T(8,128)S(1)} collective-permute-done((f32[4,32,192]{2,1,0:T(8,128)S(1)}, f32[4,32,192]{2,1,0:T(8,128)S(1)}, u32[]{:S(2)}, u32[]{:S(2)}) %collective-permute-start.11) | collective-permute-done | bytes 98336 | tf_op jit(solution)/shard_map/ppermute | solution.py:437
  70.1 0.0 collective-permute-done.13.refs_11_
  70.1 0.0 collective-permute-done.12.refs_10_
  70.1 8.6 %correlate.1 = (f32[7,7,2,8,128]{4,3,2,1,0:T(8,128)S(1)}, f32[7,7,2,8,128]{4,3,2,1,0:T(8,128)S(1)}) custom-call(f32[2,32,192]{2,1,0:T(8,128)S(1)} %get-tuple-element.31.refs_0_, f32[2,32,192]{2,1,0:T(8,128)S(1)} %collective-permute-done.8.refs_1_, f32[2,32,192]{2,1,0:T(8,128)S(1)} %collective-permute-done.9.refs_2_, ...), custom_call_target="tpu_custom_call" | custom-call | flops 3699376128 | bytes 3162112 | tf_op jit(solution)/shard_map/correlate/pallas_call | solution.py:406
  78.7 0.1 collective-permute-start.14
  78.8 1.7 %collective-permute-done.14 = f32[7,7,2,8,128]{4,3,2,1,0:T(8,128)S(1)} collective-permute-done((f32[7,7,2,8,128]{4,3,2,1,0:T(8,128)S(1)}, f32[7,7,2,8,128]{4,3,2,1,0:T(8,128)S(1)}, u32[]{:S(2)}, u32[]{:S(2)}) %collective-permute-start.14) | collective-permute-done | bytes 401440 | tf_op jit(solution)/shard_map/ppermute | solution.py:437
  80.5 0.1 add.20
  80.6 7.2 %collective-permute-start.15 = (f32[7,7,2,8,128]{4,3,2,1,0:T(8,128)S(1)}, f32[7,7,2,8,128]{4,3,2,1,0:T(8,128)S(1)}, u32[]{:S(2)}, u32[]{:S(2)}) collective-permute-start(f32[7,7,2,8,128]{4,3,2,1,0:T(8,128)S(1)} %add.20), channel_id=1, source_target_pairs={{0,2},{1,3},{2,0},{3,1},{4,6},{5,7},{6,4},{7,5},{8,10},{9,11},{10,... | collective-permute-start | bytes 1204232 | tf_op jit(solution)/shard_map/ppermute | solution.py:444
  87.8 9.6 %collective-permute-done.15 = f32[7,7,2,8,128]{4,3,2,1,0:T(8,128)S(1)} collective-permute-done((f32[7,7,2,8,128]{4,3,2,1,0:T(8,128)S(1)}, f32[7,7,2,8,128]{4,3,2,1,0:T(8,128)S(1)}, u32[]{:S(2)}, u32[]{:S(2)}) %collective-permute-start.15) | collective-permute-done | bytes 401440 | tf_op jit(solution)/shard_map/ppermute | solution.py:444
  97.4 0.1 add.21
  97.5 0.1 collective-permute-start.16
  97.5 0.8 reshape.17
  98.3 0.9 collective-permute-done.16
  99.3 0.1 broadcast_select_fusion.1
  99.3 1.0 pad_maximum_fusion
  (17 shorter events, 0.3 us)
Async XLA Ops:
  0.6 23.5 %copy-start = (f32[2,128,128]{2,1,0:T(8,128)S(1)}, f32[2,128,128]{2,1,0:T(8,128)}, u32[]{:S(2)}) copy-start(f32[2,128,128]{2,1,0:T(8,128)} %inverse_ref.3) | copy-start | bytes 393220
  2.7 5.0 %collective-permute-start = (f32[12,9,2,128]{3,1,0,2:T(8,128)S(1)}, f32[12,9,2,128]{3,1,0,2:T(8,128)S(1)}, u32[]{:S(2)}, u32[]{:S(2)}) collective-permute-start(f32[12,9,2,128]{3,1,0,2:T(8,128)S(1)} %get-tuple-element.49), channel_id=1, source_target_pairs={{1,2},{2,1},{5,6},{6,5},{9,10},{10,9},{13,14},{14,13},{17,18},{18,... | collective-permute-start | bytes 331784 | tf_op jit(solution)/shard_map/ppermute | solution.py:437
  3.4 5.4 %collective-permute-start.1 = (f32[12,9,2,128]{3,1,0,2:T(8,128)S(1)}, f32[12,9,2,128]{3,1,0,2:T(8,128)S(1)}, u32[]{:S(2)}, u32[]{:S(2)}) collective-permute-start(f32[12,9,2,128]{3,1,0,2:T(8,128)S(1)} %get-tuple-element.48), channel_id=1, source_target_pairs={{0,1},{1,0},{2,3},{3,2},{4,5},{5,4},{6,7},{7,6},{8,9},{9,8},{10,11... | collective-permute-start | bytes 331784 | tf_op jit(solution)/shard_map/ppermute | solution.py:437
  10.3 10.2 %collective-permute-start.2 = (f32[6,28,256]{2,1,0:T(8,128)S(1)}, f32[6,28,256]{2,1,0:T(8,128)S(1)}, u32[]{:S(2)}, u32[]{:S(2)}) collective-permute-start(f32[6,28,256]{2,1,0:T(8,128)S(1)} %select_n.83), channel_id=1, source_target_pairs={{4,8},{8,4},{12,16},{16,12},{20,24},{24,20},{5,9},{9,5},{13,17},{1... | collective-permute-start | bytes 516104 | tf_op jit(solution)/shard_map/ppermute | solution.py:437
  11.1 12.9 %collective-permute-start.3 = (f32[6,28,256]{2,1,0:T(8,128)S(1)}, f32[6,28,256]{2,1,0:T(8,128)S(1)}, u32[]{:S(2)}, u32[]{:S(2)}) collective-permute-start(f32[6,28,256]{2,1,0:T(8,128)S(1)} %select_n.85), channel_id=1, source_target_pairs={{0,4},{4,0},{8,12},{12,8},{16,20},{20,16},{24,28},{28,24},{1,5},{5... | collective-permute-start | bytes 516104 | tf_op jit(solution)/shard_map/ppermute | solution.py:437
  15.8 27.2 %collective-permute-start.5 = (f32[2,12,24,128]{3,2,1,0:T(8,128)S(1)}, f32[2,12,24,128]{3,2,1,0:T(8,128)S(1)}, u32[]{:S(2)}, u32[]{:S(2)}) collective-permute-start(f32[2,12,24,128]{3,2,1,0:T(8,128)S(1)} %pad.9.refs_4_), channel_id=1, source_target_pairs={{0,8},{4,12},{8,16},{12,20},{16,24},{20,28},{24,0},{28,4},{1,9},{5... | collective-permute-start | bytes 884744 | tf_op jit(solution)/shard_map/ppermute | solution.py:444
  17.5 25.6 %collective-permute-start.6 = (f32[2,12,24,128]{3,2,1,0:T(8,128)S(1)}, f32[2,12,24,128]{3,2,1,0:T(8,128)S(1)}, u32[]{:S(2)}, u32[]{:S(2)}) collective-permute-start(f32[2,12,24,128]{3,2,1,0:T(8,128)S(1)} %pad.9.refs_4_), channel_id=1, source_target_pairs={{0,16},{4,20},{8,24},{12,28},{16,0},{20,4},{24,8},{28,12},{1,17},{... | collective-permute-start | bytes 884744 | tf_op jit(solution)/shard_map/ppermute | solution.py:444
  18.6 24.5 %collective-permute-start.4 = (f32[2,12,24,128]{3,2,1,0:T(8,128)S(1)}, f32[2,12,24,128]{3,2,1,0:T(8,128)S(1)}, u32[]{:S(2)}, u32[]{:S(2)}) collective-permute-start(f32[2,12,24,128]{3,2,1,0:T(8,128)S(1)} %pad.9.refs_4_), channel_id=1, source_target_pairs={{0,4},{4,0},{8,12},{12,8},{16,20},{20,16},{24,28},{28,24},{1,5},{5... | collective-permute-start | bytes 884744 | tf_op jit(solution)/shard_map/ppermute | solution.py:437
  20.5 34.7 %collective-permute-start.7 = (f32[2,12,24,128]{3,2,1,0:T(8,128)S(1)}, f32[2,12,24,128]{3,2,1,0:T(8,128)S(1)}, u32[]{:S(2)}, u32[]{:S(2)}) collective-permute-start(f32[2,12,24,128]{3,2,1,0:T(8,128)S(1)} %pad.9.refs_4_), channel_id=1, source_target_pairs={{0,24},{4,28},{8,0},{12,4},{16,8},{20,12},{24,16},{28,20},{1,25},{... | collective-permute-start | bytes 884744 | tf_op jit(solution)/shard_map/ppermute | solution.py:444
  43.1 27.0 %collective-permute-start.12 = (f32[2,2,12,24,128]{4,3,2,1,0:T(8,128)S(1)}, f32[2,2,12,24,128]{4,3,2,1,0:T(8,128)S(1)}, u32[]{:S(2)}, u32[]{:S(2)}) collective-permute-start(f32[2,2,12,24,128]{4,3,2,1,0:T(8,128)S(1)} %pad_maximum_fusion.1), channel_id=1, source_target_pairs={{0,4},{4,0},{8,12},{12,8},{16,20},{20,16},{24,28},{28,24},{1,5},{5... | collective-permute-start | bytes 1769480 | tf_op jit(solution)/shard_map/ppermute | solution.py:437
  55.2 14.9 %collective-permute-start.13 = (f32[2,12,24,128]{3,2,1,0:T(8,128)S(1)}, f32[2,12,24,128]{3,2,1,0:T(8,128)S(1)}, u32[]{:S(2)}, u32[]{:S(2)}) collective-permute-start(f32[2,12,24,128]{3,2,1,0:T(8,128)S(1)} %collective-permute-done.7.refs_7_), channel_id=1, source_target_pairs={{0,4},{4,0},{8,12},{12,8},{16,20},{20,16},{24,28},{28,24},{1,5},{5... | collective-permute-start | bytes 884744 | tf_op jit(solution)/shard_map/ppermute | solution.py:437
  55.3 7.1 %collective-permute-start.8 = (f32[2,32,192]{2,1,0:T(8,128)S(1)}, f32[2,32,192]{2,1,0:T(8,128)S(1)}, u32[]{:S(2)}, u32[]{:S(2)}) collective-permute-start(f32[2,32,192]{2,1,0:T(8,128)S(1)} %get-tuple-element.32), channel_id=1, source_target_pairs={{0,8},{4,12},{8,16},{12,20},{16,24},{20,28},{24,0},{28,4},{1,9},{5... | collective-permute-start | bytes 147464 | tf_op jit(solution)/shard_map/ppermute | solution.py:444
  57.3 7.4 %collective-permute-start.9 = (f32[2,32,192]{2,1,0:T(8,128)S(1)}, f32[2,32,192]{2,1,0:T(8,128)S(1)}, u32[]{:S(2)}, u32[]{:S(2)}) collective-permute-start(f32[2,32,192]{2,1,0:T(8,128)S(1)} %get-tuple-element.33), channel_id=1, source_target_pairs={{0,16},{4,20},{8,24},{12,28},{16,0},{20,4},{24,8},{28,12},{1,17},{... | collective-permute-start | bytes 147464 | tf_op jit(solution)/shard_map/ppermute | solution.py:444
  59.9 5.0 %collective-permute-start.10 = (f32[2,32,192]{2,1,0:T(8,128)S(1)}, f32[2,32,192]{2,1,0:T(8,128)S(1)}, u32[]{:S(2)}, u32[]{:S(2)}) collective-permute-start(f32[2,32,192]{2,1,0:T(8,128)S(1)} %get-tuple-element.34), channel_id=1, source_target_pairs={{0,24},{4,28},{8,0},{12,4},{16,8},{20,12},{24,16},{28,20},{1,25},{... | collective-permute-start | bytes 147464 | tf_op jit(solution)/shard_map/ppermute | solution.py:444
  65.0 5.2 %collective-permute-start.11 = (f32[4,32,192]{2,1,0:T(8,128)S(1)}, f32[4,32,192]{2,1,0:T(8,128)S(1)}, u32[]{:S(2)}, u32[]{:S(2)}) collective-permute-start(f32[4,32,192]{2,1,0:T(8,128)S(1)} %pad_maximum_fusion.4), channel_id=1, source_target_pairs={{0,4},{4,0},{8,12},{12,8},{16,20},{20,16},{24,28},{28,24},{1,5},{5... | collective-permute-start | bytes 294920 | tf_op jit(solution)/shard_map/ppermute | solution.py:437
  78.7 1.8 %collective-permute-start.14 = (f32[7,7,2,8,128]{4,3,2,1,0:T(8,128)S(1)}, f32[7,7,2,8,128]{4,3,2,1,0:T(8,128)S(1)}, u32[]{:S(2)}, u32[]{:S(2)}) collective-permute-start(f32[7,7,2,8,128]{4,3,2,1,0:T(8,128)S(1)} %get-tuple-element.39), channel_id=1, source_target_pairs={{0,1},{1,0},{2,3},{3,2},{4,5},{5,4},{6,7},{7,6},{8,9},{9,8},{10,11... | collective-permute-start | bytes 1204232 | tf_op jit(solution)/shard_map/ppermute | solution.py:437
  80.6 16.8 %collective-permute-start.15 = (f32[7,7,2,8,128]{4,3,2,1,0:T(8,128)S(1)}, f32[7,7,2,8,128]{4,3,2,1,0:T(8,128)S(1)}, u32[]{:S(2)}, u32[]{:S(2)}) collective-permute-start(f32[7,7,2,8,128]{4,3,2,1,0:T(8,128)S(1)} %add.20), channel_id=1, source_target_pairs={{0,2},{1,3},{2,0},{3,1},{4,6},{5,7},{6,4},{7,5},{8,10},{9,11},{10,... | collective-permute-start | bytes 1204232 | tf_op jit(solution)/shard_map/ppermute | solution.py:444
  97.5 1.8 %collective-permute-start.16 = (f32[7,7,2,8,128]{4,3,2,1,0:T(8,128)S(1)}, f32[7,7,2,8,128]{4,3,2,1,0:T(8,128)S(1)}, u32[]{:S(2)}, u32[]{:S(2)}) collective-permute-start(f32[7,7,2,8,128]{4,3,2,1,0:T(8,128)S(1)} %add.21), channel_id=1, source_target_pairs={{0,1},{1,0},{2,3},{3,2},{4,5},{5,4},{6,7},{7,6},{8,9},{9,8},{10,11... | collective-permute-start | bytes 1204232 | tf_op jit(solution)/shard_map/ppermute | solution.py:437

commit v4 on v3

--- a/solution.py
+++ b/solution.py
@@ -73,15 +73,13 @@
     blocks_hbm,
     second_ref,
     own_source_ref,
-    high_hbm,
-    low_hbm,
+    w_high,
+    w_low,
     first,
     x_high,
     x_low,
     acc,
     raw,
-    w_high,
-    w_low,
     e_high,
     e_low,
     sems,
@@ -90,16 +88,13 @@
     reach = span // 2
     mid_rows, mid_cols = rows + 2 * reach, cols + 2 * reach
     full_rows = rows + 4 * reach
-    lanes = source_ref.shape[-1]
+    lanes = 2 * source_ref.shape[-1]
+
+    def source_at(i, j):
+        return jnp.concatenate([source_ref[0, i, j, :], source_ref[1, i, j, :]], axis=-1)
 
     def block_copy(a):
-        return pltpu.make_async_copy(blocks_hbm.at[a], raw.at[a], sems.at[0, a])
-
-    def part_copies(a):
-        return (
-            pltpu.make_async_copy(w_high.at[a], high_hbm.at[a], sems.at[1, a]),
-            pltpu.make_async_copy(w_low.at[a], low_hbm.at[a], sems.at[2, a]),
-        )
+        return pltpu.make_async_copy(blocks_hbm.at[a], raw.at[a], sems.at[a])
 
     for a in range(span):
         block_copy(a).start()
@@ -109,14 +104,14 @@
     def invert(value):
         return dot3(split(value), (e_high[...], e_low[...]))
 
-    own_source_ref[...] = source_ref[2 * reach : 2 * reach + rows, pl.ds(2 * reach, cols), :]
+    own_source_ref[...] = source_at(pl.ds(2 * reach, rows), pl.ds(2 * reach, cols))
 
     step_rows = 4
 
     @pl.loop(0, full_rows // step_rows)
     def _(s):
         at = pl.ds(s * step_rows, step_rows)
-        piece = source_ref[at].reshape(step_rows * wide, lanes)
+        piece = source_at(at, pl.ds(0, wide)).reshape(step_rows * wide, lanes)
         first[at] = invert(piece).reshape(step_rows, wide, lanes)
 
     first[full_rows] = jnp.zeros((wide, lanes), f32)
@@ -144,8 +139,6 @@
             store_block(w_high, (a, b), real_high, imag_high)
             store_block(w_low, (a, b), real_low, imag_low)
 
-        for copy in part_copies(a):
-            copy.start()
         at = pl.ds(pl.multiple_of((a // 2) * 2 * pitch, 2 * pitch), mid_rows * pitch)
         acc[...] += products(x_high[a % 2, at, :], x_low[a % 2, at, :], w_high[a], w_low[a])
 
@@ -157,23 +150,18 @@
         count = step_rows * pitch
         flat = pl.ds(pl.multiple_of(s * count, 8), count)
         centre = first[at, pl.ds(reach, pitch), :].reshape(count, lanes)
-        source = source_ref[at, pl.ds(reach, pitch), :].reshape(count, lanes)
+        source = source_at(at, pl.ds(reach, pitch)).reshape(count, lanes)
         value = centre + invert(source - centre - acc[flat, :])
         mask = inside(s * step_rows, step_rows, mid_cols, pitch, reach, rows, cols)
         value = jnp.where(mask, value, 0.0)
         second_ref[pl.ds(s * step_rows, step_rows)] = value.reshape(step_rows, pitch, lanes)
 
-    @pl.loop(0, span)
-    def _(a):
-        for copy in part_copies(a):
-            copy.wait()
-
 
 def first_sweep(source, inverse, lag_blocks, rows, cols):
     span = lag_blocks.shape[0]
     reach = span // 2
-    lanes = source.shape[-1]
-    wide = source.shape[1]
+    lanes = 2 * source.shape[-1]
+    wide = source.shape[2]
     pitch = round_up(cols + 2 * reach, 8)
     full_rows, mid_rows = rows + 4 * reach, rows + 2 * reach
     vmem = pl.BlockSpec(memory_space=pltpu.VMEM)
@@ -182,7 +170,7 @@
     return pl.pallas_call(
         functools.partial(first_sweep_kernel, (rows, cols, span, pitch, wide)),
         in_specs=[vmem, vmem, hbm],
-        out_specs=[vmem, vmem, hbm, hbm],
+        out_specs=[vmem] * 4,
         out_shape=[
             jax.ShapeDtypeStruct((mid_rows, pitch, lanes), f32),
             jax.ShapeDtypeStruct((rows, cols, lanes), f32),
@@ -195,11 +183,9 @@
             pltpu.VMEM((2, full_rows * pitch, span * lanes), bf16),
             pltpu.VMEM((mid_rows * pitch, lanes), f32),
             pltpu.VMEM(lag_blocks.shape, f32),
-            pltpu.VMEM(weights, bf16),
-            pltpu.VMEM(weights, bf16),
             pltpu.VMEM((lanes, lanes), bf16),
             pltpu.VMEM((lanes, lanes), bf16),
-            pltpu.SemaphoreType.DMA((3, span)),
+            pltpu.SemaphoreType.DMA((span,)),
         ],
         cost_estimate=pl.CostEstimate(
             flops=6 * span * span * lanes * lanes * mid_rows * pitch,
@@ -216,29 +202,19 @@
     second_ref,
     source_ref,
     inverse_ref,
-    high_hbm,
-    low_hbm,
+    w_high,
+    w_low,
     adjoint_ref,
     *rest,
 ):
     rows, cols, span, peers = sizes
     sends = rest[: peers // 2]
-    x_high, x_low, acc, turned, w_high, w_low, e_high, e_low, sems = rest[peers // 2 :]
+    x_high, x_low, acc, turned, e_high, e_low = rest[peers // 2 :]
     reach = span // 2
     mid_rows = rows + 2 * reach
     own = rows * cols
     lanes = source_ref.shape[-1]
     width = lanes // 2
-
-    def part_copies(a):
-        return (
-            pltpu.make_async_copy(high_hbm.at[a], w_high.at[a], sems.at[0, a]),
-            pltpu.make_async_copy(low_hbm.at[a], w_low.at[a], sems.at[1, a]),
-        )
-
-    for a in range(span):
-        for copy in part_copies(a):
-            copy.start()
 
     store_inverse(inverse_ref, e_high, e_low)
 
@@ -254,8 +230,6 @@
 
     @pl.loop(0, span)
     def _(a):
-        for copy in part_copies(a):
-            copy.wait()
         at = pl.ds(pl.multiple_of(a * cols, cols), own)
         acc[...] += products(x_high[at, :], x_low[at, :], w_high[a], w_low[a])
 
@@ -282,11 +256,10 @@
     mid_rows = second.shape[0]
     share = lanes // 2 // peers
     vmem = pl.BlockSpec(memory_space=pltpu.VMEM)
-    hbm = pl.BlockSpec(memory_space=pltpu.HBM)
     send = jax.ShapeDtypeStruct((2, 2 * share, rows * cols), f32)
     out = pl.pallas_call(
         functools.partial(second_sweep_kernel, (rows, cols, span, peers)),
-        in_specs=[vmem, vmem, vmem, hbm, hbm],
+        in_specs=[vmem] * 5,
         out_specs=[vmem] * (1 + peers // 2),
         out_shape=[jax.ShapeDtypeStruct((rows, cols, lanes), f32)] + [send] * (peers // 2),
         scratch_shapes=[
@@ -294,11 +267,8 @@
             pltpu.VMEM((mid_rows * cols, span * lanes), bf16),
             pltpu.VMEM((rows * cols, lanes), f32),
             pltpu.VMEM((lanes, rows * cols), f32),
-            pltpu.VMEM(high.shape, bf16),
-            pltpu.VMEM(high.shape, bf16),
             pltpu.VMEM((lanes, lanes), bf16),
             pltpu.VMEM((lanes, lanes), bf16),
-            pltpu.SemaphoreType.DMA((2, span)),
         ],
         cost_estimate=pl.CostEstimate(
             flops=6 * span * span * lanes * lanes * rows * cols,
@@ -446,8 +416,14 @@
 
 def edges(initial, last, axis):
     even = lax.axis_index(axis) % 2 == 0
-    inner = swap(jnp.where(even, last, initial), axis, 0)
+    shape = initial.shape
+    initial, last = (value.reshape(shape[0], -1, shape[-1]) for value in (initial, last))
+    inner = jnp.where(even, last, initial)
     outer = swap(jnp.where(even, initial, last), axis, 1)
+    if axis == "col":
+        inner, outer = lax.optimization_barrier((inner, outer))
+    inner = swap(inner, axis, 0)
+    inner, outer = inner.reshape(shape), outer.reshape(shape)
     return jnp.where(even, outer, inner), jnp.where(even, inner, outer)
 
 
@@ -456,24 +432,22 @@
     span = lag_blocks.shape[0]
     reach = span // 2
     halo = SWEEPS * reach
-    lanes = parts * width
     peers = lax.axis_size("row")
 
-    initial = jnp.concatenate([adjoint_source[:, :halo], saved_currents[:, :reach]], axis=1)
-    last = jnp.concatenate(
-        [adjoint_source[:, cols - halo :], saved_currents[:, cols - reach :]], axis=1
-    )
+    source = adjoint_source.transpose(2, 0, 1, 3)
+    saved = saved_currents.transpose(2, 0, 1, 3)
+    initial = jnp.concatenate([source[:, :, :halo], saved[:, :, :reach]], axis=2)
+    last = jnp.concatenate([source[:, :, cols - halo :], saved[:, :, cols - reach :]], axis=2)
     before, after = edges(initial, last, "col")
-    source = jnp.concatenate([before[:, :halo], adjoint_source, after[:, :halo]], axis=1)
-    source = source.reshape(rows, cols + 2 * halo, lanes)
-    saved = jnp.concatenate([before[:, halo:], saved_currents, after[:, halo:]], axis=1)
-    before, after = edges(source[:halo], source[rows - halo :], "row")
-    source = jnp.concatenate([before, source, after], axis=0)
+    source = jnp.concatenate([before[:, :, :halo], source, after[:, :, :halo]], axis=2)
+    saved = jnp.concatenate([before[:, :, halo:], saved, after[:, :, halo:]], axis=2)
+    before, after = edges(source[:, :halo], source[:, rows - halo :], "row")
+    source = jnp.concatenate([before, source, after], axis=1)
     wide = round_up(cols + 2 * halo, 8)
-    source = jnp.pad(source, ((0, 0), (0, wide - cols - 2 * halo), (0, 0)))
+    source = jnp.pad(source, ((0, 0), (0, 0), (0, wide - cols - 2 * halo), (0, 0)))
 
     pitch = round_up(cols + 2 * reach, 8)
-    saved = jnp.pad(saved.transpose(2, 0, 1, 3), ((0, 0), (0, 0), (0, pitch - cols - 2 * reach), (0, 0)))
+    saved = jnp.pad(saved, ((0, 0), (0, 0), (0, pitch - cols - 2 * reach), (0, 0)))
     pieces = [shifted(saved, "row", k) for k in range(0, peers, 2)]
     own_twin = swap(saved, "row", 0)
 

time: 101 us -> 93.1 us (0.922)
  Pallas kernels: 37 us -> 30.4 us
  starting transfers between devices: 35.2 us -> 34 us
  local copies, waits for them, and re-layouts: 4.46 us -> 3.32 us
    pallas_call x1, Pallas kernels: 18.9 us -> 15.6 us  [first_sweep(): pl.pallas_call(functools.partial(first_sweep_kernel, (rows, cols, span, p...]
    pallas_call x1, Pallas kernels: 9.5 us -> 6.26 us  [second_sweep(): pl.pallas_call(functools.partial(second_sweep_kernel, (rows, cols, span,...]
    ppermute x7, starting transfers between devices: 18.7 us -> 15.5 us  [shifted(): lax.ppermute(value, axis, [(i, (i + shift) % peers) for i in range(peers)])]
    ppermute x10, starting transfers between devices: 16.5 us -> 18.6 us  [swap(): return lax.ppermute(value, axis, pairs)]
    ppermute x7, waiting for transfers between devices: 13.3 us -> 14.9 us  [shifted(): lax.ppermute(value, axis, [(i, (i + shift) % peers) for i in range(peers)])]
    ppermute x10, waiting for transfers between devices: 7.85 us -> 6.61 us  [swap(): return lax.ppermute(value, axis, pairs)]
    unnamed x7 -> x8, local copies, waits for them, and re-layouts: 2.02 us -> 1.98 us
  transfers between devices with their start and end apart: 17 -> 17, of which waited for: 9 -> 9; matrix products, arithmetic and copies ran while one was open for 1% -> 1% of each run, Pallas kernels for 28% -> 24%
where the time goes in v4:
time: 93.1 us; the launch traced here: 91.8 us
  starting transfers between devices  34 us (37%)
  Pallas kernels  30.4 us (33%)
  waiting for transfers between devices  21.5 us (23%)
  local copies, waits for them, and re-layouts  3.32 us (4%)
  other arithmetic  1.58 us (2%)
  between operations  0.94 us (1%)
    ppermute x10, starting transfers between devices, swap(): return lax.ppermute(value, axis, pairs)  18.6 us
    pallas_call x1, Pallas kernels, first_sweep(): pl.pallas_call(functools.partial(first_sweep_kernel, (rows, cols, span, p...  15.6 us
    ppermute x7, starting transfers between devices, shifted(): lax.ppermute(value, axis, [(i, (i + shift) % peers) for i in range(peers)])  15.5 us
    ppermute x7, waiting for transfers between devices, shifted(): lax.ppermute(value, axis, [(i, (i + shift) % peers) for i in range(peers)])  14.9 us
    pallas_call x1, Pallas kernels, correlate(): pl.pallas_call(functools.partial(correlate_kernel, (rows, cols, span, pee...  8.62 us
    ppermute x10, waiting for transfers between devices, swap(): return lax.ppermute(value, axis, pairs)  6.61 us
    pallas_call x1, Pallas kernels, second_sweep(): pl.pallas_call(functools.partial(second_sweep_kernel, (rows, cols, span,...  6.26 us
    unnamed x8, local copies, waits for them, and re-layouts  1.98 us
  transfers between devices with their start and end apart: 17, of which 9 were waited for; matrix products, arithmetic and copies ran while one was open for 1% of the time, Pallas kernels for 24%

profile of v4, /device:TPU:0, one launch (start us, length us, event | category | flops | bytes accessed | tf_op | source)
XLA Modules:
  0.0 91.8 jit_solution(13156467442802141951)
XLA Ops:
  0.6 0.0 copy-start
  0.7 1.0 %copy.27 = f32[12,16,2,128]{3,1,0,2:T(8,128)S(1)} copy(f32[12,16,2,128]{3,2,1,0:T(2,128)} %param.4) | data formatting | bytes 393216 | tf_op args[0]
  1.7 0.9 %copy.26 = f32[12,16,2,128]{3,1,0,2:T(8,128)S(1)} copy(f32[12,16,2,128]{3,2,1,0:T(2,128)} %param.5) | data formatting | bytes 393216 | tf_op args[1]
  2.6 0.1 fusion.5
  2.7 0.1 copy.11
  2.8 0.7 collective-permute-start
  3.5 0.1 copy.10
  3.6 0.0 collective-permute-done
  3.6 6.6 %collective-permute-start.1 = (f32[2,108,128]{2,0,1:T(2,128)S(1)}, f32[2,108,128]{2,0,1:T(2,128)S(1)}, u32[]{:S(2)}, u32[]{:S(2)}) collective-permute-start(f32[2,108,128]{2,0,1:T(2,128)S(1)} %bitcast.42), channel_id=1, source_target_pairs={{0,1},{1,0},{2,3},{3,2},{4,5},{5,4},{6,7},{7,6},{8,9},{9,8},{10,11... | collective-permute-start | bytes 331784 | tf_op jit(solution)/shard_map/ppermute | solution.py:407
  10.2 1.0 %collective-permute-done.1 = f32[2,108,128]{2,0,1:T(2,128)S(1)} collective-permute-done((f32[2,108,128]{2,0,1:T(2,128)S(1)}, f32[2,108,128]{2,0,1:T(2,128)S(1)}, u32[]{:S(2)}, u32[]{:S(2)}) %collective-permute-start.1) | collective-permute-done | bytes 110624 | tf_op jit(solution)/shard_map/ppermute | solution.py:407
  11.2 0.1 pad_maximum_fusion.2
  11.3 0.1 copy.14
  11.5 0.7 collective-permute-start.2
  12.2 0.1 copy.15
  12.3 4.4 %collective-permute-start.3 = (f32[2,168,128]{2,0,1:T(2,128)S(1)}, f32[2,168,128]{2,0,1:T(2,128)S(1)}, u32[]{:S(2)}, u32[]{:S(2)}) collective-permute-start(f32[2,168,128]{2,0,1:T(2,128)S(1)} %bitcast.39), channel_id=1, source_target_pairs={{0,4},{4,0},{8,12},{12,8},{16,20},{20,16},{24,28},{28,24},{1,5},{5... | collective-permute-start | bytes 516104 | tf_op jit(solution)/shard_map/ppermute | solution.py:407
  16.7 0.1 select_maximum_fusion.2.refs_4_
  16.8 1.6 %collective-permute-start.5 = (f32[2,12,24,128]{3,2,1,0:T(8,128)S(1)}, f32[2,12,24,128]{3,2,1,0:T(8,128)S(1)}, u32[]{:S(2)}, u32[]{:S(2)}) collective-permute-start(f32[2,12,24,128]{3,2,1,0:T(8,128)S(1)} %select_maximum_fusion.2.refs_4_), channel_id=1, source_target_pairs={{0,8},{4,12},{8,16},{12,20},{16,24},{20,28},{24,0},{28,4},{1,9},{5... | collective-permute-start | bytes 884744 | tf_op jit(solution)/shard_map/ppermute | solution.py:414
  18.4 1.1 %collective-permute-start.6 = (f32[2,12,24,128]{3,2,1,0:T(8,128)S(1)}, f32[2,12,24,128]{3,2,1,0:T(8,128)S(1)}, u32[]{:S(2)}, u32[]{:S(2)}) collective-permute-start(f32[2,12,24,128]{3,2,1,0:T(8,128)S(1)} %select_maximum_fusion.2.refs_4_), channel_id=1, source_target_pairs={{0,16},{4,20},{8,24},{12,28},{16,0},{20,4},{24,8},{28,12},{1,17},{... | collective-permute-start | bytes 884744 | tf_op jit(solution)/shard_map/ppermute | solution.py:414
  19.5 1.9 %collective-permute-start.4 = (f32[2,12,24,128]{3,2,1,0:T(8,128)S(1)}, f32[2,12,24,128]{3,2,1,0:T(8,128)S(1)}, u32[]{:S(2)}, u32[]{:S(2)}) collective-permute-start(f32[2,12,24,128]{3,2,1,0:T(8,128)S(1)} %select_maximum_fusion.2.refs_4_), channel_id=1, source_target_pairs={{0,4},{4,0},{8,12},{12,8},{16,20},{20,16},{24,28},{28,24},{1,5},{5... | collective-permute-start | bytes 884744 | tf_op jit(solution)/shard_map/ppermute | solution.py:407
  21.4 0.0 collective-permute-done.2
  21.4 3.7 %collective-permute-start.7 = (f32[2,12,24,128]{3,2,1,0:T(8,128)S(1)}, f32[2,12,24,128]{3,2,1,0:T(8,128)S(1)}, u32[]{:S(2)}, u32[]{:S(2)}) collective-permute-start(f32[2,12,24,128]{3,2,1,0:T(8,128)S(1)} %select_maximum_fusion.2.refs_4_), channel_id=1, source_target_pairs={{0,24},{4,28},{8,0},{12,4},{16,8},{20,12},{24,16},{28,20},{1,25},{... | collective-permute-start | bytes 884744 | tf_op jit(solution)/shard_map/ppermute | solution.py:414
  25.1 0.0 collective-permute-done.3
  25.2 0.1 select_maximum_fusion.source_ref
  25.3 0.0 copy-done
  25.3 15.6 %first_sweep.1 = (f32[18,24,256]{2,1,0:T(8,128)S(1)}, f32[12,16,256]{2,1,0:T(8,128)S(1)}, bf16[7,7,256,256]{3,2,1,0:T(8,128)(2,1)S(1)}, bf16[7,7,256,256]{3,2,1,0:T(8,128)(2,1)S(1)}) custom-call(f32[2,24,32,128]{3,2,1,0:T(8,128)S(1)} %select_maximum_fusion.source_ref, f32[2,128,128]{2,1,0:T(8,128)S(1)} %copy-done, f32[7,7,2,128,128]{4,3,2,1,0:T(8,128)} %blocks_hbm.1), custom_call_target="tpu_custom_call" | custom-call | flops 8323596288 | bytes 19267584 | tf_op jit(solution)/shard_map/first_sweep/pallas_call | solution.py:170
  40.9 0.0 collective-permute-done.5.refs_5_
  40.9 0.8 collective-permute-done.6.refs_6_
  41.8 0.0 collective-permute-done.4.refs_9_
  41.8 0.3 collective-permute-start.12
  42.1 6.3 %second_sweep.1 = (f32[12,16,256]{2,1,0:T(8,128)S(1)}, f32[2,32,192]{2,1,0:T(8,128)S(1)}, f32[2,32,192]{2,1,0:T(8,128)S(1)}, f32[2,32,192]{2,1,0:T(8,128)S(1)}, f32[2,32,192]{2,1,0:T(8,128)S(1)}) custom-call(f32[18,24,256]{2,1,0:T(8,128)S(1)} %get-tuple-element.26.second_ref, f32[12,16,256]{2,1,0:T(8,128)S(1)} %get-tuple-element.27.source_ref, ...), custom_call_target="tpu_custom_call" | custom-call | flops 3699376128 | bytes 12845056 | tf_op jit(solution)/shard_map/second_sweep/pallas_call | solution.py:260
  48.4 0.0 collective-permute-done.7.refs_7_
  48.4 1.8 %collective-permute-start.13 = (f32[2,12,24,128]{3,2,1,0:T(8,128)S(1)}, f32[2,12,24,128]{3,2,1,0:T(8,128)S(1)}, u32[]{:S(2)}, u32[]{:S(2)}) collective-permute-start(f32[2,12,24,128]{3,2,1,0:T(8,128)S(1)} %collective-permute-done.7.refs_7_), channel_id=1, source_target_pairs={{0,4},{4,0},{8,12},{12,8},{16,20},{20,16},{24,28},{28,24},{1,5},{5... | collective-permute-start | bytes 884744 | tf_op jit(solution)/shard_map/ppermute | solution.py:407
  50.2 3.8 %collective-permute-start.8 = (f32[2,32,192]{2,1,0:T(8,128)S(1)}, f32[2,32,192]{2,1,0:T(8,128)S(1)}, u32[]{:S(2)}, u32[]{:S(2)}) collective-permute-start(f32[2,32,192]{2,1,0:T(8,128)S(1)} %get-tuple-element.36), channel_id=1, source_target_pairs={{0,8},{4,12},{8,16},{12,20},{16,24},{20,28},{24,0},{28,4},{1,9},{5... | collective-permute-start | bytes 147464 | tf_op jit(solution)/shard_map/ppermute | solution.py:414
  54.0 3.4 %collective-permute-start.9 = (f32[2,32,192]{2,1,0:T(8,128)S(1)}, f32[2,32,192]{2,1,0:T(8,128)S(1)}, u32[]{:S(2)}, u32[]{:S(2)}) collective-permute-start(f32[2,32,192]{2,1,0:T(8,128)S(1)} %get-tuple-element.37), channel_id=1, source_target_pairs={{0,16},{4,20},{8,24},{12,28},{16,0},{20,4},{24,8},{28,12},{1,17},{... | collective-permute-start | bytes 147464 | tf_op jit(solution)/shard_map/ppermute | solution.py:414
  57.4 0.0 collective-permute-start.10
  57.4 2.4 %collective-permute-done.8.refs_1_ = f32[2,32,192]{2,1,0:T(8,128)S(1)} collective-permute-done((f32[2,32,192]{2,1,0:T(8,128)S(1)}, f32[2,32,192]{2,1,0:T(8,128)S(1)}, u32[]{:S(2)}, u32[]{:S(2)}) %collective-permute-start.8) | collective-permute-done | bytes 49184 | tf_op jit(solution)/shard_map/ppermute | solution.py:414
  59.8 1.6 %collective-permute-done.9.refs_2_ = f32[2,32,192]{2,1,0:T(8,128)S(1)} collective-permute-done((f32[2,32,192]{2,1,0:T(8,128)S(1)}, f32[2,32,192]{2,1,0:T(8,128)S(1)}, u32[]{:S(2)}, u32[]{:S(2)}) %collective-permute-start.9) | collective-permute-done | bytes 49184 | tf_op jit(solution)/shard_map/ppermute | solution.py:414
  61.4 0.5 collective-permute-done.10.refs_3_
  61.9 2.1 %collective-permute-start.11 = (f32[4,32,192]{2,1,0:T(8,128)S(1)}, f32[4,32,192]{2,1,0:T(8,128)S(1)}, u32[]{:S(2)}, u32[]{:S(2)}) collective-permute-start(f32[4,32,192]{2,1,0:T(8,128)S(1)} %pad_maximum_fusion.5), channel_id=1, source_target_pairs={{0,4},{4,0},{8,12},{12,8},{16,20},{20,16},{24,28},{28,24},{1,5},{5... | collective-permute-start | bytes 294920 | tf_op jit(solution)/shard_map/ppermute | solution.py:407
  64.0 3.0 %collective-permute-done.11.refs_8_ = f32[4,32,192]{2,1,0:T(8,128)S(1)} collective-permute-done((f32[4,32,192]{2,1,0:T(8,128)S(1)}, f32[4,32,192]{2,1,0:T(8,128)S(1)}, u32[]{:S(2)}, u32[]{:S(2)}) %collective-permute-start.11) | collective-permute-done | bytes 98336 | tf_op jit(solution)/shard_map/ppermute | solution.py:407
  66.9 0.0 collective-permute-done.13.refs_11_
  66.9 0.0 collective-permute-done.12.refs_10_
  67.0 8.6 %correlate.1 = (f32[7,7,2,8,128]{4,3,2,1,0:T(8,128)S(1)}, f32[7,7,2,8,128]{4,3,2,1,0:T(8,128)S(1)}) custom-call(f32[2,32,192]{2,1,0:T(8,128)S(1)} %get-tuple-element.35.refs_0_, f32[2,32,192]{2,1,0:T(8,128)S(1)} %collective-permute-done.8.refs_1_, f32[2,32,192]{2,1,0:T(8,128)S(1)} %collective-permute-done.9.refs_2_, ...), custom_call_target="tpu_custom_call" | custom-call | flops 3699376128 | bytes 3162112 | tf_op jit(solution)/shard_map/correlate/pallas_call | solution.py:376
  75.6 0.1 collective-permute-start.14
  75.7 1.7 %collective-permute-done.14 = f32[7,7,2,8,128]{4,3,2,1,0:T(8,128)S(1)} collective-permute-done((f32[7,7,2,8,128]{4,3,2,1,0:T(8,128)S(1)}, f32[7,7,2,8,128]{4,3,2,1,0:T(8,128)S(1)}, u32[]{:S(2)}, u32[]{:S(2)}) %collective-permute-start.14) | collective-permute-done | bytes 401440 | tf_op jit(solution)/shard_map/ppermute | solution.py:407
  77.4 0.1 add.20
  77.5 1.9 %collective-permute-start.15 = (f32[7,7,2,8,128]{4,3,2,1,0:T(8,128)S(1)}, f32[7,7,2,8,128]{4,3,2,1,0:T(8,128)S(1)}, u32[]{:S(2)}, u32[]{:S(2)}) collective-permute-start(f32[7,7,2,8,128]{4,3,2,1,0:T(8,128)S(1)} %add.20), channel_id=1, source_target_pairs={{0,2},{1,3},{2,0},{3,1},{4,6},{5,7},{6,4},{7,5},{8,10},{9,11},{10,... | collective-permute-start | bytes 1204232 | tf_op jit(solution)/shard_map/ppermute | solution.py:414
  79.3 9.6 %collective-permute-done.15 = f32[7,7,2,8,128]{4,3,2,1,0:T(8,128)S(1)} collective-permute-done((f32[7,7,2,8,128]{4,3,2,1,0:T(8,128)S(1)}, f32[7,7,2,8,128]{4,3,2,1,0:T(8,128)S(1)}, u32[]{:S(2)}, u32[]{:S(2)}) %collective-permute-start.15) | collective-permute-done | bytes 401440 | tf_op jit(solution)/shard_map/ppermute | solution.py:414
  88.9 0.1 add.21
  89.0 0.1 collective-permute-start.16
  89.1 0.8 reshape.31
  89.8 0.9 %collective-permute-done.16 = f32[7,7,2,8,128]{4,3,2,1,0:T(8,128)S(1)} collective-permute-done((f32[7,7,2,8,128]{4,3,2,1,0:T(8,128)S(1)}, f32[7,7,2,8,128]{4,3,2,1,0:T(8,128)S(1)}, u32[]{:S(2)}, u32[]{:S(2)}) %collective-permute-start.16) | collective-permute-done | bytes 401440 | tf_op jit(solution)/shard_map/ppermute | solution.py:407
  90.8 0.1 broadcast_select_fusion.1
  90.8 1.0 %pad_maximum_fusion = f32[7,7,2,16,128]{4,3,2,1,0:T(8,128)} fusion(f32[7,7,2,8,128]{4,3,2,1,0:T(8,128)S(1)} %get-tuple-element.45, f32[7,7,2,8,128]{4,3,2,1,0:T(8,128)S(1)} %get-tuple-element.44), kind=kLoop, calls=%fused_computation | loop fusion | flops 200704 | bytes 1605632 | tf_op jit(solution)/shard_map/concatenate | solution.py:474
  (21 shorter events, 0.3 us)
Async XLA Ops:
  0.6 24.7 %copy-start = (f32[2,128,128]{2,1,0:T(8,128)S(1)}, f32[2,128,128]{2,1,0:T(8,128)}, u32[]{:S(2)}) copy-start(f32[2,128,128]{2,1,0:T(8,128)} %inverse_ref.3) | copy-start | bytes 393220
  2.8 0.8 collective-permute-start
  3.6 7.6 %collective-permute-start.1 = (f32[2,108,128]{2,0,1:T(2,128)S(1)}, f32[2,108,128]{2,0,1:T(2,128)S(1)}, u32[]{:S(2)}, u32[]{:S(2)}) collective-permute-start(f32[2,108,128]{2,0,1:T(2,128)S(1)} %bitcast.42), channel_id=1, source_target_pairs={{0,1},{1,0},{2,3},{3,2},{4,5},{5,4},{6,7},{7,6},{8,9},{9,8},{10,11... | collective-permute-start | bytes 331784 | tf_op jit(solution)/shard_map/ppermute | solution.py:407
  11.5 9.9 %collective-permute-start.2 = (f32[2,168,128]{2,0,1:T(2,128)S(1)}, f32[2,168,128]{2,0,1:T(2,128)S(1)}, u32[]{:S(2)}, u32[]{:S(2)}) collective-permute-start(f32[2,168,128]{2,0,1:T(2,128)S(1)} %bitcast.40), channel_id=1, source_target_pairs={{4,8},{8,4},{12,16},{16,12},{20,24},{24,20},{5,9},{9,5},{13,17},{1... | collective-permute-start | bytes 516104 | tf_op jit(solution)/shard_map/ppermute | solution.py:407
  12.3 12.8 %collective-permute-start.3 = (f32[2,168,128]{2,0,1:T(2,128)S(1)}, f32[2,168,128]{2,0,1:T(2,128)S(1)}, u32[]{:S(2)}, u32[]{:S(2)}) collective-permute-start(f32[2,168,128]{2,0,1:T(2,128)S(1)} %bitcast.39), channel_id=1, source_target_pairs={{0,4},{4,0},{8,12},{12,8},{16,20},{20,16},{24,28},{28,24},{1,5},{5... | collective-permute-start | bytes 516104 | tf_op jit(solution)/shard_map/ppermute | solution.py:407
  16.8 24.1 %collective-permute-start.5 = (f32[2,12,24,128]{3,2,1,0:T(8,128)S(1)}, f32[2,12,24,128]{3,2,1,0:T(8,128)S(1)}, u32[]{:S(2)}, u32[]{:S(2)}) collective-permute-start(f32[2,12,24,128]{3,2,1,0:T(8,128)S(1)} %select_maximum_fusion.2.refs_4_), channel_id=1, source_target_pairs={{0,8},{4,12},{8,16},{12,20},{16,24},{20,28},{24,0},{28,4},{1,9},{5... | collective-permute-start | bytes 884744 | tf_op jit(solution)/shard_map/ppermute | solution.py:414
  18.4 23.3 %collective-permute-start.6 = (f32[2,12,24,128]{3,2,1,0:T(8,128)S(1)}, f32[2,12,24,128]{3,2,1,0:T(8,128)S(1)}, u32[]{:S(2)}, u32[]{:S(2)}) collective-permute-start(f32[2,12,24,128]{3,2,1,0:T(8,128)S(1)} %select_maximum_fusion.2.refs_4_), channel_id=1, source_target_pairs={{0,16},{4,20},{8,24},{12,28},{16,0},{20,4},{24,8},{28,12},{1,17},{... | collective-permute-start | bytes 884744 | tf_op jit(solution)/shard_map/ppermute | solution.py:414
  19.5 22.3 %collective-permute-start.4 = (f32[2,12,24,128]{3,2,1,0:T(8,128)S(1)}, f32[2,12,24,128]{3,2,1,0:T(8,128)S(1)}, u32[]{:S(2)}, u32[]{:S(2)}) collective-permute-start(f32[2,12,24,128]{3,2,1,0:T(8,128)S(1)} %select_maximum_fusion.2.refs_4_), channel_id=1, source_target_pairs={{0,4},{4,0},{8,12},{12,8},{16,20},{20,16},{24,28},{28,24},{1,5},{5... | collective-permute-start | bytes 884744 | tf_op jit(solution)/shard_map/ppermute | solution.py:407
  21.4 27.0 %collective-permute-start.7 = (f32[2,12,24,128]{3,2,1,0:T(8,128)S(1)}, f32[2,12,24,128]{3,2,1,0:T(8,128)S(1)}, u32[]{:S(2)}, u32[]{:S(2)}) collective-permute-start(f32[2,12,24,128]{3,2,1,0:T(8,128)S(1)} %select_maximum_fusion.2.refs_4_), channel_id=1, source_target_pairs={{0,24},{4,28},{8,0},{12,4},{16,8},{20,12},{24,16},{28,20},{1,25},{... | collective-permute-start | bytes 884744 | tf_op jit(solution)/shard_map/ppermute | solution.py:414
  41.8 25.1 %collective-permute-start.12 = (f32[2,2,12,24,128]{4,3,2,1,0:T(8,128)S(1)}, f32[2,2,12,24,128]{4,3,2,1,0:T(8,128)S(1)}, u32[]{:S(2)}, u32[]{:S(2)}) collective-permute-start(f32[2,2,12,24,128]{4,3,2,1,0:T(8,128)S(1)} %pad_maximum_fusion.1), channel_id=1, source_target_pairs={{0,4},{4,0},{8,12},{12,8},{16,20},{20,16},{24,28},{28,24},{1,5},{5... | collective-permute-start | bytes 1769480 | tf_op jit(solution)/shard_map/ppermute | solution.py:407
  48.4 18.5 %collective-permute-start.13 = (f32[2,12,24,128]{3,2,1,0:T(8,128)S(1)}, f32[2,12,24,128]{3,2,1,0:T(8,128)S(1)}, u32[]{:S(2)}, u32[]{:S(2)}) collective-permute-start(f32[2,12,24,128]{3,2,1,0:T(8,128)S(1)} %collective-permute-done.7.refs_7_), channel_id=1, source_target_pairs={{0,4},{4,0},{8,12},{12,8},{16,20},{20,16},{24,28},{28,24},{1,5},{5... | collective-permute-start | bytes 884744 | tf_op jit(solution)/shard_map/ppermute | solution.py:407
  50.2 9.6 %collective-permute-start.8 = (f32[2,32,192]{2,1,0:T(8,128)S(1)}, f32[2,32,192]{2,1,0:T(8,128)S(1)}, u32[]{:S(2)}, u32[]{:S(2)}) collective-permute-start(f32[2,32,192]{2,1,0:T(8,128)S(1)} %get-tuple-element.36), channel_id=1, source_target_pairs={{0,8},{4,12},{8,16},{12,20},{16,24},{20,28},{24,0},{28,4},{1,9},{5... | collective-permute-start | bytes 147464 | tf_op jit(solution)/shard_map/ppermute | solution.py:414
  54.0 7.4 %collective-permute-start.9 = (f32[2,32,192]{2,1,0:T(8,128)S(1)}, f32[2,32,192]{2,1,0:T(8,128)S(1)}, u32[]{:S(2)}, u32[]{:S(2)}) collective-permute-start(f32[2,32,192]{2,1,0:T(8,128)S(1)} %get-tuple-element.37), channel_id=1, source_target_pairs={{0,16},{4,20},{8,24},{12,28},{16,0},{20,4},{24,8},{28,12},{1,17},{... | collective-permute-start | bytes 147464 | tf_op jit(solution)/shard_map/ppermute | solution.py:414
  57.4 4.5 %collective-permute-start.10 = (f32[2,32,192]{2,1,0:T(8,128)S(1)}, f32[2,32,192]{2,1,0:T(8,128)S(1)}, u32[]{:S(2)}, u32[]{:S(2)}) collective-permute-start(f32[2,32,192]{2,1,0:T(8,128)S(1)} %get-tuple-element.38), channel_id=1, source_target_pairs={{0,24},{4,28},{8,0},{12,4},{16,8},{20,12},{24,16},{28,20},{1,25},{... | collective-permute-start | bytes 147464 | tf_op jit(solution)/shard_map/ppermute | solution.py:414
  61.9 5.0 %collective-permute-start.11 = (f32[4,32,192]{2,1,0:T(8,128)S(1)}, f32[4,32,192]{2,1,0:T(8,128)S(1)}, u32[]{:S(2)}, u32[]{:S(2)}) collective-permute-start(f32[4,32,192]{2,1,0:T(8,128)S(1)} %pad_maximum_fusion.5), channel_id=1, source_target_pairs={{0,4},{4,0},{8,12},{12,8},{16,20},{20,16},{24,28},{28,24},{1,5},{5... | collective-permute-start | bytes 294920 | tf_op jit(solution)/shard_map/ppermute | solution.py:407
  75.6 1.8 %collective-permute-start.14 = (f32[7,7,2,8,128]{4,3,2,1,0:T(8,128)S(1)}, f32[7,7,2,8,128]{4,3,2,1,0:T(8,128)S(1)}, u32[]{:S(2)}, u32[]{:S(2)}) collective-permute-start(f32[7,7,2,8,128]{4,3,2,1,0:T(8,128)S(1)} %get-tuple-element.43), channel_id=1, source_target_pairs={{0,1},{1,0},{2,3},{3,2},{4,5},{5,4},{6,7},{7,6},{8,9},{9,8},{10,11... | collective-permute-start | bytes 1204232 | tf_op jit(solution)/shard_map/ppermute | solution.py:407
  77.5 11.5 %collective-permute-start.15 = (f32[7,7,2,8,128]{4,3,2,1,0:T(8,128)S(1)}, f32[7,7,2,8,128]{4,3,2,1,0:T(8,128)S(1)}, u32[]{:S(2)}, u32[]{:S(2)}) collective-permute-start(f32[7,7,2,8,128]{4,3,2,1,0:T(8,128)S(1)} %add.20), channel_id=1, source_target_pairs={{0,2},{1,3},{2,0},{3,1},{4,6},{5,7},{6,4},{7,5},{8,10},{9,11},{10,... | collective-permute-start | bytes 1204232 | tf_op jit(solution)/shard_map/ppermute | solution.py:414
  89.0 1.8 %collective-permute-start.16 = (f32[7,7,2,8,128]{4,3,2,1,0:T(8,128)S(1)}, f32[7,7,2,8,128]{4,3,2,1,0:T(8,128)S(1)}, u32[]{:S(2)}, u32[]{:S(2)}) collective-permute-start(f32[7,7,2,8,128]{4,3,2,1,0:T(8,128)S(1)} %add.21), channel_id=1, source_target_pairs={{0,1},{1,0},{2,3},{3,2},{4,5},{5,4},{6,7},{7,6},{8,9},{9,8},{10,11... | collective-permute-start | bytes 1204232 | tf_op jit(solution)/shard_map/ppermute | solution.py:407

commit v5 on v4

--- a/solution.py
+++ b/solution.py
@@ -66,23 +66,62 @@
     return dot(high, weight_high) + dot(low, weight_high) + dot(high, weight_low)
 
 
+def weights_kernel(blocks_hbm, w_high, w_low, raw, sems):
+    span = blocks_hbm.shape[0]
+
+    def block_copy(a):
+        return pltpu.make_async_copy(blocks_hbm.at[a], raw.at[a], sems.at[a])
+
+    for a in range(span):
+        block_copy(a).start()
+
+    @pl.loop(0, span)
+    def _(a):
+        block_copy(a).wait()
+
+        @pl.loop(0, span)
+        def _(b):
+            real_high, real_low = split(raw[a, b, 0])
+            imag_high, imag_low = split(raw[a, b, 1])
+            store_block(w_high, (a, b), real_high, imag_high)
+            store_block(w_low, (a, b), real_low, imag_low)
+
+
+def prepare_weights(lag_blocks):
+    span, _, parts, width, _ = lag_blocks.shape
+    vmem = pl.BlockSpec(memory_space=pltpu.VMEM)
+    out = jax.ShapeDtypeStruct((span, span, parts * width, parts * width), bf16)
+    return pl.pallas_call(
+        weights_kernel,
+        in_specs=[pl.BlockSpec(memory_space=pltpu.HBM)],
+        out_specs=[vmem, vmem],
+        out_shape=[out, out],
+        scratch_shapes=[
+            pltpu.VMEM(lag_blocks.shape, f32),
+            pltpu.SemaphoreType.DMA((span,)),
+        ],
+        cost_estimate=pl.CostEstimate(
+            flops=0, bytes_accessed=4 * lag_blocks.size, transcendentals=0
+        ),
+        compiler_params=pltpu.CompilerParams(vmem_limit_bytes=28 * 1024 * 1024),
+        name="weights",
+    )(lag_blocks)
+
+
 def first_sweep_kernel(
     sizes,
     source_ref,
     inverse_ref,
-    blocks_hbm,
+    w_high,
+    w_low,
     second_ref,
     own_source_ref,
-    w_high,
-    w_low,
     first,
     x_high,
     x_low,
     acc,
-    raw,
     e_high,
     e_low,
-    sems,
 ):
     rows, cols, span, pitch, wide = sizes
     reach = span // 2
@@ -92,12 +131,6 @@
 
     def source_at(i, j):
         return jnp.concatenate([source_ref[0, i, j, :], source_ref[1, i, j, :]], axis=-1)
-
-    def block_copy(a):
-        return pltpu.make_async_copy(blocks_hbm.at[a], raw.at[a], sems.at[a])
-
-    for a in range(span):
-        block_copy(a).start()
 
     store_inverse(inverse_ref, e_high, e_low)
 
@@ -130,15 +163,6 @@
 
     @pl.loop(0, span)
     def _(a):
-        block_copy(a).wait()
-
-        @pl.loop(0, span)
-        def _(b):
-            real_high, real_low = split(raw[a, b, 0])
-            imag_high, imag_low = split(raw[a, b, 1])
-            store_block(w_high, (a, b), real_high, imag_high)
-            store_block(w_low, (a, b), real_low, imag_low)
-
         at = pl.ds(pl.multiple_of((a // 2) * 2 * pitch, 2 * pitch), mid_rows * pitch)
         acc[...] += products(x_high[a % 2, at, :], x_low[a % 2, at, :], w_high[a], w_low[a])
 
@@ -157,44 +181,38 @@
         second_ref[pl.ds(s * step_rows, step_rows)] = value.reshape(step_rows, pitch, lanes)
 
 
-def first_sweep(source, inverse, lag_blocks, rows, cols):
-    span = lag_blocks.shape[0]
+def first_sweep(source, inverse, high, low, rows, cols):
+    span = high.shape[0]
     reach = span // 2
     lanes = 2 * source.shape[-1]
     wide = source.shape[2]
     pitch = round_up(cols + 2 * reach, 8)
     full_rows, mid_rows = rows + 4 * reach, rows + 2 * reach
     vmem = pl.BlockSpec(memory_space=pltpu.VMEM)
-    hbm = pl.BlockSpec(memory_space=pltpu.HBM)
-    weights = (span, span, lanes, lanes)
     return pl.pallas_call(
         functools.partial(first_sweep_kernel, (rows, cols, span, pitch, wide)),
-        in_specs=[vmem, vmem, hbm],
-        out_specs=[vmem] * 4,
+        in_specs=[vmem] * 4,
+        out_specs=[vmem] * 2,
         out_shape=[
             jax.ShapeDtypeStruct((mid_rows, pitch, lanes), f32),
             jax.ShapeDtypeStruct((rows, cols, lanes), f32),
-            jax.ShapeDtypeStruct(weights, bf16),
-            jax.ShapeDtypeStruct(weights, bf16),
         ],
         scratch_shapes=[
             pltpu.VMEM((full_rows + 1, wide, lanes), f32),
             pltpu.VMEM((2, full_rows * pitch, span * lanes), bf16),
             pltpu.VMEM((2, full_rows * pitch, span * lanes), bf16),
             pltpu.VMEM((mid_rows * pitch, lanes), f32),
-            pltpu.VMEM(lag_blocks.shape, f32),
             pltpu.VMEM((lanes, lanes), bf16),
             pltpu.VMEM((lanes, lanes), bf16),
-            pltpu.SemaphoreType.DMA((span,)),
         ],
         cost_estimate=pl.CostEstimate(
             flops=6 * span * span * lanes * lanes * mid_rows * pitch,
-            bytes_accessed=12 * lag_blocks.size,
+            bytes_accessed=4 * high.size,
             transcendentals=0,
         ),
         compiler_params=pltpu.CompilerParams(vmem_limit_bytes=40 * 1024 * 1024),
         name="first_sweep",
-    )(source, inverse, lag_blocks)
+    )(source, inverse, high, low)
 
 
 def second_sweep_kernel(
@@ -302,10 +320,7 @@
         return base + 1 - odd, base + odd
 
     for k in range(half_peers):
-        if k == 0:
-            twin = own_twin_ref
-        else:
-            twin = late_ref if k == half_peers - 1 else early_ref.at[k - 1]
+        twin = (own_twin_ref, early_ref)[k] if k < 2 else late_ref.at[k - 2]
         for n, (source, tile) in enumerate(zip((piece_refs[k], twin), tiles(k))):
             pltpu.make_async_copy(source, stage.at[tile], sems.at[n, k]).start()
         first, second = tiles(k)
@@ -414,17 +429,17 @@
     return lax.ppermute(value, axis, [(i, (i + shift) % peers) for i in range(peers)])
 
 
-def edges(initial, last, axis):
+def edges(initial, last, axis, beside=()):
     even = lax.axis_index(axis) % 2 == 0
     shape = initial.shape
     initial, last = (value.reshape(shape[0], -1, shape[-1]) for value in (initial, last))
     inner = jnp.where(even, last, initial)
     outer = swap(jnp.where(even, initial, last), axis, 1)
-    if axis == "col":
-        inner, outer = lax.optimization_barrier((inner, outer))
+    if beside:
+        inner, outer, beside = lax.optimization_barrier((inner, outer, beside))
     inner = swap(inner, axis, 0)
     inner, outer = inner.reshape(shape), outer.reshape(shape)
-    return jnp.where(even, outer, inner), jnp.where(even, inner, outer)
+    return jnp.where(even, outer, inner), jnp.where(even, inner, outer), beside or inner
 
 
 def on_device(adjoint_source, saved_currents, lag_blocks, element_inverse):
@@ -438,10 +453,11 @@
     saved = saved_currents.transpose(2, 0, 1, 3)
     initial = jnp.concatenate([source[:, :, :halo], saved[:, :, :reach]], axis=2)
     last = jnp.concatenate([source[:, :, cols - halo :], saved[:, :, cols - reach :]], axis=2)
-    before, after = edges(initial, last, "col")
+    weights = prepare_weights(lag_blocks)
+    before, after, (high, low) = edges(initial, last, "col", tuple(weights))
     source = jnp.concatenate([before[:, :, :halo], source, after[:, :, :halo]], axis=2)
     saved = jnp.concatenate([before[:, :, halo:], saved, after[:, :, halo:]], axis=2)
-    before, after = edges(source[:, :halo], source[:, rows - halo :], "row")
+    before, after, arrived = edges(source[:, :halo], source[:, rows - halo :], "row")
     source = jnp.concatenate([before, source, after], axis=1)
     wide = round_up(cols + 2 * halo, 8)
     source = jnp.pad(source, ((0, 0), (0, 0), (0, wide - cols - 2 * halo), (0, 0)))
@@ -449,21 +465,21 @@
     pitch = round_up(cols + 2 * reach, 8)
     saved = jnp.pad(saved, ((0, 0), (0, 0), (0, pitch - cols - 2 * reach), (0, 0)))
     pieces = [shifted(saved, "row", k) for k in range(0, peers, 2)]
-    own_twin = swap(saved, "row", 0)
-
-    second, own_source, high, low = first_sweep(source, element_inverse, lag_blocks, rows, cols)
-    second, own_twin, early = lax.optimization_barrier((second, own_twin, jnp.stack(pieces[1:-1])))
-    early_twins = swap(early, "row", 0)
+    own_twin = swap(lax.optimization_barrier((saved, arrived))[0], "row", 0)
+
+    second, own_source = first_sweep(source, element_inverse, high, low, rows, cols)
+    second, own_twin, early = lax.optimization_barrier((second, own_twin, pieces[1]))
+    early_twin = swap(early, "row", 0)
     adjoint, sends = second_sweep(second, own_source, element_inverse, high, low, peers)
-    late, sends = lax.optimization_barrier((pieces[-1], sends))
-    late_twin = swap(late, "row", 0)
+    *late, early_twin, sends = lax.optimization_barrier((*pieces[2:], early_twin, sends))
+    late_twins = swap(jnp.stack(late), "row", 0)
     shares = [shifted(send, "row", 2 * k) for k, send in enumerate(sends)]
     twin_shares = swap(jnp.stack([received[1] for received in shares]), "row", 0)
 
     elements = rows * peers * cols * lax.axis_size("col")
     factor = -1.0 / math.sqrt(elements)
     mine, other = correlate(
-        shares, twin_shares, pieces, (own_twin, early_twins, late_twin), rows, cols, span, factor
+        shares, twin_shares, pieces, (own_twin, early_twin, late_twins), rows, cols, span, factor
     )
     mine = mine + swap(other, "col", 0)
     total = mine

time: 93.1 us -> 101 us (1.085); the launches traced: 91.8 us -> 101 us
  local copies, waits for them, and re-layouts: 3.32 us -> 17.1 us
  starting transfers between devices: 34 us -> 25.9 us
  waiting for transfers between devices: 21.5 us -> 23.4 us
  Pallas kernels: 30.4 us -> 32.1 us
    unnamed x8 -> x20, local copies, waits for them, and re-layouts: 1.98 us -> 15.8 us
    ppermute x10, starting transfers between devices: 18.6 us -> 13.6 us  [swap(): return lax.ppermute(value, axis, pairs)]
    pallas_call x0 -> x1, Pallas kernels: none -> 3.48 us  [prepare_weights(): pl.pallas_call(weights_kernel, in_specs=[pl.BlockSpec(memory_space=pltpu....]
    ppermute x7, starting transfers between devices: 15.5 us -> 12.3 us  [shifted(): lax.ppermute(value, axis, [(i, (i + shift) % peers) for i in range(peers)])]
    pallas_call x1, Pallas kernels: 15.6 us -> 13.7 us  [first_sweep(): pl.pallas_call(functools.partial(first_sweep_kernel, (rows, cols, span, p...]
    ppermute x7, waiting for transfers between devices: 14.9 us -> 16.1 us  [shifted(): lax.ppermute(value, axis, [(i, (i + shift) % peers) for i in range(peers)])]
  transfers between devices with their start and end apart: 17 -> 17, of which waited for: 9 -> 8; matrix products, arithmetic and copies ran while one was open for 1% -> 1% of each run, Pallas kernels for 24% -> 23%
where the time goes in v5:
time: 101 us
  Pallas kernels  32.1 us (32%)
  starting transfers between devices  25.9 us (26%)
  waiting for transfers between devices  23.4 us (23%)
  local copies, waits for them, and re-layouts  17.1 us (17%)
  other arithmetic  1.58 us (2%)
    ppermute x7, waiting for transfers between devices, shifted(): lax.ppermute(value, axis, [(i, (i + shift) % peers) for i in range(peers)])  16.1 us
    unnamed x20, local copies, waits for them, and re-layouts  15.8 us
    pallas_call x1, Pallas kernels, first_sweep(): pl.pallas_call(functools.partial(first_sweep_kernel, (rows, cols, span, p...  13.7 us
    ppermute x10, starting transfers between devices, swap(): return lax.ppermute(value, axis, pairs)  13.6 us
    ppermute x7, starting transfers between devices, shifted(): lax.ppermute(value, axis, [(i, (i + shift) % peers) for i in range(peers)])  12.3 us
    pallas_call x1, Pallas kernels, correlate(): pl.pallas_call(functools.partial(correlate_kernel, (rows, cols, span, pee...  8.62 us
    ppermute x10, waiting for transfers between devices, swap(): return lax.ppermute(value, axis, pairs)  7.33 us
    pallas_call x1, Pallas kernels, second_sweep(): pl.pallas_call(functools.partial(second_sweep_kernel, (rows, cols, span,...  6.26 us
  transfers between devices with their start and end apart: 17, of which 8 were waited for; matrix products, arithmetic and copies ran while one was open for 1% of the time, Pallas kernels for 23%

profile of v5, /device:TPU:0, one launch (start us, length us, event | category | flops | bytes accessed | tf_op | source)
XLA Modules:
  0.0 101.0 jit_solution(11902796307641977951)
XLA Ops:
  0.6 0.9 copy.32
  1.6 0.9 copy.33
  2.6 0.1 fusion.5
  2.7 0.1 copy.11
  2.8 0.7 collective-permute-start
  3.4 0.1 copy.10
  3.5 0.0 copy-start
  3.5 2.8 %copy-done = f32[7,7,2,128,128]{4,3,2,1,0:T(8,128)S(1)} copy-done((f32[7,7,2,128,128]{4,3,2,1,0:T(8,128)S(1)}, f32[7,7,2,128,128]{4,3,2,1,0:T(8,128)}, u32[]{:S(2)}) %copy-start) | copy-done | bytes 6422552
  6.4 0.0 copy-start.6
  6.4 3.5 %weights.1 = (bf16[7,7,256,256]{3,2,1,0:T(8,128)(2,1)S(1)}, bf16[7,7,256,256]{3,2,1,0:T(8,128)(2,1)S(1)}) custom-call(f32[7,7,2,128,128]{4,3,2,1,0:T(8,128)S(1)} %copy-done), custom_call_target="tpu_custom_call" | custom-call | bytes 6422528 | tf_op jit(solution)/shard_map/weights/pallas_call | solution.py:94
  9.8 0.0 copy-start.1
  9.9 2.7 %copy-done.1 = bf16[7,7,256,256]{3,2,1,0:T(8,128)(2,1)} copy-done((bf16[7,7,256,256]{3,2,1,0:T(8,128)(2,1)}, bf16[7,7,256,256]{3,2,1,0:T(8,128)(2,1)S(1)}, u32[]{:S(2)}) %copy-start.1) | copy-done | bytes 6422552
  12.5 2.7 %copy-done.4 = bf16[7,7,256,256]{3,2,1,0:T(8,128)(2,1)} copy-done((bf16[7,7,256,256]{3,2,1,0:T(8,128)(2,1)}, bf16[7,7,256,256]{3,2,1,0:T(8,128)(2,1)S(1)}, u32[]{:S(2)}) %copy-start.4) | copy-done | bytes 6422552
  15.3 0.0 collective-permute-done
  15.3 4.3 %collective-permute-start.1 = (f32[2,108,128]{2,0,1:T(2,128)S(1)}, f32[2,108,128]{2,0,1:T(2,128)S(1)}, u32[]{:S(2)}, u32[]{:S(2)}) collective-permute-start(f32[2,108,128]{2,0,1:T(2,128)S(1)} %bitcast.36), channel_id=1, source_target_pairs={{0,1},{1,0},{2,3},{3,2},{4,5},{5,4},{6,7},{7,6},{8,9},{9,8},{10,11... | collective-permute-start | bytes 331784 | tf_op jit(solution)/shard_map/ppermute | solution.py:422
  19.6 1.0 collective-permute-done.1
  20.6 0.1 pad_maximum_fusion.2
  20.7 0.1 copy.15
  20.9 1.6 %collective-permute-start.3 = (f32[2,168,128]{2,0,1:T(2,128)S(1)}, f32[2,168,128]{2,0,1:T(2,128)S(1)}, u32[]{:S(2)}, u32[]{:S(2)}) collective-permute-start(f32[2,168,128]{2,0,1:T(2,128)S(1)} %bitcast.33), channel_id=1, source_target_pairs={{0,4},{4,0},{8,12},{12,8},{16,20},{20,16},{24,28},{28,24},{1,5},{5... | collective-permute-start | bytes 516104 | tf_op jit(solution)/shard_map/ppermute | solution.py:422
  22.5 0.1 copy.14
  22.6 0.7 collective-permute-start.2
  23.4 0.1 select_maximum_fusion.2.refs_4_
  23.4 3.3 %collective-permute-start.5 = (f32[2,12,24,128]{3,2,1,0:T(8,128)S(1)}, f32[2,12,24,128]{3,2,1,0:T(8,128)S(1)}, u32[]{:S(2)}, u32[]{:S(2)}) collective-permute-start(f32[2,12,24,128]{3,2,1,0:T(8,128)S(1)} %select_maximum_fusion.2.refs_4_), channel_id=1, source_target_pairs={{0,8},{4,12},{8,16},{12,20},{16,24},{20,28},{24,0},{28,4},{1,9},{5... | collective-permute-start | bytes 884744 | tf_op jit(solution)/shard_map/ppermute | solution.py:429
  26.7 2.6 %collective-permute-start.6 = (f32[2,12,24,128]{3,2,1,0:T(8,128)S(1)}, f32[2,12,24,128]{3,2,1,0:T(8,128)S(1)}, u32[]{:S(2)}, u32[]{:S(2)}) collective-permute-start(f32[2,12,24,128]{3,2,1,0:T(8,128)S(1)} %select_maximum_fusion.2.refs_4_), channel_id=1, source_target_pairs={{0,16},{4,20},{8,24},{12,28},{16,0},{20,4},{24,8},{28,12},{1,17},{... | collective-permute-start | bytes 884744 | tf_op jit(solution)/shard_map/ppermute | solution.py:429
  29.3 1.3 %collective-permute-start.7 = (f32[2,12,24,128]{3,2,1,0:T(8,128)S(1)}, f32[2,12,24,128]{3,2,1,0:T(8,128)S(1)}, u32[]{:S(2)}, u32[]{:S(2)}) collective-permute-start(f32[2,12,24,128]{3,2,1,0:T(8,128)S(1)} %select_maximum_fusion.2.refs_4_), channel_id=1, source_target_pairs={{0,24},{4,28},{8,0},{12,4},{16,8},{20,12},{24,16},{28,20},{1,25},{... | collective-permute-start | bytes 884744 | tf_op jit(solution)/shard_map/ppermute | solution.py:429
  30.6 0.0 collective-permute-done.3
  30.6 0.0 collective-permute-done.2
  30.7 2.7 %collective-permute-start.4 = (f32[2,12,24,128]{3,2,1,0:T(8,128)S(1)}, f32[2,12,24,128]{3,2,1,0:T(8,128)S(1)}, u32[]{:S(2)}, u32[]{:S(2)}) collective-permute-start(f32[2,12,24,128]{3,2,1,0:T(8,128)S(1)} %select_maximum_fusion.2.refs_4_), channel_id=1, source_target_pairs={{0,4},{4,0},{8,12},{12,8},{16,20},{20,16},{24,28},{28,24},{1,5},{5... | collective-permute-start | bytes 884744 | tf_op jit(solution)/shard_map/ppermute | solution.py:422
  33.4 0.1 select_maximum_fusion.source_ref
  33.5 0.0 copy-done.6
  33.5 0.0 copy-done.2
  33.5 0.0 copy-start.5
  33.5 2.8 %copy-done.5 = bf16[7,7,256,256]{3,2,1,0:T(8,128)(2,1)S(1)} copy-done((bf16[7,7,256,256]{3,2,1,0:T(8,128)(2,1)S(1)}, bf16[7,7,256,256]{3,2,1,0:T(8,128)(2,1)}, u32[]{:S(2)}) %copy-start.5) | copy-done | bytes 6422552
  36.4 13.7 %first_sweep.1 = (f32[18,24,256]{2,1,0:T(8,128)S(1)}, f32[12,16,256]{2,1,0:T(8,128)S(1)}) custom-call(f32[2,24,32,128]{3,2,1,0:T(8,128)S(1)} %select_maximum_fusion.source_ref, f32[2,128,128]{2,1,0:T(8,128)S(1)} %copy-done.6, bf16[7,7,256,256]{3,2,1,0:T(8,128)(2,1)S(1)} %copy-done.2, bf16[7,7,256,256]{3,2,1,0:T(8,128)(2,1)S(1)} %copy-done.5), custom_call_target="tpu_custom_call" | custom-call | flops 8323596288 | bytes 12845056 | tf_op jit(solution)/shard_map/first_sweep/pallas_call | solution.py:192
  50.1 0.0 collective-permute-done.5.refs_5_
  50.1 0.0 collective-permute-done.4.refs_9_
  50.1 0.1 collective-permute-start.8
  50.2 2.8 %copy-done.3 = bf16[7,7,256,256]{3,2,1,0:T(8,128)(2,1)S(1)} copy-done((bf16[7,7,256,256]{3,2,1,0:T(8,128)(2,1)S(1)}, bf16[7,7,256,256]{3,2,1,0:T(8,128)(2,1)}, u32[]{:S(2)}) %copy-start.3) | copy-done | bytes 6422552
  53.0 6.3 %second_sweep.1 = (f32[12,16,256]{2,1,0:T(8,128)S(1)}, f32[2,32,192]{2,1,0:T(8,128)S(1)}, f32[2,32,192]{2,1,0:T(8,128)S(1)}, f32[2,32,192]{2,1,0:T(8,128)S(1)}, f32[2,32,192]{2,1,0:T(8,128)S(1)}) custom-call(f32[18,24,256]{2,1,0:T(8,128)S(1)} %get-tuple-element.36.second_ref, f32[12,16,256]{2,1,0:T(8,128)S(1)} %get-tuple-element.37.source_ref, ...), custom_call_target="tpu_custom_call" | custom-call | flops 3699376128 | bytes 12845056 | tf_op jit(solution)/shard_map/second_sweep/pallas_call | solution.py:278
  59.3 0.0 collective-permute-done.6.refs_6_
  59.3 0.0 collective-permute-done.7.refs_7_
  59.3 0.0 collective-permute-done.8.refs_10_
  59.3 2.1 %collective-permute-start.13 = (f32[2,2,12,24,128]{4,3,2,1,0:T(8,128)S(1)}, f32[2,2,12,24,128]{4,3,2,1,0:T(8,128)S(1)}, u32[]{:S(2)}, u32[]{:S(2)}) collective-permute-start(f32[2,2,12,24,128]{4,3,2,1,0:T(8,128)S(1)} %pad_maximum_fusion.1), channel_id=1, source_target_pairs={{0,4},{4,0},{8,12},{12,8},{16,20},{20,16},{24,28},{28,24},{1,5},{5... | collective-permute-start | bytes 1769480 | tf_op jit(solution)/shard_map/ppermute | solution.py:422
  61.4 3.0 %collective-permute-start.11 = (f32[2,32,192]{2,1,0:T(8,128)S(1)}, f32[2,32,192]{2,1,0:T(8,128)S(1)}, u32[]{:S(2)}, u32[]{:S(2)}) collective-permute-start(f32[2,32,192]{2,1,0:T(8,128)S(1)} %get-tuple-element.47), channel_id=1, source_target_pairs={{0,24},{4,28},{8,0},{12,4},{16,8},{20,12},{24,16},{28,20},{1,25},{... | collective-permute-start | bytes 147464 | tf_op jit(solution)/shard_map/ppermute | solution.py:429
  64.4 0.7 collective-permute-start.10
  65.1 0.9 collective-permute-start.9
  66.1 1.3 %collective-permute-done.11.refs_3_ = f32[2,32,192]{2,1,0:T(8,128)S(1)} collective-permute-done((f32[2,32,192]{2,1,0:T(8,128)S(1)}, f32[2,32,192]{2,1,0:T(8,128)S(1)}, u32[]{:S(2)}, u32[]{:S(2)}) %collective-permute-start.11) | collective-permute-done | bytes 49184 | tf_op jit(solution)/shard_map/ppermute | solution.py:429
  67.3 2.3 %collective-permute-done.10.refs_2_ = f32[2,32,192]{2,1,0:T(8,128)S(1)} collective-permute-done((f32[2,32,192]{2,1,0:T(8,128)S(1)}, f32[2,32,192]{2,1,0:T(8,128)S(1)}, u32[]{:S(2)}, u32[]{:S(2)}) %collective-permute-start.10) | collective-permute-done | bytes 49184 | tf_op jit(solution)/shard_map/ppermute | solution.py:429
  69.6 1.6 %collective-permute-done.9.refs_1_ = f32[2,32,192]{2,1,0:T(8,128)S(1)} collective-permute-done((f32[2,32,192]{2,1,0:T(8,128)S(1)}, f32[2,32,192]{2,1,0:T(8,128)S(1)}, u32[]{:S(2)}, u32[]{:S(2)}) %collective-permute-start.9) | collective-permute-done | bytes 49184 | tf_op jit(solution)/shard_map/ppermute | solution.py:429
  71.2 1.3 %collective-permute-start.12 = (f32[4,32,192]{2,1,0:T(8,128)S(1)}, f32[4,32,192]{2,1,0:T(8,128)S(1)}, u32[]{:S(2)}, u32[]{:S(2)}) collective-permute-start(f32[4,32,192]{2,1,0:T(8,128)S(1)} %pad_maximum_fusion.5), channel_id=1, source_target_pairs={{0,4},{4,0},{8,12},{12,8},{16,20},{20,16},{24,28},{28,24},{1,5},{5... | collective-permute-start | bytes 294920 | tf_op jit(solution)/shard_map/ppermute | solution.py:422
  72.6 3.7 %collective-permute-done.12.refs_8_ = f32[4,32,192]{2,1,0:T(8,128)S(1)} collective-permute-done((f32[4,32,192]{2,1,0:T(8,128)S(1)}, f32[4,32,192]{2,1,0:T(8,128)S(1)}, u32[]{:S(2)}, u32[]{:S(2)}) %collective-permute-start.12) | collective-permute-done | bytes 98336 | tf_op jit(solution)/shard_map/ppermute | solution.py:422
  76.2 0.0 collective-permute-done.13.refs_11_
  76.2 8.6 %correlate.1 = (f32[7,7,2,8,128]{4,3,2,1,0:T(8,128)S(1)}, f32[7,7,2,8,128]{4,3,2,1,0:T(8,128)S(1)}) custom-call(f32[2,32,192]{2,1,0:T(8,128)S(1)} %get-tuple-element.44.refs_0_, f32[2,32,192]{2,1,0:T(8,128)S(1)} %collective-permute-done.9.refs_1_, f32[2,32,192]{2,1,0:T(8,128)S(1)} %collective-permute-done.10.refs_2_, ...), custom_call_target="tpu_custom_call" | custom-call | flops 3699376128 | bytes 3162112 | tf_op jit(solution)/shard_map/correlate/pallas_call | solution.py:391
  84.9 0.1 collective-permute-start.14
  84.9 1.7 %collective-permute-done.14 = f32[7,7,2,8,128]{4,3,2,1,0:T(8,128)S(1)} collective-permute-done((f32[7,7,2,8,128]{4,3,2,1,0:T(8,128)S(1)}, f32[7,7,2,8,128]{4,3,2,1,0:T(8,128)S(1)}, u32[]{:S(2)}, u32[]{:S(2)}) %collective-permute-start.14) | collective-permute-done | bytes 401440 | tf_op jit(solution)/shard_map/ppermute | solution.py:422
  86.7 0.1 add.20
  86.7 0.4 collective-permute-start.15
  87.2 11.0 %collective-permute-done.15 = f32[7,7,2,8,128]{4,3,2,1,0:T(8,128)S(1)} collective-permute-done((f32[7,7,2,8,128]{4,3,2,1,0:T(8,128)S(1)}, f32[7,7,2,8,128]{4,3,2,1,0:T(8,128)S(1)}, u32[]{:S(2)}, u32[]{:S(2)}) %collective-permute-start.15) | collective-permute-done | bytes 401440 | tf_op jit(solution)/shard_map/ppermute | solution.py:429
  98.1 0.1 add.21
  98.2 0.1 collective-permute-start.16
  98.3 0.8 reshape.33
  99.1 0.9 collective-permute-done.16
  100.0 0.1 broadcast_select_fusion.1
  100.1 1.0 pad_maximum_fusion
  (22 shorter events, 0.3 us)
Async XLA Ops:
  2.8 12.5 %collective-permute-start = (f32[2,108,128]{2,0,1:T(2,128)S(1)}, f32[2,108,128]{2,0,1:T(2,128)S(1)}, u32[]{:S(2)}, u32[]{:S(2)}) collective-permute-start(f32[2,108,128]{2,0,1:T(2,128)S(1)} %bitcast.38), channel_id=1, source_target_pairs={{1,2},{2,1},{5,6},{6,5},{9,10},{10,9},{13,14},{14,13},{17,18},{18,... | collective-permute-start | bytes 331784 | tf_op jit(solution)/shard_map/ppermute | solution.py:422
  3.5 2.8 %copy-start = (f32[7,7,2,128,128]{4,3,2,1,0:T(8,128)S(1)}, f32[7,7,2,128,128]{4,3,2,1,0:T(8,128)}, u32[]{:S(2)}) copy-start(f32[7,7,2,128,128]{4,3,2,1,0:T(8,128)} %blocks_hbm.1) | copy-start | bytes 19267588
  6.4 27.2 %copy-start.6 = (f32[2,128,128]{2,1,0:T(8,128)S(1)}, f32[2,128,128]{2,1,0:T(8,128)}, u32[]{:S(2)}) copy-start(f32[2,128,128]{2,1,0:T(8,128)} %inverse_ref.3) | copy-start | bytes 393220
  9.8 2.7 %copy-start.1 = (bf16[7,7,256,256]{3,2,1,0:T(8,128)(2,1)}, bf16[7,7,256,256]{3,2,1,0:T(8,128)(2,1)S(1)}, u32[]{:S(2)}) copy-start(bf16[7,7,256,256]{3,2,1,0:T(8,128)(2,1)S(1)} %get-tuple-element.32.w_high) | copy-start | bytes 19267588
  12.5 2.7 %copy-start.4 = (bf16[7,7,256,256]{3,2,1,0:T(8,128)(2,1)}, bf16[7,7,256,256]{3,2,1,0:T(8,128)(2,1)S(1)}, u32[]{:S(2)}) copy-start(bf16[7,7,256,256]{3,2,1,0:T(8,128)(2,1)S(1)} %get-tuple-element.33.w_low) | copy-start | bytes 19267588
  15.3 5.3 %collective-permute-start.1 = (f32[2,108,128]{2,0,1:T(2,128)S(1)}, f32[2,108,128]{2,0,1:T(2,128)S(1)}, u32[]{:S(2)}, u32[]{:S(2)}) collective-permute-start(f32[2,108,128]{2,0,1:T(2,128)S(1)} %bitcast.36), channel_id=1, source_target_pairs={{0,1},{1,0},{2,3},{3,2},{4,5},{5,4},{6,7},{7,6},{8,9},{9,8},{10,11... | collective-permute-start | bytes 331784 | tf_op jit(solution)/shard_map/ppermute | solution.py:422
  19.6 14.0 %copy-start.2 = (bf16[7,7,256,256]{3,2,1,0:T(8,128)(2,1)S(1)}, bf16[7,7,256,256]{3,2,1,0:T(8,128)(2,1)}, u32[]{:S(2)}) copy-start(bf16[7,7,256,256]{3,2,1,0:T(8,128)(2,1)} %copy-done.1) | copy-start | bytes 19267588
  20.9 9.8 %collective-permute-start.3 = (f32[2,168,128]{2,0,1:T(2,128)S(1)}, f32[2,168,128]{2,0,1:T(2,128)S(1)}, u32[]{:S(2)}, u32[]{:S(2)}) collective-permute-start(f32[2,168,128]{2,0,1:T(2,128)S(1)} %bitcast.33), channel_id=1, source_target_pairs={{0,4},{4,0},{8,12},{12,8},{16,20},{20,16},{24,28},{28,24},{1,5},{5... | collective-permute-start | bytes 516104 | tf_op jit(solution)/shard_map/ppermute | solution.py:422
  22.6 8.0 %collective-permute-start.2 = (f32[2,168,128]{2,0,1:T(2,128)S(1)}, f32[2,168,128]{2,0,1:T(2,128)S(1)}, u32[]{:S(2)}, u32[]{:S(2)}) collective-permute-start(f32[2,168,128]{2,0,1:T(2,128)S(1)} %bitcast.34), channel_id=1, source_target_pairs={{4,8},{8,4},{12,16},{16,12},{20,24},{24,20},{5,9},{9,5},{13,17},{1... | collective-permute-start | bytes 516104 | tf_op jit(solution)/shard_map/ppermute | solution.py:422
  23.4 26.7 %collective-permute-start.5 = (f32[2,12,24,128]{3,2,1,0:T(8,128)S(1)}, f32[2,12,24,128]{3,2,1,0:T(8,128)S(1)}, u32[]{:S(2)}, u32[]{:S(2)}) collective-permute-start(f32[2,12,24,128]{3,2,1,0:T(8,128)S(1)} %select_maximum_fusion.2.refs_4_), channel_id=1, source_target_pairs={{0,8},{4,12},{8,16},{12,20},{16,24},{20,28},{24,0},{28,4},{1,9},{5... | collective-permute-start | bytes 884744 | tf_op jit(solution)/shard_map/ppermute | solution.py:429
  26.7 32.6 %collective-permute-start.6 = (f32[2,12,24,128]{3,2,1,0:T(8,128)S(1)}, f32[2,12,24,128]{3,2,1,0:T(8,128)S(1)}, u32[]{:S(2)}, u32[]{:S(2)}) collective-permute-start(f32[2,12,24,128]{3,2,1,0:T(8,128)S(1)} %select_maximum_fusion.2.refs_4_), channel_id=1, source_target_pairs={{0,16},{4,20},{8,24},{12,28},{16,0},{20,4},{24,8},{28,12},{1,17},{... | collective-permute-start | bytes 884744 | tf_op jit(solution)/shard_map/ppermute | solution.py:429
  29.3 30.0 %collective-permute-start.7 = (f32[2,12,24,128]{3,2,1,0:T(8,128)S(1)}, f32[2,12,24,128]{3,2,1,0:T(8,128)S(1)}, u32[]{:S(2)}, u32[]{:S(2)}) collective-permute-start(f32[2,12,24,128]{3,2,1,0:T(8,128)S(1)} %select_maximum_fusion.2.refs_4_), channel_id=1, source_target_pairs={{0,24},{4,28},{8,0},{12,4},{16,8},{20,12},{24,16},{28,20},{1,25},{... | collective-permute-start | bytes 884744 | tf_op jit(solution)/shard_map/ppermute | solution.py:429
  30.7 19.4 %collective-permute-start.4 = (f32[2,12,24,128]{3,2,1,0:T(8,128)S(1)}, f32[2,12,24,128]{3,2,1,0:T(8,128)S(1)}, u32[]{:S(2)}, u32[]{:S(2)}) collective-permute-start(f32[2,12,24,128]{3,2,1,0:T(8,128)S(1)} %select_maximum_fusion.2.refs_4_), channel_id=1, source_target_pairs={{0,4},{4,0},{8,12},{12,8},{16,20},{20,16},{24,28},{28,24},{1,5},{5... | collective-permute-start | bytes 884744 | tf_op jit(solution)/shard_map/ppermute | solution.py:422
  33.5 2.8 %copy-start.5 = (bf16[7,7,256,256]{3,2,1,0:T(8,128)(2,1)S(1)}, bf16[7,7,256,256]{3,2,1,0:T(8,128)(2,1)}, u32[]{:S(2)}) copy-start(bf16[7,7,256,256]{3,2,1,0:T(8,128)(2,1)} %copy-done.4) | copy-start | bytes 19267588
  50.1 9.2 %collective-permute-start.8 = (f32[2,12,24,128]{3,2,1,0:T(8,128)S(1)}, f32[2,12,24,128]{3,2,1,0:T(8,128)S(1)}, u32[]{:S(2)}, u32[]{:S(2)}) collective-permute-start(f32[2,12,24,128]{3,2,1,0:T(8,128)S(1)} %collective-permute-done.5.refs_5_), channel_id=1, source_target_pairs={{0,4},{4,0},{8,12},{12,8},{16,20},{20,16},{24,28},{28,24},{1,5},{5... | collective-permute-start | bytes 884744 | tf_op jit(solution)/shard_map/ppermute | solution.py:422
  50.2 2.8 %copy-start.3 = (bf16[7,7,256,256]{3,2,1,0:T(8,128)(2,1)S(1)}, bf16[7,7,256,256]{3,2,1,0:T(8,128)(2,1)}, u32[]{:S(2)}) copy-start(bf16[7,7,256,256]{3,2,1,0:T(8,128)(2,1)} %copy-done.1) | copy-start | bytes 19267588
  59.3 16.9 %collective-permute-start.13 = (f32[2,2,12,24,128]{4,3,2,1,0:T(8,128)S(1)}, f32[2,2,12,24,128]{4,3,2,1,0:T(8,128)S(1)}, u32[]{:S(2)}, u32[]{:S(2)}) collective-permute-start(f32[2,2,12,24,128]{4,3,2,1,0:T(8,128)S(1)} %pad_maximum_fusion.1), channel_id=1, source_target_pairs={{0,4},{4,0},{8,12},{12,8},{16,20},{20,16},{24,28},{28,24},{1,5},{5... | collective-permute-start | bytes 1769480 | tf_op jit(solution)/shard_map/ppermute | solution.py:422
  61.4 5.9 %collective-permute-start.11 = (f32[2,32,192]{2,1,0:T(8,128)S(1)}, f32[2,32,192]{2,1,0:T(8,128)S(1)}, u32[]{:S(2)}, u32[]{:S(2)}) collective-permute-start(f32[2,32,192]{2,1,0:T(8,128)S(1)} %get-tuple-element.47), channel_id=1, source_target_pairs={{0,24},{4,28},{8,0},{12,4},{16,8},{20,12},{24,16},{28,20},{1,25},{... | collective-permute-start | bytes 147464 | tf_op jit(solution)/shard_map/ppermute | solution.py:429
  64.4 5.2 %collective-permute-start.10 = (f32[2,32,192]{2,1,0:T(8,128)S(1)}, f32[2,32,192]{2,1,0:T(8,128)S(1)}, u32[]{:S(2)}, u32[]{:S(2)}) collective-permute-start(f32[2,32,192]{2,1,0:T(8,128)S(1)} %get-tuple-element.46), channel_id=1, source_target_pairs={{0,16},{4,20},{8,24},{12,28},{16,0},{20,4},{24,8},{28,12},{1,17},{... | collective-permute-start | bytes 147464 | tf_op jit(solution)/shard_map/ppermute | solution.py:429
  65.1 6.1 %collective-permute-start.9 = (f32[2,32,192]{2,1,0:T(8,128)S(1)}, f32[2,32,192]{2,1,0:T(8,128)S(1)}, u32[]{:S(2)}, u32[]{:S(2)}) collective-permute-start(f32[2,32,192]{2,1,0:T(8,128)S(1)} %get-tuple-element.45), channel_id=1, source_target_pairs={{0,8},{4,12},{8,16},{12,20},{16,24},{20,28},{24,0},{28,4},{1,9},{5... | collective-permute-start | bytes 147464 | tf_op jit(solution)/shard_map/ppermute | solution.py:429
  71.2 5.0 %collective-permute-start.12 = (f32[4,32,192]{2,1,0:T(8,128)S(1)}, f32[4,32,192]{2,1,0:T(8,128)S(1)}, u32[]{:S(2)}, u32[]{:S(2)}) collective-permute-start(f32[4,32,192]{2,1,0:T(8,128)S(1)} %pad_maximum_fusion.5), channel_id=1, source_target_pairs={{0,4},{4,0},{8,12},{12,8},{16,20},{20,16},{24,28},{28,24},{1,5},{5... | collective-permute-start | bytes 294920 | tf_op jit(solution)/shard_map/ppermute | solution.py:422
  84.9 1.8 %collective-permute-start.14 = (f32[7,7,2,8,128]{4,3,2,1,0:T(8,128)S(1)}, f32[7,7,2,8,128]{4,3,2,1,0:T(8,128)S(1)}, u32[]{:S(2)}, u32[]{:S(2)}) collective-permute-start(f32[7,7,2,8,128]{4,3,2,1,0:T(8,128)S(1)} %get-tuple-element.53), channel_id=1, source_target_pairs={{0,1},{1,0},{2,3},{3,2},{4,5},{5,4},{6,7},{7,6},{8,9},{9,8},{10,11... | collective-permute-start | bytes 1204232 | tf_op jit(solution)/shard_map/ppermute | solution.py:422
  86.7 11.4 %collective-permute-start.15 = (f32[7,7,2,8,128]{4,3,2,1,0:T(8,128)S(1)}, f32[7,7,2,8,128]{4,3,2,1,0:T(8,128)S(1)}, u32[]{:S(2)}, u32[]{:S(2)}) collective-permute-start(f32[7,7,2,8,128]{4,3,2,1,0:T(8,128)S(1)} %add.20), channel_id=1, source_target_pairs={{0,2},{1,3},{2,0},{3,1},{4,6},{5,7},{6,4},{7,5},{8,10},{9,11},{10,... | collective-permute-start | bytes 1204232 | tf_op jit(solution)/shard_map/ppermute | solution.py:429
  98.2 1.8 %collective-permute-start.16 = (f32[7,7,2,8,128]{4,3,2,1,0:T(8,128)S(1)}, f32[7,7,2,8,128]{4,3,2,1,0:T(8,128)S(1)}, u32[]{:S(2)}, u32[]{:S(2)}) collective-permute-start(f32[7,7,2,8,128]{4,3,2,1,0:T(8,128)S(1)} %add.21), channel_id=1, source_target_pairs={{0,1},{1,0},{2,3},{3,2},{4,5},{5,4},{6,7},{7,6},{8,9},{9,8},{10,11... | collective-permute-start | bytes 1204232 | tf_op jit(solution)/shard_map/ppermute | solution.py:422

commit v6 on v4

--- a/solution.py
+++ b/solution.py
@@ -302,10 +302,7 @@
         return base + 1 - odd, base + odd
 
     for k in range(half_peers):
-        if k == 0:
-            twin = own_twin_ref
-        else:
-            twin = late_ref if k == half_peers - 1 else early_ref.at[k - 1]
+        twin = (own_twin_ref, early_ref)[k] if k < 2 else late_ref.at[k - 2]
         for n, (source, tile) in enumerate(zip((piece_refs[k], twin), tiles(k))):
             pltpu.make_async_copy(source, stage.at[tile], sems.at[n, k]).start()
         first, second = tiles(k)
@@ -424,7 +421,7 @@
         inner, outer = lax.optimization_barrier((inner, outer))
     inner = swap(inner, axis, 0)
     inner, outer = inner.reshape(shape), outer.reshape(shape)
-    return jnp.where(even, outer, inner), jnp.where(even, inner, outer)
+    return jnp.where(even, outer, inner), jnp.where(even, inner, outer), inner
 
 
 def on_device(adjoint_source, saved_currents, lag_blocks, element_inverse):
@@ -438,10 +435,10 @@
     saved = saved_currents.transpose(2, 0, 1, 3)
     initial = jnp.concatenate([source[:, :, :halo], saved[:, :, :reach]], axis=2)
     last = jnp.concatenate([source[:, :, cols - halo :], saved[:, :, cols - reach :]], axis=2)
-    before, after = edges(initial, last, "col")
+    before, after, _ = edges(initial, last, "col")
     source = jnp.concatenate([before[:, :, :halo], source, after[:, :, :halo]], axis=2)
     saved = jnp.concatenate([before[:, :, halo:], saved, after[:, :, halo:]], axis=2)
-    before, after = edges(source[:, :halo], source[:, rows - halo :], "row")
+    before, after, arrived = edges(source[:, :halo], source[:, rows - halo :], "row")
     source = jnp.concatenate([before, source, after], axis=1)
     wide = round_up(cols + 2 * halo, 8)
     source = jnp.pad(source, ((0, 0), (0, 0), (0, wide - cols - 2 * halo), (0, 0)))
@@ -449,21 +446,21 @@
     pitch = round_up(cols + 2 * reach, 8)
     saved = jnp.pad(saved, ((0, 0), (0, 0), (0, pitch - cols - 2 * reach), (0, 0)))
     pieces = [shifted(saved, "row", k) for k in range(0, peers, 2)]
-    own_twin = swap(saved, "row", 0)
+    own_twin = swap(lax.optimization_barrier((saved, arrived))[0], "row", 0)
 
     second, own_source, high, low = first_sweep(source, element_inverse, lag_blocks, rows, cols)
-    second, own_twin, early = lax.optimization_barrier((second, own_twin, jnp.stack(pieces[1:-1])))
-    early_twins = swap(early, "row", 0)
+    second, own_twin, early = lax.optimization_barrier((second, own_twin, pieces[1]))
+    early_twin = swap(early, "row", 0)
     adjoint, sends = second_sweep(second, own_source, element_inverse, high, low, peers)
-    late, sends = lax.optimization_barrier((pieces[-1], sends))
-    late_twin = swap(late, "row", 0)
+    *late, early_twin, sends = lax.optimization_barrier((*pieces[2:], early_twin, sends))
+    late_twins = swap(jnp.stack(late), "row", 0)
     shares = [shifted(send, "row", 2 * k) for k, send in enumerate(sends)]
     twin_shares = swap(jnp.stack([received[1] for received in shares]), "row", 0)
 
     elements = rows * peers * cols * lax.axis_size("col")
     factor = -1.0 / math.sqrt(elements)
     mine, other = correlate(
-        shares, twin_shares, pieces, (own_twin, early_twins, late_twin), rows, cols, span, factor
+        shares, twin_shares, pieces, (own_twin, early_twin, late_twins), rows, cols, span, factor
     )
     mine = mine + swap(other, "col", 0)
     total = mine

time: 93.1 us -> 88.6 us (0.952); the launches traced: 91.8 us -> 88.4 us
  starting transfers between devices: 34 us -> 31.2 us
    ppermute x10, starting transfers between devices: 18.6 us -> 14 us  [swap(): return lax.ppermute(value, axis, pairs)]
    ppermute x7, waiting for transfers between devices: 14.9 us -> 11.5 us  [shifted(): lax.ppermute(value, axis, [(i, (i + shift) % peers) for i in range(peers)])]
    ppermute x10, waiting for transfers between devices: 6.61 us -> 9.47 us  [swap(): return lax.ppermute(value, axis, pairs)]
    ppermute x7, starting transfers between devices: 15.5 us -> 17.2 us  [shifted(): lax.ppermute(value, axis, [(i, (i + shift) % peers) for i in range(peers)])]
  transfers between devices with their start and end apart: 17 -> 17, of which waited for: 9 -> 7; matrix products, arithmetic and copies ran while one was open for 1% -> 1% of each run, Pallas kernels for 24% -> 25%
where the time goes in v6:
time: 88.6 us; the launch traced here: 88.4 us
  starting transfers between devices  31.2 us (35%)
  Pallas kernels  30.5 us (34%)
  waiting for transfers between devices  20.9 us (24%)
  local copies, waits for them, and re-layouts  3.29 us (4%)
  other arithmetic  1.58 us (2%)
  between operations  0.96 us (1%)
    ppermute x7, starting transfers between devices, shifted(): lax.ppermute(value, axis, [(i, (i + shift) % peers) for i in range(peers)])  17.2 us
    pallas_call x1, Pallas kernels, first_sweep(): pl.pallas_call(functools.partial(first_sweep_kernel, (rows, cols, span, p...  15.6 us
    ppermute x10, starting transfers between devices, swap(): return lax.ppermute(value, axis, pairs)  14 us
    ppermute x7, waiting for transfers between devices, shifted(): lax.ppermute(value, axis, [(i, (i + shift) % peers) for i in range(peers)])  11.5 us
    ppermute x10, waiting for transfers between devices, swap(): return lax.ppermute(value, axis, pairs)  9.47 us
    pallas_call x1, Pallas kernels, correlate(): pl.pallas_call(functools.partial(correlate_kernel, (rows, cols, span, pee...  8.62 us
    pallas_call x1, Pallas kernels, second_sweep(): pl.pallas_call(functools.partial(second_sweep_kernel, (rows, cols, span,...  6.27 us
    unnamed x8, local copies, waits for them, and re-layouts  1.98 us
  transfers between devices with their start and end apart: 17, of which 7 were waited for; matrix products, arithmetic and copies ran while one was open for 1% of the time, Pallas kernels for 25%

profile of v6, /device:TPU:0, one launch (start us, length us, event | category | flops | bytes accessed | tf_op | source)
XLA Modules:
  0.0 88.4 jit_solution(3174427868927830210)
XLA Ops:
  0.6 0.0 copy-start
  0.7 1.0 %copy.33 = f32[12,16,2,128]{3,1,0,2:T(8,128)S(1)} copy(f32[12,16,2,128]{3,2,1,0:T(2,128)} %param.4) | data formatting | bytes 393216 | tf_op args[0]
  1.7 0.9 %copy.32 = f32[12,16,2,128]{3,1,0,2:T(8,128)S(1)} copy(f32[12,16,2,128]{3,2,1,0:T(2,128)} %param.5) | data formatting | bytes 393216 | tf_op args[1]
  2.6 0.1 fusion.5
  2.7 0.1 copy.11
  2.8 0.7 collective-permute-start
  3.5 0.1 copy.10
  3.6 0.0 collective-permute-done
  3.6 6.6 %collective-permute-start.1 = (f32[2,108,128]{2,0,1:T(2,128)S(1)}, f32[2,108,128]{2,0,1:T(2,128)S(1)}, u32[]{:S(2)}, u32[]{:S(2)}) collective-permute-start(f32[2,108,128]{2,0,1:T(2,128)S(1)} %bitcast.36), channel_id=1, source_target_pairs={{0,1},{1,0},{2,3},{3,2},{4,5},{5,4},{6,7},{7,6},{8,9},{9,8},{10,11... | collective-permute-start | bytes 331784 | tf_op jit(solution)/shard_map/ppermute | solution.py:404
  10.2 1.0 %collective-permute-done.1 = f32[2,108,128]{2,0,1:T(2,128)S(1)} collective-permute-done((f32[2,108,128]{2,0,1:T(2,128)S(1)}, f32[2,108,128]{2,0,1:T(2,128)S(1)}, u32[]{:S(2)}, u32[]{:S(2)}) %collective-permute-start.1) | collective-permute-done | bytes 110624 | tf_op jit(solution)/shard_map/ppermute | solution.py:404
  11.2 0.1 pad_maximum_fusion.2
  11.3 0.1 copy.15
  11.5 1.6 %collective-permute-start.3 = (f32[2,168,128]{2,0,1:T(2,128)S(1)}, f32[2,168,128]{2,0,1:T(2,128)S(1)}, u32[]{:S(2)}, u32[]{:S(2)}) collective-permute-start(f32[2,168,128]{2,0,1:T(2,128)S(1)} %bitcast.33), channel_id=1, source_target_pairs={{0,4},{4,0},{8,12},{12,8},{16,20},{20,16},{24,28},{28,24},{1,5},{5... | collective-permute-start | bytes 516104 | tf_op jit(solution)/shard_map/ppermute | solution.py:404
  13.1 0.1 copy.14
  13.2 0.7 collective-permute-start.2
  14.0 0.1 select_maximum_fusion.2.refs_4_
  14.0 3.3 %collective-permute-start.5 = (f32[2,12,24,128]{3,2,1,0:T(8,128)S(1)}, f32[2,12,24,128]{3,2,1,0:T(8,128)S(1)}, u32[]{:S(2)}, u32[]{:S(2)}) collective-permute-start(f32[2,12,24,128]{3,2,1,0:T(8,128)S(1)} %select_maximum_fusion.2.refs_4_), channel_id=1, source_target_pairs={{0,8},{4,12},{8,16},{12,20},{16,24},{20,28},{24,0},{28,4},{1,9},{5... | collective-permute-start | bytes 884744 | tf_op jit(solution)/shard_map/ppermute | solution.py:411
  17.3 2.6 %collective-permute-start.6 = (f32[2,12,24,128]{3,2,1,0:T(8,128)S(1)}, f32[2,12,24,128]{3,2,1,0:T(8,128)S(1)}, u32[]{:S(2)}, u32[]{:S(2)}) collective-permute-start(f32[2,12,24,128]{3,2,1,0:T(8,128)S(1)} %select_maximum_fusion.2.refs_4_), channel_id=1, source_target_pairs={{0,16},{4,20},{8,24},{12,28},{16,0},{20,4},{24,8},{28,12},{1,17},{... | collective-permute-start | bytes 884744 | tf_op jit(solution)/shard_map/ppermute | solution.py:411
  19.9 1.3 %collective-permute-start.7 = (f32[2,12,24,128]{3,2,1,0:T(8,128)S(1)}, f32[2,12,24,128]{3,2,1,0:T(8,128)S(1)}, u32[]{:S(2)}, u32[]{:S(2)}) collective-permute-start(f32[2,12,24,128]{3,2,1,0:T(8,128)S(1)} %select_maximum_fusion.2.refs_4_), channel_id=1, source_target_pairs={{0,24},{4,28},{8,0},{12,4},{16,8},{20,12},{24,16},{28,20},{1,25},{... | collective-permute-start | bytes 884744 | tf_op jit(solution)/shard_map/ppermute | solution.py:411
  21.2 0.0 collective-permute-done.3
  21.2 0.0 collective-permute-done.2
  21.3 2.7 %collective-permute-start.4 = (f32[2,12,24,128]{3,2,1,0:T(8,128)S(1)}, f32[2,12,24,128]{3,2,1,0:T(8,128)S(1)}, u32[]{:S(2)}, u32[]{:S(2)}) collective-permute-start(f32[2,12,24,128]{3,2,1,0:T(8,128)S(1)} %select_maximum_fusion.2.refs_4_), channel_id=1, source_target_pairs={{0,4},{4,0},{8,12},{12,8},{16,20},{20,16},{24,28},{28,24},{1,5},{5... | collective-permute-start | bytes 884744 | tf_op jit(solution)/shard_map/ppermute | solution.py:404
  24.0 0.1 select_maximum_fusion.source_ref
  24.1 0.0 copy-done
  24.1 15.6 %first_sweep.1 = (f32[18,24,256]{2,1,0:T(8,128)S(1)}, f32[12,16,256]{2,1,0:T(8,128)S(1)}, bf16[7,7,256,256]{3,2,1,0:T(8,128)(2,1)S(1)}, bf16[7,7,256,256]{3,2,1,0:T(8,128)(2,1)S(1)}) custom-call(f32[2,24,32,128]{3,2,1,0:T(8,128)S(1)} %select_maximum_fusion.source_ref, f32[2,128,128]{2,1,0:T(8,128)S(1)} %copy-done, f32[7,7,2,128,128]{4,3,2,1,0:T(8,128)} %blocks_hbm.1), custom_call_target="tpu_custom_call" | custom-call | flops 8323596288 | bytes 19267584 | tf_op jit(solution)/shard_map/first_sweep/pallas_call | solution.py:170
  39.7 0.0 collective-permute-done.5.refs_5_
  39.7 0.0 collective-permute-done.4.refs_9_
  39.7 0.1 collective-permute-start.8
  39.8 6.3 %second_sweep.1 = (f32[12,16,256]{2,1,0:T(8,128)S(1)}, f32[2,32,192]{2,1,0:T(8,128)S(1)}, f32[2,32,192]{2,1,0:T(8,128)S(1)}, f32[2,32,192]{2,1,0:T(8,128)S(1)}, f32[2,32,192]{2,1,0:T(8,128)S(1)}) custom-call(f32[18,24,256]{2,1,0:T(8,128)S(1)} %get-tuple-element.30.second_ref, f32[12,16,256]{2,1,0:T(8,128)S(1)} %get-tuple-element.31.source_ref, ...), custom_call_target="tpu_custom_call" | custom-call | flops 3699376128 | bytes 12845056 | tf_op jit(solution)/shard_map/second_sweep/pallas_call | solution.py:260
  46.1 0.0 collective-permute-done.6.refs_6_
  46.1 0.0 collective-permute-done.7.refs_7_
  46.1 1.3 %collective-permute-done.8.refs_10_ = f32[2,12,24,128]{3,2,1,0:T(8,128)S(1)} collective-permute-done((f32[2,12,24,128]{3,2,1,0:T(8,128)S(1)}, f32[2,12,24,128]{3,2,1,0:T(8,128)S(1)}, u32[]{:S(2)}, u32[]{:S(2)}) %collective-permute-start.8) | collective-permute-done | bytes 294944 | tf_op jit(solution)/shard_map/ppermute | solution.py:404
  47.4 0.8 collective-permute-start.13
  48.2 2.2 %collective-permute-start.9 = (f32[2,32,192]{2,1,0:T(8,128)S(1)}, f32[2,32,192]{2,1,0:T(8,128)S(1)}, u32[]{:S(2)}, u32[]{:S(2)}) collective-permute-start(f32[2,32,192]{2,1,0:T(8,128)S(1)} %get-tuple-element.41), channel_id=1, source_target_pairs={{0,8},{4,12},{8,16},{12,20},{16,24},{20,28},{24,0},{28,4},{1,9},{5... | collective-permute-start | bytes 147464 | tf_op jit(solution)/shard_map/ppermute | solution.py:411
  50.5 2.6 %collective-permute-start.10 = (f32[2,32,192]{2,1,0:T(8,128)S(1)}, f32[2,32,192]{2,1,0:T(8,128)S(1)}, u32[]{:S(2)}, u32[]{:S(2)}) collective-permute-start(f32[2,32,192]{2,1,0:T(8,128)S(1)} %get-tuple-element.42), channel_id=1, source_target_pairs={{0,16},{4,20},{8,24},{12,28},{16,0},{20,4},{24,8},{28,12},{1,17},{... | collective-permute-start | bytes 147464 | tf_op jit(solution)/shard_map/ppermute | solution.py:411
  53.1 2.9 %collective-permute-start.11 = (f32[2,32,192]{2,1,0:T(8,128)S(1)}, f32[2,32,192]{2,1,0:T(8,128)S(1)}, u32[]{:S(2)}, u32[]{:S(2)}) collective-permute-start(f32[2,32,192]{2,1,0:T(8,128)S(1)} %get-tuple-element.43), channel_id=1, source_target_pairs={{0,24},{4,28},{8,0},{12,4},{16,8},{20,12},{24,16},{28,20},{1,25},{... | collective-permute-start | bytes 147464 | tf_op jit(solution)/shard_map/ppermute | solution.py:411
  56.1 0.0 collective-permute-done.9.refs_1_
  56.1 0.0 collective-permute-done.10.refs_2_
  56.1 1.9 %collective-permute-done.11.refs_3_ = f32[2,32,192]{2,1,0:T(8,128)S(1)} collective-permute-done((f32[2,32,192]{2,1,0:T(8,128)S(1)}, f32[2,32,192]{2,1,0:T(8,128)S(1)}, u32[]{:S(2)}, u32[]{:S(2)}) %collective-permute-start.11) | collective-permute-done | bytes 49184 | tf_op jit(solution)/shard_map/ppermute | solution.py:411
  58.0 0.7 collective-permute-start.12
  58.7 4.6 %collective-permute-done.12.refs_8_ = f32[4,32,192]{2,1,0:T(8,128)S(1)} collective-permute-done((f32[4,32,192]{2,1,0:T(8,128)S(1)}, f32[4,32,192]{2,1,0:T(8,128)S(1)}, u32[]{:S(2)}, u32[]{:S(2)}) %collective-permute-start.12) | collective-permute-done | bytes 98336 | tf_op jit(solution)/shard_map/ppermute | solution.py:404
  63.3 0.0 collective-permute-done.13.refs_11_
  63.3 8.6 %correlate.1 = (f32[7,7,2,8,128]{4,3,2,1,0:T(8,128)S(1)}, f32[7,7,2,8,128]{4,3,2,1,0:T(8,128)S(1)}) custom-call(f32[2,32,192]{2,1,0:T(8,128)S(1)} %get-tuple-element.40.refs_0_, f32[2,32,192]{2,1,0:T(8,128)S(1)} %collective-permute-done.9.refs_1_, f32[2,32,192]{2,1,0:T(8,128)S(1)} %collective-permute-done.10.refs_2_, ...), custom_call_target="tpu_custom_call" | custom-call | flops 3699376128 | bytes 3162112 | tf_op jit(solution)/shard_map/correlate/pallas_call | solution.py:373
  71.9 0.1 collective-permute-start.14
  72.0 1.7 %collective-permute-done.14 = f32[7,7,2,8,128]{4,3,2,1,0:T(8,128)S(1)} collective-permute-done((f32[7,7,2,8,128]{4,3,2,1,0:T(8,128)S(1)}, f32[7,7,2,8,128]{4,3,2,1,0:T(8,128)S(1)}, u32[]{:S(2)}, u32[]{:S(2)}) %collective-permute-start.14) | collective-permute-done | bytes 401440 | tf_op jit(solution)/shard_map/ppermute | solution.py:404
  73.7 0.1 add.20
  73.8 2.2 %collective-permute-start.15 = (f32[7,7,2,8,128]{4,3,2,1,0:T(8,128)S(1)}, f32[7,7,2,8,128]{4,3,2,1,0:T(8,128)S(1)}, u32[]{:S(2)}, u32[]{:S(2)}) collective-permute-start(f32[7,7,2,8,128]{4,3,2,1,0:T(8,128)S(1)} %add.20), channel_id=1, source_target_pairs={{0,2},{1,3},{2,0},{3,1},{4,6},{5,7},{6,4},{7,5},{8,10},{9,11},{10,... | collective-permute-start | bytes 1204232 | tf_op jit(solution)/shard_map/ppermute | solution.py:411
  75.9 9.6 %collective-permute-done.15 = f32[7,7,2,8,128]{4,3,2,1,0:T(8,128)S(1)} collective-permute-done((f32[7,7,2,8,128]{4,3,2,1,0:T(8,128)S(1)}, f32[7,7,2,8,128]{4,3,2,1,0:T(8,128)S(1)}, u32[]{:S(2)}, u32[]{:S(2)}) %collective-permute-start.15) | collective-permute-done | bytes 401440 | tf_op jit(solution)/shard_map/ppermute | solution.py:411
  85.5 0.1 add.21
  85.6 0.1 collective-permute-start.16
  85.7 0.8 reshape.33
  86.5 0.9 %collective-permute-done.16 = f32[7,7,2,8,128]{4,3,2,1,0:T(8,128)S(1)} collective-permute-done((f32[7,7,2,8,128]{4,3,2,1,0:T(8,128)S(1)}, f32[7,7,2,8,128]{4,3,2,1,0:T(8,128)S(1)}, u32[]{:S(2)}, u32[]{:S(2)}) %collective-permute-start.16) | collective-permute-done | bytes 401440 | tf_op jit(solution)/shard_map/ppermute | solution.py:404
  87.4 0.1 broadcast_select_fusion.1
  87.5 1.0 %pad_maximum_fusion = f32[7,7,2,16,128]{4,3,2,1,0:T(8,128)} fusion(f32[7,7,2,8,128]{4,3,2,1,0:T(8,128)S(1)} %get-tuple-element.51, f32[7,7,2,8,128]{4,3,2,1,0:T(8,128)S(1)} %get-tuple-element.50), kind=kLoop, calls=%fused_computation | loop fusion | flops 200704 | bytes 1605632 | tf_op jit(solution)/shard_map/concatenate | solution.py:471
  (19 shorter events, 0.3 us)
Async XLA Ops:
  0.6 23.5 %copy-start = (f32[2,128,128]{2,1,0:T(8,128)S(1)}, f32[2,128,128]{2,1,0:T(8,128)}, u32[]{:S(2)}) copy-start(f32[2,128,128]{2,1,0:T(8,128)} %inverse_ref.3) | copy-start | bytes 393220
  2.8 0.8 collective-permute-start
  3.6 7.6 %collective-permute-start.1 = (f32[2,108,128]{2,0,1:T(2,128)S(1)}, f32[2,108,128]{2,0,1:T(2,128)S(1)}, u32[]{:S(2)}, u32[]{:S(2)}) collective-permute-start(f32[2,108,128]{2,0,1:T(2,128)S(1)} %bitcast.36), channel_id=1, source_target_pairs={{0,1},{1,0},{2,3},{3,2},{4,5},{5,4},{6,7},{7,6},{8,9},{9,8},{10,11... | collective-permute-start | bytes 331784 | tf_op jit(solution)/shard_map/ppermute | solution.py:404
  11.5 9.8 %collective-permute-start.3 = (f32[2,168,128]{2,0,1:T(2,128)S(1)}, f32[2,168,128]{2,0,1:T(2,128)S(1)}, u32[]{:S(2)}, u32[]{:S(2)}) collective-permute-start(f32[2,168,128]{2,0,1:T(2,128)S(1)} %bitcast.33), channel_id=1, source_target_pairs={{0,4},{4,0},{8,12},{12,8},{16,20},{20,16},{24,28},{28,24},{1,5},{5... | collective-permute-start | bytes 516104 | tf_op jit(solution)/shard_map/ppermute | solution.py:404
  13.2 8.0 %collective-permute-start.2 = (f32[2,168,128]{2,0,1:T(2,128)S(1)}, f32[2,168,128]{2,0,1:T(2,128)S(1)}, u32[]{:S(2)}, u32[]{:S(2)}) collective-permute-start(f32[2,168,128]{2,0,1:T(2,128)S(1)} %bitcast.34), channel_id=1, source_target_pairs={{4,8},{8,4},{12,16},{16,12},{20,24},{24,20},{5,9},{9,5},{13,17},{1... | collective-permute-start | bytes 516104 | tf_op jit(solution)/shard_map/ppermute | solution.py:404
  14.0 25.7 %collective-permute-start.5 = (f32[2,12,24,128]{3,2,1,0:T(8,128)S(1)}, f32[2,12,24,128]{3,2,1,0:T(8,128)S(1)}, u32[]{:S(2)}, u32[]{:S(2)}) collective-permute-start(f32[2,12,24,128]{3,2,1,0:T(8,128)S(1)} %select_maximum_fusion.2.refs_4_), channel_id=1, source_target_pairs={{0,8},{4,12},{8,16},{12,20},{16,24},{20,28},{24,0},{28,4},{1,9},{5... | collective-permute-start | bytes 884744 | tf_op jit(solution)/shard_map/ppermute | solution.py:411
  17.3 28.8 %collective-permute-start.6 = (f32[2,12,24,128]{3,2,1,0:T(8,128)S(1)}, f32[2,12,24,128]{3,2,1,0:T(8,128)S(1)}, u32[]{:S(2)}, u32[]{:S(2)}) collective-permute-start(f32[2,12,24,128]{3,2,1,0:T(8,128)S(1)} %select_maximum_fusion.2.refs_4_), channel_id=1, source_target_pairs={{0,16},{4,20},{8,24},{12,28},{16,0},{20,4},{24,8},{28,12},{1,17},{... | collective-permute-start | bytes 884744 | tf_op jit(solution)/shard_map/ppermute | solution.py:411
  19.9 26.2 %collective-permute-start.7 = (f32[2,12,24,128]{3,2,1,0:T(8,128)S(1)}, f32[2,12,24,128]{3,2,1,0:T(8,128)S(1)}, u32[]{:S(2)}, u32[]{:S(2)}) collective-permute-start(f32[2,12,24,128]{3,2,1,0:T(8,128)S(1)} %select_maximum_fusion.2.refs_4_), channel_id=1, source_target_pairs={{0,24},{4,28},{8,0},{12,4},{16,8},{20,12},{24,16},{28,20},{1,25},{... | collective-permute-start | bytes 884744 | tf_op jit(solution)/shard_map/ppermute | solution.py:411
  21.3 18.4 %collective-permute-start.4 = (f32[2,12,24,128]{3,2,1,0:T(8,128)S(1)}, f32[2,12,24,128]{3,2,1,0:T(8,128)S(1)}, u32[]{:S(2)}, u32[]{:S(2)}) collective-permute-start(f32[2,12,24,128]{3,2,1,0:T(8,128)S(1)} %select_maximum_fusion.2.refs_4_), channel_id=1, source_target_pairs={{0,4},{4,0},{8,12},{12,8},{16,20},{20,16},{24,28},{28,24},{1,5},{5... | collective-permute-start | bytes 884744 | tf_op jit(solution)/shard_map/ppermute | solution.py:404
  39.7 7.6 %collective-permute-start.8 = (f32[2,12,24,128]{3,2,1,0:T(8,128)S(1)}, f32[2,12,24,128]{3,2,1,0:T(8,128)S(1)}, u32[]{:S(2)}, u32[]{:S(2)}) collective-permute-start(f32[2,12,24,128]{3,2,1,0:T(8,128)S(1)} %collective-permute-done.5.refs_5_), channel_id=1, source_target_pairs={{0,4},{4,0},{8,12},{12,8},{16,20},{20,16},{24,28},{28,24},{1,5},{5... | collective-permute-start | bytes 884744 | tf_op jit(solution)/shard_map/ppermute | solution.py:404
  47.4 15.9 %collective-permute-start.13 = (f32[2,2,12,24,128]{4,3,2,1,0:T(8,128)S(1)}, f32[2,2,12,24,128]{4,3,2,1,0:T(8,128)S(1)}, u32[]{:S(2)}, u32[]{:S(2)}) collective-permute-start(f32[2,2,12,24,128]{4,3,2,1,0:T(8,128)S(1)} %pad_maximum_fusion.1), channel_id=1, source_target_pairs={{0,4},{4,0},{8,12},{12,8},{16,20},{20,16},{24,28},{28,24},{1,5},{5... | collective-permute-start | bytes 1769480 | tf_op jit(solution)/shard_map/ppermute | solution.py:404
  48.2 7.8 %collective-permute-start.9 = (f32[2,32,192]{2,1,0:T(8,128)S(1)}, f32[2,32,192]{2,1,0:T(8,128)S(1)}, u32[]{:S(2)}, u32[]{:S(2)}) collective-permute-start(f32[2,32,192]{2,1,0:T(8,128)S(1)} %get-tuple-element.41), channel_id=1, source_target_pairs={{0,8},{4,12},{8,16},{12,20},{16,24},{20,28},{24,0},{28,4},{1,9},{5... | collective-permute-start | bytes 147464 | tf_op jit(solution)/shard_map/ppermute | solution.py:411
  50.5 5.6 %collective-permute-start.10 = (f32[2,32,192]{2,1,0:T(8,128)S(1)}, f32[2,32,192]{2,1,0:T(8,128)S(1)}, u32[]{:S(2)}, u32[]{:S(2)}) collective-permute-start(f32[2,32,192]{2,1,0:T(8,128)S(1)} %get-tuple-element.42), channel_id=1, source_target_pairs={{0,16},{4,20},{8,24},{12,28},{16,0},{20,4},{24,8},{28,12},{1,17},{... | collective-permute-start | bytes 147464 | tf_op jit(solution)/shard_map/ppermute | solution.py:411
  53.1 4.8 %collective-permute-start.11 = (f32[2,32,192]{2,1,0:T(8,128)S(1)}, f32[2,32,192]{2,1,0:T(8,128)S(1)}, u32[]{:S(2)}, u32[]{:S(2)}) collective-permute-start(f32[2,32,192]{2,1,0:T(8,128)S(1)} %get-tuple-element.43), channel_id=1, source_target_pairs={{0,24},{4,28},{8,0},{12,4},{16,8},{20,12},{24,16},{28,20},{1,25},{... | collective-permute-start | bytes 147464 | tf_op jit(solution)/shard_map/ppermute | solution.py:411
  58.0 5.3 %collective-permute-start.12 = (f32[4,32,192]{2,1,0:T(8,128)S(1)}, f32[4,32,192]{2,1,0:T(8,128)S(1)}, u32[]{:S(2)}, u32[]{:S(2)}) collective-permute-start(f32[4,32,192]{2,1,0:T(8,128)S(1)} %pad_maximum_fusion.5), channel_id=1, source_target_pairs={{0,4},{4,0},{8,12},{12,8},{16,20},{20,16},{24,28},{28,24},{1,5},{5... | collective-permute-start | bytes 294920 | tf_op jit(solution)/shard_map/ppermute | solution.py:404
  71.9 1.8 %collective-permute-start.14 = (f32[7,7,2,8,128]{4,3,2,1,0:T(8,128)S(1)}, f32[7,7,2,8,128]{4,3,2,1,0:T(8,128)S(1)}, u32[]{:S(2)}, u32[]{:S(2)}) collective-permute-start(f32[7,7,2,8,128]{4,3,2,1,0:T(8,128)S(1)} %get-tuple-element.49), channel_id=1, source_target_pairs={{0,1},{1,0},{2,3},{3,2},{4,5},{5,4},{6,7},{7,6},{8,9},{9,8},{10,11... | collective-permute-start | bytes 1204232 | tf_op jit(solution)/shard_map/ppermute | solution.py:404
  73.8 11.8 %collective-permute-start.15 = (f32[7,7,2,8,128]{4,3,2,1,0:T(8,128)S(1)}, f32[7,7,2,8,128]{4,3,2,1,0:T(8,128)S(1)}, u32[]{:S(2)}, u32[]{:S(2)}) collective-permute-start(f32[7,7,2,8,128]{4,3,2,1,0:T(8,128)S(1)} %add.20), channel_id=1, source_target_pairs={{0,2},{1,3},{2,0},{3,1},{4,6},{5,7},{6,4},{7,5},{8,10},{9,11},{10,... | collective-permute-start | bytes 1204232 | tf_op jit(solution)/shard_map/ppermute | solution.py:411
  85.6 1.8 %collective-permute-start.16 = (f32[7,7,2,8,128]{4,3,2,1,0:T(8,128)S(1)}, f32[7,7,2,8,128]{4,3,2,1,0:T(8,128)S(1)}, u32[]{:S(2)}, u32[]{:S(2)}) collective-permute-start(f32[7,7,2,8,128]{4,3,2,1,0:T(8,128)S(1)} %add.21), channel_id=1, source_target_pairs={{0,1},{1,0},{2,3},{3,2},{4,5},{5,4},{6,7},{7,6},{8,9},{9,8},{10,11... | collective-permute-start | bytes 1204232 | tf_op jit(solution)/shard_map/ppermute | solution.py:404

commit v7 on v4

--- a/solution.py
+++ b/solution.py
@@ -304,8 +304,10 @@
     for k in range(half_peers):
         if k == 0:
             twin = own_twin_ref
+        elif k in (1, half_peers - 1):
+            twin = early_ref.at[0 if k == 1 else 1]
         else:
-            twin = late_ref if k == half_peers - 1 else early_ref.at[k - 1]
+            twin = late_ref.at[k - 2]
         for n, (source, tile) in enumerate(zip((piece_refs[k], twin), tiles(k))):
             pltpu.make_async_copy(source, stage.at[tile], sems.at[n, k]).start()
         first, second = tiles(k)
@@ -340,7 +342,8 @@
             to = pl.ds(pl.multiple_of(tile * own + i * cols, cols), cols)
             for b in range(span):
                 for h in range(2):
-                    high, low = split(stage[tile, h, i, pl.ds(span - 1 - b, cols), :])
+                    start = i * (cols + span - 1) + span - 1 - b
+                    high, low = split(stage[tile, h, pl.ds(start, cols), :])
                     s_high[b, to, h * width : (h + 1) * width] = high
                     s_low[b, to, h * width : (h + 1) * width] = low
 
@@ -414,17 +417,22 @@
     return lax.ppermute(value, axis, [(i, (i + shift) % peers) for i in range(peers)])
 
 
-def edges(initial, last, axis):
+def edges(initial, last, axis, rider=None, beside=None):
     even = lax.axis_index(axis) % 2 == 0
     shape = initial.shape
     initial, last = (value.reshape(shape[0], -1, shape[-1]) for value in (initial, last))
     inner = jnp.where(even, last, initial)
     outer = swap(jnp.where(even, initial, last), axis, 1)
-    if axis == "col":
-        inner, outer = lax.optimization_barrier((inner, outer))
-    inner = swap(inner, axis, 0)
-    inner, outer = inner.reshape(shape), outer.reshape(shape)
-    return jnp.where(even, outer, inner), jnp.where(even, inner, outer)
+    count = inner.shape[1]
+    if beside is None:
+        inner = swap(jnp.concatenate([inner, rider], axis=1), axis, 0)
+        inner, rider = inner[:, :count], inner[:, count:]
+    else:
+        inner, outer, rider = lax.optimization_barrier((inner, outer, beside))
+        inner = swap(inner, axis, 0)
+    inner = inner.reshape(shape)
+    outer = outer.reshape(shape)
+    return jnp.where(even, outer, inner), jnp.where(even, inner, outer), rider
 
 
 def on_device(adjoint_source, saved_currents, lag_blocks, element_inverse):
@@ -436,34 +444,42 @@
 
     source = adjoint_source.transpose(2, 0, 1, 3)
     saved = saved_currents.transpose(2, 0, 1, 3)
+    twin_own = swap(saved, "row", 0)
     initial = jnp.concatenate([source[:, :, :halo], saved[:, :, :reach]], axis=2)
     last = jnp.concatenate([source[:, :, cols - halo :], saved[:, :, cols - reach :]], axis=2)
-    before, after = edges(initial, last, "col")
+    before, after, twin_own = edges(initial, last, "col", beside=twin_own)
     source = jnp.concatenate([before[:, :, :halo], source, after[:, :, :halo]], axis=2)
     saved = jnp.concatenate([before[:, :, halo:], saved, after[:, :, halo:]], axis=2)
-    before, after = edges(source[:, :halo], source[:, rows - halo :], "row")
+    sides = jnp.concatenate([saved[:, :, :reach], saved[:, :, cols + reach :]], axis=2)
+    twin_sides = sides.reshape(parts, -1, width)
+    before, after, arrived = edges(source[:, :halo], source[:, rows - halo :], "row", twin_sides)
     source = jnp.concatenate([before, source, after], axis=1)
     wide = round_up(cols + 2 * halo, 8)
     source = jnp.pad(source, ((0, 0), (0, 0), (0, wide - cols - 2 * halo), (0, 0)))
-
-    pitch = round_up(cols + 2 * reach, 8)
-    saved = jnp.pad(saved, ((0, 0), (0, 0), (0, pitch - cols - 2 * reach), (0, 0)))
-    pieces = [shifted(saved, "row", k) for k in range(0, peers, 2)]
-    own_twin = swap(saved, "row", 0)
+    twin_sides = arrived.reshape(sides.shape)
+    own_twin = jnp.concatenate([twin_sides[:, :, :reach], twin_own, twin_sides[:, :, reach:]], axis=2)
+    own_twin = own_twin.reshape(parts, -1, width)
+
+    saved = saved.reshape(parts, -1, width)
+    pieces = [saved] + [None] * (peers // 2 - 1)
+    middle = lax.optimization_barrier((saved, arrived))[0]
+    for k in range(1, peers // 2):
+        near = k in (1, peers // 2 - 1)
+        pieces[k] = shifted(saved if near else middle, "row", 2 * k)
 
     second, own_source, high, low = first_sweep(source, element_inverse, lag_blocks, rows, cols)
-    second, own_twin, early = lax.optimization_barrier((second, own_twin, jnp.stack(pieces[1:-1])))
+    second, own_twin, early = lax.optimization_barrier((second, own_twin, jnp.stack([pieces[1], pieces[-1]])))
     early_twins = swap(early, "row", 0)
     adjoint, sends = second_sweep(second, own_source, element_inverse, high, low, peers)
-    late, sends = lax.optimization_barrier((pieces[-1], sends))
-    late_twin = swap(late, "row", 0)
+    *late, sends = lax.optimization_barrier((*pieces[2:-1], sends))
+    late_twins = swap(jnp.stack(late), "row", 0)
     shares = [shifted(send, "row", 2 * k) for k, send in enumerate(sends)]
     twin_shares = swap(jnp.stack([received[1] for received in shares]), "row", 0)
 
     elements = rows * peers * cols * lax.axis_size("col")
     factor = -1.0 / math.sqrt(elements)
     mine, other = correlate(
-        shares, twin_shares, pieces, (own_twin, early_twins, late_twin), rows, cols, span, factor
+        shares, twin_shares, pieces, (own_twin, early_twins, late_twins), rows, cols, span, factor
     )
     mine = mine + swap(other, "col", 0)
     total = mine

time: 93.1 us -> 91.2 us (0.980); the launches traced: 91.8 us -> 91 us
  starting transfers between devices: 34 us -> 26.4 us
  waiting for transfers between devices: 21.5 us -> 27.6 us
    ppermute x10, starting transfers between devices: 18.6 us -> 9.88 us  [swap(): return lax.ppermute(value, axis, pairs)]
    ppermute x10, waiting for transfers between devices: 6.61 us -> 13.7 us  [swap(): return lax.ppermute(value, axis, pairs)]
    ppermute x7, starting transfers between devices: 15.5 us -> 16.5 us  [shifted(): lax.ppermute(value, axis, [(i, (i + shift) % peers) for i in range(peers)])]
    ppermute x7, waiting for transfers between devices: 14.9 us -> 13.9 us  [shifted(): lax.ppermute(value, axis, [(i, (i + shift) % peers) for i in range(peers)])]
    unnamed x8 -> x10, local copies, waits for them, and re-layouts: 1.98 us -> 2.01 us
  transfers between devices with their start and end apart: 17 -> 17, of which waited for: 9 -> 9; matrix products, arithmetic and copies ran while one was open for 1% -> 3% of each run, Pallas kernels for 24% -> 24%
where the time goes in v7:
time: 91.2 us; the launch traced here: 91 us
  Pallas kernels  30.2 us (33%)
  waiting for transfers between devices  27.6 us (30%)
  starting transfers between devices  26.4 us (29%)
  local copies, waits for them, and re-layouts  3.92 us (4%)
  other arithmetic  1.84 us (2%)
  between operations  1.04 us (1%)
    ppermute x7, starting transfers between devices, shifted(): lax.ppermute(value, axis, [(i, (i + shift) % peers) for i in range(peers)])  16.5 us
    pallas_call x1, Pallas kernels, first_sweep(): pl.pallas_call(functools.partial(first_sweep_kernel, (rows, cols, span, p...  15.6 us
    ppermute x7, waiting for transfers between devices, shifted(): lax.ppermute(value, axis, [(i, (i + shift) % peers) for i in range(peers)])  13.9 us
    ppermute x10, waiting for transfers between devices, swap(): return lax.ppermute(value, axis, pairs)  13.7 us
    ppermute x10, starting transfers between devices, swap(): return lax.ppermute(value, axis, pairs)  9.88 us
    pallas_call x1, Pallas kernels, correlate(): pl.pallas_call(functools.partial(correlate_kernel, (rows, cols, span, pee...  8.36 us
    pallas_call x1, Pallas kernels, second_sweep(): pl.pallas_call(functools.partial(second_sweep_kernel, (rows, cols, span,...  6.25 us
    unnamed x10, local copies, waits for them, and re-layouts  2.01 us
  transfers between devices with their start and end apart: 17, of which 9 were waited for; matrix products, arithmetic and copies ran while one was open for 3% of the time, Pallas kernels for 24%

profile of v7, /device:TPU:0, one launch (start us, length us, event | category | flops | bytes accessed | tf_op | source)
XLA Modules:
  0.0 91.0 jit_solution(14171826547796828823)
XLA Ops:
  0.6 0.0 copy-start
  0.6 1.0 %copy.38 = f32[12,16,2,128]{3,1,0,2:T(8,128)S(1)} copy(f32[12,16,2,128]{3,2,1,0:T(2,128)} %param.5) | data formatting | bytes 393216 | tf_op args[1]
  1.6 3.0 %collective-permute-start.1 = (f32[2,12,16,128]{3,2,1,0:T(8,128)S(1)}, f32[2,12,16,128]{3,2,1,0:T(8,128)S(1)}, u32[]{:S(2)}, u32[]{:S(2)}) collective-permute-start(f32[2,12,16,128]{3,2,1,0:T(8,128)S(1)} %bitcast.33), channel_id=1, source_target_pairs={{0,4},{4,0},{8,12},{12,8},{16,20},{20,16},{24,28},{28,24},{1,5},{5... | collective-permute-start | bytes 589832 | tf_op jit(solution)/shard_map/ppermute | solution.py:410
  4.7 0.9 %copy.39 = f32[12,16,2,128]{3,1,0,2:T(8,128)S(1)} copy(f32[12,16,2,128]{3,2,1,0:T(2,128)} %param.4) | data formatting | bytes 393216 | tf_op args[0]
  5.7 0.1 fusion.5
  5.7 0.1 copy.11
  5.8 0.7 collective-permute-start
  6.5 0.1 copy.10
  6.6 0.0 collective-permute-done
  6.6 2.9 %collective-permute-done.1 = f32[2,12,16,128]{3,2,1,0:T(8,128)S(1)} collective-permute-done((f32[2,12,16,128]{3,2,1,0:T(8,128)S(1)}, f32[2,12,16,128]{3,2,1,0:T(8,128)S(1)}, u32[]{:S(2)}, u32[]{:S(2)}) %collective-permute-start.1) | collective-permute-done | bytes 196640 | tf_op jit(solution)/shard_map/ppermute | solution.py:410
  9.6 2.2 %collective-permute-start.2 = (f32[2,108,128]{2,0,1:T(2,128)S(1)}, f32[2,108,128]{2,0,1:T(2,128)S(1)}, u32[]{:S(2)}, u32[]{:S(2)}) collective-permute-start(f32[2,108,128]{2,0,1:T(2,128)S(1)} %bitcast.48), channel_id=1, source_target_pairs={{0,1},{1,0},{2,3},{3,2},{4,5},{5,4},{6,7},{7,6},{8,9},{9,8},{10,11... | collective-permute-start | bytes 331784 | tf_op jit(solution)/shard_map/ppermute | solution.py:410
  11.8 1.0 %collective-permute-done.2 = f32[2,108,128]{2,0,1:T(2,128)S(1)} collective-permute-done((f32[2,108,128]{2,0,1:T(2,128)S(1)}, f32[2,108,128]{2,0,1:T(2,128)S(1)}, u32[]{:S(2)}, u32[]{:S(2)}) %collective-permute-start.2) | collective-permute-done | bytes 110624 | tf_op jit(solution)/shard_map/ppermute | solution.py:410
  12.9 0.1 copy.18
  13.0 0.1 pad_maximum_fusion.2
  13.1 0.1 copy.15
  13.3 0.1 pad_maximum_fusion.5
  13.4 0.6 collective-permute-start.4
  14.0 0.1 copy.14
  14.1 0.7 collective-permute-start.3
  14.8 0.2 copy.24
  15.1 4.3 %collective-permute-start.5 = (f32[2,264,128]{2,1,0:T(8,128)S(1)}, f32[2,264,128]{2,1,0:T(8,128)S(1)}, u32[]{:S(2)}, u32[]{:S(2)}) collective-permute-start(f32[2,264,128]{2,1,0:T(8,128)S(1)} %copy.25.refs_4_), channel_id=1, source_target_pairs={{0,8},{4,12},{8,16},{12,20},{16,24},{20,28},{24,0},{28,4},{1,9},{5... | collective-permute-start | bytes 811016 | tf_op jit(solution)/shard_map/ppermute | solution.py:417
  19.3 2.1 %collective-permute-start.6 = (f32[2,264,128]{2,1,0:T(8,128)S(1)}, f32[2,264,128]{2,1,0:T(8,128)S(1)}, u32[]{:S(2)}, u32[]{:S(2)}) collective-permute-start(f32[2,264,128]{2,1,0:T(8,128)S(1)} %copy.25.refs_4_), channel_id=1, source_target_pairs={{0,24},{4,28},{8,0},{12,4},{16,8},{20,12},{24,16},{28,20},{1,25},{... | collective-permute-start | bytes 811016 | tf_op jit(solution)/shard_map/ppermute | solution.py:417
  21.4 0.0 collective-permute-done.3
  21.4 1.9 %collective-permute-done.4 = f32[2,240,128]{2,0,1:T(2,128)S(1)} collective-permute-done((f32[2,240,128]{2,0,1:T(2,128)S(1)}, f32[2,240,128]{2,0,1:T(2,128)S(1)}, u32[]{:S(2)}, u32[]{:S(2)}) %collective-permute-start.4) | collective-permute-done | bytes 245792 | tf_op jit(solution)/shard_map/ppermute | solution.py:410
  23.4 0.1 broadcast_select_fusion.3
  23.6 4.6 %collective-permute-start.7 = (f32[2,264,128]{2,1,0:T(8,128)S(1)}, f32[2,264,128]{2,1,0:T(8,128)S(1)}, u32[]{:S(2)}, u32[]{:S(2)}) collective-permute-start(f32[2,264,128]{2,1,0:T(8,128)S(1)} %copy.27), channel_id=1, source_target_pairs={{0,16},{4,20},{8,24},{12,28},{16,0},{20,4},{24,8},{28,12},{1,17},{... | collective-permute-start | bytes 811016 | tf_op jit(solution)/shard_map/ppermute | solution.py:417
  28.2 0.1 select_maximum_fusion.source_ref
  28.3 0.0 copy-done
  28.3 15.6 %first_sweep.1 = (f32[18,24,256]{2,1,0:T(8,128)S(1)}, f32[12,16,256]{2,1,0:T(8,128)S(1)}, bf16[7,7,256,256]{3,2,1,0:T(8,128)(2,1)S(1)}, bf16[7,7,256,256]{3,2,1,0:T(8,128)(2,1)S(1)}) custom-call(f32[2,24,32,128]{3,2,1,0:T(8,128)S(1)} %select_maximum_fusion.source_ref, f32[2,128,128]{2,1,0:T(8,128)S(1)} %copy-done, f32[7,7,2,128,128]{4,3,2,1,0:T(8,128)} %blocks_hbm.1), custom_call_target="tpu_custom_call" | custom-call | flops 8323596288 | bytes 19267584 | tf_op jit(solution)/shard_map/first_sweep/pallas_call | solution.py:170
  44.0 0.2 copy.23
  44.3 0.0 collective-permute-done.5.refs_5_
  44.3 0.0 collective-permute-done.6.refs_7_
  44.3 0.6 collective-permute-start.12
  44.9 6.2 %second_sweep.1 = (f32[12,16,256]{2,1,0:T(8,128)S(1)}, f32[2,32,192]{2,1,0:T(8,128)S(1)}, f32[2,32,192]{2,1,0:T(8,128)S(1)}, f32[2,32,192]{2,1,0:T(8,128)S(1)}, f32[2,32,192]{2,1,0:T(8,128)S(1)}) custom-call(f32[18,24,256]{2,1,0:T(8,128)S(1)} %get-tuple-element.29.second_ref, f32[12,16,256]{2,1,0:T(8,128)S(1)} %get-tuple-element.30.source_ref, ...), custom_call_target="tpu_custom_call" | custom-call | flops 3699376128 | bytes 12845056 | tf_op jit(solution)/shard_map/second_sweep/pallas_call | solution.py:260
  51.2 0.0 collective-permute-done.7.refs_6_
  51.2 1.6 %collective-permute-start.13 = (f32[1,2,264,128]{3,2,1,0:T(8,128)S(1)}, f32[1,2,264,128]{3,2,1,0:T(8,128)S(1)}, u32[]{:S(2)}, u32[]{:S(2)}) collective-permute-start(f32[1,2,264,128]{3,2,1,0:T(8,128)S(1)} %bitcast.27), channel_id=1, source_target_pairs={{0,4},{4,0},{8,12},{12,8},{16,20},{20,16},{24,28},{28,24},{1,5},{5... | collective-permute-start | bytes 811016 | tf_op jit(solution)/shard_map/ppermute | solution.py:410
  52.7 1.6 %collective-permute-start.8 = (f32[2,32,192]{2,1,0:T(8,128)S(1)}, f32[2,32,192]{2,1,0:T(8,128)S(1)}, u32[]{:S(2)}, u32[]{:S(2)}) collective-permute-start(f32[2,32,192]{2,1,0:T(8,128)S(1)} %get-tuple-element.40), channel_id=1, source_target_pairs={{0,8},{4,12},{8,16},{12,20},{16,24},{20,28},{24,0},{28,4},{1,9},{5... | collective-permute-start | bytes 147464 | tf_op jit(solution)/shard_map/ppermute | solution.py:417
  54.3 0.3 collective-permute-start.9
  54.7 2.0 %collective-permute-start.10 = (f32[2,32,192]{2,1,0:T(8,128)S(1)}, f32[2,32,192]{2,1,0:T(8,128)S(1)}, u32[]{:S(2)}, u32[]{:S(2)}) collective-permute-start(f32[2,32,192]{2,1,0:T(8,128)S(1)} %get-tuple-element.42), channel_id=1, source_target_pairs={{0,24},{4,28},{8,0},{12,4},{16,8},{20,12},{24,16},{28,20},{1,25},{... | collective-permute-start | bytes 147464 | tf_op jit(solution)/shard_map/ppermute | solution.py:417
  56.7 2.2 %collective-permute-done.8.refs_1_ = f32[2,32,192]{2,1,0:T(8,128)S(1)} collective-permute-done((f32[2,32,192]{2,1,0:T(8,128)S(1)}, f32[2,32,192]{2,1,0:T(8,128)S(1)}, u32[]{:S(2)}, u32[]{:S(2)}) %collective-permute-start.8) | collective-permute-done | bytes 49184 | tf_op jit(solution)/shard_map/ppermute | solution.py:417
  58.9 1.8 %collective-permute-done.9.refs_2_ = f32[2,32,192]{2,1,0:T(8,128)S(1)} collective-permute-done((f32[2,32,192]{2,1,0:T(8,128)S(1)}, f32[2,32,192]{2,1,0:T(8,128)S(1)}, u32[]{:S(2)}, u32[]{:S(2)}) %collective-permute-start.9) | collective-permute-done | bytes 49184 | tf_op jit(solution)/shard_map/ppermute | solution.py:417
  60.8 0.0 collective-permute-done.10.refs_3_
  60.8 0.4 collective-permute-start.11
  61.2 5.2 %collective-permute-done.11.refs_8_ = f32[4,32,192]{2,1,0:T(8,128)S(1)} collective-permute-done((f32[4,32,192]{2,1,0:T(8,128)S(1)}, f32[4,32,192]{2,1,0:T(8,128)S(1)}, u32[]{:S(2)}, u32[]{:S(2)}) %collective-permute-start.11) | collective-permute-done | bytes 98336 | tf_op jit(solution)/shard_map/ppermute | solution.py:410
  66.4 0.0 collective-permute-done.13.refs_11_
  66.4 0.0 collective-permute-done.12.refs_10_
  66.4 8.4 %correlate.1 = (f32[7,7,2,8,128]{4,3,2,1,0:T(8,128)S(1)}, f32[7,7,2,8,128]{4,3,2,1,0:T(8,128)S(1)}) custom-call(f32[2,32,192]{2,1,0:T(8,128)S(1)} %get-tuple-element.39.refs_0_, f32[2,32,192]{2,1,0:T(8,128)S(1)} %collective-permute-done.8.refs_1_, f32[2,32,192]{2,1,0:T(8,128)S(1)} %collective-permute-done.9.refs_2_, ...), custom_call_target="tpu_custom_call" | custom-call | flops 3699376128 | bytes 2965504 | tf_op jit(solution)/shard_map/correlate/pallas_call | solution.py:379
  74.8 0.1 collective-permute-start.14
  74.9 1.7 %collective-permute-done.14 = f32[7,7,2,8,128]{4,3,2,1,0:T(8,128)S(1)} collective-permute-done((f32[7,7,2,8,128]{4,3,2,1,0:T(8,128)S(1)}, f32[7,7,2,8,128]{4,3,2,1,0:T(8,128)S(1)}, u32[]{:S(2)}, u32[]{:S(2)}) %collective-permute-start.14) | collective-permute-done | bytes 401440 | tf_op jit(solution)/shard_map/ppermute | solution.py:410
  76.6 0.1 add.18
  76.7 1.6 %collective-permute-start.15 = (f32[7,7,2,8,128]{4,3,2,1,0:T(8,128)S(1)}, f32[7,7,2,8,128]{4,3,2,1,0:T(8,128)S(1)}, u32[]{:S(2)}, u32[]{:S(2)}) collective-permute-start(f32[7,7,2,8,128]{4,3,2,1,0:T(8,128)S(1)} %add.18), channel_id=1, source_target_pairs={{0,2},{1,3},{2,0},{3,1},{4,6},{5,7},{6,4},{7,5},{8,10},{9,11},{10,... | collective-permute-start | bytes 1204232 | tf_op jit(solution)/shard_map/ppermute | solution.py:417
  78.3 9.8 %collective-permute-done.15 = f32[7,7,2,8,128]{4,3,2,1,0:T(8,128)S(1)} collective-permute-done((f32[7,7,2,8,128]{4,3,2,1,0:T(8,128)S(1)}, f32[7,7,2,8,128]{4,3,2,1,0:T(8,128)S(1)}, u32[]{:S(2)}, u32[]{:S(2)}) %collective-permute-start.15) | collective-permute-done | bytes 401440 | tf_op jit(solution)/shard_map/ppermute | solution.py:417
  88.1 0.1 add.19
  88.2 0.1 collective-permute-start.16
  88.2 0.8 reshape.47
  89.0 0.9 %collective-permute-done.16 = f32[7,7,2,8,128]{4,3,2,1,0:T(8,128)S(1)} collective-permute-done((f32[7,7,2,8,128]{4,3,2,1,0:T(8,128)S(1)}, f32[7,7,2,8,128]{4,3,2,1,0:T(8,128)S(1)}, u32[]{:S(2)}, u32[]{:S(2)}) %collective-permute-start.16) | collective-permute-done | bytes 401440 | tf_op jit(solution)/shard_map/ppermute | solution.py:410
  90.0 0.1 broadcast_select_fusion.1
  90.0 1.0 %pad_maximum_fusion = f32[7,7,2,16,128]{4,3,2,1,0:T(8,128)} fusion(f32[7,7,2,8,128]{4,3,2,1,0:T(8,128)S(1)} %get-tuple-element.49, f32[7,7,2,8,128]{4,3,2,1,0:T(8,128)S(1)} %get-tuple-element.48), kind=kLoop, calls=%fused_computation | loop fusion | flops 200704 | bytes 1605632 | tf_op jit(solution)/shard_map/concatenate | solution.py:490
  (30 shorter events, 0.5 us)
Async XLA Ops:
  0.6 27.7 %copy-start = (f32[2,128,128]{2,1,0:T(8,128)S(1)}, f32[2,128,128]{2,1,0:T(8,128)}, u32[]{:S(2)}) copy-start(f32[2,128,128]{2,1,0:T(8,128)} %inverse_ref.3) | copy-start | bytes 393220
  1.6 7.9 %collective-permute-start.1 = (f32[2,12,16,128]{3,2,1,0:T(8,128)S(1)}, f32[2,12,16,128]{3,2,1,0:T(8,128)S(1)}, u32[]{:S(2)}, u32[]{:S(2)}) collective-permute-start(f32[2,12,16,128]{3,2,1,0:T(8,128)S(1)} %bitcast.33), channel_id=1, source_target_pairs={{0,4},{4,0},{8,12},{12,8},{16,20},{20,16},{24,28},{28,24},{1,5},{5... | collective-permute-start | bytes 589832 | tf_op jit(solution)/shard_map/ppermute | solution.py:410
  5.8 0.8 collective-permute-start
  9.6 3.2 %collective-permute-start.2 = (f32[2,108,128]{2,0,1:T(2,128)S(1)}, f32[2,108,128]{2,0,1:T(2,128)S(1)}, u32[]{:S(2)}, u32[]{:S(2)}) collective-permute-start(f32[2,108,128]{2,0,1:T(2,128)S(1)} %bitcast.48), channel_id=1, source_target_pairs={{0,1},{1,0},{2,3},{3,2},{4,5},{5,4},{6,7},{7,6},{8,9},{9,8},{10,11... | collective-permute-start | bytes 331784 | tf_op jit(solution)/shard_map/ppermute | solution.py:410
  13.4 10.0 %collective-permute-start.4 = (f32[2,240,128]{2,0,1:T(2,128)S(1)}, f32[2,240,128]{2,0,1:T(2,128)S(1)}, u32[]{:S(2)}, u32[]{:S(2)}) collective-permute-start(f32[2,240,128]{2,0,1:T(2,128)S(1)} %pad_maximum_fusion.5), channel_id=1, source_target_pairs={{0,4},{4,0},{8,12},{12,8},{16,20},{20,16},{24,28},{28,24},{1,5},{5... | collective-permute-start | bytes 737288 | tf_op jit(solution)/shard_map/ppermute | solution.py:410
  14.1 7.3 %collective-permute-start.3 = (f32[2,168,128]{2,0,1:T(2,128)S(1)}, f32[2,168,128]{2,0,1:T(2,128)S(1)}, u32[]{:S(2)}, u32[]{:S(2)}) collective-permute-start(f32[2,168,128]{2,0,1:T(2,128)S(1)} %bitcast.46), channel_id=1, source_target_pairs={{4,8},{8,4},{12,16},{16,12},{20,24},{24,20},{5,9},{9,5},{13,17},{1... | collective-permute-start | bytes 516104 | tf_op jit(solution)/shard_map/ppermute | solution.py:410
  15.1 29.2 %collective-permute-start.5 = (f32[2,264,128]{2,1,0:T(8,128)S(1)}, f32[2,264,128]{2,1,0:T(8,128)S(1)}, u32[]{:S(2)}, u32[]{:S(2)}) collective-permute-start(f32[2,264,128]{2,1,0:T(8,128)S(1)} %copy.25.refs_4_), channel_id=1, source_target_pairs={{0,8},{4,12},{8,16},{12,20},{16,24},{20,28},{24,0},{28,4},{1,9},{5... | collective-permute-start | bytes 811016 | tf_op jit(solution)/shard_map/ppermute | solution.py:417
  19.3 24.9 %collective-permute-start.6 = (f32[2,264,128]{2,1,0:T(8,128)S(1)}, f32[2,264,128]{2,1,0:T(8,128)S(1)}, u32[]{:S(2)}, u32[]{:S(2)}) collective-permute-start(f32[2,264,128]{2,1,0:T(8,128)S(1)} %copy.25.refs_4_), channel_id=1, source_target_pairs={{0,24},{4,28},{8,0},{12,4},{16,8},{20,12},{24,16},{28,20},{1,25},{... | collective-permute-start | bytes 811016 | tf_op jit(solution)/shard_map/ppermute | solution.py:417
  23.6 27.6 %collective-permute-start.7 = (f32[2,264,128]{2,1,0:T(8,128)S(1)}, f32[2,264,128]{2,1,0:T(8,128)S(1)}, u32[]{:S(2)}, u32[]{:S(2)}) collective-permute-start(f32[2,264,128]{2,1,0:T(8,128)S(1)} %copy.27), channel_id=1, source_target_pairs={{0,16},{4,20},{8,24},{12,28},{16,0},{20,4},{24,8},{28,12},{1,17},{... | collective-permute-start | bytes 811016 | tf_op jit(solution)/shard_map/ppermute | solution.py:417
  44.3 22.1 %collective-permute-start.12 = (f32[2,2,264,128]{3,2,1,0:T(8,128)S(1)}, f32[2,2,264,128]{3,2,1,0:T(8,128)S(1)}, u32[]{:S(2)}, u32[]{:S(2)}) collective-permute-start(f32[2,2,264,128]{3,2,1,0:T(8,128)S(1)} %pad_maximum_fusion.1), channel_id=1, source_target_pairs={{0,4},{4,0},{8,12},{12,8},{16,20},{20,16},{24,28},{28,24},{1,5},{5... | collective-permute-start | bytes 1622024 | tf_op jit(solution)/shard_map/ppermute | solution.py:410
  51.2 15.3 %collective-permute-start.13 = (f32[1,2,264,128]{3,2,1,0:T(8,128)S(1)}, f32[1,2,264,128]{3,2,1,0:T(8,128)S(1)}, u32[]{:S(2)}, u32[]{:S(2)}) collective-permute-start(f32[1,2,264,128]{3,2,1,0:T(8,128)S(1)} %bitcast.27), channel_id=1, source_target_pairs={{0,4},{4,0},{8,12},{12,8},{16,20},{20,16},{24,28},{28,24},{1,5},{5... | collective-permute-start | bytes 811016 | tf_op jit(solution)/shard_map/ppermute | solution.py:410
  52.7 6.2 %collective-permute-start.8 = (f32[2,32,192]{2,1,0:T(8,128)S(1)}, f32[2,32,192]{2,1,0:T(8,128)S(1)}, u32[]{:S(2)}, u32[]{:S(2)}) collective-permute-start(f32[2,32,192]{2,1,0:T(8,128)S(1)} %get-tuple-element.40), channel_id=1, source_target_pairs={{0,8},{4,12},{8,16},{12,20},{16,24},{20,28},{24,0},{28,4},{1,9},{5... | collective-permute-start | bytes 147464 | tf_op jit(solution)/shard_map/ppermute | solution.py:417
  54.3 6.4 %collective-permute-start.9 = (f32[2,32,192]{2,1,0:T(8,128)S(1)}, f32[2,32,192]{2,1,0:T(8,128)S(1)}, u32[]{:S(2)}, u32[]{:S(2)}) collective-permute-start(f32[2,32,192]{2,1,0:T(8,128)S(1)} %get-tuple-element.41), channel_id=1, source_target_pairs={{0,16},{4,20},{8,24},{12,28},{16,0},{20,4},{24,8},{28,12},{1,17},{... | collective-permute-start | bytes 147464 | tf_op jit(solution)/shard_map/ppermute | solution.py:417
  54.7 6.1 %collective-permute-start.10 = (f32[2,32,192]{2,1,0:T(8,128)S(1)}, f32[2,32,192]{2,1,0:T(8,128)S(1)}, u32[]{:S(2)}, u32[]{:S(2)}) collective-permute-start(f32[2,32,192]{2,1,0:T(8,128)S(1)} %get-tuple-element.42), channel_id=1, source_target_pairs={{0,24},{4,28},{8,0},{12,4},{16,8},{20,12},{24,16},{28,20},{1,25},{... | collective-permute-start | bytes 147464 | tf_op jit(solution)/shard_map/ppermute | solution.py:417
  60.8 5.6 %collective-permute-start.11 = (f32[4,32,192]{2,1,0:T(8,128)S(1)}, f32[4,32,192]{2,1,0:T(8,128)S(1)}, u32[]{:S(2)}, u32[]{:S(2)}) collective-permute-start(f32[4,32,192]{2,1,0:T(8,128)S(1)} %pad_maximum_fusion.8), channel_id=1, source_target_pairs={{0,4},{4,0},{8,12},{12,8},{16,20},{20,16},{24,28},{28,24},{1,5},{5... | collective-permute-start | bytes 294920 | tf_op jit(solution)/shard_map/ppermute | solution.py:410
  74.8 1.8 %collective-permute-start.14 = (f32[7,7,2,8,128]{4,3,2,1,0:T(8,128)S(1)}, f32[7,7,2,8,128]{4,3,2,1,0:T(8,128)S(1)}, u32[]{:S(2)}, u32[]{:S(2)}) collective-permute-start(f32[7,7,2,8,128]{4,3,2,1,0:T(8,128)S(1)} %get-tuple-element.47), channel_id=1, source_target_pairs={{0,1},{1,0},{2,3},{3,2},{4,5},{5,4},{6,7},{7,6},{8,9},{9,8},{10,11... | collective-permute-start | bytes 1204232 | tf_op jit(solution)/shard_map/ppermute | solution.py:410
  76.7 11.4 %collective-permute-start.15 = (f32[7,7,2,8,128]{4,3,2,1,0:T(8,128)S(1)}, f32[7,7,2,8,128]{4,3,2,1,0:T(8,128)S(1)}, u32[]{:S(2)}, u32[]{:S(2)}) collective-permute-start(f32[7,7,2,8,128]{4,3,2,1,0:T(8,128)S(1)} %add.18), channel_id=1, source_target_pairs={{0,2},{1,3},{2,0},{3,1},{4,6},{5,7},{6,4},{7,5},{8,10},{9,11},{10,... | collective-permute-start | bytes 1204232 | tf_op jit(solution)/shard_map/ppermute | solution.py:417
  88.2 1.8 %collective-permute-start.16 = (f32[7,7,2,8,128]{4,3,2,1,0:T(8,128)S(1)}, f32[7,7,2,8,128]{4,3,2,1,0:T(8,128)S(1)}, u32[]{:S(2)}, u32[]{:S(2)}) collective-permute-start(f32[7,7,2,8,128]{4,3,2,1,0:T(8,128)S(1)} %add.19), channel_id=1, source_target_pairs={{0,1},{1,0},{2,3},{3,2},{4,5},{5,4},{6,7},{7,6},{8,9},{9,8},{10,11... | collective-permute-start | bytes 1204232 | tf_op jit(solution)/shard_map/ppermute | solution.py:410

commit v8 on v7

--- a/solution.py
+++ b/solution.py
@@ -428,7 +428,9 @@
         inner = swap(jnp.concatenate([inner, rider], axis=1), axis, 0)
         inner, rider = inner[:, :count], inner[:, count:]
     else:
-        inner, outer, rider = lax.optimization_barrier((inner, outer, beside))
+        inner, beside = lax.optimization_barrier((inner, beside))
+        rider = swap(beside, "row", 0)
+        inner, outer, rider = lax.optimization_barrier((inner, outer, rider))
         inner = swap(inner, axis, 0)
     inner = inner.reshape(shape)
     outer = outer.reshape(shape)
@@ -444,10 +446,9 @@
 
     source = adjoint_source.transpose(2, 0, 1, 3)
     saved = saved_currents.transpose(2, 0, 1, 3)
-    twin_own = swap(saved, "row", 0)
     initial = jnp.concatenate([source[:, :, :halo], saved[:, :, :reach]], axis=2)
     last = jnp.concatenate([source[:, :, cols - halo :], saved[:, :, cols - reach :]], axis=2)
-    before, after, twin_own = edges(initial, last, "col", beside=twin_own)
+    before, after, twin_own = edges(initial, last, "col", beside=saved)
     source = jnp.concatenate([before[:, :, :halo], source, after[:, :, :halo]], axis=2)
     saved = jnp.concatenate([before[:, :, halo:], saved, after[:, :, halo:]], axis=2)
     sides = jnp.concatenate([saved[:, :, :reach], saved[:, :, cols + reach :]], axis=2)
@@ -461,11 +462,10 @@
     own_twin = own_twin.reshape(parts, -1, width)
 
     saved = saved.reshape(parts, -1, width)
-    pieces = [saved] + [None] * (peers // 2 - 1)
-    middle = lax.optimization_barrier((saved, arrived))[0]
-    for k in range(1, peers // 2):
-        near = k in (1, peers // 2 - 1)
-        pieces[k] = shifted(saved if near else middle, "row", 2 * k)
+    pieces = {0: saved}
+    for k in sorted(range(1, peers // 2), key=lambda k: min(k, peers // 2 - k)):
+        pieces[k] = shifted(saved, "row", 2 * k)
+    pieces = [pieces[k] for k in range(peers // 2)]
 
     second, own_source, high, low = first_sweep(source, element_inverse, lag_blocks, rows, cols)
     second, own_twin, early = lax.optimization_barrier((second, own_twin, jnp.stack([pieces[1], pieces[-1]])))

time: 91.2 us -> 88.7 us (0.973)
  starting transfers between devices: 26.4 us -> 24.8 us
    ppermute x7, starting transfers between devices: 16.5 us -> 15.4 us  [shifted(): lax.ppermute(value, axis, [(i, (i + shift) % peers) for i in range(peers)])]
    ppermute x7, waiting for transfers between devices: 13.9 us -> 12.8 us  [shifted(): lax.ppermute(value, axis, [(i, (i + shift) % peers) for i in range(peers)])]
  transfers between devices with their start and end apart: 17 -> 17, of which waited for: 9 -> 10; matrix products, arithmetic and copies ran while one was open for 3% -> 2% of each run, Pallas kernels for 24% -> 25%
where the time goes in v8:
time: 88.7 us; the launch traced here: 88.5 us
  Pallas kernels  30.2 us (34%)
  waiting for transfers between devices  26.7 us (30%)
  starting transfers between devices  24.8 us (28%)
  local copies, waits for them, and re-layouts  3.9 us (4%)
  other arithmetic  1.84 us (2%)
  between operations  1.04 us (1%)
    pallas_call x1, Pallas kernels, first_sweep(): pl.pallas_call(functools.partial(first_sweep_kernel, (rows, cols, span, p...  15.6 us
    ppermute x7, starting transfers between devices, shifted(): lax.ppermute(value, axis, [(i, (i + shift) % peers) for i in range(peers)])  15.4 us
    ppermute x10, waiting for transfers between devices, swap(): return lax.ppermute(value, axis, pairs)  14 us
    ppermute x7, waiting for transfers between devices, shifted(): lax.ppermute(value, axis, [(i, (i + shift) % peers) for i in range(peers)])  12.8 us
    ppermute x10, starting transfers between devices, swap(): return lax.ppermute(value, axis, pairs)  9.35 us
    pallas_call x1, Pallas kernels, correlate(): pl.pallas_call(functools.partial(correlate_kernel, (rows, cols, span, pee...  8.36 us
    pallas_call x1, Pallas kernels, second_sweep(): pl.pallas_call(functools.partial(second_sweep_kernel, (rows, cols, span,...  6.25 us
    unnamed x10, local copies, waits for them, and re-layouts  2.01 us
  transfers between devices with their start and end apart: 17, of which 10 were waited for; matrix products, arithmetic and copies ran while one was open for 2% of the time, Pallas kernels for 25%

profile of v8, /device:TPU:0, one launch (start us, length us, event | category | flops | bytes accessed | tf_op | source)
XLA Modules:
  0.0 88.5 jit_solution(12901495627936276452)
XLA Ops:
  0.6 0.0 copy-start
  0.7 1.0 %copy.39 = f32[12,16,2,128]{3,1,0,2:T(8,128)S(1)} copy(f32[12,16,2,128]{3,2,1,0:T(2,128)} %param.4) | data formatting | bytes 393216 | tf_op args[0]
  1.7 0.9 %copy.38 = f32[12,16,2,128]{3,1,0,2:T(8,128)S(1)} copy(f32[12,16,2,128]{3,2,1,0:T(2,128)} %param.5) | data formatting | bytes 393216 | tf_op args[1]
  2.6 0.1 fusion.5
  2.7 0.1 copy.10
  2.8 3.0 %collective-permute-start.1 = (f32[2,12,16,128]{3,2,1,0:T(8,128)S(1)}, f32[2,12,16,128]{3,2,1,0:T(8,128)S(1)}, u32[]{:S(2)}, u32[]{:S(2)}) collective-permute-start(f32[2,12,16,128]{3,2,1,0:T(8,128)S(1)} %bitcast.32), channel_id=1, source_target_pairs={{0,4},{4,0},{8,12},{12,8},{16,20},{20,16},{24,28},{28,24},{1,5},{5... | collective-permute-start | bytes 589832 | tf_op jit(solution)/shard_map/ppermute | solution.py:410
  5.8 0.1 copy.11
  5.9 0.7 collective-permute-start
  6.6 0.0 collective-permute-done
  6.6 4.1 %collective-permute-done.1 = f32[2,12,16,128]{3,2,1,0:T(8,128)S(1)} collective-permute-done((f32[2,12,16,128]{3,2,1,0:T(8,128)S(1)}, f32[2,12,16,128]{3,2,1,0:T(8,128)S(1)}, u32[]{:S(2)}, u32[]{:S(2)}) %collective-permute-start.1) | collective-permute-done | bytes 196640 | tf_op jit(solution)/shard_map/ppermute | solution.py:410
  10.7 1.1 %collective-permute-start.2 = (f32[2,108,128]{2,0,1:T(2,128)S(1)}, f32[2,108,128]{2,0,1:T(2,128)S(1)}, u32[]{:S(2)}, u32[]{:S(2)}) collective-permute-start(f32[2,108,128]{2,0,1:T(2,128)S(1)} %bitcast.46), channel_id=1, source_target_pairs={{0,1},{1,0},{2,3},{3,2},{4,5},{5,4},{6,7},{7,6},{8,9},{9,8},{10,11... | collective-permute-start | bytes 331784 | tf_op jit(solution)/shard_map/ppermute | solution.py:410
  11.9 1.0 %collective-permute-done.2 = f32[2,108,128]{2,0,1:T(2,128)S(1)} collective-permute-done((f32[2,108,128]{2,0,1:T(2,128)S(1)}, f32[2,108,128]{2,0,1:T(2,128)S(1)}, u32[]{:S(2)}, u32[]{:S(2)}) %collective-permute-start.2) | collective-permute-done | bytes 110624 | tf_op jit(solution)/shard_map/ppermute | solution.py:410
  13.0 0.1 copy.18
  13.1 0.1 pad_maximum_fusion.2
  13.2 0.1 copy.15
  13.3 0.1 pad_maximum_fusion.5
  13.5 1.0 %collective-permute-start.4 = (f32[2,240,128]{2,0,1:T(2,128)S(1)}, f32[2,240,128]{2,0,1:T(2,128)S(1)}, u32[]{:S(2)}, u32[]{:S(2)}) collective-permute-start(f32[2,240,128]{2,0,1:T(2,128)S(1)} %pad_maximum_fusion.5), channel_id=1, source_target_pairs={{0,4},{4,0},{8,12},{12,8},{16,20},{20,16},{24,28},{28,24},{1,5},{5... | collective-permute-start | bytes 737288 | tf_op jit(solution)/shard_map/ppermute | solution.py:410
  14.5 0.1 copy.14
  14.6 0.7 collective-permute-start.3
  15.4 0.2 copy.24
  15.6 3.8 %collective-permute-start.5 = (f32[2,264,128]{2,1,0:T(8,128)S(1)}, f32[2,264,128]{2,1,0:T(8,128)S(1)}, u32[]{:S(2)}, u32[]{:S(2)}) collective-permute-start(f32[2,264,128]{2,1,0:T(8,128)S(1)} %copy.25.refs_4_), channel_id=1, source_target_pairs={{0,8},{4,12},{8,16},{12,20},{16,24},{20,28},{24,0},{28,4},{1,9},{5... | collective-permute-start | bytes 811016 | tf_op jit(solution)/shard_map/ppermute | solution.py:417
  19.4 2.1 %collective-permute-start.6 = (f32[2,264,128]{2,1,0:T(8,128)S(1)}, f32[2,264,128]{2,1,0:T(8,128)S(1)}, u32[]{:S(2)}, u32[]{:S(2)}) collective-permute-start(f32[2,264,128]{2,1,0:T(8,128)S(1)} %copy.25.refs_4_), channel_id=1, source_target_pairs={{0,24},{4,28},{8,0},{12,4},{16,8},{20,12},{24,16},{28,20},{1,25},{... | collective-permute-start | bytes 811016 | tf_op jit(solution)/shard_map/ppermute | solution.py:417
  21.5 0.9 %collective-permute-start.7 = (f32[2,264,128]{2,1,0:T(8,128)S(1)}, f32[2,264,128]{2,1,0:T(8,128)S(1)}, u32[]{:S(2)}, u32[]{:S(2)}) collective-permute-start(f32[2,264,128]{2,1,0:T(8,128)S(1)} %copy.25.refs_4_), channel_id=1, source_target_pairs={{0,16},{4,20},{8,24},{12,28},{16,0},{20,4},{24,8},{28,12},{1,17},{... | collective-permute-start | bytes 811016 | tf_op jit(solution)/shard_map/ppermute | solution.py:417
  22.5 0.0 collective-permute-done.3
  22.5 1.3 %collective-permute-done.4 = f32[2,240,128]{2,0,1:T(2,128)S(1)} collective-permute-done((f32[2,240,128]{2,0,1:T(2,128)S(1)}, f32[2,240,128]{2,0,1:T(2,128)S(1)}, u32[]{:S(2)}, u32[]{:S(2)}) %collective-permute-start.4) | collective-permute-done | bytes 245792 | tf_op jit(solution)/shard_map/ppermute | solution.py:410
  23.7 0.1 broadcast_select_fusion.3
  23.9 0.1 select_maximum_fusion.source_ref
  24.0 0.0 copy-done
  24.1 15.6 %first_sweep.1 = (f32[18,24,256]{2,1,0:T(8,128)S(1)}, f32[12,16,256]{2,1,0:T(8,128)S(1)}, bf16[7,7,256,256]{3,2,1,0:T(8,128)(2,1)S(1)}, bf16[7,7,256,256]{3,2,1,0:T(8,128)(2,1)S(1)}) custom-call(f32[2,24,32,128]{3,2,1,0:T(8,128)S(1)} %select_maximum_fusion.source_ref, f32[2,128,128]{2,1,0:T(8,128)S(1)} %copy-done, f32[7,7,2,128,128]{4,3,2,1,0:T(8,128)} %blocks_hbm.1), custom_call_target="tpu_custom_call" | custom-call | flops 8323596288 | bytes 19267584 | tf_op jit(solution)/shard_map/first_sweep/pallas_call | solution.py:170
  39.8 0.2 copy.23
  40.0 0.0 collective-permute-done.5.refs_5_
  40.0 0.0 collective-permute-done.6.refs_7_
  40.1 2.5 %collective-permute-start.12 = (f32[2,2,264,128]{3,2,1,0:T(8,128)S(1)}, f32[2,2,264,128]{3,2,1,0:T(8,128)S(1)}, u32[]{:S(2)}, u32[]{:S(2)}) collective-permute-start(f32[2,2,264,128]{3,2,1,0:T(8,128)S(1)} %pad_maximum_fusion.1), channel_id=1, source_target_pairs={{0,4},{4,0},{8,12},{12,8},{16,20},{20,16},{24,28},{28,24},{1,5},{5... | collective-permute-start | bytes 1622024 | tf_op jit(solution)/shard_map/ppermute | solution.py:410
  42.6 6.2 %second_sweep.1 = (f32[12,16,256]{2,1,0:T(8,128)S(1)}, f32[2,32,192]{2,1,0:T(8,128)S(1)}, f32[2,32,192]{2,1,0:T(8,128)S(1)}, f32[2,32,192]{2,1,0:T(8,128)S(1)}, f32[2,32,192]{2,1,0:T(8,128)S(1)}) custom-call(f32[18,24,256]{2,1,0:T(8,128)S(1)} %get-tuple-element.32.second_ref, f32[12,16,256]{2,1,0:T(8,128)S(1)} %get-tuple-element.33.source_ref, ...), custom_call_target="tpu_custom_call" | custom-call | flops 3699376128 | bytes 12845056 | tf_op jit(solution)/shard_map/second_sweep/pallas_call | solution.py:260
  48.8 0.0 collective-permute-done.7.refs_6_
  48.8 0.1 collective-permute-start.13
  48.9 2.8 %collective-permute-start.8 = (f32[2,32,192]{2,1,0:T(8,128)S(1)}, f32[2,32,192]{2,1,0:T(8,128)S(1)}, u32[]{:S(2)}, u32[]{:S(2)}) collective-permute-start(f32[2,32,192]{2,1,0:T(8,128)S(1)} %get-tuple-element.42), channel_id=1, source_target_pairs={{0,8},{4,12},{8,16},{12,20},{16,24},{20,28},{24,0},{28,4},{1,9},{5... | collective-permute-start | bytes 147464 | tf_op jit(solution)/shard_map/ppermute | solution.py:417
  51.7 2.6 %collective-permute-start.9 = (f32[2,32,192]{2,1,0:T(8,128)S(1)}, f32[2,32,192]{2,1,0:T(8,128)S(1)}, u32[]{:S(2)}, u32[]{:S(2)}) collective-permute-start(f32[2,32,192]{2,1,0:T(8,128)S(1)} %get-tuple-element.43), channel_id=1, source_target_pairs={{0,16},{4,20},{8,24},{12,28},{16,0},{20,4},{24,8},{28,12},{1,17},{... | collective-permute-start | bytes 147464 | tf_op jit(solution)/shard_map/ppermute | solution.py:417
  54.3 1.3 %collective-permute-start.10 = (f32[2,32,192]{2,1,0:T(8,128)S(1)}, f32[2,32,192]{2,1,0:T(8,128)S(1)}, u32[]{:S(2)}, u32[]{:S(2)}) collective-permute-start(f32[2,32,192]{2,1,0:T(8,128)S(1)} %get-tuple-element.44), channel_id=1, source_target_pairs={{0,24},{4,28},{8,0},{12,4},{16,8},{20,12},{24,16},{28,20},{1,25},{... | collective-permute-start | bytes 147464 | tf_op jit(solution)/shard_map/ppermute | solution.py:417
  55.7 1.0 %collective-permute-done.8.refs_1_ = f32[2,32,192]{2,1,0:T(8,128)S(1)} collective-permute-done((f32[2,32,192]{2,1,0:T(8,128)S(1)}, f32[2,32,192]{2,1,0:T(8,128)S(1)}, u32[]{:S(2)}, u32[]{:S(2)}) %collective-permute-start.8) | collective-permute-done | bytes 49184 | tf_op jit(solution)/shard_map/ppermute | solution.py:417
  56.7 2.0 %collective-permute-done.9.refs_2_ = f32[2,32,192]{2,1,0:T(8,128)S(1)} collective-permute-done((f32[2,32,192]{2,1,0:T(8,128)S(1)}, f32[2,32,192]{2,1,0:T(8,128)S(1)}, u32[]{:S(2)}, u32[]{:S(2)}) %collective-permute-start.9) | collective-permute-done | bytes 49184 | tf_op jit(solution)/shard_map/ppermute | solution.py:417
  58.6 0.2 collective-permute-done.10.refs_3_
  58.9 0.1 collective-permute-start.11
  59.0 4.9 %collective-permute-done.11.refs_8_ = f32[4,32,192]{2,1,0:T(8,128)S(1)} collective-permute-done((f32[4,32,192]{2,1,0:T(8,128)S(1)}, f32[4,32,192]{2,1,0:T(8,128)S(1)}, u32[]{:S(2)}, u32[]{:S(2)}) %collective-permute-start.11) | collective-permute-done | bytes 98336 | tf_op jit(solution)/shard_map/ppermute | solution.py:410
  63.9 0.0 collective-permute-done.13.refs_11_
  63.9 0.0 collective-permute-done.12.refs_10_
  63.9 8.4 %correlate.1 = (f32[7,7,2,8,128]{4,3,2,1,0:T(8,128)S(1)}, f32[7,7,2,8,128]{4,3,2,1,0:T(8,128)S(1)}) custom-call(f32[2,32,192]{2,1,0:T(8,128)S(1)} %get-tuple-element.41.refs_0_, f32[2,32,192]{2,1,0:T(8,128)S(1)} %collective-permute-done.8.refs_1_, f32[2,32,192]{2,1,0:T(8,128)S(1)} %collective-permute-done.9.refs_2_, ...), custom_call_target="tpu_custom_call" | custom-call | flops 3699376128 | bytes 2965504 | tf_op jit(solution)/shard_map/correlate/pallas_call | solution.py:379
  72.3 0.1 collective-permute-start.14
  72.4 1.7 %collective-permute-done.14 = f32[7,7,2,8,128]{4,3,2,1,0:T(8,128)S(1)} collective-permute-done((f32[7,7,2,8,128]{4,3,2,1,0:T(8,128)S(1)}, f32[7,7,2,8,128]{4,3,2,1,0:T(8,128)S(1)}, u32[]{:S(2)}, u32[]{:S(2)}) %collective-permute-start.14) | collective-permute-done | bytes 401440 | tf_op jit(solution)/shard_map/ppermute | solution.py:410
  74.1 0.1 add.18
  74.2 1.8 %collective-permute-start.15 = (f32[7,7,2,8,128]{4,3,2,1,0:T(8,128)S(1)}, f32[7,7,2,8,128]{4,3,2,1,0:T(8,128)S(1)}, u32[]{:S(2)}, u32[]{:S(2)}) collective-permute-start(f32[7,7,2,8,128]{4,3,2,1,0:T(8,128)S(1)} %add.18), channel_id=1, source_target_pairs={{0,2},{1,3},{2,0},{3,1},{4,6},{5,7},{6,4},{7,5},{8,10},{9,11},{10,... | collective-permute-start | bytes 1204232 | tf_op jit(solution)/shard_map/ppermute | solution.py:417
  76.0 9.6 %collective-permute-done.15 = f32[7,7,2,8,128]{4,3,2,1,0:T(8,128)S(1)} collective-permute-done((f32[7,7,2,8,128]{4,3,2,1,0:T(8,128)S(1)}, f32[7,7,2,8,128]{4,3,2,1,0:T(8,128)S(1)}, u32[]{:S(2)}, u32[]{:S(2)}) %collective-permute-start.15) | collective-permute-done | bytes 401440 | tf_op jit(solution)/shard_map/ppermute | solution.py:417
  85.6 0.1 add.19
  85.7 0.1 collective-permute-start.16
  85.7 0.8 reshape.47
  86.5 0.9 %collective-permute-done.16 = f32[7,7,2,8,128]{4,3,2,1,0:T(8,128)S(1)} collective-permute-done((f32[7,7,2,8,128]{4,3,2,1,0:T(8,128)S(1)}, f32[7,7,2,8,128]{4,3,2,1,0:T(8,128)S(1)}, u32[]{:S(2)}, u32[]{:S(2)}) %collective-permute-start.16) | collective-permute-done | bytes 401440 | tf_op jit(solution)/shard_map/ppermute | solution.py:410
  87.5 0.1 broadcast_select_fusion.1
  87.5 1.0 %pad_maximum_fusion = f32[7,7,2,16,128]{4,3,2,1,0:T(8,128)} fusion(f32[7,7,2,8,128]{4,3,2,1,0:T(8,128)S(1)} %get-tuple-element.51, f32[7,7,2,8,128]{4,3,2,1,0:T(8,128)S(1)} %get-tuple-element.50), kind=kLoop, calls=%fused_computation | loop fusion | flops 200704 | bytes 1605632 | tf_op jit(solution)/shard_map/concatenate | solution.py:490
  (29 shorter events, 0.5 us)
Async XLA Ops:
  0.6 23.4 %copy-start = (f32[2,128,128]{2,1,0:T(8,128)S(1)}, f32[2,128,128]{2,1,0:T(8,128)}, u32[]{:S(2)}) copy-start(f32[2,128,128]{2,1,0:T(8,128)} %inverse_ref.3) | copy-start | bytes 393220
  2.8 7.9 %collective-permute-start.1 = (f32[2,12,16,128]{3,2,1,0:T(8,128)S(1)}, f32[2,12,16,128]{3,2,1,0:T(8,128)S(1)}, u32[]{:S(2)}, u32[]{:S(2)}) collective-permute-start(f32[2,12,16,128]{3,2,1,0:T(8,128)S(1)} %bitcast.32), channel_id=1, source_target_pairs={{0,4},{4,0},{8,12},{12,8},{16,20},{20,16},{24,28},{28,24},{1,5},{5... | collective-permute-start | bytes 589832 | tf_op jit(solution)/shard_map/ppermute | solution.py:410
  5.9 0.7 collective-permute-start
  10.7 2.1 %collective-permute-start.2 = (f32[2,108,128]{2,0,1:T(2,128)S(1)}, f32[2,108,128]{2,0,1:T(2,128)S(1)}, u32[]{:S(2)}, u32[]{:S(2)}) collective-permute-start(f32[2,108,128]{2,0,1:T(2,128)S(1)} %bitcast.46), channel_id=1, source_target_pairs={{0,1},{1,0},{2,3},{3,2},{4,5},{5,4},{6,7},{7,6},{8,9},{9,8},{10,11... | collective-permute-start | bytes 331784 | tf_op jit(solution)/shard_map/ppermute | solution.py:410
  13.5 10.3 %collective-permute-start.4 = (f32[2,240,128]{2,0,1:T(2,128)S(1)}, f32[2,240,128]{2,0,1:T(2,128)S(1)}, u32[]{:S(2)}, u32[]{:S(2)}) collective-permute-start(f32[2,240,128]{2,0,1:T(2,128)S(1)} %pad_maximum_fusion.5), channel_id=1, source_target_pairs={{0,4},{4,0},{8,12},{12,8},{16,20},{20,16},{24,28},{28,24},{1,5},{5... | collective-permute-start | bytes 737288 | tf_op jit(solution)/shard_map/ppermute | solution.py:410
  14.6 7.8 %collective-permute-start.3 = (f32[2,168,128]{2,0,1:T(2,128)S(1)}, f32[2,168,128]{2,0,1:T(2,128)S(1)}, u32[]{:S(2)}, u32[]{:S(2)}) collective-permute-start(f32[2,168,128]{2,0,1:T(2,128)S(1)} %bitcast.45), channel_id=1, source_target_pairs={{4,8},{8,4},{12,16},{16,12},{20,24},{24,20},{5,9},{9,5},{13,17},{1... | collective-permute-start | bytes 516104 | tf_op jit(solution)/shard_map/ppermute | solution.py:410
  15.6 24.4 %collective-permute-start.5 = (f32[2,264,128]{2,1,0:T(8,128)S(1)}, f32[2,264,128]{2,1,0:T(8,128)S(1)}, u32[]{:S(2)}, u32[]{:S(2)}) collective-permute-start(f32[2,264,128]{2,1,0:T(8,128)S(1)} %copy.25.refs_4_), channel_id=1, source_target_pairs={{0,8},{4,12},{8,16},{12,20},{16,24},{20,28},{24,0},{28,4},{1,9},{5... | collective-permute-start | bytes 811016 | tf_op jit(solution)/shard_map/ppermute | solution.py:417
  19.4 20.6 %collective-permute-start.6 = (f32[2,264,128]{2,1,0:T(8,128)S(1)}, f32[2,264,128]{2,1,0:T(8,128)S(1)}, u32[]{:S(2)}, u32[]{:S(2)}) collective-permute-start(f32[2,264,128]{2,1,0:T(8,128)S(1)} %copy.25.refs_4_), channel_id=1, source_target_pairs={{0,24},{4,28},{8,0},{12,4},{16,8},{20,12},{24,16},{28,20},{1,25},{... | collective-permute-start | bytes 811016 | tf_op jit(solution)/shard_map/ppermute | solution.py:417
  21.5 27.3 %collective-permute-start.7 = (f32[2,264,128]{2,1,0:T(8,128)S(1)}, f32[2,264,128]{2,1,0:T(8,128)S(1)}, u32[]{:S(2)}, u32[]{:S(2)}) collective-permute-start(f32[2,264,128]{2,1,0:T(8,128)S(1)} %copy.25.refs_4_), channel_id=1, source_target_pairs={{0,16},{4,20},{8,24},{12,28},{16,0},{20,4},{24,8},{28,12},{1,17},{... | collective-permute-start | bytes 811016 | tf_op jit(solution)/shard_map/ppermute | solution.py:417
  40.1 23.9 %collective-permute-start.12 = (f32[2,2,264,128]{3,2,1,0:T(8,128)S(1)}, f32[2,2,264,128]{3,2,1,0:T(8,128)S(1)}, u32[]{:S(2)}, u32[]{:S(2)}) collective-permute-start(f32[2,2,264,128]{3,2,1,0:T(8,128)S(1)} %pad_maximum_fusion.1), channel_id=1, source_target_pairs={{0,4},{4,0},{8,12},{12,8},{16,20},{20,16},{24,28},{28,24},{1,5},{5... | collective-permute-start | bytes 1622024 | tf_op jit(solution)/shard_map/ppermute | solution.py:410
  48.8 15.1 %collective-permute-start.13 = (f32[1,2,264,128]{3,2,1,0:T(8,128)S(1)}, f32[1,2,264,128]{3,2,1,0:T(8,128)S(1)}, u32[]{:S(2)}, u32[]{:S(2)}) collective-permute-start(f32[1,2,264,128]{3,2,1,0:T(8,128)S(1)} %bitcast.27), channel_id=1, source_target_pairs={{0,4},{4,0},{8,12},{12,8},{16,20},{20,16},{24,28},{28,24},{1,5},{5... | collective-permute-start | bytes 811016 | tf_op jit(solution)/shard_map/ppermute | solution.py:410
  48.9 7.7 %collective-permute-start.8 = (f32[2,32,192]{2,1,0:T(8,128)S(1)}, f32[2,32,192]{2,1,0:T(8,128)S(1)}, u32[]{:S(2)}, u32[]{:S(2)}) collective-permute-start(f32[2,32,192]{2,1,0:T(8,128)S(1)} %get-tuple-element.42), channel_id=1, source_target_pairs={{0,8},{4,12},{8,16},{12,20},{16,24},{20,28},{24,0},{28,4},{1,9},{5... | collective-permute-start | bytes 147464 | tf_op jit(solution)/shard_map/ppermute | solution.py:417
  51.7 6.9 %collective-permute-start.9 = (f32[2,32,192]{2,1,0:T(8,128)S(1)}, f32[2,32,192]{2,1,0:T(8,128)S(1)}, u32[]{:S(2)}, u32[]{:S(2)}) collective-permute-start(f32[2,32,192]{2,1,0:T(8,128)S(1)} %get-tuple-element.43), channel_id=1, source_target_pairs={{0,16},{4,20},{8,24},{12,28},{16,0},{20,4},{24,8},{28,12},{1,17},{... | collective-permute-start | bytes 147464 | tf_op jit(solution)/shard_map/ppermute | solution.py:417
  54.3 4.5 %collective-permute-start.10 = (f32[2,32,192]{2,1,0:T(8,128)S(1)}, f32[2,32,192]{2,1,0:T(8,128)S(1)}, u32[]{:S(2)}, u32[]{:S(2)}) collective-permute-start(f32[2,32,192]{2,1,0:T(8,128)S(1)} %get-tuple-element.44), channel_id=1, source_target_pairs={{0,24},{4,28},{8,0},{12,4},{16,8},{20,12},{24,16},{28,20},{1,25},{... | collective-permute-start | bytes 147464 | tf_op jit(solution)/shard_map/ppermute | solution.py:417
  58.9 5.0 %collective-permute-start.11 = (f32[4,32,192]{2,1,0:T(8,128)S(1)}, f32[4,32,192]{2,1,0:T(8,128)S(1)}, u32[]{:S(2)}, u32[]{:S(2)}) collective-permute-start(f32[4,32,192]{2,1,0:T(8,128)S(1)} %pad_maximum_fusion.8), channel_id=1, source_target_pairs={{0,4},{4,0},{8,12},{12,8},{16,20},{20,16},{24,28},{28,24},{1,5},{5... | collective-permute-start | bytes 294920 | tf_op jit(solution)/shard_map/ppermute | solution.py:410
  72.3 1.8 %collective-permute-start.14 = (f32[7,7,2,8,128]{4,3,2,1,0:T(8,128)S(1)}, f32[7,7,2,8,128]{4,3,2,1,0:T(8,128)S(1)}, u32[]{:S(2)}, u32[]{:S(2)}) collective-permute-start(f32[7,7,2,8,128]{4,3,2,1,0:T(8,128)S(1)} %get-tuple-element.49), channel_id=1, source_target_pairs={{0,1},{1,0},{2,3},{3,2},{4,5},{5,4},{6,7},{7,6},{8,9},{9,8},{10,11... | collective-permute-start | bytes 1204232 | tf_op jit(solution)/shard_map/ppermute | solution.py:410
  74.2 11.4 %collective-permute-start.15 = (f32[7,7,2,8,128]{4,3,2,1,0:T(8,128)S(1)}, f32[7,7,2,8,128]{4,3,2,1,0:T(8,128)S(1)}, u32[]{:S(2)}, u32[]{:S(2)}) collective-permute-start(f32[7,7,2,8,128]{4,3,2,1,0:T(8,128)S(1)} %add.18), channel_id=1, source_target_pairs={{0,2},{1,3},{2,0},{3,1},{4,6},{5,7},{6,4},{7,5},{8,10},{9,11},{10,... | collective-permute-start | bytes 1204232 | tf_op jit(solution)/shard_map/ppermute | solution.py:417
  85.7 1.8 %collective-permute-start.16 = (f32[7,7,2,8,128]{4,3,2,1,0:T(8,128)S(1)}, f32[7,7,2,8,128]{4,3,2,1,0:T(8,128)S(1)}, u32[]{:S(2)}, u32[]{:S(2)}) collective-permute-start(f32[7,7,2,8,128]{4,3,2,1,0:T(8,128)S(1)} %add.19), channel_id=1, source_target_pairs={{0,1},{1,0},{2,3},{3,2},{4,5},{5,4},{6,7},{7,6},{8,9},{9,8},{10,11... | collective-permute-start | bytes 1204232 | tf_op jit(solution)/shard_map/ppermute | solution.py:410

commit v9 on v8

--- a/solution.py
+++ b/solution.py
@@ -30,6 +30,10 @@
 
 def round_up(count, unit):
     return (count + unit - 1) // unit * unit
+
+
+def chip_along_z(z, shift, count):
+    return (z + shift + count) % count
 
 
 def store_block(ref, index, real, imag):
@@ -70,7 +74,7 @@
     sizes,
     source_ref,
     inverse_ref,
-    blocks_hbm,
+    blocks_ref,
     second_ref,
     own_source_ref,
     w_high,
@@ -79,10 +83,8 @@
     x_high,
     x_low,
     acc,
-    raw,
     e_high,
     e_low,
-    sems,
 ):
     rows, cols, span, pitch, wide = sizes
     reach = span // 2
@@ -92,12 +94,6 @@
 
     def source_at(i, j):
         return jnp.concatenate([source_ref[0, i, j, :], source_ref[1, i, j, :]], axis=-1)
-
-    def block_copy(a):
-        return pltpu.make_async_copy(blocks_hbm.at[a], raw.at[a], sems.at[a])
-
-    for a in range(span):
-        block_copy(a).start()
 
     store_inverse(inverse_ref, e_high, e_low)
 
@@ -130,12 +126,9 @@
 
     @pl.loop(0, span)
     def _(a):
-        block_copy(a).wait()
-
-        @pl.loop(0, span)
-        def _(b):
-            real_high, real_low = split(raw[a, b, 0])
-            imag_high, imag_low = split(raw[a, b, 1])
+        for b in range(span):
+            real_high, real_low = split(blocks_ref[a, b, 0])
+            imag_high, imag_low = split(blocks_ref[a, b, 1])
             store_block(w_high, (a, b), real_high, imag_high)
             store_block(w_low, (a, b), real_low, imag_low)
 
@@ -165,11 +158,10 @@
     pitch = round_up(cols + 2 * reach, 8)
     full_rows, mid_rows = rows + 4 * reach, rows + 2 * reach
     vmem = pl.BlockSpec(memory_space=pltpu.VMEM)
-    hbm = pl.BlockSpec(memory_space=pltpu.HBM)
     weights = (span, span, lanes, lanes)
     return pl.pallas_call(
         functools.partial(first_sweep_kernel, (rows, cols, span, pitch, wide)),
-        in_specs=[vmem, vmem, hbm],
+        in_specs=[vmem] * 3,
         out_specs=[vmem] * 4,
         out_shape=[
             jax.ShapeDtypeStruct((mid_rows, pitch, lanes), f32),
@@ -182,17 +174,15 @@
             pltpu.VMEM((2, full_rows * pitch, span * lanes), bf16),
             pltpu.VMEM((2, full_rows * pitch, span * lanes), bf16),
             pltpu.VMEM((mid_rows * pitch, lanes), f32),
-            pltpu.VMEM(lag_blocks.shape, f32),
             pltpu.VMEM((lanes, lanes), bf16),
             pltpu.VMEM((lanes, lanes), bf16),
-            pltpu.SemaphoreType.DMA((span,)),
         ],
         cost_estimate=pl.CostEstimate(
             flops=6 * span * span * lanes * lanes * mid_rows * pitch,
             bytes_accessed=12 * lag_blocks.size,
             transcendentals=0,
         ),
-        compiler_params=pltpu.CompilerParams(vmem_limit_bytes=40 * 1024 * 1024),
+        compiler_params=pltpu.CompilerParams(vmem_limit_bytes=32 * 1024 * 1024),
         name="first_sweep",
     )(source, inverse, lag_blocks)
 
@@ -241,10 +231,10 @@
 
     share = width // peers
     me = lax.axis_index("row")
-    twin = me + 1 - 2 * lax.rem(me, 2)
+    parity = me % 2
     for k in range(peers // 2):
-        for n, target in enumerate((me, twin)):
-            peer = lax.rem(target + 2 * k, peers)
+        base = 2 * chip_along_z(me // 2, k, peers // 2)
+        for n, peer in enumerate((base + parity, base + 1 - parity)):
             for part in range(2):
                 at = pl.multiple_of(part * width + peer * share, share)
                 sends[k][n, part * share : (part + 1) * share, :] = turned[pl.ds(at, share), :]
@@ -275,67 +265,38 @@
             bytes_accessed=4 * high.size,
             transcendentals=0,
         ),
-        compiler_params=pltpu.CompilerParams(vmem_limit_bytes=28 * 1024 * 1024),
+        compiler_params=pltpu.CompilerParams(vmem_limit_bytes=18 * 1024 * 1024),
         name="second_sweep",
     )(second, source, inverse, high, low)
     return out[0], out[1:]
 
 
-def correlate_kernel(sizes, factor, *refs):
+def spread_kernel(sizes, *refs):
     rows, cols, span, peers = sizes
     half_peers = peers // 2
-    shares, piece_refs = refs[:half_peers], refs[half_peers:peers]
-    twin_shares_ref, own_twin_ref, early_ref, late_ref = refs[peers : peers + 4]
-    mine_ref, other_ref = refs[peers + 4 : peers + 6]
-    placed, flat, l_high, l_low, stage, s_high, s_low, sems = refs[peers + 6 :]
-    reach = span // 2
+    piece_refs = refs[:half_peers]
+    own_twin_ref, early_ref, late_ref, s_high, s_low, stage, sems = refs[half_peers:]
     own = rows * cols
-    double = shares[0].shape[1]
-    share = double // 2
     width = stage.shape[-1]
     me = lax.axis_index("row")
-    even = me - lax.rem(me, 2)
-    odd = 1 - lax.rem(me, 2)
+    parity = me % 2
 
     def tiles(k):
-        base = lax.rem(even - 2 * k + peers, peers)
-        return base + 1 - odd, base + odd
+        base = 2 * chip_along_z(me // 2, -k, half_peers)
+        return base + parity, base + 1 - parity
 
     for k in range(half_peers):
         if k == 0:
             twin = own_twin_ref
-        elif k in (1, half_peers - 1):
-            twin = early_ref.at[0 if k == 1 else 1]
         else:
-            twin = late_ref.at[k - 2]
-        for n, (source, tile) in enumerate(zip((piece_refs[k], twin), tiles(k))):
-            pltpu.make_async_copy(source, stage.at[tile], sems.at[n, k]).start()
-        first, second = tiles(k)
-        placed[first] = shares[k][0]
-        placed[second] = twin_shares_ref[k]
-
-    total = peers * own
-    side = round_up(reach * cols, 128)
-    flat[:, :side] = jnp.zeros((double, side), f32)
-    flat[:, side + total :] = jnp.zeros((double, side), f32)
-    for tile in range(peers):
-        flat[:, side + tile * own : side + (tile + 1) * own] = placed[tile]
-
-    @pl.loop(0, 2)
-    def _(part):
-        rows_at = pl.ds(pl.multiple_of(part * share, 8), share)
-        for a in range(span):
-            start = side + (a - reach) * cols
-            high, low = split(flat[rows_at, start : start + total])
-            l_high[a, part] = high
-            l_low[a, part] = low
+            near = k in (1, half_peers - 1)
+            twin = early_ref.at[0 if k == 1 else 1] if near else late_ref.at[k - 2]
+        for source, tile in zip((piece_refs[k], twin), tiles(k)):
+            pltpu.make_async_copy(source, stage.at[tile], sems.at[tile]).start()
 
     @pl.loop(0, peers)
-    def _(at):
-        n, k = lax.rem(at, 2), at // 2
-        first, second = tiles(k)
-        tile = jnp.where(n == 0, first, second)
-        pltpu.make_async_copy(own_twin_ref, stage.at[tile], sems.at[n, k]).wait()
+    def _(tile):
+        pltpu.make_async_copy(own_twin_ref, stage.at[tile], sems.at[tile]).wait()
 
         @pl.loop(0, rows)
         def _(i):
@@ -347,11 +308,72 @@
                     s_high[b, to, h * width : (h + 1) * width] = high
                     s_low[b, to, h * width : (h + 1) * width] = low
 
+
+def spread(pieces, twins, rows, cols, span):
+    peers = 2 * len(pieces)
+    piece = pieces[0]
+    vmem = pl.BlockSpec(memory_space=pltpu.VMEM)
+    hbm = pl.BlockSpec(memory_space=pltpu.HBM)
+    out = jax.ShapeDtypeStruct((span, peers * rows * cols, 2 * piece.shape[-1]), bf16)
+    return pl.pallas_call(
+        functools.partial(spread_kernel, (rows, cols, span, peers)),
+        in_specs=[hbm] * (len(pieces) + len(twins)),
+        out_specs=[vmem, vmem],
+        out_shape=[out, out],
+        scratch_shapes=[
+            pltpu.VMEM((peers,) + piece.shape, f32),
+            pltpu.SemaphoreType.DMA((peers,)),
+        ],
+        cost_estimate=pl.CostEstimate(
+            flops=0, bytes_accessed=4 * peers * piece.size, transcendentals=0
+        ),
+        compiler_params=pltpu.CompilerParams(vmem_limit_bytes=15 * 1024 * 1024),
+        name="spread",
+    )(*pieces, *twins)
+
+
+def correlate_kernel(sizes, lags, factor, *refs):
+    rows, cols, span, peers = sizes
+    half_peers = peers // 2
+    shares = refs[:half_peers]
+    twin_shares_ref, s_high, s_low, mine_ref, other_ref = refs[half_peers : half_peers + 5]
+    placed, flat, l_high, l_low = refs[half_peers + 5 :]
+    reach = span // 2
+    own = rows * cols
+    double = shares[0].shape[1]
+    share = double // 2
+    width = s_high.shape[-1] // 2
+    me = lax.axis_index("row")
+    parity = me % 2
+
+    for k in range(half_peers):
+        base = 2 * chip_along_z(me // 2, -k, half_peers)
+        placed[base + parity] = shares[k][0]
+        placed[base + 1 - parity] = twin_shares_ref[k]
+
+    total = peers * own
+    side = round_up(reach * cols, 128)
+    flat[:, :side] = jnp.zeros((double, side), f32)
+    flat[:, side + total :] = jnp.zeros((double, side), f32)
+    for tile in range(peers):
+        flat[:, side + tile * own : side + (tile + 1) * own] = placed[tile]
+
+    @pl.loop(0, 2)
+    def _(part):
+        rows_at = pl.ds(pl.multiple_of(part * share, 8), share)
+        for a in range(span):
+            start = side + (a - reach) * cols
+            high, low = split(flat[rows_at, start : start + total])
+            l_high[a, part] = high
+            l_low[a, part] = low
+
     half = share // 2
     upper = lax.axis_index("col") % 2 == 1
-
-    @pl.loop(0, span)
-    def _(b):
+    first_lag, count = lags
+
+    @pl.loop(0, count)
+    def _(n):
+        b = first_lag + n
         left = tuple(ref[...].reshape(span * double, total) for ref in (l_high, l_low))
         product = dot3(left, (s_high[b], s_low[b])) * factor
         for a in range(span):
@@ -360,25 +382,22 @@
             real = top[:, :width] + bottom[:, width:]
             imag = bottom[:, :width] - top[:, width:]
             for c, value in enumerate((real, imag)):
-                mine_ref[a, b, c] = jnp.where(upper, value[half:], value[:half])
-                other_ref[a, b, c] = jnp.where(upper, value[:half], value[half:])
-
-
-def correlate(shares, twin_shares, pieces, twins, rows, cols, span, factor):
+                mine_ref[a, n, c] = jnp.where(upper, value[half:], value[:half])
+                other_ref[a, n, c] = jnp.where(upper, value[:half], value[half:])
+
+
+def correlate(shares, twin_shares, s_high, s_low, lags, rows, cols, factor):
     peers = 2 * len(shares)
+    span, total, lanes = s_high.shape
     reach = span // 2
     double, own = twin_shares.shape[1:]
     share = double // 2
-    own_twin = twins[0]
-    width = own_twin.shape[-1]
-    total = peers * own
     side = round_up(reach * cols, 128)
     vmem = pl.BlockSpec(memory_space=pltpu.VMEM)
-    hbm = pl.BlockSpec(memory_space=pltpu.HBM)
-    out = jax.ShapeDtypeStruct((span, span, 2, share // 2, width), f32)
+    out = jax.ShapeDtypeStruct((span, lags[1], 2, share // 2, lanes // 2), f32)
     return pl.pallas_call(
-        functools.partial(correlate_kernel, (rows, cols, span, peers), factor),
-        in_specs=[vmem] * (peers // 2) + [hbm] * (peers // 2) + [vmem, hbm, hbm, hbm],
+        functools.partial(correlate_kernel, (rows, cols, span, peers), lags, factor),
+        in_specs=[vmem] * (peers // 2 + 3),
         out_specs=[vmem, vmem],
         out_shape=[out, out],
         scratch_shapes=[
@@ -386,19 +405,15 @@
             pltpu.VMEM((double, total + 2 * side), f32),
             pltpu.VMEM((span, 2, share, total), bf16),
             pltpu.VMEM((span, 2, share, total), bf16),
-            pltpu.VMEM((peers,) + own_twin.shape, f32),
-            pltpu.VMEM((span, total, 2 * width), bf16),
-            pltpu.VMEM((span, total, 2 * width), bf16),
-            pltpu.SemaphoreType.DMA((2, peers // 2)),
         ],
         cost_estimate=pl.CostEstimate(
-            flops=6 * span * double * total * span * 2 * width,
-            bytes_accessed=4 * (2 * out.size + peers * own_twin.size),
+            flops=6 * span * double * total * lags[1] * lanes if lags[0] == 0 else 1,
+            bytes_accessed=8 * out.size if lags[0] == 0 else 1,
             transcendentals=0,
         ),
-        compiler_params=pltpu.CompilerParams(vmem_limit_bytes=28 * 1024 * 1024),
+        compiler_params=pltpu.CompilerParams(vmem_limit_bytes=17 * 1024 * 1024),
         name="correlate",
-    )(*shares, *pieces, twin_shares, *twins)
+    )(*shares, twin_shares, s_high, s_low)
 
 
 def swap(value, axis, first):
@@ -476,17 +491,22 @@
     shares = [shifted(send, "row", 2 * k) for k, send in enumerate(sends)]
     twin_shares = swap(jnp.stack([received[1] for received in shares]), "row", 0)
 
+    s_high, s_low = spread(pieces, (own_twin, early_twins, late_twins), rows, cols, span)
+
     elements = rows * peers * cols * lax.axis_size("col")
     factor = -1.0 / math.sqrt(elements)
-    mine, other = correlate(
-        shares, twin_shares, pieces, (own_twin, early_twins, late_twins), rows, cols, span, factor
-    )
-    mine = mine + swap(other, "col", 0)
-    total = mine
-    for k in range(2, lax.axis_size("col"), 2):
-        total = total + shifted(mine, "col", k)
+    even = lax.axis_index("col") % 2 == 0
+    totals = []
+    for lags in ((0, span),):
+        mine, other = correlate(shares, twin_shares, s_high, s_low, lags, rows, cols, factor)
+        mine = mine + swap(other, "col", 0)
+        twin_shares, mine = lax.optimization_barrier((twin_shares, mine))
+        total = mine
+        for k in range(2, lax.axis_size("col"), 2):
+            total = total + shifted(mine, "col", k)
+        totals.append(total)
+    total = jnp.concatenate(totals, axis=1)
     twin = swap(total, "col", 0)
-    even = lax.axis_index("col") % 2 == 0
     lag_grad = jnp.concatenate(
         [jnp.where(even, total, twin), jnp.where(even, twin, total)], axis=3
     )

time: 88.7 us -> 85.2 us (0.961)
  waiting for transfers between devices: 26.7 us -> 23.3 us
  Pallas kernels: 30.2 us -> 29.1 us
    ppermute x10, waiting for transfers between devices: 14 us -> 10.5 us  [swap(): return lax.ppermute(value, axis, pairs)]
    pallas_call x1, Pallas kernels: 8.36 us -> 5.56 us  [correlate(): pl.pallas_call(functools.partial(correlate_kernel, (rows, cols, span, pee...]
    pallas_call x0 -> x1, Pallas kernels: none -> 2.73 us  [spread(): pl.pallas_call(functools.partial(spread_kernel, (rows, cols, span, peers)...]
    pallas_call x1, Pallas kernels: 15.6 us -> 14.5 us  [first_sweep(): pl.pallas_call(functools.partial(first_sweep_kernel, (rows, cols, span, p...]
    unnamed x10 -> x12, local copies, waits for them, and re-layouts: 2.01 us -> 2.01 us
  transfers between devices with their start and end apart: 17 -> 17, of which waited for: 10 -> 11; matrix products, arithmetic and copies ran while one was open for 2% -> 2% of each run, Pallas kernels for 25% -> 28%
where the time goes in v9:
time: 85.2 us; the launch traced here: 84.6 us
  Pallas kernels  29.1 us (34%)
  starting transfers between devices  25.5 us (30%)
  waiting for transfers between devices  23.3 us (27%)
  local copies, waits for them, and re-layouts  3.9 us (5%)
  other arithmetic  1.82 us (2%)
  between operations  1.05 us (1%)
    ppermute x7, starting transfers between devices, shifted(): lax.ppermute(value, axis, [(i, (i + shift) % peers) for i in range(peers)])  15.5 us
    pallas_call x1, Pallas kernels, first_sweep(): pl.pallas_call(functools.partial(first_sweep_kernel, (rows, cols, span, p...  14.5 us
    ppermute x7, waiting for transfers between devices, shifted(): lax.ppermute(value, axis, [(i, (i + shift) % peers) for i in range(peers)])  12.8 us
    ppermute x10, waiting for transfers between devices, swap(): return lax.ppermute(value, axis, pairs)  10.5 us
    ppermute x10, starting transfers between devices, swap(): return lax.ppermute(value, axis, pairs)  10 us
    pallas_call x1, Pallas kernels, second_sweep(): pl.pallas_call(functools.partial(second_sweep_kernel, (rows, cols, span,...  6.26 us
    pallas_call x1, Pallas kernels, correlate(): pl.pallas_call(functools.partial(correlate_kernel, (rows, cols, span, pee...  5.56 us
    pallas_call x1, Pallas kernels, spread(): pl.pallas_call(functools.partial(spread_kernel, (rows, cols, span, peers)...  2.73 us
  transfers between devices with their start and end apart: 17, of which 11 were waited for; matrix products, arithmetic and copies ran while one was open for 2% of the time, Pallas kernels for 28%

profile of v9, /device:TPU:0, one launch (start us, length us, event | category | flops | bytes accessed | tf_op | source)
XLA Modules:
  0.0 84.6 jit_solution(7215512532068821456)
XLA Ops:
  0.6 0.0 copy-start.1
  0.7 1.0 %copy.39 = f32[12,16,2,128]{3,1,0,2:T(8,128)S(1)} copy(f32[12,16,2,128]{3,2,1,0:T(2,128)} %param.4) | data formatting | bytes 393216 | tf_op args[0]
  1.7 0.9 %copy.38 = f32[12,16,2,128]{3,1,0,2:T(8,128)S(1)} copy(f32[12,16,2,128]{3,2,1,0:T(2,128)} %param.5) | data formatting | bytes 393216 | tf_op args[1]
  2.6 0.1 fusion.5
  2.7 0.1 copy.10
  2.8 3.0 %collective-permute-start.1 = (f32[2,12,16,128]{3,2,1,0:T(8,128)S(1)}, f32[2,12,16,128]{3,2,1,0:T(8,128)S(1)}, u32[]{:S(2)}, u32[]{:S(2)}) collective-permute-start(f32[2,12,16,128]{3,2,1,0:T(8,128)S(1)} %bitcast.32), channel_id=1, source_target_pairs={{0,4},{4,0},{8,12},{12,8},{16,20},{20,16},{24,28},{28,24},{1,5},{5... | collective-permute-start | bytes 589832 | tf_op jit(solution)/shard_map/ppermute | solution.py:425
  5.8 0.1 copy.11
  5.9 0.7 collective-permute-start
  6.6 0.0 collective-permute-done
  6.6 4.1 %collective-permute-done.1 = f32[2,12,16,128]{3,2,1,0:T(8,128)S(1)} collective-permute-done((f32[2,12,16,128]{3,2,1,0:T(8,128)S(1)}, f32[2,12,16,128]{3,2,1,0:T(8,128)S(1)}, u32[]{:S(2)}, u32[]{:S(2)}) %collective-permute-start.1) | collective-permute-done | bytes 196640 | tf_op jit(solution)/shard_map/ppermute | solution.py:425
  10.7 1.1 %collective-permute-start.2 = (f32[2,108,128]{2,0,1:T(2,128)S(1)}, f32[2,108,128]{2,0,1:T(2,128)S(1)}, u32[]{:S(2)}, u32[]{:S(2)}) collective-permute-start(f32[2,108,128]{2,0,1:T(2,128)S(1)} %bitcast.46), channel_id=1, source_target_pairs={{0,1},{1,0},{2,3},{3,2},{4,5},{5,4},{6,7},{7,6},{8,9},{9,8},{10,11... | collective-permute-start | bytes 331784 | tf_op jit(solution)/shard_map/ppermute | solution.py:425
  11.9 0.0 copy-start
  11.9 1.0 %collective-permute-done.2 = f32[2,108,128]{2,0,1:T(2,128)S(1)} collective-permute-done((f32[2,108,128]{2,0,1:T(2,128)S(1)}, f32[2,108,128]{2,0,1:T(2,128)S(1)}, u32[]{:S(2)}, u32[]{:S(2)}) %collective-permute-start.2) | collective-permute-done | bytes 110624 | tf_op jit(solution)/shard_map/ppermute | solution.py:425
  13.0 0.1 copy.18
  13.1 0.1 pad_maximum_fusion.2
  13.2 0.1 copy.15
  13.3 0.1 pad_maximum_fusion.5
  13.5 1.0 %collective-permute-start.4 = (f32[2,240,128]{2,0,1:T(2,128)S(1)}, f32[2,240,128]{2,0,1:T(2,128)S(1)}, u32[]{:S(2)}, u32[]{:S(2)}) collective-permute-start(f32[2,240,128]{2,0,1:T(2,128)S(1)} %pad_maximum_fusion.5), channel_id=1, source_target_pairs={{0,4},{4,0},{8,12},{12,8},{16,20},{20,16},{24,28},{28,24},{1,5},{5... | collective-permute-start | bytes 737288 | tf_op jit(solution)/shard_map/ppermute | solution.py:425
  14.5 0.1 copy.14
  14.6 0.7 collective-permute-start.3
  15.4 0.2 copy.24
  15.6 3.8 %collective-permute-start.5 = (f32[2,264,128]{2,1,0:T(8,128)S(1)}, f32[2,264,128]{2,1,0:T(8,128)S(1)}, u32[]{:S(2)}, u32[]{:S(2)}) collective-permute-start(f32[2,264,128]{2,1,0:T(8,128)S(1)} %copy.25.refs_0_), channel_id=1, source_target_pairs={{0,8},{4,12},{8,16},{12,20},{16,24},{20,28},{24,0},{28,4},{1,9},{5... | collective-permute-start | bytes 811016 | tf_op jit(solution)/shard_map/ppermute | solution.py:432
  19.4 2.1 %collective-permute-start.6 = (f32[2,264,128]{2,1,0:T(8,128)S(1)}, f32[2,264,128]{2,1,0:T(8,128)S(1)}, u32[]{:S(2)}, u32[]{:S(2)}) collective-permute-start(f32[2,264,128]{2,1,0:T(8,128)S(1)} %copy.25.refs_0_), channel_id=1, source_target_pairs={{0,24},{4,28},{8,0},{12,4},{16,8},{20,12},{24,16},{28,20},{1,25},{... | collective-permute-start | bytes 811016 | tf_op jit(solution)/shard_map/ppermute | solution.py:432
  21.5 0.9 %collective-permute-start.7 = (f32[2,264,128]{2,1,0:T(8,128)S(1)}, f32[2,264,128]{2,1,0:T(8,128)S(1)}, u32[]{:S(2)}, u32[]{:S(2)}) collective-permute-start(f32[2,264,128]{2,1,0:T(8,128)S(1)} %copy.25.refs_0_), channel_id=1, source_target_pairs={{0,16},{4,20},{8,24},{12,28},{16,0},{20,4},{24,8},{28,12},{1,17},{... | collective-permute-start | bytes 811016 | tf_op jit(solution)/shard_map/ppermute | solution.py:432
  22.5 0.0 collective-permute-done.3
  22.5 1.3 %collective-permute-done.4 = f32[2,240,128]{2,0,1:T(2,128)S(1)} collective-permute-done((f32[2,240,128]{2,0,1:T(2,128)S(1)}, f32[2,240,128]{2,0,1:T(2,128)S(1)}, u32[]{:S(2)}, u32[]{:S(2)}) %collective-permute-start.4) | collective-permute-done | bytes 245792 | tf_op jit(solution)/shard_map/ppermute | solution.py:425
  23.7 0.1 broadcast_select_fusion.3
  23.9 0.1 select_maximum_fusion.source_ref
  24.0 0.0 copy-done.1
  24.0 0.0 copy-done
  24.1 14.5 %first_sweep.1 = (f32[18,24,256]{2,1,0:T(8,128)S(1)}, f32[12,16,256]{2,1,0:T(8,128)S(1)}, bf16[7,7,256,256]{3,2,1,0:T(8,128)(2,1)S(1)}, bf16[7,7,256,256]{3,2,1,0:T(8,128)(2,1)S(1)}) custom-call(f32[2,24,32,128]{3,2,1,0:T(8,128)S(1)} %select_maximum_fusion.source_ref, f32[2,128,128]{2,1,0:T(8,128)S(1)} %copy-done.1, f32[7,7,2,128,128]{4,3,2,1,0:T(8,128)S(1)} %copy-done), custom_call_target="tpu_custom_call" | custom-call | flops 8323596288 | bytes 19267584 | tf_op jit(solution)/shard_map/first_sweep/pallas_call | solution.py:162
  38.7 0.2 copy.23
  38.9 0.0 collective-permute-done.5.refs_1_
  38.9 0.0 collective-permute-done.6.refs_3_
  39.0 2.5 %collective-permute-start.12 = (f32[2,2,264,128]{3,2,1,0:T(8,128)S(1)}, f32[2,2,264,128]{3,2,1,0:T(8,128)S(1)}, u32[]{:S(2)}, u32[]{:S(2)}) collective-permute-start(f32[2,2,264,128]{3,2,1,0:T(8,128)S(1)} %pad_maximum_fusion.1), channel_id=1, source_target_pairs={{0,4},{4,0},{8,12},{12,8},{16,20},{20,16},{24,28},{28,24},{1,5},{5... | collective-permute-start | bytes 1622024 | tf_op jit(solution)/shard_map/ppermute | solution.py:425
  41.5 6.3 %second_sweep.1 = (f32[12,16,256]{2,1,0:T(8,128)S(1)}, f32[2,32,192]{2,1,0:T(8,128)S(1)}, f32[2,32,192]{2,1,0:T(8,128)S(1)}, f32[2,32,192]{2,1,0:T(8,128)S(1)}, f32[2,32,192]{2,1,0:T(8,128)S(1)}) custom-call(f32[18,24,256]{2,1,0:T(8,128)S(1)} %get-tuple-element.35.second_ref, f32[12,16,256]{2,1,0:T(8,128)S(1)} %get-tuple-element.36.source_ref, ...), custom_call_target="tpu_custom_call" | custom-call | flops 3699376128 | bytes 12845056 | tf_op jit(solution)/shard_map/second_sweep/pallas_call | solution.py:250
  47.8 0.0 collective-permute-done.7.refs_2_
  47.8 0.1 collective-permute-start.13
  47.9 2.8 %collective-permute-start.8 = (f32[2,32,192]{2,1,0:T(8,128)S(1)}, f32[2,32,192]{2,1,0:T(8,128)S(1)}, u32[]{:S(2)}, u32[]{:S(2)}) collective-permute-start(f32[2,32,192]{2,1,0:T(8,128)S(1)} %get-tuple-element.45), channel_id=1, source_target_pairs={{0,8},{4,12},{8,16},{12,20},{16,24},{20,28},{24,0},{28,4},{1,9},{5... | collective-permute-start | bytes 147464 | tf_op jit(solution)/shard_map/ppermute | solution.py:432
  50.7 2.6 %collective-permute-start.9 = (f32[2,32,192]{2,1,0:T(8,128)S(1)}, f32[2,32,192]{2,1,0:T(8,128)S(1)}, u32[]{:S(2)}, u32[]{:S(2)}) collective-permute-start(f32[2,32,192]{2,1,0:T(8,128)S(1)} %get-tuple-element.46), channel_id=1, source_target_pairs={{0,16},{4,20},{8,24},{12,28},{16,0},{20,4},{24,8},{28,12},{1,17},{... | collective-permute-start | bytes 147464 | tf_op jit(solution)/shard_map/ppermute | solution.py:432
  53.3 1.4 %collective-permute-start.10 = (f32[2,32,192]{2,1,0:T(8,128)S(1)}, f32[2,32,192]{2,1,0:T(8,128)S(1)}, u32[]{:S(2)}, u32[]{:S(2)}) collective-permute-start(f32[2,32,192]{2,1,0:T(8,128)S(1)} %get-tuple-element.47), channel_id=1, source_target_pairs={{0,24},{4,28},{8,0},{12,4},{16,8},{20,12},{24,16},{28,20},{1,25},{... | collective-permute-start | bytes 147464 | tf_op jit(solution)/shard_map/ppermute | solution.py:432
  54.7 0.9 %collective-permute-done.8.refs_1_ = f32[2,32,192]{2,1,0:T(8,128)S(1)} collective-permute-done((f32[2,32,192]{2,1,0:T(8,128)S(1)}, f32[2,32,192]{2,1,0:T(8,128)S(1)}, u32[]{:S(2)}, u32[]{:S(2)}) %collective-permute-start.8) | collective-permute-done | bytes 49184 | tf_op jit(solution)/shard_map/ppermute | solution.py:432
  55.6 2.0 %collective-permute-done.9.refs_2_ = f32[2,32,192]{2,1,0:T(8,128)S(1)} collective-permute-done((f32[2,32,192]{2,1,0:T(8,128)S(1)}, f32[2,32,192]{2,1,0:T(8,128)S(1)}, u32[]{:S(2)}, u32[]{:S(2)}) %collective-permute-start.9) | collective-permute-done | bytes 49184 | tf_op jit(solution)/shard_map/ppermute | solution.py:432
  57.6 0.2 collective-permute-done.10.refs_3_
  57.8 0.8 collective-permute-start.11
  58.6 0.6 collective-permute-done.13.refs_6_
  59.2 0.0 collective-permute-done.12.refs_5_
  59.2 2.7 %spread.1 = (bf16[7,1536,256]{2,1,0:T(8,128)(2,1)S(1)}, bf16[7,1536,256]{2,1,0:T(8,128)(2,1)S(1)}) custom-call(f32[2,264,128]{2,1,0:T(8,128)S(1)} %copy.25.refs_0_, f32[2,264,128]{2,1,0:T(8,128)S(1)} %collective-permute-done.5.refs_1_, f32[2,264,128]{2,1,0:T(8,128)S(1)} %collective-permute-done.7.refs_2_, f32[2,264,128]{2,1,0:T(8,128)S(1)} %collective-permute-done.6.refs_3_, ...), custom_call_target="tpu_custom_call" | custom-call | bytes 2162688 | tf_op jit(solution)/shard_map/spread/pallas_call | solution.py:318
  62.0 0.9 %collective-permute-done.11.refs_4_ = f32[4,32,192]{2,1,0:T(8,128)S(1)} collective-permute-done((f32[4,32,192]{2,1,0:T(8,128)S(1)}, f32[4,32,192]{2,1,0:T(8,128)S(1)}, u32[]{:S(2)}, u32[]{:S(2)}) %collective-permute-start.11) | collective-permute-done | bytes 98336 | tf_op jit(solution)/shard_map/ppermute | solution.py:425
  62.9 5.6 %correlate.1 = (f32[7,7,2,8,128]{4,3,2,1,0:T(8,128)S(1)}, f32[7,7,2,8,128]{4,3,2,1,0:T(8,128)S(1)}) custom-call(f32[2,32,192]{2,1,0:T(8,128)S(1)} %get-tuple-element.44.refs_0_, f32[2,32,192]{2,1,0:T(8,128)S(1)} %collective-permute-done.8.refs_1_, f32[2,32,192]{2,1,0:T(8,128)S(1)} %collective-permute-done.9.refs_2_, ...), custom_call_target="tpu_custom_call" | custom-call | flops 3699376128 | bytes 802816 | tf_op jit(solution)/shard_map/correlate/pallas_call | solution.py:398
  68.4 0.1 collective-permute-start.14
  68.5 1.7 %collective-permute-done.14 = f32[7,7,2,8,128]{4,3,2,1,0:T(8,128)S(1)} collective-permute-done((f32[7,7,2,8,128]{4,3,2,1,0:T(8,128)S(1)}, f32[7,7,2,8,128]{4,3,2,1,0:T(8,128)S(1)}, u32[]{:S(2)}, u32[]{:S(2)}) %collective-permute-start.14) | collective-permute-done | bytes 401440 | tf_op jit(solution)/shard_map/ppermute | solution.py:425
  70.2 0.1 add.18
  70.3 1.8 %collective-permute-start.15 = (f32[7,7,2,8,128]{4,3,2,1,0:T(8,128)S(1)}, f32[7,7,2,8,128]{4,3,2,1,0:T(8,128)S(1)}, u32[]{:S(2)}, u32[]{:S(2)}) collective-permute-start(f32[7,7,2,8,128]{4,3,2,1,0:T(8,128)S(1)} %add.18), channel_id=1, source_target_pairs={{0,2},{1,3},{2,0},{3,1},{4,6},{5,7},{6,4},{7,5},{8,10},{9,11},{10,... | collective-permute-start | bytes 1204232 | tf_op jit(solution)/shard_map/ppermute | solution.py:432
  72.1 9.6 %collective-permute-done.15 = f32[7,7,2,8,128]{4,3,2,1,0:T(8,128)S(1)} collective-permute-done((f32[7,7,2,8,128]{4,3,2,1,0:T(8,128)S(1)}, f32[7,7,2,8,128]{4,3,2,1,0:T(8,128)S(1)}, u32[]{:S(2)}, u32[]{:S(2)}) %collective-permute-start.15) | collective-permute-done | bytes 401440 | tf_op jit(solution)/shard_map/ppermute | solution.py:432
  81.7 0.1 add.19
  81.8 0.1 collective-permute-start.16
  81.9 0.8 reshape.47
  82.6 0.9 %collective-permute-done.16 = f32[7,7,2,8,128]{4,3,2,1,0:T(8,128)S(1)} collective-permute-done((f32[7,7,2,8,128]{4,3,2,1,0:T(8,128)S(1)}, f32[7,7,2,8,128]{4,3,2,1,0:T(8,128)S(1)}, u32[]{:S(2)}, u32[]{:S(2)}) %collective-permute-start.16) | collective-permute-done | bytes 401440 | tf_op jit(solution)/shard_map/ppermute | solution.py:425
  83.6 0.1 broadcast_select_fusion.1
  83.7 1.0 %pad_maximum_fusion = f32[7,7,2,16,128]{4,3,2,1,0:T(8,128)} fusion(f32[7,7,2,8,128]{4,3,2,1,0:T(8,128)S(1)} %get-tuple-element.57, f32[7,7,2,8,128]{4,3,2,1,0:T(8,128)S(1)} %get-tuple-element.56), kind=kLoop, calls=%fused_computation | loop fusion | flops 200704 | bytes 1605632 | tf_op jit(solution)/shard_map/concatenate | solution.py:510
  (29 shorter events, 0.5 us)
Async XLA Ops:
  0.6 23.4 %copy-start.1 = (f32[2,128,128]{2,1,0:T(8,128)S(1)}, f32[2,128,128]{2,1,0:T(8,128)}, u32[]{:S(2)}) copy-start(f32[2,128,128]{2,1,0:T(8,128)} %inverse_ref.3) | copy-start | bytes 393220
  2.8 7.9 %collective-permute-start.1 = (f32[2,12,16,128]{3,2,1,0:T(8,128)S(1)}, f32[2,12,16,128]{3,2,1,0:T(8,128)S(1)}, u32[]{:S(2)}, u32[]{:S(2)}) collective-permute-start(f32[2,12,16,128]{3,2,1,0:T(8,128)S(1)} %bitcast.32), channel_id=1, source_target_pairs={{0,4},{4,0},{8,12},{12,8},{16,20},{20,16},{24,28},{28,24},{1,5},{5... | collective-permute-start | bytes 589832 | tf_op jit(solution)/shard_map/ppermute | solution.py:425
  5.9 0.7 collective-permute-start
  10.7 2.1 %collective-permute-start.2 = (f32[2,108,128]{2,0,1:T(2,128)S(1)}, f32[2,108,128]{2,0,1:T(2,128)S(1)}, u32[]{:S(2)}, u32[]{:S(2)}) collective-permute-start(f32[2,108,128]{2,0,1:T(2,128)S(1)} %bitcast.46), channel_id=1, source_target_pairs={{0,1},{1,0},{2,3},{3,2},{4,5},{5,4},{6,7},{7,6},{8,9},{9,8},{10,11... | collective-permute-start | bytes 331784 | tf_op jit(solution)/shard_map/ppermute | solution.py:425
  11.9 12.2 %copy-start = (f32[7,7,2,128,128]{4,3,2,1,0:T(8,128)S(1)}, f32[7,7,2,128,128]{4,3,2,1,0:T(8,128)}, u32[]{:S(2)}) copy-start(f32[7,7,2,128,128]{4,3,2,1,0:T(8,128)} %blocks_ref.1) | copy-start | bytes 19267588
  13.5 10.3 %collective-permute-start.4 = (f32[2,240,128]{2,0,1:T(2,128)S(1)}, f32[2,240,128]{2,0,1:T(2,128)S(1)}, u32[]{:S(2)}, u32[]{:S(2)}) collective-permute-start(f32[2,240,128]{2,0,1:T(2,128)S(1)} %pad_maximum_fusion.5), channel_id=1, source_target_pairs={{0,4},{4,0},{8,12},{12,8},{16,20},{20,16},{24,28},{28,24},{1,5},{5... | collective-permute-start | bytes 737288 | tf_op jit(solution)/shard_map/ppermute | solution.py:425
  14.6 7.8 %collective-permute-start.3 = (f32[2,168,128]{2,0,1:T(2,128)S(1)}, f32[2,168,128]{2,0,1:T(2,128)S(1)}, u32[]{:S(2)}, u32[]{:S(2)}) collective-permute-start(f32[2,168,128]{2,0,1:T(2,128)S(1)} %bitcast.45), channel_id=1, source_target_pairs={{4,8},{8,4},{12,16},{16,12},{20,24},{24,20},{5,9},{9,5},{13,17},{1... | collective-permute-start | bytes 516104 | tf_op jit(solution)/shard_map/ppermute | solution.py:425
  15.6 23.3 %collective-permute-start.5 = (f32[2,264,128]{2,1,0:T(8,128)S(1)}, f32[2,264,128]{2,1,0:T(8,128)S(1)}, u32[]{:S(2)}, u32[]{:S(2)}) collective-permute-start(f32[2,264,128]{2,1,0:T(8,128)S(1)} %copy.25.refs_0_), channel_id=1, source_target_pairs={{0,8},{4,12},{8,16},{12,20},{16,24},{20,28},{24,0},{28,4},{1,9},{5... | collective-permute-start | bytes 811016 | tf_op jit(solution)/shard_map/ppermute | solution.py:432
  19.4 19.5 %collective-permute-start.6 = (f32[2,264,128]{2,1,0:T(8,128)S(1)}, f32[2,264,128]{2,1,0:T(8,128)S(1)}, u32[]{:S(2)}, u32[]{:S(2)}) collective-permute-start(f32[2,264,128]{2,1,0:T(8,128)S(1)} %copy.25.refs_0_), channel_id=1, source_target_pairs={{0,24},{4,28},{8,0},{12,4},{16,8},{20,12},{24,16},{28,20},{1,25},{... | collective-permute-start | bytes 811016 | tf_op jit(solution)/shard_map/ppermute | solution.py:432
  21.5 26.2 %collective-permute-start.7 = (f32[2,264,128]{2,1,0:T(8,128)S(1)}, f32[2,264,128]{2,1,0:T(8,128)S(1)}, u32[]{:S(2)}, u32[]{:S(2)}) collective-permute-start(f32[2,264,128]{2,1,0:T(8,128)S(1)} %copy.25.refs_0_), channel_id=1, source_target_pairs={{0,16},{4,20},{8,24},{12,28},{16,0},{20,4},{24,8},{28,12},{1,17},{... | collective-permute-start | bytes 811016 | tf_op jit(solution)/shard_map/ppermute | solution.py:432
  39.0 20.2 %collective-permute-start.12 = (f32[2,2,264,128]{3,2,1,0:T(8,128)S(1)}, f32[2,2,264,128]{3,2,1,0:T(8,128)S(1)}, u32[]{:S(2)}, u32[]{:S(2)}) collective-permute-start(f32[2,2,264,128]{3,2,1,0:T(8,128)S(1)} %pad_maximum_fusion.1), channel_id=1, source_target_pairs={{0,4},{4,0},{8,12},{12,8},{16,20},{20,16},{24,28},{28,24},{1,5},{5... | collective-permute-start | bytes 1622024 | tf_op jit(solution)/shard_map/ppermute | solution.py:425
  47.8 11.5 %collective-permute-start.13 = (f32[1,2,264,128]{3,2,1,0:T(8,128)S(1)}, f32[1,2,264,128]{3,2,1,0:T(8,128)S(1)}, u32[]{:S(2)}, u32[]{:S(2)}) collective-permute-start(f32[1,2,264,128]{3,2,1,0:T(8,128)S(1)} %bitcast.27), channel_id=1, source_target_pairs={{0,4},{4,0},{8,12},{12,8},{16,20},{20,16},{24,28},{28,24},{1,5},{5... | collective-permute-start | bytes 811016 | tf_op jit(solution)/shard_map/ppermute | solution.py:425
  47.9 7.7 %collective-permute-start.8 = (f32[2,32,192]{2,1,0:T(8,128)S(1)}, f32[2,32,192]{2,1,0:T(8,128)S(1)}, u32[]{:S(2)}, u32[]{:S(2)}) collective-permute-start(f32[2,32,192]{2,1,0:T(8,128)S(1)} %get-tuple-element.45), channel_id=1, source_target_pairs={{0,8},{4,12},{8,16},{12,20},{16,24},{20,28},{24,0},{28,4},{1,9},{5... | collective-permute-start | bytes 147464 | tf_op jit(solution)/shard_map/ppermute | solution.py:432
  50.7 6.9 %collective-permute-start.9 = (f32[2,32,192]{2,1,0:T(8,128)S(1)}, f32[2,32,192]{2,1,0:T(8,128)S(1)}, u32[]{:S(2)}, u32[]{:S(2)}) collective-permute-start(f32[2,32,192]{2,1,0:T(8,128)S(1)} %get-tuple-element.46), channel_id=1, source_target_pairs={{0,16},{4,20},{8,24},{12,28},{16,0},{20,4},{24,8},{28,12},{1,17},{... | collective-permute-start | bytes 147464 | tf_op jit(solution)/shard_map/ppermute | solution.py:432
  53.3 4.5 %collective-permute-start.10 = (f32[2,32,192]{2,1,0:T(8,128)S(1)}, f32[2,32,192]{2,1,0:T(8,128)S(1)}, u32[]{:S(2)}, u32[]{:S(2)}) collective-permute-start(f32[2,32,192]{2,1,0:T(8,128)S(1)} %get-tuple-element.47), channel_id=1, source_target_pairs={{0,24},{4,28},{8,0},{12,4},{16,8},{20,12},{24,16},{28,20},{1,25},{... | collective-permute-start | bytes 147464 | tf_op jit(solution)/shard_map/ppermute | solution.py:432
  57.8 5.0 %collective-permute-start.11 = (f32[4,32,192]{2,1,0:T(8,128)S(1)}, f32[4,32,192]{2,1,0:T(8,128)S(1)}, u32[]{:S(2)}, u32[]{:S(2)}) collective-permute-start(f32[4,32,192]{2,1,0:T(8,128)S(1)} %pad_maximum_fusion.8), channel_id=1, source_target_pairs={{0,4},{4,0},{8,12},{12,8},{16,20},{20,16},{24,28},{28,24},{1,5},{5... | collective-permute-start | bytes 294920 | tf_op jit(solution)/shard_map/ppermute | solution.py:425
  68.4 1.8 %collective-permute-start.14 = (f32[7,7,2,8,128]{4,3,2,1,0:T(8,128)S(1)}, f32[7,7,2,8,128]{4,3,2,1,0:T(8,128)S(1)}, u32[]{:S(2)}, u32[]{:S(2)}) collective-permute-start(f32[7,7,2,8,128]{4,3,2,1,0:T(8,128)S(1)} %get-tuple-element.54), channel_id=1, source_target_pairs={{0,1},{1,0},{2,3},{3,2},{4,5},{5,4},{6,7},{7,6},{8,9},{9,8},{10,11... | collective-permute-start | bytes 1204232 | tf_op jit(solution)/shard_map/ppermute | solution.py:425
  70.3 11.4 %collective-permute-start.15 = (f32[7,7,2,8,128]{4,3,2,1,0:T(8,128)S(1)}, f32[7,7,2,8,128]{4,3,2,1,0:T(8,128)S(1)}, u32[]{:S(2)}, u32[]{:S(2)}) collective-permute-start(f32[7,7,2,8,128]{4,3,2,1,0:T(8,128)S(1)} %add.18), channel_id=1, source_target_pairs={{0,2},{1,3},{2,0},{3,1},{4,6},{5,7},{6,4},{7,5},{8,10},{9,11},{10,... | collective-permute-start | bytes 1204232 | tf_op jit(solution)/shard_map/ppermute | solution.py:432
  81.8 1.8 %collective-permute-start.16 = (f32[7,7,2,8,128]{4,3,2,1,0:T(8,128)S(1)}, f32[7,7,2,8,128]{4,3,2,1,0:T(8,128)S(1)}, u32[]{:S(2)}, u32[]{:S(2)}) collective-permute-start(f32[7,7,2,8,128]{4,3,2,1,0:T(8,128)S(1)} %add.19), channel_id=1, source_target_pairs={{0,1},{1,0},{2,3},{3,2},{4,5},{5,4},{6,7},{7,6},{8,9},{9,8},{10,11... | collective-permute-start | bytes 1204232 | tf_op jit(solution)/shard_map/ppermute | solution.py:425

commit v10 on v9

--- a/solution.py
+++ b/solution.py
@@ -416,6 +416,25 @@
     )(*shares, twin_shares, s_high, s_low)
 
 
+def parts_first_kernel(field_ref, out_ref):
+    for part in range(2):
+        out_ref[part] = field_ref[:, pl.ds(part, out_ref.shape[2], 2), :]
+
+
+def parts_first(field):
+    rows, cols, parts, width = field.shape
+    vmem = pl.BlockSpec(memory_space=pltpu.VMEM)
+    return pl.pallas_call(
+        parts_first_kernel,
+        in_specs=[vmem],
+        out_specs=vmem,
+        out_shape=jax.ShapeDtypeStruct((parts, rows, cols, width), f32),
+        cost_estimate=pl.CostEstimate(flops=0, bytes_accessed=8 * field.size, transcendentals=0),
+        compiler_params=pltpu.CompilerParams(vmem_limit_bytes=4 * 1024 * 1024),
+        name="parts_first",
+    )(field.reshape(rows, cols * parts, width))
+
+
 def swap(value, axis, first):
     pairs = []
     for low in range(first, lax.axis_size(axis) - 1, 2):
@@ -432,24 +451,21 @@
     return lax.ppermute(value, axis, [(i, (i + shift) % peers) for i in range(peers)])
 
 
-def edges(initial, last, axis, rider=None, beside=None):
+def edges(initial, last, axis):
     even = lax.axis_index(axis) % 2 == 0
     shape = initial.shape
     initial, last = (value.reshape(shape[0], -1, shape[-1]) for value in (initial, last))
-    inner = jnp.where(even, last, initial)
-    outer = swap(jnp.where(even, initial, last), axis, 1)
-    count = inner.shape[1]
-    if beside is None:
-        inner = swap(jnp.concatenate([inner, rider], axis=1), axis, 0)
-        inner, rider = inner[:, :count], inner[:, count:]
-    else:
-        inner, beside = lax.optimization_barrier((inner, beside))
-        rider = swap(beside, "row", 0)
-        inner, outer, rider = lax.optimization_barrier((inner, outer, rider))
-        inner = swap(inner, axis, 0)
-    inner = inner.reshape(shape)
-    outer = outer.reshape(shape)
-    return jnp.where(even, outer, inner), jnp.where(even, inner, outer), rider
+    outer = swap(jnp.where(even, initial, last), axis, 1).reshape(shape)
+    inner = swap(jnp.where(even, last, initial), axis, 0).reshape(shape)
+    return jnp.where(even, outer, inner), jnp.where(even, inner, outer)
+
+
+def extended(value, axis, dim, width):
+    length = value.shape[dim]
+    initial = lax.slice_in_dim(value, 0, width, axis=dim)
+    last = lax.slice_in_dim(value, length - width, length, axis=dim)
+    before, after = edges(initial, last, axis)
+    return jnp.concatenate([before, value, after], axis=dim)
 
 
 def on_device(adjoint_source, saved_currents, lag_blocks, element_inverse):
@@ -460,27 +476,20 @@
     peers = lax.axis_size("row")
 
     source = adjoint_source.transpose(2, 0, 1, 3)
-    saved = saved_currents.transpose(2, 0, 1, 3)
-    initial = jnp.concatenate([source[:, :, :halo], saved[:, :, :reach]], axis=2)
-    last = jnp.concatenate([source[:, :, cols - halo :], saved[:, :, cols - reach :]], axis=2)
-    before, after, twin_own = edges(initial, last, "col", beside=saved)
-    source = jnp.concatenate([before[:, :, :halo], source, after[:, :, :halo]], axis=2)
-    saved = jnp.concatenate([before[:, :, halo:], saved, after[:, :, halo:]], axis=2)
-    sides = jnp.concatenate([saved[:, :, :reach], saved[:, :, cols + reach :]], axis=2)
-    twin_sides = sides.reshape(parts, -1, width)
-    before, after, arrived = edges(source[:, :halo], source[:, rows - halo :], "row", twin_sides)
-    source = jnp.concatenate([before, source, after], axis=1)
+    saved = parts_first(saved_currents)
+    source = extended(source, "row", 1, halo)
+    saved = extended(saved, "col", 2, reach)
+    saved = lax.optimization_barrier((saved, source))[0]
+    source = extended(source, "col", 2, halo)
     wide = round_up(cols + 2 * halo, 8)
     source = jnp.pad(source, ((0, 0), (0, 0), (0, wide - cols - 2 * halo), (0, 0)))
-    twin_sides = arrived.reshape(sides.shape)
-    own_twin = jnp.concatenate([twin_sides[:, :, :reach], twin_own, twin_sides[:, :, reach:]], axis=2)
-    own_twin = own_twin.reshape(parts, -1, width)
 
     saved = saved.reshape(parts, -1, width)
     pieces = {0: saved}
     for k in sorted(range(1, peers // 2), key=lambda k: min(k, peers // 2 - k)):
         pieces[k] = shifted(saved, "row", 2 * k)
     pieces = [pieces[k] for k in range(peers // 2)]
+    own_twin = swap(saved, "row", 0)
 
     second, own_source, high, low = first_sweep(source, element_inverse, lag_blocks, rows, cols)
     second, own_twin, early = lax.optimization_barrier((second, own_twin, jnp.stack([pieces[1], pieces[-1]])))

time: 85.2 us -> 83 us (0.974)
  waiting for transfers between devices: 23.3 us -> 19.2 us
  starting transfers between devices: 25.5 us -> 28.8 us
    ppermute x10 -> x12, starting transfers between devices: 10 us -> 17.4 us  [swap(): return lax.ppermute(value, axis, pairs)]
    ppermute x10 -> x12, waiting for transfers between devices: 10.5 us -> 5.71 us  [swap(): return lax.ppermute(value, axis, pairs)]
    ppermute x7, starting transfers between devices: 15.5 us -> 11.4 us  [shifted(): lax.ppermute(value, axis, [(i, (i + shift) % peers) for i in range(peers)])]
    unnamed x12 -> x7, local copies, waits for them, and re-layouts: 2.01 us -> 1.91 us
  transfers between devices with their start and end apart: 17 -> 19, of which waited for: 11 -> 6; matrix products, arithmetic and copies ran while one was open for 2% -> 2% of each run, Pallas kernels for 28% -> 28%
where the time goes in v10:
time: 83 us; the launch traced here: 82.8 us
  Pallas kernels  29.1 us (35%)
  starting transfers between devices  28.8 us (35%)
  waiting for transfers between devices  19.2 us (23%)
  local copies, waits for them, and re-layouts  3.28 us (4%)
  other arithmetic  1.52 us (2%)
  between operations  0.96 us (1%)
    ppermute x12, starting transfers between devices, swap(): return lax.ppermute(value, axis, pairs)  17.4 us
    pallas_call x1, Pallas kernels, first_sweep(): pl.pallas_call(functools.partial(first_sweep_kernel, (rows, cols, span, p...  14.5 us
    ppermute x7, waiting for transfers between devices, shifted(): lax.ppermute(value, axis, [(i, (i + shift) % peers) for i in range(peers)])  13.4 us
    ppermute x7, starting transfers between devices, shifted(): lax.ppermute(value, axis, [(i, (i + shift) % peers) for i in range(peers)])  11.4 us
    pallas_call x1, Pallas kernels, second_sweep(): pl.pallas_call(functools.partial(second_sweep_kernel, (rows, cols, span,...  6.25 us
    ppermute x12, waiting for transfers between devices, swap(): return lax.ppermute(value, axis, pairs)  5.71 us
    pallas_call x1, Pallas kernels, correlate(): pl.pallas_call(functools.partial(correlate_kernel, (rows, cols, span, pee...  5.57 us
    pallas_call x1, Pallas kernels, spread(): pl.pallas_call(functools.partial(spread_kernel, (rows, cols, span, peers)...  2.73 us
  transfers between devices with their start and end apart: 19, of which 6 were waited for; matrix products, arithmetic and copies ran while one was open for 2% of the time, Pallas kernels for 28%

profile of v10, /device:TPU:0, one launch (start us, length us, event | category | flops | bytes accessed | tf_op | source)
XLA Modules:
  0.0 82.8 jit_solution(3322348023180672892)
XLA Ops:
  0.6 0.0 copy-start.2
  0.7 1.0 %copy.23 = f32[12,16,2,128]{3,1,0,2:T(8,128)S(1)} copy(f32[12,16,2,128]{3,2,1,0:T(2,128)} %param.4) | data formatting | bytes 393216 | tf_op args[0]
  1.7 0.7 collective-permute-start
  2.3 5.8 %collective-permute-start.1 = (f32[2,96,128]{2,1,0:T(8,128)S(1)}, f32[2,96,128]{2,1,0:T(8,128)S(1)}, u32[]{:S(2)}, u32[]{:S(2)}) collective-permute-start(f32[2,96,128]{2,1,0:T(8,128)S(1)} %bitcast.48), channel_id=1, source_target_pairs={{0,4},{4,0},{8,12},{12,8},{16,20},{20,16},{24,28},{28,24},{1,5},{5... | collective-permute-start | bytes 294920 | tf_op jit(solution)/shard_map/ppermute | solution.py:444
  8.1 0.0 copy-start
  8.1 0.9 %copy-done = f32[12,16,2,128]{3,2,1,0:T(2,128)S(1)} copy-done((f32[12,16,2,128]{3,2,1,0:T(2,128)S(1)}, f32[12,16,2,128]{3,2,1,0:T(2,128)}, u32[]{:S(2)}) %copy-start) | copy-done | bytes 196632
  9.1 0.0 copy-start.1
  9.1 0.8 collective-permute-start.4
  10.0 3.0 %collective-permute-start.5 = (f32[2,36,128]{2,0,1:T(2,128)S(1)}, f32[2,36,128]{2,0,1:T(2,128)S(1)}, u32[]{:S(2)}, u32[]{:S(2)}) collective-permute-start(f32[2,36,128]{2,0,1:T(2,128)S(1)} %bitcast.53), channel_id=1, source_target_pairs={{0,1},{1,0},{2,3},{3,2},{4,5},{5,4},{6,7},{7,6},{8,9},{9,8},{10,11... | collective-permute-start | bytes 110600 | tf_op jit(solution)/shard_map/ppermute | solution.py:444
  13.0 0.0 collective-permute-done
  13.0 0.0 collective-permute-done.1
  13.1 0.1 copy.8
  13.2 0.7 collective-permute-start.2
  13.9 0.1 copy.9
  14.0 1.5 %collective-permute-start.3 = (f32[2,144,128]{2,0,1:T(2,128)S(1)}, f32[2,144,128]{2,0,1:T(2,128)S(1)}, u32[]{:S(2)}, u32[]{:S(2)}) collective-permute-start(f32[2,144,128]{2,0,1:T(2,128)S(1)} %bitcast.44), channel_id=1, source_target_pairs={{0,1},{1,0},{2,3},{3,2},{4,5},{5,4},{6,7},{7,6},{8,9},{9,8},{10,11... | collective-permute-start | bytes 442376 | tf_op jit(solution)/shard_map/ppermute | solution.py:444
  15.5 0.0 collective-permute-done.4
  15.5 0.0 collective-permute-done.5
  15.6 0.2 copy.16
  15.9 2.6 %collective-permute-start.7 = (f32[2,264,128]{2,1,0:T(8,128)S(1)}, f32[2,264,128]{2,1,0:T(8,128)S(1)}, u32[]{:S(2)}, u32[]{:S(2)}) collective-permute-start(f32[2,264,128]{2,1,0:T(8,128)S(1)} %copy.17.refs_0_), channel_id=1, source_target_pairs={{0,8},{4,12},{8,16},{12,20},{16,24},{20,28},{24,0},{28,4},{1,9},{5... | collective-permute-start | bytes 811016 | tf_op jit(solution)/shard_map/ppermute | solution.py:451
  18.5 2.1 %collective-permute-start.8 = (f32[2,264,128]{2,1,0:T(8,128)S(1)}, f32[2,264,128]{2,1,0:T(8,128)S(1)}, u32[]{:S(2)}, u32[]{:S(2)}) collective-permute-start(f32[2,264,128]{2,1,0:T(8,128)S(1)} %copy.17.refs_0_), channel_id=1, source_target_pairs={{0,24},{4,28},{8,0},{12,4},{16,8},{20,12},{24,16},{28,20},{1,25},{... | collective-permute-start | bytes 811016 | tf_op jit(solution)/shard_map/ppermute | solution.py:451
  20.6 1.7 %collective-permute-start.6 = (f32[2,264,128]{2,1,0:T(8,128)S(1)}, f32[2,264,128]{2,1,0:T(8,128)S(1)}, u32[]{:S(2)}, u32[]{:S(2)}) collective-permute-start(f32[2,264,128]{2,1,0:T(8,128)S(1)} %copy.17.refs_0_), channel_id=1, source_target_pairs={{0,4},{4,0},{8,12},{12,8},{16,20},{20,16},{24,28},{28,24},{1,5},{5... | collective-permute-start | bytes 811016 | tf_op jit(solution)/shard_map/ppermute | solution.py:444
  22.2 0.0 collective-permute-done.2
  22.2 0.8 collective-permute-start.9
  23.0 0.0 collective-permute-done.3
  23.1 0.1 select_maximum_fusion.source_ref
  23.3 0.0 copy-done.2
  23.3 0.0 copy-done.1
  23.3 14.5 %first_sweep.1 = (f32[18,24,256]{2,1,0:T(8,128)S(1)}, f32[12,16,256]{2,1,0:T(8,128)S(1)}, bf16[7,7,256,256]{3,2,1,0:T(8,128)(2,1)S(1)}, bf16[7,7,256,256]{3,2,1,0:T(8,128)(2,1)S(1)}) custom-call(f32[2,24,32,128]{3,2,1,0:T(8,128)S(1)} %select_maximum_fusion.source_ref, f32[2,128,128]{2,1,0:T(8,128)S(1)} %copy-done.2, f32[7,7,2,128,128]{4,3,2,1,0:T(8,128)S(1)} %copy-done.1), custom_call_target="tpu_custom_call" | custom-call | flops 8323596288 | bytes 19267584 | tf_op jit(solution)/shard_map/first_sweep/pallas_call | solution.py:162
  37.8 0.0 collective-permute-done.7.refs_1_
  37.8 0.0 collective-permute-done.8.refs_3_
  37.9 0.0 collective-permute-done.6.refs_4_
  37.9 0.6 collective-permute-start.14
  38.5 6.2 %second_sweep.1 = (f32[12,16,256]{2,1,0:T(8,128)S(1)}, f32[2,32,192]{2,1,0:T(8,128)S(1)}, f32[2,32,192]{2,1,0:T(8,128)S(1)}, f32[2,32,192]{2,1,0:T(8,128)S(1)}, f32[2,32,192]{2,1,0:T(8,128)S(1)}) custom-call(f32[18,24,256]{2,1,0:T(8,128)S(1)} %get-tuple-element.27.second_ref, f32[12,16,256]{2,1,0:T(8,128)S(1)} %get-tuple-element.28.source_ref, ...), custom_call_target="tpu_custom_call" | custom-call | flops 3699376128 | bytes 12845056 | tf_op jit(solution)/shard_map/second_sweep/pallas_call | solution.py:250
  44.7 0.0 collective-permute-done.9.refs_2_
  44.7 1.6 %collective-permute-start.15 = (f32[1,2,264,128]{3,2,1,0:T(8,128)S(1)}, f32[1,2,264,128]{3,2,1,0:T(8,128)S(1)}, u32[]{:S(2)}, u32[]{:S(2)}) collective-permute-start(f32[1,2,264,128]{3,2,1,0:T(8,128)S(1)} %bitcast.30), channel_id=1, source_target_pairs={{0,4},{4,0},{8,12},{12,8},{16,20},{20,16},{24,28},{28,24},{1,5},{5... | collective-permute-start | bytes 811016 | tf_op jit(solution)/shard_map/ppermute | solution.py:444
  46.3 0.7 collective-permute-start.10
  47.0 1.9 %collective-permute-start.11 = (f32[2,32,192]{2,1,0:T(8,128)S(1)}, f32[2,32,192]{2,1,0:T(8,128)S(1)}, u32[]{:S(2)}, u32[]{:S(2)}) collective-permute-start(f32[2,32,192]{2,1,0:T(8,128)S(1)} %get-tuple-element.38), channel_id=1, source_target_pairs={{0,16},{4,20},{8,24},{12,28},{16,0},{20,4},{24,8},{28,12},{1,17},{... | collective-permute-start | bytes 147464 | tf_op jit(solution)/shard_map/ppermute | solution.py:451
  48.9 2.9 %collective-permute-start.12 = (f32[2,32,192]{2,1,0:T(8,128)S(1)}, f32[2,32,192]{2,1,0:T(8,128)S(1)}, u32[]{:S(2)}, u32[]{:S(2)}) collective-permute-start(f32[2,32,192]{2,1,0:T(8,128)S(1)} %get-tuple-element.39), channel_id=1, source_target_pairs={{0,24},{4,28},{8,0},{12,4},{16,8},{20,12},{24,16},{28,20},{1,25},{... | collective-permute-start | bytes 147464 | tf_op jit(solution)/shard_map/ppermute | solution.py:451
  51.8 1.2 %collective-permute-done.10.refs_1_ = f32[2,32,192]{2,1,0:T(8,128)S(1)} collective-permute-done((f32[2,32,192]{2,1,0:T(8,128)S(1)}, f32[2,32,192]{2,1,0:T(8,128)S(1)}, u32[]{:S(2)}, u32[]{:S(2)}) %collective-permute-start.10) | collective-permute-done | bytes 49184 | tf_op jit(solution)/shard_map/ppermute | solution.py:451
  53.0 1.3 %collective-permute-done.11.refs_2_ = f32[2,32,192]{2,1,0:T(8,128)S(1)} collective-permute-done((f32[2,32,192]{2,1,0:T(8,128)S(1)}, f32[2,32,192]{2,1,0:T(8,128)S(1)}, u32[]{:S(2)}, u32[]{:S(2)}) %collective-permute-start.11) | collective-permute-done | bytes 49184 | tf_op jit(solution)/shard_map/ppermute | solution.py:451
  54.3 0.0 collective-permute-done.12.refs_3_
  54.3 1.0 %collective-permute-start.13 = (f32[4,32,192]{2,1,0:T(8,128)S(1)}, f32[4,32,192]{2,1,0:T(8,128)S(1)}, u32[]{:S(2)}, u32[]{:S(2)}) collective-permute-start(f32[4,32,192]{2,1,0:T(8,128)S(1)} %pad_maximum_fusion.4), channel_id=1, source_target_pairs={{0,4},{4,0},{8,12},{12,8},{16,20},{20,16},{24,28},{28,24},{1,5},{5... | collective-permute-start | bytes 294920 | tf_op jit(solution)/shard_map/ppermute | solution.py:444
  55.3 3.0 %collective-permute-done.15.refs_6_ = f32[1,2,264,128]{3,2,1,0:T(8,128)S(1)} collective-permute-done((f32[1,2,264,128]{3,2,1,0:T(8,128)S(1)}, f32[1,2,264,128]{3,2,1,0:T(8,128)S(1)}, u32[]{:S(2)}, u32[]{:S(2)}) %collective-permute-start.15) | collective-permute-done | bytes 270368 | tf_op jit(solution)/shard_map/ppermute | solution.py:444
  58.3 0.0 collective-permute-done.14.refs_5_
  58.3 2.7 %spread.1 = (bf16[7,1536,256]{2,1,0:T(8,128)(2,1)S(1)}, bf16[7,1536,256]{2,1,0:T(8,128)(2,1)S(1)}) custom-call(f32[2,264,128]{2,1,0:T(8,128)S(1)} %copy.17.refs_0_, f32[2,264,128]{2,1,0:T(8,128)S(1)} %collective-permute-done.7.refs_1_, f32[2,264,128]{2,1,0:T(8,128)S(1)} %collective-permute-done.9.refs_2_, f32[2,264,128]{2,1,0:T(8,128)S(1)} %collective-permute-done.8.refs_3_, ...), custom_call_target="tpu_custom_call" | custom-call | bytes 2162688 | tf_op jit(solution)/shard_map/spread/pallas_call | solution.py:318
  61.1 0.0 collective-permute-done.13.refs_4_
  61.1 5.6 %correlate.1 = (f32[7,7,2,8,128]{4,3,2,1,0:T(8,128)S(1)}, f32[7,7,2,8,128]{4,3,2,1,0:T(8,128)S(1)}) custom-call(f32[2,32,192]{2,1,0:T(8,128)S(1)} %get-tuple-element.36.refs_0_, f32[2,32,192]{2,1,0:T(8,128)S(1)} %collective-permute-done.10.refs_1_, f32[2,32,192]{2,1,0:T(8,128)S(1)} %collective-permute-done.11.refs_2_, ...), custom_call_target="tpu_custom_call" | custom-call | flops 3699376128 | bytes 802816 | tf_op jit(solution)/shard_map/correlate/pallas_call | solution.py:398
  66.7 0.1 collective-permute-start.16
  66.8 1.7 %collective-permute-done.16 = f32[7,7,2,8,128]{4,3,2,1,0:T(8,128)S(1)} collective-permute-done((f32[7,7,2,8,128]{4,3,2,1,0:T(8,128)S(1)}, f32[7,7,2,8,128]{4,3,2,1,0:T(8,128)S(1)}, u32[]{:S(2)}, u32[]{:S(2)}) %collective-permute-start.16) | collective-permute-done | bytes 401440 | tf_op jit(solution)/shard_map/ppermute | solution.py:444
  68.5 0.1 add.19
  68.5 0.4 collective-permute-start.17
  69.0 11.0 %collective-permute-done.17 = f32[7,7,2,8,128]{4,3,2,1,0:T(8,128)S(1)} collective-permute-done((f32[7,7,2,8,128]{4,3,2,1,0:T(8,128)S(1)}, f32[7,7,2,8,128]{4,3,2,1,0:T(8,128)S(1)}, u32[]{:S(2)}, u32[]{:S(2)}) %collective-permute-start.17) | collective-permute-done | bytes 401440 | tf_op jit(solution)/shard_map/ppermute | solution.py:451
  79.9 0.1 add.20
  80.0 0.1 collective-permute-start.18
  80.1 0.8 reshape.51
  80.9 0.9 %collective-permute-done.18 = f32[7,7,2,8,128]{4,3,2,1,0:T(8,128)S(1)} collective-permute-done((f32[7,7,2,8,128]{4,3,2,1,0:T(8,128)S(1)}, f32[7,7,2,8,128]{4,3,2,1,0:T(8,128)S(1)}, u32[]{:S(2)}, u32[]{:S(2)}) %collective-permute-start.18) | collective-permute-done | bytes 401440 | tf_op jit(solution)/shard_map/ppermute | solution.py:444
  81.8 0.1 broadcast_select_fusion.1
  81.9 1.0 %pad_maximum_fusion = f32[7,7,2,16,128]{4,3,2,1,0:T(8,128)} fusion(f32[7,7,2,8,128]{4,3,2,1,0:T(8,128)S(1)} %get-tuple-element.49, f32[7,7,2,8,128]{4,3,2,1,0:T(8,128)S(1)} %get-tuple-element.48), kind=kLoop, calls=%fused_computation | loop fusion | flops 200704 | bytes 1605632 | tf_op jit(solution)/shard_map/concatenate | solution.py:519
  (22 shorter events, 0.4 us)
Async XLA Ops:
  0.6 22.6 %copy-start.2 = (f32[2,128,128]{2,1,0:T(8,128)S(1)}, f32[2,128,128]{2,1,0:T(8,128)}, u32[]{:S(2)}) copy-start(f32[2,128,128]{2,1,0:T(8,128)} %inverse_ref.3) | copy-start | bytes 393220
  1.7 11.4 %collective-permute-start = (f32[2,96,128]{2,1,0:T(8,128)S(1)}, f32[2,96,128]{2,1,0:T(8,128)S(1)}, u32[]{:S(2)}, u32[]{:S(2)}) collective-permute-start(f32[2,96,128]{2,1,0:T(8,128)S(1)} %bitcast.49), channel_id=1, source_target_pairs={{4,8},{8,4},{12,16},{16,12},{20,24},{24,20},{5,9},{9,5},{13,17},{1... | collective-permute-start | bytes 294920 | tf_op jit(solution)/shard_map/ppermute | solution.py:444
  2.3 10.7 %collective-permute-start.1 = (f32[2,96,128]{2,1,0:T(8,128)S(1)}, f32[2,96,128]{2,1,0:T(8,128)S(1)}, u32[]{:S(2)}, u32[]{:S(2)}) collective-permute-start(f32[2,96,128]{2,1,0:T(8,128)S(1)} %bitcast.48), channel_id=1, source_target_pairs={{0,4},{4,0},{8,12},{12,8},{16,20},{20,16},{24,28},{28,24},{1,5},{5... | collective-permute-start | bytes 294920 | tf_op jit(solution)/shard_map/ppermute | solution.py:444
  8.1 0.9 %copy-start = (f32[12,16,2,128]{3,2,1,0:T(2,128)S(1)}, f32[12,16,2,128]{3,2,1,0:T(2,128)}, u32[]{:S(2)}) copy-start(f32[12,16,2,128]{3,2,1,0:T(2,128)} %param.5) | copy-start | bytes 589828
  9.1 14.2 %copy-start.1 = (f32[7,7,2,128,128]{4,3,2,1,0:T(8,128)S(1)}, f32[7,7,2,128,128]{4,3,2,1,0:T(8,128)}, u32[]{:S(2)}) copy-start(f32[7,7,2,128,128]{4,3,2,1,0:T(8,128)} %blocks_ref.1) | copy-start | bytes 19267588
  9.1 6.4 %collective-permute-start.4 = (f32[2,36,128]{2,0,1:T(2,128)S(1)}, f32[2,36,128]{2,0,1:T(2,128)S(1)}, u32[]{:S(2)}, u32[]{:S(2)}) collective-permute-start(f32[2,36,128]{2,0,1:T(2,128)S(1)} %bitcast.51), channel_id=1, source_target_pairs={{1,2},{2,1},{5,6},{6,5},{9,10},{10,9},{13,14},{14,13},{17,18},{18,... | collective-permute-start | bytes 110600 | tf_op jit(solution)/shard_map/ppermute | solution.py:444
  10.0 5.6 %collective-permute-start.5 = (f32[2,36,128]{2,0,1:T(2,128)S(1)}, f32[2,36,128]{2,0,1:T(2,128)S(1)}, u32[]{:S(2)}, u32[]{:S(2)}) collective-permute-start(f32[2,36,128]{2,0,1:T(2,128)S(1)} %bitcast.53), channel_id=1, source_target_pairs={{0,1},{1,0},{2,3},{3,2},{4,5},{5,4},{6,7},{7,6},{8,9},{9,8},{10,11... | collective-permute-start | bytes 110600 | tf_op jit(solution)/shard_map/ppermute | solution.py:444
  13.2 9.0 %collective-permute-start.2 = (f32[2,144,128]{2,0,1:T(2,128)S(1)}, f32[2,144,128]{2,0,1:T(2,128)S(1)}, u32[]{:S(2)}, u32[]{:S(2)}) collective-permute-start(f32[2,144,128]{2,0,1:T(2,128)S(1)} %bitcast.45), channel_id=1, source_target_pairs={{1,2},{2,1},{5,6},{6,5},{9,10},{10,9},{13,14},{14,13},{17,18},{18,... | collective-permute-start | bytes 442376 | tf_op jit(solution)/shard_map/ppermute | solution.py:444
  14.0 9.0 %collective-permute-start.3 = (f32[2,144,128]{2,0,1:T(2,128)S(1)}, f32[2,144,128]{2,0,1:T(2,128)S(1)}, u32[]{:S(2)}, u32[]{:S(2)}) collective-permute-start(f32[2,144,128]{2,0,1:T(2,128)S(1)} %bitcast.44), channel_id=1, source_target_pairs={{0,1},{1,0},{2,3},{3,2},{4,5},{5,4},{6,7},{7,6},{8,9},{9,8},{10,11... | collective-permute-start | bytes 442376 | tf_op jit(solution)/shard_map/ppermute | solution.py:444
  15.9 21.9 %collective-permute-start.7 = (f32[2,264,128]{2,1,0:T(8,128)S(1)}, f32[2,264,128]{2,1,0:T(8,128)S(1)}, u32[]{:S(2)}, u32[]{:S(2)}) collective-permute-start(f32[2,264,128]{2,1,0:T(8,128)S(1)} %copy.17.refs_0_), channel_id=1, source_target_pairs={{0,8},{4,12},{8,16},{12,20},{16,24},{20,28},{24,0},{28,4},{1,9},{5... | collective-permute-start | bytes 811016 | tf_op jit(solution)/shard_map/ppermute | solution.py:451
  18.5 19.4 %collective-permute-start.8 = (f32[2,264,128]{2,1,0:T(8,128)S(1)}, f32[2,264,128]{2,1,0:T(8,128)S(1)}, u32[]{:S(2)}, u32[]{:S(2)}) collective-permute-start(f32[2,264,128]{2,1,0:T(8,128)S(1)} %copy.17.refs_0_), channel_id=1, source_target_pairs={{0,24},{4,28},{8,0},{12,4},{16,8},{20,12},{24,16},{28,20},{1,25},{... | collective-permute-start | bytes 811016 | tf_op jit(solution)/shard_map/ppermute | solution.py:451
  20.6 17.3 %collective-permute-start.6 = (f32[2,264,128]{2,1,0:T(8,128)S(1)}, f32[2,264,128]{2,1,0:T(8,128)S(1)}, u32[]{:S(2)}, u32[]{:S(2)}) collective-permute-start(f32[2,264,128]{2,1,0:T(8,128)S(1)} %copy.17.refs_0_), channel_id=1, source_target_pairs={{0,4},{4,0},{8,12},{12,8},{16,20},{20,16},{24,28},{28,24},{1,5},{5... | collective-permute-start | bytes 811016 | tf_op jit(solution)/shard_map/ppermute | solution.py:444
  22.2 22.5 %collective-permute-start.9 = (f32[2,264,128]{2,1,0:T(8,128)S(1)}, f32[2,264,128]{2,1,0:T(8,128)S(1)}, u32[]{:S(2)}, u32[]{:S(2)}) collective-permute-start(f32[2,264,128]{2,1,0:T(8,128)S(1)} %copy.17.refs_0_), channel_id=1, source_target_pairs={{0,16},{4,20},{8,24},{12,28},{16,0},{20,4},{24,8},{28,12},{1,17},{... | collective-permute-start | bytes 811016 | tf_op jit(solution)/shard_map/ppermute | solution.py:451
  37.9 20.5 %collective-permute-start.14 = (f32[2,2,264,128]{3,2,1,0:T(8,128)S(1)}, f32[2,2,264,128]{3,2,1,0:T(8,128)S(1)}, u32[]{:S(2)}, u32[]{:S(2)}) collective-permute-start(f32[2,2,264,128]{3,2,1,0:T(8,128)S(1)} %pad_maximum_fusion.1), channel_id=1, source_target_pairs={{0,4},{4,0},{8,12},{12,8},{16,20},{20,16},{24,28},{28,24},{1,5},{5... | collective-permute-start | bytes 1622024 | tf_op jit(solution)/shard_map/ppermute | solution.py:444
  44.7 13.6 %collective-permute-start.15 = (f32[1,2,264,128]{3,2,1,0:T(8,128)S(1)}, f32[1,2,264,128]{3,2,1,0:T(8,128)S(1)}, u32[]{:S(2)}, u32[]{:S(2)}) collective-permute-start(f32[1,2,264,128]{3,2,1,0:T(8,128)S(1)} %bitcast.30), channel_id=1, source_target_pairs={{0,4},{4,0},{8,12},{12,8},{16,20},{20,16},{24,28},{28,24},{1,5},{5... | collective-permute-start | bytes 811016 | tf_op jit(solution)/shard_map/ppermute | solution.py:444
  46.3 6.7 %collective-permute-start.10 = (f32[2,32,192]{2,1,0:T(8,128)S(1)}, f32[2,32,192]{2,1,0:T(8,128)S(1)}, u32[]{:S(2)}, u32[]{:S(2)}) collective-permute-start(f32[2,32,192]{2,1,0:T(8,128)S(1)} %get-tuple-element.37), channel_id=1, source_target_pairs={{0,8},{4,12},{8,16},{12,20},{16,24},{20,28},{24,0},{28,4},{1,9},{5... | collective-permute-start | bytes 147464 | tf_op jit(solution)/shard_map/ppermute | solution.py:451
  47.0 7.3 %collective-permute-start.11 = (f32[2,32,192]{2,1,0:T(8,128)S(1)}, f32[2,32,192]{2,1,0:T(8,128)S(1)}, u32[]{:S(2)}, u32[]{:S(2)}) collective-permute-start(f32[2,32,192]{2,1,0:T(8,128)S(1)} %get-tuple-element.38), channel_id=1, source_target_pairs={{0,16},{4,20},{8,24},{12,28},{16,0},{20,4},{24,8},{28,12},{1,17},{... | collective-permute-start | bytes 147464 | tf_op jit(solution)/shard_map/ppermute | solution.py:451
  48.9 5.4 %collective-permute-start.12 = (f32[2,32,192]{2,1,0:T(8,128)S(1)}, f32[2,32,192]{2,1,0:T(8,128)S(1)}, u32[]{:S(2)}, u32[]{:S(2)}) collective-permute-start(f32[2,32,192]{2,1,0:T(8,128)S(1)} %get-tuple-element.39), channel_id=1, source_target_pairs={{0,24},{4,28},{8,0},{12,4},{16,8},{20,12},{24,16},{28,20},{1,25},{... | collective-permute-start | bytes 147464 | tf_op jit(solution)/shard_map/ppermute | solution.py:451
  54.3 6.8 %collective-permute-start.13 = (f32[4,32,192]{2,1,0:T(8,128)S(1)}, f32[4,32,192]{2,1,0:T(8,128)S(1)}, u32[]{:S(2)}, u32[]{:S(2)}) collective-permute-start(f32[4,32,192]{2,1,0:T(8,128)S(1)} %pad_maximum_fusion.4), channel_id=1, source_target_pairs={{0,4},{4,0},{8,12},{12,8},{16,20},{20,16},{24,28},{28,24},{1,5},{5... | collective-permute-start | bytes 294920 | tf_op jit(solution)/shard_map/ppermute | solution.py:444
  66.7 1.8 %collective-permute-start.16 = (f32[7,7,2,8,128]{4,3,2,1,0:T(8,128)S(1)}, f32[7,7,2,8,128]{4,3,2,1,0:T(8,128)S(1)}, u32[]{:S(2)}, u32[]{:S(2)}) collective-permute-start(f32[7,7,2,8,128]{4,3,2,1,0:T(8,128)S(1)} %get-tuple-element.46), channel_id=1, source_target_pairs={{0,1},{1,0},{2,3},{3,2},{4,5},{5,4},{6,7},{7,6},{8,9},{9,8},{10,11... | collective-permute-start | bytes 1204232 | tf_op jit(solution)/shard_map/ppermute | solution.py:444
  68.5 11.4 %collective-permute-start.17 = (f32[7,7,2,8,128]{4,3,2,1,0:T(8,128)S(1)}, f32[7,7,2,8,128]{4,3,2,1,0:T(8,128)S(1)}, u32[]{:S(2)}, u32[]{:S(2)}) collective-permute-start(f32[7,7,2,8,128]{4,3,2,1,0:T(8,128)S(1)} %add.19), channel_id=1, source_target_pairs={{0,2},{1,3},{2,0},{3,1},{4,6},{5,7},{6,4},{7,5},{8,10},{9,11},{10,... | collective-permute-start | bytes 1204232 | tf_op jit(solution)/shard_map/ppermute | solution.py:451
  80.0 1.8 %collective-permute-start.18 = (f32[7,7,2,8,128]{4,3,2,1,0:T(8,128)S(1)}, f32[7,7,2,8,128]{4,3,2,1,0:T(8,128)S(1)}, u32[]{:S(2)}, u32[]{:S(2)}) collective-permute-start(f32[7,7,2,8,128]{4,3,2,1,0:T(8,128)S(1)} %add.20), channel_id=1, source_target_pairs={{0,1},{1,0},{2,3},{3,2},{4,5},{5,4},{6,7},{7,6},{8,9},{9,8},{10,11... | collective-permute-start | bytes 1204232 | tf_op jit(solution)/shard_map/ppermute | solution.py:444

commit v11 on v10

--- a/solution.py
+++ b/solution.py
@@ -271,32 +271,31 @@
     return out[0], out[1:]
 
 
-def spread_kernel(sizes, *refs):
+def tiles_of(k, peers):
+    me = lax.axis_index("row")
+    parity = me % 2
+    base = 2 * chip_along_z(me // 2, -k, peers // 2)
+    return base + parity, base + 1 - parity
+
+
+def spread_kernel(sizes, places, filled, *refs):
     rows, cols, span, peers = sizes
-    half_peers = peers // 2
-    piece_refs = refs[:half_peers]
-    own_twin_ref, early_ref, late_ref, s_high, s_low, stage, sems = refs[half_peers:]
+    count = len(places)
+    sources = refs[:count]
+    s_high, s_low, stage, sems = refs[count + filled :]
     own = rows * cols
     width = stage.shape[-1]
-    me = lax.axis_index("row")
-    parity = me % 2
-
-    def tiles(k):
-        base = 2 * chip_along_z(me // 2, -k, half_peers)
-        return base + parity, base + 1 - parity
-
-    for k in range(half_peers):
-        if k == 0:
-            twin = own_twin_ref
-        else:
-            near = k in (1, half_peers - 1)
-            twin = early_ref.at[0 if k == 1 else 1] if near else late_ref.at[k - 2]
-        for source, tile in zip((piece_refs[k], twin), tiles(k)):
-            pltpu.make_async_copy(source, stage.at[tile], sems.at[tile]).start()
-
-    @pl.loop(0, peers)
-    def _(tile):
-        pltpu.make_async_copy(own_twin_ref, stage.at[tile], sems.at[tile]).wait()
+    copies = []
+    at = 0
+    for source, place in zip(sources, places):
+        for n, (k, twin) in enumerate(place):
+            piece = source.at[n] if len(source.shape) == 4 else source
+            copies.append((pltpu.make_async_copy(piece, stage.at[at], sems.at[at]), tiles_of(k, peers)[twin]))
+            copies[-1][0].start()
+            at += 1
+
+    for at, (copy, tile) in enumerate(copies):
+        copy.wait()
 
         @pl.loop(0, rows)
         def _(i):
@@ -304,32 +303,34 @@
             for b in range(span):
                 for h in range(2):
                     start = i * (cols + span - 1) + span - 1 - b
-                    high, low = split(stage[tile, h, pl.ds(start, cols), :])
+                    high, low = split(stage[at, h, pl.ds(start, cols), :])
                     s_high[b, to, h * width : (h + 1) * width] = high
                     s_low[b, to, h * width : (h + 1) * width] = low
 
 
-def spread(pieces, twins, rows, cols, span):
-    peers = 2 * len(pieces)
-    piece = pieces[0]
+def spread(placed, rows, cols, span, peers, filled=()):
+    sources, places = zip(*placed)
+    piece = sources[0].shape[-3:]
     vmem = pl.BlockSpec(memory_space=pltpu.VMEM)
     hbm = pl.BlockSpec(memory_space=pltpu.HBM)
-    out = jax.ShapeDtypeStruct((span, peers * rows * cols, 2 * piece.shape[-1]), bf16)
+    out = jax.ShapeDtypeStruct((span, peers * rows * cols, 2 * piece[-1]), bf16)
+    count = sum(len(place) for place in places)
     return pl.pallas_call(
-        functools.partial(spread_kernel, (rows, cols, span, peers)),
-        in_specs=[hbm] * (len(pieces) + len(twins)),
+        functools.partial(spread_kernel, (rows, cols, span, peers), places, len(filled)),
+        in_specs=[hbm] * len(sources) + [vmem] * len(filled),
         out_specs=[vmem, vmem],
         out_shape=[out, out],
+        input_output_aliases={len(sources) + n: n for n in range(len(filled))},
         scratch_shapes=[
-            pltpu.VMEM((peers,) + piece.shape, f32),
-            pltpu.SemaphoreType.DMA((peers,)),
+            pltpu.VMEM((count,) + piece, f32),
+            pltpu.SemaphoreType.DMA((count,)),
         ],
         cost_estimate=pl.CostEstimate(
-            flops=0, bytes_accessed=4 * peers * piece.size, transcendentals=0
+            flops=0, bytes_accessed=4 * count * math.prod(piece), transcendentals=0
         ),
-        compiler_params=pltpu.CompilerParams(vmem_limit_bytes=15 * 1024 * 1024),
+        compiler_params=pltpu.CompilerParams(vmem_limit_bytes=30 * 1024 * 1024),
         name="spread",
-    )(*pieces, *twins)
+    )(*sources, *filled)
 
 
 def correlate_kernel(sizes, lags, factor, *refs):
@@ -343,13 +344,11 @@
     double = shares[0].shape[1]
     share = double // 2
     width = s_high.shape[-1] // 2
-    me = lax.axis_index("row")
-    parity = me % 2
 
     for k in range(half_peers):
-        base = 2 * chip_along_z(me // 2, -k, half_peers)
-        placed[base + parity] = shares[k][0]
-        placed[base + 1 - parity] = twin_shares_ref[k]
+        tile, twin = tiles_of(k, peers)
+        placed[tile] = shares[k][0]
+        placed[twin] = twin_shares_ref[k]
 
     total = peers * own
     side = round_up(reach * cols, 128)
@@ -457,15 +456,15 @@
     initial, last = (value.reshape(shape[0], -1, shape[-1]) for value in (initial, last))
     outer = swap(jnp.where(even, initial, last), axis, 1).reshape(shape)
     inner = swap(jnp.where(even, last, initial), axis, 0).reshape(shape)
-    return jnp.where(even, outer, inner), jnp.where(even, inner, outer)
+    return jnp.where(even, outer, inner), jnp.where(even, inner, outer), inner
 
 
 def extended(value, axis, dim, width):
     length = value.shape[dim]
     initial = lax.slice_in_dim(value, 0, width, axis=dim)
     last = lax.slice_in_dim(value, length - width, length, axis=dim)
-    before, after = edges(initial, last, axis)
-    return jnp.concatenate([before, value, after], axis=dim)
+    before, after, inner = edges(initial, last, axis)
+    return jnp.concatenate([before, value, after], axis=dim), inner
 
 
 def on_device(adjoint_source, saved_currents, lag_blocks, element_inverse):
@@ -477,19 +476,21 @@
 
     source = adjoint_source.transpose(2, 0, 1, 3)
     saved = parts_first(saved_currents)
-    source = extended(source, "row", 1, halo)
-    saved = extended(saved, "col", 2, reach)
+    source, _ = extended(source, "row", 1, halo)
+    saved, _ = extended(saved, "col", 2, reach)
     saved = lax.optimization_barrier((saved, source))[0]
-    source = extended(source, "col", 2, halo)
+    source, inner = extended(source, "col", 2, halo)
     wide = round_up(cols + 2 * halo, 8)
     source = jnp.pad(source, ((0, 0), (0, 0), (0, wide - cols - 2 * halo), (0, 0)))
 
     saved = saved.reshape(parts, -1, width)
     pieces = {0: saved}
+    behind = lax.optimization_barrier((saved, inner))[0]
     for k in sorted(range(1, peers // 2), key=lambda k: min(k, peers // 2 - k)):
-        pieces[k] = shifted(saved, "row", 2 * k)
+        near = k in (1, peers // 2 - 1)
+        pieces[k] = shifted(saved if near else behind, "row", 2 * k)
     pieces = [pieces[k] for k in range(peers // 2)]
-    own_twin = swap(saved, "row", 0)
+    own_twin = swap(lax.optimization_barrier((saved, source))[0], "row", 0)
 
     second, own_source, high, low = first_sweep(source, element_inverse, lag_blocks, rows, cols)
     second, own_twin, early = lax.optimization_barrier((second, own_twin, jnp.stack([pieces[1], pieces[-1]])))
@@ -500,7 +501,12 @@
     shares = [shifted(send, "row", 2 * k) for k, send in enumerate(sends)]
     twin_shares = swap(jnp.stack([received[1] for received in shares]), "row", 0)
 
-    s_high, s_low = spread(pieces, (own_twin, early_twins, late_twins), rows, cols, span)
+    last = peers // 2 - 1
+    arrived = [(piece, ((k, 0),)) for k, piece in enumerate(pieces)]
+    arrived += [(own_twin, ((0, 1),)), (early_twins, ((1, 1), (last, 1)))]
+    spreads = spread(arrived, rows, cols, span, peers)
+    late = [(late_twins, tuple((k, 1) for k in range(2, last)))]
+    s_high, s_low = spread(late, rows, cols, span, peers, tuple(spreads))
 
     elements = rows * peers * cols * lax.axis_size("col")
     factor = -1.0 / math.sqrt(elements)
@@ -510,12 +516,13 @@
         mine, other = correlate(shares, twin_shares, s_high, s_low, lags, rows, cols, factor)
         mine = mine + swap(other, "col", 0)
         twin_shares, mine = lax.optimization_barrier((twin_shares, mine))
-        total = mine
-        for k in range(2, lax.axis_size("col"), 2):
-            total = total + shifted(mine, "col", k)
-        totals.append(total)
-    total = jnp.concatenate(totals, axis=1)
-    twin = swap(total, "col", 0)
+        for piece in (mine[: span // 2 + 1], mine[span // 2 + 1 :]):
+            total = piece
+            for k in range(2, lax.axis_size("col"), 2):
+                total = total + shifted(piece, "col", k)
+            totals.append(total)
+    twins = [swap(total, "col", 0) for total in totals]
+    total, twin = jnp.concatenate(totals, axis=0), jnp.concatenate(twins, axis=0)
     lag_grad = jnp.concatenate(
         [jnp.where(even, total, twin), jnp.where(even, twin, total)], axis=3
     )

time: 83 us -> 81 us (0.976)
  starting transfers between devices: 28.8 us -> 26.3 us
    ppermute x12 -> x13, starting transfers between devices: 17.4 us -> 13.8 us  [swap(): return lax.ppermute(value, axis, pairs)]
    ppermute x7 -> x8, waiting for transfers between devices: 13.4 us -> 14.8 us  [shifted(): lax.ppermute(value, axis, [(i, (i + shift) % peers) for i in range(peers)])]
    ppermute x7 -> x8, starting transfers between devices: 11.4 us -> 12.5 us  [shifted(): lax.ppermute(value, axis, [(i, (i + shift) % peers) for i in range(peers)])]
    ppermute x12 -> x13, waiting for transfers between devices: 5.71 us -> 4.83 us  [swap(): return lax.ppermute(value, axis, pairs)]
    pallas_call x1 -> x2, Pallas kernels: 2.73 us -> 2.57 us  [spread(): pl.pallas_call(functools.partial(spread_kernel, (rows, cols, span, peers)...]
    unnamed x7 -> x8, local copies, waits for them, and re-layouts: 1.91 us -> 1.92 us
  transfers between devices with their start and end apart: 19 -> 21, of which waited for: 6 -> 8; matrix products, arithmetic and copies ran while one was open for 2% -> 2% of each run, Pallas kernels for 28% -> 29%
where the time goes in v11:
time: 81 us; the launch traced here: 80.8 us
  Pallas kernels  29 us (36%)
  starting transfers between devices  26.3 us (32%)
  waiting for transfers between devices  19.6 us (24%)
  local copies, waits for them, and re-layouts  3.32 us (4%)
  other arithmetic  1.54 us (2%)
  between operations  1.05 us (1%)
    ppermute x8, waiting for transfers between devices, shifted(): lax.ppermute(value, axis, [(i, (i + shift) % peers) for i in range(peers)])  14.8 us
    pallas_call x1, Pallas kernels, first_sweep(): pl.pallas_call(functools.partial(first_sweep_kernel, (rows, cols, span, p...  14.5 us
    ppermute x13, starting transfers between devices, swap(): return lax.ppermute(value, axis, pairs)  13.8 us
    ppermute x8, starting transfers between devices, shifted(): lax.ppermute(value, axis, [(i, (i + shift) % peers) for i in range(peers)])  12.5 us
    pallas_call x1, Pallas kernels, second_sweep(): pl.pallas_call(functools.partial(second_sweep_kernel, (rows, cols, span,...  6.32 us
    pallas_call x1, Pallas kernels, correlate(): pl.pallas_call(functools.partial(correlate_kernel, (rows, cols, span, pee...  5.56 us
    ppermute x13, waiting for transfers between devices, swap(): return lax.ppermute(value, axis, pairs)  4.83 us
    pallas_call x2, Pallas kernels, spread(): pl.pallas_call(functools.partial(spread_kernel, (rows, cols, span, peers)...  2.57 us
  transfers between devices with their start and end apart: 21, of which 8 were waited for; matrix products, arithmetic and copies ran while one was open for 2% of the time, Pallas kernels for 29%

profile of v11, /device:TPU:0, one launch (start us, length us, event | category | flops | bytes accessed | tf_op | source)
XLA Modules:
  0.0 80.8 jit_solution(17031830527794708974)
XLA Ops:
  0.6 0.0 copy-start.2
  0.7 1.0 %copy.31 = f32[12,16,2,128]{3,1,0,2:T(8,128)S(1)} copy(f32[12,16,2,128]{3,2,1,0:T(2,128)} %param.4) | data formatting | bytes 393216 | tf_op args[0]
  1.7 3.0 %collective-permute-start.1 = (f32[2,96,128]{2,1,0:T(8,128)S(1)}, f32[2,96,128]{2,1,0:T(8,128)S(1)}, u32[]{:S(2)}, u32[]{:S(2)}) collective-permute-start(f32[2,96,128]{2,1,0:T(8,128)S(1)} %bitcast.45), channel_id=1, source_target_pairs={{0,4},{4,0},{8,12},{12,8},{16,20},{20,16},{24,28},{28,24},{1,5},{5... | collective-permute-start | bytes 294920 | tf_op jit(solution)/shard_map/ppermute | solution.py:443
  4.7 0.7 collective-permute-start
  5.4 0.0 copy-start
  5.4 0.9 %copy-done = f32[12,16,2,128]{3,2,1,0:T(2,128)S(1)} copy-done((f32[12,16,2,128]{3,2,1,0:T(2,128)S(1)}, f32[12,16,2,128]{3,2,1,0:T(2,128)}, u32[]{:S(2)}) %copy-start) | copy-done | bytes 196632
  6.3 0.0 copy-start.1
  6.4 0.1 collective-permute-start.5
  6.5 0.8 collective-permute-start.4
  7.3 0.2 collective-permute-done.1
  7.5 0.0 collective-permute-done
  7.6 0.1 copy.10
  7.7 0.1 copy.11
  7.8 2.9 %collective-permute-start.3 = (f32[2,144,128]{2,0,1:T(2,128)S(1)}, f32[2,144,128]{2,0,1:T(2,128)S(1)}, u32[]{:S(2)}, u32[]{:S(2)}) collective-permute-start(f32[2,144,128]{2,0,1:T(2,128)S(1)} %bitcast.41), channel_id=1, source_target_pairs={{0,1},{1,0},{2,3},{3,2},{4,5},{5,4},{6,7},{7,6},{8,9},{9,8},{10,11... | collective-permute-start | bytes 442376 | tf_op jit(solution)/shard_map/ppermute | solution.py:443
  10.7 0.7 collective-permute-start.2
  11.4 0.0 collective-permute-done.5
  11.4 0.0 collective-permute-done.4
  11.5 0.2 copy.20
  11.7 5.5 %collective-permute-start.8 = (f32[2,264,128]{2,1,0:T(8,128)S(1)}, f32[2,264,128]{2,1,0:T(8,128)S(1)}, u32[]{:S(2)}, u32[]{:S(2)}) collective-permute-start(f32[2,264,128]{2,1,0:T(8,128)S(1)} %copy.22.refs_0_), channel_id=1, source_target_pairs={{0,24},{4,28},{8,0},{12,4},{16,8},{20,12},{24,16},{28,20},{1,25},{... | collective-permute-start | bytes 811016 | tf_op jit(solution)/shard_map/ppermute | solution.py:450
  17.2 0.0 collective-permute-start.7
  17.2 0.0 collective-permute-done.3
  17.2 0.0 collective-permute-done.2
  17.3 0.1 select_maximum_fusion.source_ref
  17.5 1.1 %collective-permute-start.9 = (f32[2,264,128]{2,1,0:T(8,128)S(1)}, f32[2,264,128]{2,1,0:T(8,128)S(1)}, u32[]{:S(2)}, u32[]{:S(2)}) collective-permute-start(f32[2,264,128]{2,1,0:T(8,128)S(1)} %copy.24), channel_id=1, source_target_pairs={{0,16},{4,20},{8,24},{12,28},{16,0},{20,4},{24,8},{28,12},{1,17},{... | collective-permute-start | bytes 811016 | tf_op jit(solution)/shard_map/ppermute | solution.py:450
  18.5 2.5 %collective-permute-start.6 = (f32[2,264,128]{2,1,0:T(8,128)S(1)}, f32[2,264,128]{2,1,0:T(8,128)S(1)}, u32[]{:S(2)}, u32[]{:S(2)}) collective-permute-start(f32[2,264,128]{2,1,0:T(8,128)S(1)} %copy.21), channel_id=1, source_target_pairs={{0,4},{4,0},{8,12},{12,8},{16,20},{20,16},{24,28},{28,24},{1,5},{5... | collective-permute-start | bytes 811016 | tf_op jit(solution)/shard_map/ppermute | solution.py:443
  21.0 0.0 copy-done.2
  21.0 0.0 copy-done.1
  21.0 14.5 %first_sweep.1 = (f32[18,24,256]{2,1,0:T(8,128)S(1)}, f32[12,16,256]{2,1,0:T(8,128)S(1)}, bf16[7,7,256,256]{3,2,1,0:T(8,128)(2,1)S(1)}, bf16[7,7,256,256]{3,2,1,0:T(8,128)(2,1)S(1)}) custom-call(f32[2,24,32,128]{3,2,1,0:T(8,128)S(1)} %select_maximum_fusion.source_ref, f32[2,128,128]{2,1,0:T(8,128)S(1)} %copy-done.2, f32[7,7,2,128,128]{4,3,2,1,0:T(8,128)S(1)} %copy-done.1), custom_call_target="tpu_custom_call" | custom-call | flops 8323596288 | bytes 19267584 | tf_op jit(solution)/shard_map/first_sweep/pallas_call | solution.py:162
  35.5 0.0 collective-permute-done.8.refs_3_
  35.6 0.0 collective-permute-done.7.refs_1_
  35.6 0.0 collective-permute-done.6.refs_4_
  35.6 0.1 collective-permute-start.15
  35.7 6.3 %second_sweep.1 = (f32[12,16,256]{2,1,0:T(8,128)S(1)}, f32[2,32,192]{2,1,0:T(8,128)S(1)}, f32[2,32,192]{2,1,0:T(8,128)S(1)}, f32[2,32,192]{2,1,0:T(8,128)S(1)}, f32[2,32,192]{2,1,0:T(8,128)S(1)}) custom-call(f32[18,24,256]{2,1,0:T(8,128)S(1)} %get-tuple-element.32.second_ref, f32[12,16,256]{2,1,0:T(8,128)S(1)} %get-tuple-element.33.source_ref, ...), custom_call_target="tpu_custom_call" | custom-call | flops 3699376128 | bytes 12845056 | tf_op jit(solution)/shard_map/second_sweep/pallas_call | solution.py:250
  42.0 0.0 collective-permute-done.9.refs_2_
  42.0 2.1 %collective-permute-start.14 = (f32[1,2,264,128]{3,2,1,0:T(8,128)S(1)}, f32[1,2,264,128]{3,2,1,0:T(8,128)S(1)}, u32[]{:S(2)}, u32[]{:S(2)}) collective-permute-start(f32[1,2,264,128]{3,2,1,0:T(8,128)S(1)} %bitcast.26), channel_id=1, source_target_pairs={{0,4},{4,0},{8,12},{12,8},{16,20},{20,16},{24,28},{28,24},{1,5},{5... | collective-permute-start | bytes 811016 | tf_op jit(solution)/shard_map/ppermute | solution.py:443
  44.1 1.0 %collective-permute-start.10 = (f32[2,32,192]{2,1,0:T(8,128)S(1)}, f32[2,32,192]{2,1,0:T(8,128)S(1)}, u32[]{:S(2)}, u32[]{:S(2)}) collective-permute-start(f32[2,32,192]{2,1,0:T(8,128)S(1)} %get-tuple-element.43), channel_id=1, source_target_pairs={{0,8},{4,12},{8,16},{12,20},{16,24},{20,28},{24,0},{28,4},{1,9},{5... | collective-permute-start | bytes 147464 | tf_op jit(solution)/shard_map/ppermute | solution.py:450
  45.1 0.9 %collective-permute-start.11 = (f32[2,32,192]{2,1,0:T(8,128)S(1)}, f32[2,32,192]{2,1,0:T(8,128)S(1)}, u32[]{:S(2)}, u32[]{:S(2)}) collective-permute-start(f32[2,32,192]{2,1,0:T(8,128)S(1)} %get-tuple-element.44), channel_id=1, source_target_pairs={{0,16},{4,20},{8,24},{12,28},{16,0},{20,4},{24,8},{28,12},{1,17},{... | collective-permute-start | bytes 147464 | tf_op jit(solution)/shard_map/ppermute | solution.py:450
  46.0 1.9 %collective-permute-start.12 = (f32[2,32,192]{2,1,0:T(8,128)S(1)}, f32[2,32,192]{2,1,0:T(8,128)S(1)}, u32[]{:S(2)}, u32[]{:S(2)}) collective-permute-start(f32[2,32,192]{2,1,0:T(8,128)S(1)} %get-tuple-element.45), channel_id=1, source_target_pairs={{0,24},{4,28},{8,0},{12,4},{16,8},{20,12},{24,16},{28,20},{1,25},{... | collective-permute-start | bytes 147464 | tf_op jit(solution)/shard_map/ppermute | solution.py:450
  47.9 2.3 %collective-permute-done.10.refs_1_ = f32[2,32,192]{2,1,0:T(8,128)S(1)} collective-permute-done((f32[2,32,192]{2,1,0:T(8,128)S(1)}, f32[2,32,192]{2,1,0:T(8,128)S(1)}, u32[]{:S(2)}, u32[]{:S(2)}) %collective-permute-start.10) | collective-permute-done | bytes 49184 | tf_op jit(solution)/shard_map/ppermute | solution.py:450
  50.2 3.4 %collective-permute-done.11.refs_2_ = f32[2,32,192]{2,1,0:T(8,128)S(1)} collective-permute-done((f32[2,32,192]{2,1,0:T(8,128)S(1)}, f32[2,32,192]{2,1,0:T(8,128)S(1)}, u32[]{:S(2)}, u32[]{:S(2)}) %collective-permute-start.11) | collective-permute-done | bytes 49184 | tf_op jit(solution)/shard_map/ppermute | solution.py:450
  53.6 0.0 collective-permute-done.12.refs_3_
  53.7 0.9 %collective-permute-start.13 = (f32[4,32,192]{2,1,0:T(8,128)S(1)}, f32[4,32,192]{2,1,0:T(8,128)S(1)}, u32[]{:S(2)}, u32[]{:S(2)}) collective-permute-start(f32[4,32,192]{2,1,0:T(8,128)S(1)} %pad_maximum_fusion.5), channel_id=1, source_target_pairs={{0,4},{4,0},{8,12},{12,8},{16,20},{20,16},{24,28},{28,24},{1,5},{5... | collective-permute-start | bytes 294920 | tf_op jit(solution)/shard_map/ppermute | solution.py:443
  54.5 0.0 collective-permute-done.15.refs_5_
  54.6 2.2 %spread.2 = (bf16[7,1536,256]{2,1,0:T(8,128)(2,1)S(1)}, bf16[7,1536,256]{2,1,0:T(8,128)(2,1)S(1)}) custom-call(f32[2,264,128]{2,1,0:T(8,128)S(1)} %copy.22.refs_0_, f32[2,264,128]{2,1,0:T(8,128)S(1)} %collective-permute-done.7.refs_1_, f32[2,264,128]{2,1,0:T(8,128)S(1)} %collective-permute-done.9.refs_2_, f32[2,264,128]{2,1,0:T(8,128)S(1)} %collective-permute-done.8.refs_3_, ...), custom_call_target="tpu_custom_call" | custom-call | bytes 1892352 | tf_op jit(solution)/shard_map/spread/pallas_call | solution.py:318
  56.8 0.0 collective-permute-done.14.refs_0_
  56.8 0.3 spread.3
  57.1 2.3 %collective-permute-done.13.refs_4_ = f32[4,32,192]{2,1,0:T(8,128)S(1)} collective-permute-done((f32[4,32,192]{2,1,0:T(8,128)S(1)}, f32[4,32,192]{2,1,0:T(8,128)S(1)}, u32[]{:S(2)}, u32[]{:S(2)}) %collective-permute-start.13) | collective-permute-done | bytes 98336 | tf_op jit(solution)/shard_map/ppermute | solution.py:443
  59.4 5.6 %correlate.1 = (f32[7,7,2,8,128]{4,3,2,1,0:T(8,128)S(1)}, f32[7,7,2,8,128]{4,3,2,1,0:T(8,128)S(1)}) custom-call(f32[2,32,192]{2,1,0:T(8,128)S(1)} %get-tuple-element.42.refs_0_, f32[2,32,192]{2,1,0:T(8,128)S(1)} %collective-permute-done.10.refs_1_, f32[2,32,192]{2,1,0:T(8,128)S(1)} %collective-permute-done.11.refs_2_, ...), custom_call_target="tpu_custom_call" | custom-call | flops 3699376128 | bytes 802816 | tf_op jit(solution)/shard_map/correlate/pallas_call | solution.py:397
  65.0 0.1 collective-permute-start.16
  65.1 1.7 %collective-permute-done.16 = f32[7,7,2,8,128]{4,3,2,1,0:T(8,128)S(1)} collective-permute-done((f32[7,7,2,8,128]{4,3,2,1,0:T(8,128)S(1)}, f32[7,7,2,8,128]{4,3,2,1,0:T(8,128)S(1)}, u32[]{:S(2)}, u32[]{:S(2)}) %collective-permute-start.16) | collective-permute-done | bytes 401440 | tf_op jit(solution)/shard_map/ppermute | solution.py:443
  66.8 0.1 add.22
  66.9 0.7 collective-permute-start.17
  67.6 1.5 %collective-permute-start.18 = (f32[3,7,2,8,128]{4,3,2,1,0:T(8,128)S(1)}, f32[3,7,2,8,128]{4,3,2,1,0:T(8,128)S(1)}, u32[]{:S(2)}, u32[]{:S(2)}) collective-permute-start(f32[3,7,2,8,128]{4,3,2,1,0:T(8,128)S(1)} %slice.47), channel_id=1, source_target_pairs={{0,2},{1,3},{2,0},{3,1},{4,6},{5,7},{6,4},{7,5},{8,10},{9,11},{10,... | collective-permute-start | bytes 516104 | tf_op jit(solution)/shard_map/ppermute | solution.py:450
  69.1 6.3 %collective-permute-done.17 = f32[4,7,2,8,128]{4,3,2,1,0:T(8,128)S(1)} collective-permute-done((f32[4,7,2,8,128]{4,3,2,1,0:T(8,128)S(1)}, f32[4,7,2,8,128]{4,3,2,1,0:T(8,128)S(1)}, u32[]{:S(2)}, u32[]{:S(2)}) %collective-permute-start.17) | collective-permute-done | bytes 229408 | tf_op jit(solution)/shard_map/ppermute | solution.py:450
  75.4 0.1 collective-permute-start.19
  75.5 2.8 %collective-permute-done.18 = f32[3,7,2,8,128]{4,3,2,1,0:T(8,128)S(1)} collective-permute-done((f32[3,7,2,8,128]{4,3,2,1,0:T(8,128)S(1)}, f32[3,7,2,8,128]{4,3,2,1,0:T(8,128)S(1)}, u32[]{:S(2)}, u32[]{:S(2)}) %collective-permute-start.18) | collective-permute-done | bytes 172064 | tf_op jit(solution)/shard_map/ppermute | solution.py:450
  78.3 0.1 collective-permute-start.20
  78.4 0.8 reshape.53
  79.2 0.0 collective-permute-done.19
  79.2 0.6 collective-permute-done.20
  79.8 0.1 fusion.6
  79.9 1.0 %pad_maximum_fusion = f32[7,7,2,16,128]{4,3,2,1,0:T(8,128)} fusion(f32[7,7,2,8,128]{4,3,2,1,0:T(8,128)S(1)} %get-tuple-element.57, f32[7,7,2,8,128]{4,3,2,1,0:T(8,128)S(1)} %get-tuple-element.56), kind=kLoop, calls=%fused_computation | loop fusion | flops 200704 | bytes 1605632 | tf_op jit(solution)/shard_map/concatenate | solution.py:526
  (28 shorter events, 0.5 us)
Async XLA Ops:
  0.6 20.4 %copy-start.2 = (f32[2,128,128]{2,1,0:T(8,128)S(1)}, f32[2,128,128]{2,1,0:T(8,128)}, u32[]{:S(2)}) copy-start(f32[2,128,128]{2,1,0:T(8,128)} %inverse_ref.3) | copy-start | bytes 393220
  1.7 5.8 %collective-permute-start.1 = (f32[2,96,128]{2,1,0:T(8,128)S(1)}, f32[2,96,128]{2,1,0:T(8,128)S(1)}, u32[]{:S(2)}, u32[]{:S(2)}) collective-permute-start(f32[2,96,128]{2,1,0:T(8,128)S(1)} %bitcast.45), channel_id=1, source_target_pairs={{0,4},{4,0},{8,12},{12,8},{16,20},{20,16},{24,28},{28,24},{1,5},{5... | collective-permute-start | bytes 294920 | tf_op jit(solution)/shard_map/ppermute | solution.py:443
  4.7 2.8 %collective-permute-start = (f32[2,96,128]{2,1,0:T(8,128)S(1)}, f32[2,96,128]{2,1,0:T(8,128)S(1)}, u32[]{:S(2)}, u32[]{:S(2)}) collective-permute-start(f32[2,96,128]{2,1,0:T(8,128)S(1)} %bitcast.44), channel_id=1, source_target_pairs={{4,8},{8,4},{12,16},{16,12},{20,24},{24,20},{5,9},{9,5},{13,17},{1... | collective-permute-start | bytes 294920 | tf_op jit(solution)/shard_map/ppermute | solution.py:443
  5.4 0.9 %copy-start = (f32[12,16,2,128]{3,2,1,0:T(2,128)S(1)}, f32[12,16,2,128]{3,2,1,0:T(2,128)}, u32[]{:S(2)}) copy-start(f32[12,16,2,128]{3,2,1,0:T(2,128)} %param.5) | copy-start | bytes 589828
  6.3 14.7 %copy-start.1 = (f32[7,7,2,128,128]{4,3,2,1,0:T(8,128)S(1)}, f32[7,7,2,128,128]{4,3,2,1,0:T(8,128)}, u32[]{:S(2)}) copy-start(f32[7,7,2,128,128]{4,3,2,1,0:T(8,128)} %blocks_ref.1) | copy-start | bytes 19267588
  6.4 5.0 %collective-permute-start.5 = (f32[2,36,128]{2,0,1:T(2,128)S(1)}, f32[2,36,128]{2,0,1:T(2,128)S(1)}, u32[]{:S(2)}, u32[]{:S(2)}) collective-permute-start(f32[2,36,128]{2,0,1:T(2,128)S(1)} %bitcast.47), channel_id=1, source_target_pairs={{0,1},{1,0},{2,3},{3,2},{4,5},{5,4},{6,7},{7,6},{8,9},{9,8},{10,11... | collective-permute-start | bytes 110600 | tf_op jit(solution)/shard_map/ppermute | solution.py:443
  6.5 4.9 %collective-permute-start.4 = (f32[2,36,128]{2,0,1:T(2,128)S(1)}, f32[2,36,128]{2,0,1:T(2,128)S(1)}, u32[]{:S(2)}, u32[]{:S(2)}) collective-permute-start(f32[2,36,128]{2,0,1:T(2,128)S(1)} %bitcast.49), channel_id=1, source_target_pairs={{1,2},{2,1},{5,6},{6,5},{9,10},{10,9},{13,14},{14,13},{17,18},{18,... | collective-permute-start | bytes 110600 | tf_op jit(solution)/shard_map/ppermute | solution.py:443
  7.8 9.4 %collective-permute-start.3 = (f32[2,144,128]{2,0,1:T(2,128)S(1)}, f32[2,144,128]{2,0,1:T(2,128)S(1)}, u32[]{:S(2)}, u32[]{:S(2)}) collective-permute-start(f32[2,144,128]{2,0,1:T(2,128)S(1)} %bitcast.41), channel_id=1, source_target_pairs={{0,1},{1,0},{2,3},{3,2},{4,5},{5,4},{6,7},{7,6},{8,9},{9,8},{10,11... | collective-permute-start | bytes 442376 | tf_op jit(solution)/shard_map/ppermute | solution.py:443
  10.7 6.5 %collective-permute-start.2 = (f32[2,144,128]{2,0,1:T(2,128)S(1)}, f32[2,144,128]{2,0,1:T(2,128)S(1)}, u32[]{:S(2)}, u32[]{:S(2)}) collective-permute-start(f32[2,144,128]{2,0,1:T(2,128)S(1)} %bitcast.38), channel_id=1, source_target_pairs={{1,2},{2,1},{5,6},{6,5},{9,10},{10,9},{13,14},{14,13},{17,18},{18,... | collective-permute-start | bytes 442376 | tf_op jit(solution)/shard_map/ppermute | solution.py:443
  11.7 23.8 %collective-permute-start.8 = (f32[2,264,128]{2,1,0:T(8,128)S(1)}, f32[2,264,128]{2,1,0:T(8,128)S(1)}, u32[]{:S(2)}, u32[]{:S(2)}) collective-permute-start(f32[2,264,128]{2,1,0:T(8,128)S(1)} %copy.22.refs_0_), channel_id=1, source_target_pairs={{0,24},{4,28},{8,0},{12,4},{16,8},{20,12},{24,16},{28,20},{1,25},{... | collective-permute-start | bytes 811016 | tf_op jit(solution)/shard_map/ppermute | solution.py:450
  17.2 18.3 %collective-permute-start.7 = (f32[2,264,128]{2,1,0:T(8,128)S(1)}, f32[2,264,128]{2,1,0:T(8,128)S(1)}, u32[]{:S(2)}, u32[]{:S(2)}) collective-permute-start(f32[2,264,128]{2,1,0:T(8,128)S(1)} %copy.22.refs_0_), channel_id=1, source_target_pairs={{0,8},{4,12},{8,16},{12,20},{16,24},{20,28},{24,0},{28,4},{1,9},{5... | collective-permute-start | bytes 811016 | tf_op jit(solution)/shard_map/ppermute | solution.py:450
  17.5 24.5 %collective-permute-start.9 = (f32[2,264,128]{2,1,0:T(8,128)S(1)}, f32[2,264,128]{2,1,0:T(8,128)S(1)}, u32[]{:S(2)}, u32[]{:S(2)}) collective-permute-start(f32[2,264,128]{2,1,0:T(8,128)S(1)} %copy.24), channel_id=1, source_target_pairs={{0,16},{4,20},{8,24},{12,28},{16,0},{20,4},{24,8},{28,12},{1,17},{... | collective-permute-start | bytes 811016 | tf_op jit(solution)/shard_map/ppermute | solution.py:450
  18.5 17.1 %collective-permute-start.6 = (f32[2,264,128]{2,1,0:T(8,128)S(1)}, f32[2,264,128]{2,1,0:T(8,128)S(1)}, u32[]{:S(2)}, u32[]{:S(2)}) collective-permute-start(f32[2,264,128]{2,1,0:T(8,128)S(1)} %copy.21), channel_id=1, source_target_pairs={{0,4},{4,0},{8,12},{12,8},{16,20},{20,16},{24,28},{28,24},{1,5},{5... | collective-permute-start | bytes 811016 | tf_op jit(solution)/shard_map/ppermute | solution.py:443
  35.6 18.9 %collective-permute-start.15 = (f32[2,2,264,128]{3,2,1,0:T(8,128)S(1)}, f32[2,2,264,128]{3,2,1,0:T(8,128)S(1)}, u32[]{:S(2)}, u32[]{:S(2)}) collective-permute-start(f32[2,2,264,128]{3,2,1,0:T(8,128)S(1)} %pad_maximum_fusion.1), channel_id=1, source_target_pairs={{0,4},{4,0},{8,12},{12,8},{16,20},{20,16},{24,28},{28,24},{1,5},{5... | collective-permute-start | bytes 1622024 | tf_op jit(solution)/shard_map/ppermute | solution.py:443
  42.0 14.8 %collective-permute-start.14 = (f32[1,2,264,128]{3,2,1,0:T(8,128)S(1)}, f32[1,2,264,128]{3,2,1,0:T(8,128)S(1)}, u32[]{:S(2)}, u32[]{:S(2)}) collective-permute-start(f32[1,2,264,128]{3,2,1,0:T(8,128)S(1)} %bitcast.26), channel_id=1, source_target_pairs={{0,4},{4,0},{8,12},{12,8},{16,20},{20,16},{24,28},{28,24},{1,5},{5... | collective-permute-start | bytes 811016 | tf_op jit(solution)/shard_map/ppermute | solution.py:443
  44.1 6.1 %collective-permute-start.10 = (f32[2,32,192]{2,1,0:T(8,128)S(1)}, f32[2,32,192]{2,1,0:T(8,128)S(1)}, u32[]{:S(2)}, u32[]{:S(2)}) collective-permute-start(f32[2,32,192]{2,1,0:T(8,128)S(1)} %get-tuple-element.43), channel_id=1, source_target_pairs={{0,8},{4,12},{8,16},{12,20},{16,24},{20,28},{24,0},{28,4},{1,9},{5... | collective-permute-start | bytes 147464 | tf_op jit(solution)/shard_map/ppermute | solution.py:450
  45.1 8.5 %collective-permute-start.11 = (f32[2,32,192]{2,1,0:T(8,128)S(1)}, f32[2,32,192]{2,1,0:T(8,128)S(1)}, u32[]{:S(2)}, u32[]{:S(2)}) collective-permute-start(f32[2,32,192]{2,1,0:T(8,128)S(1)} %get-tuple-element.44), channel_id=1, source_target_pairs={{0,16},{4,20},{8,24},{12,28},{16,0},{20,4},{24,8},{28,12},{1,17},{... | collective-permute-start | bytes 147464 | tf_op jit(solution)/shard_map/ppermute | solution.py:450
  46.0 7.6 %collective-permute-start.12 = (f32[2,32,192]{2,1,0:T(8,128)S(1)}, f32[2,32,192]{2,1,0:T(8,128)S(1)}, u32[]{:S(2)}, u32[]{:S(2)}) collective-permute-start(f32[2,32,192]{2,1,0:T(8,128)S(1)} %get-tuple-element.45), channel_id=1, source_target_pairs={{0,24},{4,28},{8,0},{12,4},{16,8},{20,12},{24,16},{28,20},{1,25},{... | collective-permute-start | bytes 147464 | tf_op jit(solution)/shard_map/ppermute | solution.py:450
  53.7 5.8 %collective-permute-start.13 = (f32[4,32,192]{2,1,0:T(8,128)S(1)}, f32[4,32,192]{2,1,0:T(8,128)S(1)}, u32[]{:S(2)}, u32[]{:S(2)}) collective-permute-start(f32[4,32,192]{2,1,0:T(8,128)S(1)} %pad_maximum_fusion.5), channel_id=1, source_target_pairs={{0,4},{4,0},{8,12},{12,8},{16,20},{20,16},{24,28},{28,24},{1,5},{5... | collective-permute-start | bytes 294920 | tf_op jit(solution)/shard_map/ppermute | solution.py:443
  65.0 1.8 %collective-permute-start.16 = (f32[7,7,2,8,128]{4,3,2,1,0:T(8,128)S(1)}, f32[7,7,2,8,128]{4,3,2,1,0:T(8,128)S(1)}, u32[]{:S(2)}, u32[]{:S(2)}) collective-permute-start(f32[7,7,2,8,128]{4,3,2,1,0:T(8,128)S(1)} %get-tuple-element.54), channel_id=1, source_target_pairs={{0,1},{1,0},{2,3},{3,2},{4,5},{5,4},{6,7},{7,6},{8,9},{9,8},{10,11... | collective-permute-start | bytes 1204232 | tf_op jit(solution)/shard_map/ppermute | solution.py:443
  66.9 8.5 %collective-permute-start.17 = (f32[4,7,2,8,128]{4,3,2,1,0:T(8,128)S(1)}, f32[4,7,2,8,128]{4,3,2,1,0:T(8,128)S(1)}, u32[]{:S(2)}, u32[]{:S(2)}) collective-permute-start(f32[4,7,2,8,128]{4,3,2,1,0:T(8,128)S(1)} %slice.46), channel_id=1, source_target_pairs={{0,2},{1,3},{2,0},{3,1},{4,6},{5,7},{6,4},{7,5},{8,10},{9,11},{10,... | collective-permute-start | bytes 688136 | tf_op jit(solution)/shard_map/ppermute | solution.py:450
  67.6 10.7 %collective-permute-start.18 = (f32[3,7,2,8,128]{4,3,2,1,0:T(8,128)S(1)}, f32[3,7,2,8,128]{4,3,2,1,0:T(8,128)S(1)}, u32[]{:S(2)}, u32[]{:S(2)}) collective-permute-start(f32[3,7,2,8,128]{4,3,2,1,0:T(8,128)S(1)} %slice.47), channel_id=1, source_target_pairs={{0,2},{1,3},{2,0},{3,1},{4,6},{5,7},{6,4},{7,5},{8,10},{9,11},{10,... | collective-permute-start | bytes 516104 | tf_op jit(solution)/shard_map/ppermute | solution.py:450
  75.4 3.7 %collective-permute-start.19 = (f32[4,7,2,8,128]{4,3,2,1,0:T(8,128)S(1)}, f32[4,7,2,8,128]{4,3,2,1,0:T(8,128)S(1)}, u32[]{:S(2)}, u32[]{:S(2)}) collective-permute-start(f32[4,7,2,8,128]{4,3,2,1,0:T(8,128)S(1)} %slice_add_fusion.1), channel_id=1, source_target_pairs={{0,1},{1,0},{2,3},{3,2},{4,5},{5,4},{6,7},{7,6},{8,9},{9,8},{10,11... | collective-permute-start | bytes 688136 | tf_op jit(solution)/shard_map/ppermute | solution.py:443
  78.3 1.5 %collective-permute-start.20 = (f32[3,7,2,8,128]{4,3,2,1,0:T(8,128)S(1)}, f32[3,7,2,8,128]{4,3,2,1,0:T(8,128)S(1)}, u32[]{:S(2)}, u32[]{:S(2)}) collective-permute-start(f32[3,7,2,8,128]{4,3,2,1,0:T(8,128)S(1)} %slice_add_fusion), channel_id=1, source_target_pairs={{0,1},{1,0},{2,3},{3,2},{4,5},{5,4},{6,7},{7,6},{8,9},{9,8},{10,11... | collective-permute-start | bytes 516104 | tf_op jit(solution)/shard_map/ppermute | solution.py:443

commit v12 on v11

--- a/solution.py
+++ b/solution.py
@@ -26,6 +26,10 @@
 def dot3(left, right):
     (left_high, left_low), (right_high, right_low) = left, right
     return dot(left_high, right_high) + dot(left_low, right_high) + dot(left_high, right_low)
+
+
+def largest_divisor(count, most):
+    return max(n for n in range(1, most + 1) if count % n == 0)
 
 
 def round_up(count, unit):
@@ -102,7 +106,7 @@
 
     own_source_ref[...] = source_at(pl.ds(2 * reach, rows), pl.ds(2 * reach, cols))
 
-    step_rows = 4
+    step_rows = largest_divisor(full_rows, 12)
 
     @pl.loop(0, full_rows // step_rows)
     def _(s):
@@ -135,7 +139,7 @@
         at = pl.ds(pl.multiple_of((a // 2) * 2 * pitch, 2 * pitch), mid_rows * pitch)
         acc[...] += products(x_high[a % 2, at, :], x_low[a % 2, at, :], w_high[a], w_low[a])
 
-    step_rows = 3
+    step_rows = largest_divisor(mid_rows, 18)
 
     @pl.loop(0, mid_rows // step_rows)
     def _(s):
@@ -208,11 +212,15 @@
 
     store_inverse(inverse_ref, e_high, e_low)
 
-    @pl.loop(0, mid_rows)
-    def _(i):
+    step_rows = largest_divisor(mid_rows, 3)
+
+    @pl.loop(0, mid_rows // step_rows)
+    def _(s):
         for b in range(span):
-            high, low = split(second_ref[i, pl.ds(b, cols), :])
-            to = pl.ds(pl.multiple_of(i * cols, cols), cols)
+            at = pl.ds(s * step_rows, step_rows)
+            value = second_ref[at, pl.ds(b, cols), :].reshape(step_rows * cols, lanes)
+            high, low = split(value)
+            to = pl.ds(pl.multiple_of(s * step_rows * cols, cols), step_rows * cols)
             x_high[to, b * lanes : (b + 1) * lanes] = high
             x_low[to, b * lanes : (b + 1) * lanes] = low
 
@@ -490,7 +498,7 @@
         near = k in (1, peers // 2 - 1)
         pieces[k] = shifted(saved if near else behind, "row", 2 * k)
     pieces = [pieces[k] for k in range(peers // 2)]
-    own_twin = swap(lax.optimization_barrier((saved, source))[0], "row", 0)
+    own_twin = swap(saved, "row", 0)
 
     second, own_source, high, low = first_sweep(source, element_inverse, lag_blocks, rows, cols)
     second, own_twin, early = lax.optimization_barrier((second, own_twin, jnp.stack([pieces[1], pieces[-1]])))

time: 81 us -> 79.5 us (0.981)
  Pallas kernels: 29 us -> 27 us
  starting transfers between devices: 26.3 us -> 27.6 us
    ppermute x8, starting transfers between devices: 12.5 us -> 14.1 us  [shifted(): lax.ppermute(value, axis, [(i, (i + shift) % peers) for i in range(peers)])]
    pallas_call x1, Pallas kernels: 14.5 us -> 13 us  [first_sweep(): pl.pallas_call(functools.partial(first_sweep_kernel, (rows, cols, span, p...]
    ppermute x8, waiting for transfers between devices: 14.8 us -> 13.8 us  [shifted(): lax.ppermute(value, axis, [(i, (i + shift) % peers) for i in range(peers)])]
  transfers between devices with their start and end apart: 21 -> 21, of which waited for: 8 -> 9; matrix products, arithmetic and copies ran while one was open for 2% -> 2% of each run, Pallas kernels for 29% -> 27%
where the time goes in v12:
time: 79.5 us; the launch traced here: 79.3 us
  starting transfers between devices  27.6 us (35%)
  Pallas kernels  27 us (34%)
  waiting for transfers between devices  18.9 us (24%)
  local copies, waits for them, and re-layouts  3.3 us (4%)
  other arithmetic  1.54 us (2%)
  between operations  1.04 us (1%)
    ppermute x8, starting transfers between devices, shifted(): lax.ppermute(value, axis, [(i, (i + shift) % peers) for i in range(peers)])  14.1 us
    ppermute x8, waiting for transfers between devices, shifted(): lax.ppermute(value, axis, [(i, (i + shift) % peers) for i in range(peers)])  13.8 us
    ppermute x13, starting transfers between devices, swap(): return lax.ppermute(value, axis, pairs)  13.4 us
    pallas_call x1, Pallas kernels, first_sweep(): pl.pallas_call(functools.partial(first_sweep_kernel, (rows, cols, span, p...  13 us
    pallas_call x1, Pallas kernels, second_sweep(): pl.pallas_call(functools.partial(second_sweep_kernel, (rows, cols, span,...  5.86 us
    pallas_call x1, Pallas kernels, correlate(): pl.pallas_call(functools.partial(correlate_kernel, (rows, cols, span, pee...  5.56 us
    ppermute x13, waiting for transfers between devices, swap(): return lax.ppermute(value, axis, pairs)  5.08 us
    pallas_call x2, Pallas kernels, spread(): pl.pallas_call(functools.partial(spread_kernel, (rows, cols, span, peers)...  2.57 us
  transfers between devices with their start and end apart: 21, of which 9 were waited for; matrix products, arithmetic and copies ran while one was open for 2% of the time, Pallas kernels for 27%

profile of v12, /device:TPU:0, one launch (start us, length us, event | category | flops | bytes accessed | tf_op | source)
XLA Modules:
  0.0 79.3 jit_solution(11698904859521614301)
XLA Ops:
  0.6 0.0 copy-start.2
  0.7 1.0 %copy.31 = f32[12,16,2,128]{3,1,0,2:T(8,128)S(1)} copy(f32[12,16,2,128]{3,2,1,0:T(2,128)} %param.4) | data formatting | bytes 393216 | tf_op args[0]
  1.7 3.0 %collective-permute-start.1 = (f32[2,96,128]{2,1,0:T(8,128)S(1)}, f32[2,96,128]{2,1,0:T(8,128)S(1)}, u32[]{:S(2)}, u32[]{:S(2)}) collective-permute-start(f32[2,96,128]{2,1,0:T(8,128)S(1)} %bitcast.44), channel_id=1, source_target_pairs={{0,4},{4,0},{8,12},{12,8},{16,20},{20,16},{24,28},{28,24},{1,5},{5... | collective-permute-start | bytes 294920 | tf_op jit(solution)/shard_map/ppermute | solution.py:451
  4.7 0.7 collective-permute-start
  5.4 0.0 copy-start
  5.4 0.9 %copy-done = f32[12,16,2,128]{3,2,1,0:T(2,128)S(1)} copy-done((f32[12,16,2,128]{3,2,1,0:T(2,128)S(1)}, f32[12,16,2,128]{3,2,1,0:T(2,128)}, u32[]{:S(2)}) %copy-start) | copy-done | bytes 196632
  6.3 0.0 copy-start.1
  6.4 0.1 collective-permute-start.5
  6.5 0.8 %collective-permute-start.4 = (f32[2,36,128]{2,0,1:T(2,128)S(1)}, f32[2,36,128]{2,0,1:T(2,128)S(1)}, u32[]{:S(2)}, u32[]{:S(2)}) collective-permute-start(f32[2,36,128]{2,0,1:T(2,128)S(1)} %bitcast.48), channel_id=1, source_target_pairs={{1,2},{2,1},{5,6},{6,5},{9,10},{10,9},{13,14},{14,13},{17,18},{18,... | collective-permute-start | bytes 110600 | tf_op jit(solution)/shard_map/ppermute | solution.py:451
  7.3 0.2 collective-permute-done.1
  7.5 0.0 collective-permute-done
  7.6 0.1 copy.10
  7.7 0.1 copy.11
  7.8 2.9 %collective-permute-start.3 = (f32[2,144,128]{2,0,1:T(2,128)S(1)}, f32[2,144,128]{2,0,1:T(2,128)S(1)}, u32[]{:S(2)}, u32[]{:S(2)}) collective-permute-start(f32[2,144,128]{2,0,1:T(2,128)S(1)} %bitcast.40), channel_id=1, source_target_pairs={{0,1},{1,0},{2,3},{3,2},{4,5},{5,4},{6,7},{7,6},{8,9},{9,8},{10,11... | collective-permute-start | bytes 442376 | tf_op jit(solution)/shard_map/ppermute | solution.py:451
  10.7 0.7 collective-permute-start.2
  11.4 0.0 collective-permute-done.5
  11.4 0.0 collective-permute-done.4
  11.5 0.2 copy.20
  11.7 5.5 %collective-permute-start.8 = (f32[2,264,128]{2,1,0:T(8,128)S(1)}, f32[2,264,128]{2,1,0:T(8,128)S(1)}, u32[]{:S(2)}, u32[]{:S(2)}) collective-permute-start(f32[2,264,128]{2,1,0:T(8,128)S(1)} %copy.21.refs_0_), channel_id=1, source_target_pairs={{0,24},{4,28},{8,0},{12,4},{16,8},{20,12},{24,16},{28,20},{1,25},{... | collective-permute-start | bytes 811016 | tf_op jit(solution)/shard_map/ppermute | solution.py:458
  17.2 0.0 collective-permute-start.7
  17.2 0.9 %collective-permute-start.6 = (f32[2,264,128]{2,1,0:T(8,128)S(1)}, f32[2,264,128]{2,1,0:T(8,128)S(1)}, u32[]{:S(2)}, u32[]{:S(2)}) collective-permute-start(f32[2,264,128]{2,1,0:T(8,128)S(1)} %copy.21.refs_0_), channel_id=1, source_target_pairs={{0,4},{4,0},{8,12},{12,8},{16,20},{20,16},{24,28},{28,24},{1,5},{5... | collective-permute-start | bytes 811016 | tf_op jit(solution)/shard_map/ppermute | solution.py:451
  18.1 0.0 collective-permute-done.3
  18.1 0.0 collective-permute-done.2
  18.2 2.7 %collective-permute-start.9 = (f32[2,264,128]{2,1,0:T(8,128)S(1)}, f32[2,264,128]{2,1,0:T(8,128)S(1)}, u32[]{:S(2)}, u32[]{:S(2)}) collective-permute-start(f32[2,264,128]{2,1,0:T(8,128)S(1)} %copy.24), channel_id=1, source_target_pairs={{0,16},{4,20},{8,24},{12,28},{16,0},{20,4},{24,8},{28,12},{1,17},{... | collective-permute-start | bytes 811016 | tf_op jit(solution)/shard_map/ppermute | solution.py:458
  20.8 0.1 select_maximum_fusion.source_ref
  21.0 0.0 copy-done.2
  21.0 0.0 copy-done.1
  21.0 13.0 %first_sweep.1 = (f32[18,24,256]{2,1,0:T(8,128)S(1)}, f32[12,16,256]{2,1,0:T(8,128)S(1)}, bf16[7,7,256,256]{3,2,1,0:T(8,128)(2,1)S(1)}, bf16[7,7,256,256]{3,2,1,0:T(8,128)(2,1)S(1)}) custom-call(f32[2,24,32,128]{3,2,1,0:T(8,128)S(1)} %select_maximum_fusion.source_ref, f32[2,128,128]{2,1,0:T(8,128)S(1)} %copy-done.2, f32[7,7,2,128,128]{4,3,2,1,0:T(8,128)S(1)} %copy-done.1), custom_call_target="tpu_custom_call" | custom-call | flops 8323596288 | bytes 19267584 | tf_op jit(solution)/shard_map/first_sweep/pallas_call | solution.py:166
  34.0 0.0 collective-permute-done.8.refs_3_
  34.0 0.0 collective-permute-done.7.refs_1_
  34.1 0.0 collective-permute-done.6.refs_4_
  34.1 0.1 collective-permute-start.15
  34.1 5.9 %second_sweep.1 = (f32[12,16,256]{2,1,0:T(8,128)S(1)}, f32[2,32,192]{2,1,0:T(8,128)S(1)}, f32[2,32,192]{2,1,0:T(8,128)S(1)}, f32[2,32,192]{2,1,0:T(8,128)S(1)}, f32[2,32,192]{2,1,0:T(8,128)S(1)}) custom-call(f32[18,24,256]{2,1,0:T(8,128)S(1)} %get-tuple-element.30.second_ref, f32[12,16,256]{2,1,0:T(8,128)S(1)} %get-tuple-element.31.source_ref, ...), custom_call_target="tpu_custom_call" | custom-call | flops 3699376128 | bytes 12845056 | tf_op jit(solution)/shard_map/second_sweep/pallas_call | solution.py:258
  40.0 0.1 collective-permute-done.9.refs_2_
  40.2 2.9 %collective-permute-start.14 = (f32[1,2,264,128]{3,2,1,0:T(8,128)S(1)}, f32[1,2,264,128]{3,2,1,0:T(8,128)S(1)}, u32[]{:S(2)}, u32[]{:S(2)}) collective-permute-start(f32[1,2,264,128]{3,2,1,0:T(8,128)S(1)} %bitcast.26), channel_id=1, source_target_pairs={{0,4},{4,0},{8,12},{12,8},{16,20},{20,16},{24,28},{28,24},{1,5},{5... | collective-permute-start | bytes 811016 | tf_op jit(solution)/shard_map/ppermute | solution.py:451
  43.1 0.0 collective-permute-start.10
  43.1 2.1 %collective-permute-start.11 = (f32[2,32,192]{2,1,0:T(8,128)S(1)}, f32[2,32,192]{2,1,0:T(8,128)S(1)}, u32[]{:S(2)}, u32[]{:S(2)}) collective-permute-start(f32[2,32,192]{2,1,0:T(8,128)S(1)} %get-tuple-element.42), channel_id=1, source_target_pairs={{0,16},{4,20},{8,24},{12,28},{16,0},{20,4},{24,8},{28,12},{1,17},{... | collective-permute-start | bytes 147464 | tf_op jit(solution)/shard_map/ppermute | solution.py:458
  45.1 1.8 %collective-permute-start.12 = (f32[2,32,192]{2,1,0:T(8,128)S(1)}, f32[2,32,192]{2,1,0:T(8,128)S(1)}, u32[]{:S(2)}, u32[]{:S(2)}) collective-permute-start(f32[2,32,192]{2,1,0:T(8,128)S(1)} %get-tuple-element.43), channel_id=1, source_target_pairs={{0,24},{4,28},{8,0},{12,4},{16,8},{20,12},{24,16},{28,20},{1,25},{... | collective-permute-start | bytes 147464 | tf_op jit(solution)/shard_map/ppermute | solution.py:458
  46.9 2.4 %collective-permute-done.10.refs_1_ = f32[2,32,192]{2,1,0:T(8,128)S(1)} collective-permute-done((f32[2,32,192]{2,1,0:T(8,128)S(1)}, f32[2,32,192]{2,1,0:T(8,128)S(1)}, u32[]{:S(2)}, u32[]{:S(2)}) %collective-permute-start.10) | collective-permute-done | bytes 49184 | tf_op jit(solution)/shard_map/ppermute | solution.py:458
  49.3 2.1 %collective-permute-done.11.refs_2_ = f32[2,32,192]{2,1,0:T(8,128)S(1)} collective-permute-done((f32[2,32,192]{2,1,0:T(8,128)S(1)}, f32[2,32,192]{2,1,0:T(8,128)S(1)}, u32[]{:S(2)}, u32[]{:S(2)}) %collective-permute-start.11) | collective-permute-done | bytes 49184 | tf_op jit(solution)/shard_map/ppermute | solution.py:458
  51.4 0.0 collective-permute-done.12.refs_3_
  51.5 1.3 %collective-permute-start.13 = (f32[4,32,192]{2,1,0:T(8,128)S(1)}, f32[4,32,192]{2,1,0:T(8,128)S(1)}, u32[]{:S(2)}, u32[]{:S(2)}) collective-permute-start(f32[4,32,192]{2,1,0:T(8,128)S(1)} %pad_maximum_fusion.5), channel_id=1, source_target_pairs={{0,4},{4,0},{8,12},{12,8},{16,20},{20,16},{24,28},{28,24},{1,5},{5... | collective-permute-start | bytes 294920 | tf_op jit(solution)/shard_map/ppermute | solution.py:451
  52.7 0.0 collective-permute-done.15.refs_5_
  52.7 2.2 %spread.2 = (bf16[7,1536,256]{2,1,0:T(8,128)(2,1)S(1)}, bf16[7,1536,256]{2,1,0:T(8,128)(2,1)S(1)}) custom-call(f32[2,264,128]{2,1,0:T(8,128)S(1)} %copy.21.refs_0_, f32[2,264,128]{2,1,0:T(8,128)S(1)} %collective-permute-done.7.refs_1_, f32[2,264,128]{2,1,0:T(8,128)S(1)} %collective-permute-done.9.refs_2_, f32[2,264,128]{2,1,0:T(8,128)S(1)} %collective-permute-done.8.refs_3_, ...), custom_call_target="tpu_custom_call" | custom-call | bytes 1892352 | tf_op jit(solution)/shard_map/spread/pallas_call | solution.py:326
  55.0 0.0 collective-permute-done.14.refs_0_
  55.0 0.3 spread.3
  55.3 2.5 %collective-permute-done.13.refs_4_ = f32[4,32,192]{2,1,0:T(8,128)S(1)} collective-permute-done((f32[4,32,192]{2,1,0:T(8,128)S(1)}, f32[4,32,192]{2,1,0:T(8,128)S(1)}, u32[]{:S(2)}, u32[]{:S(2)}) %collective-permute-start.13) | collective-permute-done | bytes 98336 | tf_op jit(solution)/shard_map/ppermute | solution.py:451
  57.9 5.6 %correlate.1 = (f32[7,7,2,8,128]{4,3,2,1,0:T(8,128)S(1)}, f32[7,7,2,8,128]{4,3,2,1,0:T(8,128)S(1)}) custom-call(f32[2,32,192]{2,1,0:T(8,128)S(1)} %get-tuple-element.40.refs_0_, f32[2,32,192]{2,1,0:T(8,128)S(1)} %collective-permute-done.10.refs_1_, f32[2,32,192]{2,1,0:T(8,128)S(1)} %collective-permute-done.11.refs_2_, ...), custom_call_target="tpu_custom_call" | custom-call | flops 3699376128 | bytes 802816 | tf_op jit(solution)/shard_map/correlate/pallas_call | solution.py:405
  63.5 0.1 collective-permute-start.16
  63.5 1.7 %collective-permute-done.16 = f32[7,7,2,8,128]{4,3,2,1,0:T(8,128)S(1)} collective-permute-done((f32[7,7,2,8,128]{4,3,2,1,0:T(8,128)S(1)}, f32[7,7,2,8,128]{4,3,2,1,0:T(8,128)S(1)}, u32[]{:S(2)}, u32[]{:S(2)}) %collective-permute-start.16) | collective-permute-done | bytes 401440 | tf_op jit(solution)/shard_map/ppermute | solution.py:451
  65.3 0.1 add.22
  65.4 0.5 collective-permute-start.17
  65.9 1.7 %collective-permute-start.18 = (f32[3,7,2,8,128]{4,3,2,1,0:T(8,128)S(1)}, f32[3,7,2,8,128]{4,3,2,1,0:T(8,128)S(1)}, u32[]{:S(2)}, u32[]{:S(2)}) collective-permute-start(f32[3,7,2,8,128]{4,3,2,1,0:T(8,128)S(1)} %slice.47), channel_id=1, source_target_pairs={{0,2},{1,3},{2,0},{3,1},{4,6},{5,7},{6,4},{7,5},{8,10},{9,11},{10,... | collective-permute-start | bytes 516104 | tf_op jit(solution)/shard_map/ppermute | solution.py:458
  67.5 6.3 %collective-permute-done.17 = f32[4,7,2,8,128]{4,3,2,1,0:T(8,128)S(1)} collective-permute-done((f32[4,7,2,8,128]{4,3,2,1,0:T(8,128)S(1)}, f32[4,7,2,8,128]{4,3,2,1,0:T(8,128)S(1)}, u32[]{:S(2)}, u32[]{:S(2)}) %collective-permute-start.17) | collective-permute-done | bytes 229408 | tf_op jit(solution)/shard_map/ppermute | solution.py:458
  73.9 0.1 collective-permute-start.19
  74.0 2.7 %collective-permute-done.18 = f32[3,7,2,8,128]{4,3,2,1,0:T(8,128)S(1)} collective-permute-done((f32[3,7,2,8,128]{4,3,2,1,0:T(8,128)S(1)}, f32[3,7,2,8,128]{4,3,2,1,0:T(8,128)S(1)}, u32[]{:S(2)}, u32[]{:S(2)}) %collective-permute-start.18) | collective-permute-done | bytes 172064 | tf_op jit(solution)/shard_map/ppermute | solution.py:458
  76.8 0.1 collective-permute-start.20
  76.9 0.8 reshape.53
  77.6 0.0 collective-permute-done.19
  77.7 0.6 collective-permute-done.20
  78.3 0.1 fusion.6
  78.3 1.0 %pad_maximum_fusion = f32[7,7,2,16,128]{4,3,2,1,0:T(8,128)} fusion(f32[7,7,2,8,128]{4,3,2,1,0:T(8,128)S(1)} %get-tuple-element.55, f32[7,7,2,8,128]{4,3,2,1,0:T(8,128)S(1)} %get-tuple-element.54), kind=kLoop, calls=%fused_computation | loop fusion | flops 200704 | bytes 1605632 | tf_op jit(solution)/shard_map/concatenate | solution.py:534
  (27 shorter events, 0.5 us)
Async XLA Ops:
  0.6 20.4 %copy-start.2 = (f32[2,128,128]{2,1,0:T(8,128)S(1)}, f32[2,128,128]{2,1,0:T(8,128)}, u32[]{:S(2)}) copy-start(f32[2,128,128]{2,1,0:T(8,128)} %inverse_ref.3) | copy-start | bytes 393220
  1.7 5.8 %collective-permute-start.1 = (f32[2,96,128]{2,1,0:T(8,128)S(1)}, f32[2,96,128]{2,1,0:T(8,128)S(1)}, u32[]{:S(2)}, u32[]{:S(2)}) collective-permute-start(f32[2,96,128]{2,1,0:T(8,128)S(1)} %bitcast.44), channel_id=1, source_target_pairs={{0,4},{4,0},{8,12},{12,8},{16,20},{20,16},{24,28},{28,24},{1,5},{5... | collective-permute-start | bytes 294920 | tf_op jit(solution)/shard_map/ppermute | solution.py:451
  4.7 2.8 %collective-permute-start = (f32[2,96,128]{2,1,0:T(8,128)S(1)}, f32[2,96,128]{2,1,0:T(8,128)S(1)}, u32[]{:S(2)}, u32[]{:S(2)}) collective-permute-start(f32[2,96,128]{2,1,0:T(8,128)S(1)} %bitcast.43), channel_id=1, source_target_pairs={{4,8},{8,4},{12,16},{16,12},{20,24},{24,20},{5,9},{9,5},{13,17},{1... | collective-permute-start | bytes 294920 | tf_op jit(solution)/shard_map/ppermute | solution.py:451
  5.4 0.9 %copy-start = (f32[12,16,2,128]{3,2,1,0:T(2,128)S(1)}, f32[12,16,2,128]{3,2,1,0:T(2,128)}, u32[]{:S(2)}) copy-start(f32[12,16,2,128]{3,2,1,0:T(2,128)} %param.5) | copy-start | bytes 589828
  6.3 14.7 %copy-start.1 = (f32[7,7,2,128,128]{4,3,2,1,0:T(8,128)S(1)}, f32[7,7,2,128,128]{4,3,2,1,0:T(8,128)}, u32[]{:S(2)}) copy-start(f32[7,7,2,128,128]{4,3,2,1,0:T(8,128)} %blocks_ref.1) | copy-start | bytes 19267588
  6.4 5.0 %collective-permute-start.5 = (f32[2,36,128]{2,0,1:T(2,128)S(1)}, f32[2,36,128]{2,0,1:T(2,128)S(1)}, u32[]{:S(2)}, u32[]{:S(2)}) collective-permute-start(f32[2,36,128]{2,0,1:T(2,128)S(1)} %bitcast.46), channel_id=1, source_target_pairs={{0,1},{1,0},{2,3},{3,2},{4,5},{5,4},{6,7},{7,6},{8,9},{9,8},{10,11... | collective-permute-start | bytes 110600 | tf_op jit(solution)/shard_map/ppermute | solution.py:451
  6.5 4.9 %collective-permute-start.4 = (f32[2,36,128]{2,0,1:T(2,128)S(1)}, f32[2,36,128]{2,0,1:T(2,128)S(1)}, u32[]{:S(2)}, u32[]{:S(2)}) collective-permute-start(f32[2,36,128]{2,0,1:T(2,128)S(1)} %bitcast.48), channel_id=1, source_target_pairs={{1,2},{2,1},{5,6},{6,5},{9,10},{10,9},{13,14},{14,13},{17,18},{18,... | collective-permute-start | bytes 110600 | tf_op jit(solution)/shard_map/ppermute | solution.py:451
  7.8 10.3 %collective-permute-start.3 = (f32[2,144,128]{2,0,1:T(2,128)S(1)}, f32[2,144,128]{2,0,1:T(2,128)S(1)}, u32[]{:S(2)}, u32[]{:S(2)}) collective-permute-start(f32[2,144,128]{2,0,1:T(2,128)S(1)} %bitcast.40), channel_id=1, source_target_pairs={{0,1},{1,0},{2,3},{3,2},{4,5},{5,4},{6,7},{7,6},{8,9},{9,8},{10,11... | collective-permute-start | bytes 442376 | tf_op jit(solution)/shard_map/ppermute | solution.py:451
  10.7 7.4 %collective-permute-start.2 = (f32[2,144,128]{2,0,1:T(2,128)S(1)}, f32[2,144,128]{2,0,1:T(2,128)S(1)}, u32[]{:S(2)}, u32[]{:S(2)}) collective-permute-start(f32[2,144,128]{2,0,1:T(2,128)S(1)} %bitcast.37), channel_id=1, source_target_pairs={{1,2},{2,1},{5,6},{6,5},{9,10},{10,9},{13,14},{14,13},{17,18},{18,... | collective-permute-start | bytes 442376 | tf_op jit(solution)/shard_map/ppermute | solution.py:451
  11.7 22.2 %collective-permute-start.8 = (f32[2,264,128]{2,1,0:T(8,128)S(1)}, f32[2,264,128]{2,1,0:T(8,128)S(1)}, u32[]{:S(2)}, u32[]{:S(2)}) collective-permute-start(f32[2,264,128]{2,1,0:T(8,128)S(1)} %copy.21.refs_0_), channel_id=1, source_target_pairs={{0,24},{4,28},{8,0},{12,4},{16,8},{20,12},{24,16},{28,20},{1,25},{... | collective-permute-start | bytes 811016 | tf_op jit(solution)/shard_map/ppermute | solution.py:458
  17.2 16.8 %collective-permute-start.7 = (f32[2,264,128]{2,1,0:T(8,128)S(1)}, f32[2,264,128]{2,1,0:T(8,128)S(1)}, u32[]{:S(2)}, u32[]{:S(2)}) collective-permute-start(f32[2,264,128]{2,1,0:T(8,128)S(1)} %copy.21.refs_0_), channel_id=1, source_target_pairs={{0,8},{4,12},{8,16},{12,20},{16,24},{20,28},{24,0},{28,4},{1,9},{5... | collective-permute-start | bytes 811016 | tf_op jit(solution)/shard_map/ppermute | solution.py:458
  17.2 16.8 %collective-permute-start.6 = (f32[2,264,128]{2,1,0:T(8,128)S(1)}, f32[2,264,128]{2,1,0:T(8,128)S(1)}, u32[]{:S(2)}, u32[]{:S(2)}) collective-permute-start(f32[2,264,128]{2,1,0:T(8,128)S(1)} %copy.21.refs_0_), channel_id=1, source_target_pairs={{0,4},{4,0},{8,12},{12,8},{16,20},{20,16},{24,28},{28,24},{1,5},{5... | collective-permute-start | bytes 811016 | tf_op jit(solution)/shard_map/ppermute | solution.py:451
  18.2 22.0 %collective-permute-start.9 = (f32[2,264,128]{2,1,0:T(8,128)S(1)}, f32[2,264,128]{2,1,0:T(8,128)S(1)}, u32[]{:S(2)}, u32[]{:S(2)}) collective-permute-start(f32[2,264,128]{2,1,0:T(8,128)S(1)} %copy.24), channel_id=1, source_target_pairs={{0,16},{4,20},{8,24},{12,28},{16,0},{20,4},{24,8},{28,12},{1,17},{... | collective-permute-start | bytes 811016 | tf_op jit(solution)/shard_map/ppermute | solution.py:458
  34.1 18.7 %collective-permute-start.15 = (f32[2,2,264,128]{3,2,1,0:T(8,128)S(1)}, f32[2,2,264,128]{3,2,1,0:T(8,128)S(1)}, u32[]{:S(2)}, u32[]{:S(2)}) collective-permute-start(f32[2,2,264,128]{3,2,1,0:T(8,128)S(1)} %pad_maximum_fusion.1), channel_id=1, source_target_pairs={{0,4},{4,0},{8,12},{12,8},{16,20},{20,16},{24,28},{28,24},{1,5},{5... | collective-permute-start | bytes 1622024 | tf_op jit(solution)/shard_map/ppermute | solution.py:451
  40.2 14.8 %collective-permute-start.14 = (f32[1,2,264,128]{3,2,1,0:T(8,128)S(1)}, f32[1,2,264,128]{3,2,1,0:T(8,128)S(1)}, u32[]{:S(2)}, u32[]{:S(2)}) collective-permute-start(f32[1,2,264,128]{3,2,1,0:T(8,128)S(1)} %bitcast.26), channel_id=1, source_target_pairs={{0,4},{4,0},{8,12},{12,8},{16,20},{20,16},{24,28},{28,24},{1,5},{5... | collective-permute-start | bytes 811016 | tf_op jit(solution)/shard_map/ppermute | solution.py:451
  43.1 6.2 %collective-permute-start.10 = (f32[2,32,192]{2,1,0:T(8,128)S(1)}, f32[2,32,192]{2,1,0:T(8,128)S(1)}, u32[]{:S(2)}, u32[]{:S(2)}) collective-permute-start(f32[2,32,192]{2,1,0:T(8,128)S(1)} %get-tuple-element.41), channel_id=1, source_target_pairs={{0,8},{4,12},{8,16},{12,20},{16,24},{20,28},{24,0},{28,4},{1,9},{5... | collective-permute-start | bytes 147464 | tf_op jit(solution)/shard_map/ppermute | solution.py:458
  43.1 8.4 %collective-permute-start.11 = (f32[2,32,192]{2,1,0:T(8,128)S(1)}, f32[2,32,192]{2,1,0:T(8,128)S(1)}, u32[]{:S(2)}, u32[]{:S(2)}) collective-permute-start(f32[2,32,192]{2,1,0:T(8,128)S(1)} %get-tuple-element.42), channel_id=1, source_target_pairs={{0,16},{4,20},{8,24},{12,28},{16,0},{20,4},{24,8},{28,12},{1,17},{... | collective-permute-start | bytes 147464 | tf_op jit(solution)/shard_map/ppermute | solution.py:458
  45.1 6.3 %collective-permute-start.12 = (f32[2,32,192]{2,1,0:T(8,128)S(1)}, f32[2,32,192]{2,1,0:T(8,128)S(1)}, u32[]{:S(2)}, u32[]{:S(2)}) collective-permute-start(f32[2,32,192]{2,1,0:T(8,128)S(1)} %get-tuple-element.43), channel_id=1, source_target_pairs={{0,24},{4,28},{8,0},{12,4},{16,8},{20,12},{24,16},{28,20},{1,25},{... | collective-permute-start | bytes 147464 | tf_op jit(solution)/shard_map/ppermute | solution.py:458
  51.5 6.4 %collective-permute-start.13 = (f32[4,32,192]{2,1,0:T(8,128)S(1)}, f32[4,32,192]{2,1,0:T(8,128)S(1)}, u32[]{:S(2)}, u32[]{:S(2)}) collective-permute-start(f32[4,32,192]{2,1,0:T(8,128)S(1)} %pad_maximum_fusion.5), channel_id=1, source_target_pairs={{0,4},{4,0},{8,12},{12,8},{16,20},{20,16},{24,28},{28,24},{1,5},{5... | collective-permute-start | bytes 294920 | tf_op jit(solution)/shard_map/ppermute | solution.py:451
  63.5 1.8 %collective-permute-start.16 = (f32[7,7,2,8,128]{4,3,2,1,0:T(8,128)S(1)}, f32[7,7,2,8,128]{4,3,2,1,0:T(8,128)S(1)}, u32[]{:S(2)}, u32[]{:S(2)}) collective-permute-start(f32[7,7,2,8,128]{4,3,2,1,0:T(8,128)S(1)} %get-tuple-element.52), channel_id=1, source_target_pairs={{0,1},{1,0},{2,3},{3,2},{4,5},{5,4},{6,7},{7,6},{8,9},{9,8},{10,11... | collective-permute-start | bytes 1204232 | tf_op jit(solution)/shard_map/ppermute | solution.py:451
  65.4 8.5 %collective-permute-start.17 = (f32[4,7,2,8,128]{4,3,2,1,0:T(8,128)S(1)}, f32[4,7,2,8,128]{4,3,2,1,0:T(8,128)S(1)}, u32[]{:S(2)}, u32[]{:S(2)}) collective-permute-start(f32[4,7,2,8,128]{4,3,2,1,0:T(8,128)S(1)} %slice.46), channel_id=1, source_target_pairs={{0,2},{1,3},{2,0},{3,1},{4,6},{5,7},{6,4},{7,5},{8,10},{9,11},{10,... | collective-permute-start | bytes 688136 | tf_op jit(solution)/shard_map/ppermute | solution.py:458
  65.9 10.9 %collective-permute-start.18 = (f32[3,7,2,8,128]{4,3,2,1,0:T(8,128)S(1)}, f32[3,7,2,8,128]{4,3,2,1,0:T(8,128)S(1)}, u32[]{:S(2)}, u32[]{:S(2)}) collective-permute-start(f32[3,7,2,8,128]{4,3,2,1,0:T(8,128)S(1)} %slice.47), channel_id=1, source_target_pairs={{0,2},{1,3},{2,0},{3,1},{4,6},{5,7},{6,4},{7,5},{8,10},{9,11},{10,... | collective-permute-start | bytes 516104 | tf_op jit(solution)/shard_map/ppermute | solution.py:458
  73.9 3.7 %collective-permute-start.19 = (f32[4,7,2,8,128]{4,3,2,1,0:T(8,128)S(1)}, f32[4,7,2,8,128]{4,3,2,1,0:T(8,128)S(1)}, u32[]{:S(2)}, u32[]{:S(2)}) collective-permute-start(f32[4,7,2,8,128]{4,3,2,1,0:T(8,128)S(1)} %slice_add_fusion.1), channel_id=1, source_target_pairs={{0,1},{1,0},{2,3},{3,2},{4,5},{5,4},{6,7},{7,6},{8,9},{9,8},{10,11... | collective-permute-start | bytes 688136 | tf_op jit(solution)/shard_map/ppermute | solution.py:451
  76.8 1.5 %collective-permute-start.20 = (f32[3,7,2,8,128]{4,3,2,1,0:T(8,128)S(1)}, f32[3,7,2,8,128]{4,3,2,1,0:T(8,128)S(1)}, u32[]{:S(2)}, u32[]{:S(2)}) collective-permute-start(f32[3,7,2,8,128]{4,3,2,1,0:T(8,128)S(1)} %slice_add_fusion), channel_id=1, source_target_pairs={{0,1},{1,0},{2,3},{3,2},{4,5},{5,4},{6,7},{7,6},{8,9},{9,8},{10,11... | collective-permute-start | bytes 516104 | tf_op jit(solution)/shard_map/ppermute | solution.py:451

commit v13 on v12

--- a/solution.py
+++ b/solution.py
@@ -226,10 +226,16 @@
 
     acc[...] = jnp.zeros_like(acc)
 
-    @pl.loop(0, span)
-    def _(a):
+    def one_lag(a):
         at = pl.ds(pl.multiple_of(a * cols, cols), own)
-        acc[...] += products(x_high[at, :], x_low[at, :], w_high[a], w_low[a])
+        return products(x_high[at, :], x_low[at, :], w_high[a], w_low[a])
+
+    @pl.loop(0, span // 2)
+    def _(pair):
+        acc[...] += one_lag(2 * pair) + one_lag(2 * pair + 1)
+
+    if span % 2:
+        acc[...] += one_lag(span - 1)
 
     centre = second_ref[reach : reach + rows, pl.ds(reach, cols), :].reshape(own, lanes)
     source = source_ref[...].reshape(own, lanes)
@@ -378,8 +384,7 @@
     upper = lax.axis_index("col") % 2 == 1
     first_lag, count = lags
 
-    @pl.loop(0, count)
-    def _(n):
+    def one_lag(n):
         b = first_lag + n
         left = tuple(ref[...].reshape(span * double, total) for ref in (l_high, l_low))
         product = dot3(left, (s_high[b], s_low[b])) * factor
@@ -391,6 +396,9 @@
             for c, value in enumerate((real, imag)):
                 mine_ref[a, n, c] = jnp.where(upper, value[half:], value[:half])
                 other_ref[a, n, c] = jnp.where(upper, value[:half], value[half:])
+
+    for n in range(count):
+        one_lag(n)
 
 
 def correlate(shares, twin_shares, s_high, s_low, lags, rows, cols, factor):
@@ -504,6 +512,7 @@
     second, own_twin, early = lax.optimization_barrier((second, own_twin, jnp.stack([pieces[1], pieces[-1]])))
     early_twins = swap(early, "row", 0)
     adjoint, sends = second_sweep(second, own_source, element_inverse, high, low, peers)
+    adjoint = adjoint.reshape(adjoint_source.shape)
     *late, sends = lax.optimization_barrier((*pieces[2:-1], sends))
     late_twins = swap(jnp.stack(late), "row", 0)
     shares = [shifted(send, "row", 2 * k) for k, send in enumerate(sends)]
@@ -523,7 +532,7 @@
     for lags in ((0, span),):
         mine, other = correlate(shares, twin_shares, s_high, s_low, lags, rows, cols, factor)
         mine = mine + swap(other, "col", 0)
-        twin_shares, mine = lax.optimization_barrier((twin_shares, mine))
+        mine, adjoint = lax.optimization_barrier((mine, adjoint))
         for piece in (mine[: span // 2 + 1], mine[span // 2 + 1 :]):
             total = piece
             for k in range(2, lax.axis_size("col"), 2):
@@ -534,7 +543,7 @@
     lag_grad = jnp.concatenate(
         [jnp.where(even, total, twin), jnp.where(even, twin, total)], axis=3
     )
-    return (adjoint.reshape(adjoint_source.shape), lag_grad)
+    return (adjoint, lag_grad)
 
 
 def solution(mesh):

time: 79.5 us -> 78.4 us (0.986)
  Pallas kernels: 27 us -> 25.4 us
  waiting for transfers between devices: 18.9 us -> 19.7 us
    pallas_call x1, Pallas kernels: 5.56 us -> 4.5 us  [correlate(): pl.pallas_call(functools.partial(correlate_kernel, (rows, cols, span, pee...]
    ppermute x8, waiting for transfers between devices: 13.8 us -> 14.6 us  [shifted(): lax.ppermute(value, axis, [(i, (i + shift) % peers) for i in range(peers)])]
where the time goes in v13:
time: 78.4 us; the launch traced here: 78.2 us
  starting transfers between devices  27.2 us (35%)
  Pallas kernels  25.4 us (32%)
  waiting for transfers between devices  19.7 us (25%)
  local copies, waits for them, and re-layouts  3.3 us (4%)
  other arithmetic  1.52 us (2%)
  between operations  1.08 us (1%)
    ppermute x8, waiting for transfers between devices, shifted(): lax.ppermute(value, axis, [(i, (i + shift) % peers) for i in range(peers)])  14.6 us
    ppermute x8, starting transfers between devices, shifted(): lax.ppermute(value, axis, [(i, (i + shift) % peers) for i in range(peers)])  14.1 us
    ppermute x13, starting transfers between devices, swap(): return lax.ppermute(value, axis, pairs)  13.1 us
    pallas_call x1, Pallas kernels, first_sweep(): pl.pallas_call(functools.partial(first_sweep_kernel, (rows, cols, span, p...  13 us
    pallas_call x1, Pallas kernels, second_sweep(): pl.pallas_call(functools.partial(second_sweep_kernel, (rows, cols, span,...  5.33 us
    ppermute x13, waiting for transfers between devices, swap(): return lax.ppermute(value, axis, pairs)  5.08 us
    pallas_call x1, Pallas kernels, correlate(): pl.pallas_call(functools.partial(correlate_kernel, (rows, cols, span, pee...  4.5 us
    pallas_call x2, Pallas kernels, spread(): pl.pallas_call(functools.partial(spread_kernel, (rows, cols, span, peers)...  2.57 us
  transfers between devices with their start and end apart: 21, of which 9 were waited for; matrix products, arithmetic and copies ran while one was open for 2% of the time, Pallas kernels for 27%

profile of v13, /device:TPU:0, one launch (start us, length us, event | category | flops | bytes accessed | tf_op | source)
XLA Modules:
  0.0 78.2 jit_solution(12929549342123446552)
XLA Ops:
  0.6 0.0 copy-start.2
  0.7 1.0 %copy.31 = f32[12,16,2,128]{3,1,0,2:T(8,128)S(1)} copy(f32[12,16,2,128]{3,2,1,0:T(2,128)} %param.4) | data formatting | bytes 393216 | tf_op args[0]
  1.7 3.0 %collective-permute-start.3 = (f32[2,96,128]{2,1,0:T(8,128)S(1)}, f32[2,96,128]{2,1,0:T(8,128)S(1)}, u32[]{:S(2)}, u32[]{:S(2)}) collective-permute-start(f32[2,96,128]{2,1,0:T(8,128)S(1)} %bitcast.44), channel_id=1, source_target_pairs={{0,4},{4,0},{8,12},{12,8},{16,20},{20,16},{24,28},{28,24},{1,5},{5... | collective-permute-start | bytes 294920 | tf_op jit(solution)/shard_map/ppermute | solution.py:459
  4.7 0.7 collective-permute-start.2
  5.4 0.0 copy-start
  5.4 0.9 %copy-done = f32[12,16,2,128]{3,2,1,0:T(2,128)S(1)} copy-done((f32[12,16,2,128]{3,2,1,0:T(2,128)S(1)}, f32[12,16,2,128]{3,2,1,0:T(2,128)}, u32[]{:S(2)}) %copy-start) | copy-done | bytes 196632
  6.3 0.0 copy-start.1
  6.4 0.1 collective-permute-start.1
  6.5 0.8 %collective-permute-start = (f32[2,36,128]{2,0,1:T(2,128)S(1)}, f32[2,36,128]{2,0,1:T(2,128)S(1)}, u32[]{:S(2)}, u32[]{:S(2)}) collective-permute-start(f32[2,36,128]{2,0,1:T(2,128)S(1)} %bitcast.48), channel_id=1, source_target_pairs={{1,2},{2,1},{5,6},{6,5},{9,10},{10,9},{13,14},{14,13},{17,18},{18,... | collective-permute-start | bytes 110600 | tf_op jit(solution)/shard_map/ppermute | solution.py:459
  7.3 0.2 collective-permute-done.3
  7.5 0.0 collective-permute-done.2
  7.6 0.1 copy.17
  7.7 0.1 copy.15
  7.8 2.9 %collective-permute-start.4 = (f32[2,144,128]{2,0,1:T(2,128)S(1)}, f32[2,144,128]{2,0,1:T(2,128)S(1)}, u32[]{:S(2)}, u32[]{:S(2)}) collective-permute-start(f32[2,144,128]{2,0,1:T(2,128)S(1)} %bitcast.40), channel_id=1, source_target_pairs={{0,1},{1,0},{2,3},{3,2},{4,5},{5,4},{6,7},{7,6},{8,9},{9,8},{10,11... | collective-permute-start | bytes 442376 | tf_op jit(solution)/shard_map/ppermute | solution.py:459
  10.7 0.7 collective-permute-start.6
  11.4 0.0 collective-permute-done.1
  11.4 0.0 collective-permute-done
  11.5 0.2 copy.14
  11.7 5.5 %collective-permute-start.9 = (f32[2,264,128]{2,1,0:T(8,128)S(1)}, f32[2,264,128]{2,1,0:T(8,128)S(1)}, u32[]{:S(2)}, u32[]{:S(2)}) collective-permute-start(f32[2,264,128]{2,1,0:T(8,128)S(1)} %copy.22.refs_0_), channel_id=1, source_target_pairs={{0,24},{4,28},{8,0},{12,4},{16,8},{20,12},{24,16},{28,20},{1,25},{... | collective-permute-start | bytes 811016 | tf_op jit(solution)/shard_map/ppermute | solution.py:466
  17.2 0.0 collective-permute-start.8
  17.2 0.9 %collective-permute-start.7 = (f32[2,264,128]{2,1,0:T(8,128)S(1)}, f32[2,264,128]{2,1,0:T(8,128)S(1)}, u32[]{:S(2)}, u32[]{:S(2)}) collective-permute-start(f32[2,264,128]{2,1,0:T(8,128)S(1)} %copy.22.refs_0_), channel_id=1, source_target_pairs={{0,4},{4,0},{8,12},{12,8},{16,20},{20,16},{24,28},{28,24},{1,5},{5... | collective-permute-start | bytes 811016 | tf_op jit(solution)/shard_map/ppermute | solution.py:459
  18.1 0.0 collective-permute-done.4
  18.1 0.0 collective-permute-done.6
  18.2 2.7 %collective-permute-start.5 = (f32[2,264,128]{2,1,0:T(8,128)S(1)}, f32[2,264,128]{2,1,0:T(8,128)S(1)}, u32[]{:S(2)}, u32[]{:S(2)}) collective-permute-start(f32[2,264,128]{2,1,0:T(8,128)S(1)} %copy.16), channel_id=1, source_target_pairs={{0,16},{4,20},{8,24},{12,28},{16,0},{20,4},{24,8},{28,12},{1,17},{... | collective-permute-start | bytes 811016 | tf_op jit(solution)/shard_map/ppermute | solution.py:466
  20.8 0.1 select_maximum_fusion.source_ref
  21.0 0.0 copy-done.2
  21.0 0.0 copy-done.1
  21.0 13.0 %first_sweep.1 = (f32[18,24,256]{2,1,0:T(8,128)S(1)}, f32[12,16,256]{2,1,0:T(8,128)S(1)}, bf16[7,7,256,256]{3,2,1,0:T(8,128)(2,1)S(1)}, bf16[7,7,256,256]{3,2,1,0:T(8,128)(2,1)S(1)}) custom-call(f32[2,24,32,128]{3,2,1,0:T(8,128)S(1)} %select_maximum_fusion.source_ref, f32[2,128,128]{2,1,0:T(8,128)S(1)} %copy-done.2, f32[7,7,2,128,128]{4,3,2,1,0:T(8,128)S(1)} %copy-done.1), custom_call_target="tpu_custom_call" | custom-call | flops 8323596288 | bytes 19267584 | tf_op jit(solution)/shard_map/first_sweep/pallas_call | solution.py:166
  34.0 0.0 collective-permute-done.9.refs_3_
  34.0 0.0 collective-permute-done.8.refs_1_
  34.1 0.0 collective-permute-done.7.refs_4_
  34.1 0.1 collective-permute-start.15
  34.1 5.3 %second_sweep.1 = (f32[12,16,256]{2,1,0:T(8,128)S(1)}, f32[2,32,192]{2,1,0:T(8,128)S(1)}, f32[2,32,192]{2,1,0:T(8,128)S(1)}, f32[2,32,192]{2,1,0:T(8,128)S(1)}, f32[2,32,192]{2,1,0:T(8,128)S(1)}) custom-call(f32[18,24,256]{2,1,0:T(8,128)S(1)} %get-tuple-element.32.second_ref, f32[12,16,256]{2,1,0:T(8,128)S(1)} %get-tuple-element.33.source_ref, ...), custom_call_target="tpu_custom_call" | custom-call | flops 3699376128 | bytes 12845056 | tf_op jit(solution)/shard_map/second_sweep/pallas_call | solution.py:264
  39.5 0.7 collective-permute-done.5.refs_2_
  40.2 2.9 %collective-permute-start.14 = (f32[1,2,264,128]{3,2,1,0:T(8,128)S(1)}, f32[1,2,264,128]{3,2,1,0:T(8,128)S(1)}, u32[]{:S(2)}, u32[]{:S(2)}) collective-permute-start(f32[1,2,264,128]{3,2,1,0:T(8,128)S(1)} %bitcast.26), channel_id=1, source_target_pairs={{0,4},{4,0},{8,12},{12,8},{16,20},{20,16},{24,28},{28,24},{1,5},{5... | collective-permute-start | bytes 811016 | tf_op jit(solution)/shard_map/ppermute | solution.py:459
  43.1 0.0 collective-permute-start.10
  43.1 2.1 %collective-permute-start.11 = (f32[2,32,192]{2,1,0:T(8,128)S(1)}, f32[2,32,192]{2,1,0:T(8,128)S(1)}, u32[]{:S(2)}, u32[]{:S(2)}) collective-permute-start(f32[2,32,192]{2,1,0:T(8,128)S(1)} %get-tuple-element.42), channel_id=1, source_target_pairs={{0,16},{4,20},{8,24},{12,28},{16,0},{20,4},{24,8},{28,12},{1,17},{... | collective-permute-start | bytes 147464 | tf_op jit(solution)/shard_map/ppermute | solution.py:466
  45.1 1.8 %collective-permute-start.12 = (f32[2,32,192]{2,1,0:T(8,128)S(1)}, f32[2,32,192]{2,1,0:T(8,128)S(1)}, u32[]{:S(2)}, u32[]{:S(2)}) collective-permute-start(f32[2,32,192]{2,1,0:T(8,128)S(1)} %get-tuple-element.43), channel_id=1, source_target_pairs={{0,24},{4,28},{8,0},{12,4},{16,8},{20,12},{24,16},{28,20},{1,25},{... | collective-permute-start | bytes 147464 | tf_op jit(solution)/shard_map/ppermute | solution.py:466
  46.9 2.4 %collective-permute-done.10.refs_1_ = f32[2,32,192]{2,1,0:T(8,128)S(1)} collective-permute-done((f32[2,32,192]{2,1,0:T(8,128)S(1)}, f32[2,32,192]{2,1,0:T(8,128)S(1)}, u32[]{:S(2)}, u32[]{:S(2)}) %collective-permute-start.10) | collective-permute-done | bytes 49184 | tf_op jit(solution)/shard_map/ppermute | solution.py:466
  49.3 2.4 %collective-permute-done.11.refs_2_ = f32[2,32,192]{2,1,0:T(8,128)S(1)} collective-permute-done((f32[2,32,192]{2,1,0:T(8,128)S(1)}, f32[2,32,192]{2,1,0:T(8,128)S(1)}, u32[]{:S(2)}, u32[]{:S(2)}) %collective-permute-start.11) | collective-permute-done | bytes 49184 | tf_op jit(solution)/shard_map/ppermute | solution.py:466
  51.7 0.0 collective-permute-done.12.refs_3_
  51.8 1.0 %collective-permute-start.13 = (f32[4,32,192]{2,1,0:T(8,128)S(1)}, f32[4,32,192]{2,1,0:T(8,128)S(1)}, u32[]{:S(2)}, u32[]{:S(2)}) collective-permute-start(f32[4,32,192]{2,1,0:T(8,128)S(1)} %pad_maximum_fusion.5), channel_id=1, source_target_pairs={{0,4},{4,0},{8,12},{12,8},{16,20},{20,16},{24,28},{28,24},{1,5},{5... | collective-permute-start | bytes 294920 | tf_op jit(solution)/shard_map/ppermute | solution.py:459
  52.7 0.0 collective-permute-done.15.refs_5_
  52.7 2.2 %spread.2 = (bf16[7,1536,256]{2,1,0:T(8,128)(2,1)S(1)}, bf16[7,1536,256]{2,1,0:T(8,128)(2,1)S(1)}) custom-call(f32[2,264,128]{2,1,0:T(8,128)S(1)} %copy.22.refs_0_, f32[2,264,128]{2,1,0:T(8,128)S(1)} %collective-permute-done.8.refs_1_, f32[2,264,128]{2,1,0:T(8,128)S(1)} %collective-permute-done.5.refs_2_, f32[2,264,128]{2,1,0:T(8,128)S(1)} %collective-permute-done.9.refs_3_, ...), custom_call_target="tpu_custom_call" | custom-call | bytes 1892352 | tf_op jit(solution)/shard_map/spread/pallas_call | solution.py:332
  55.0 0.0 collective-permute-done.14.refs_0_
  55.0 0.3 spread.3
  55.3 2.5 %collective-permute-done.13.refs_4_ = f32[4,32,192]{2,1,0:T(8,128)S(1)} collective-permute-done((f32[4,32,192]{2,1,0:T(8,128)S(1)}, f32[4,32,192]{2,1,0:T(8,128)S(1)}, u32[]{:S(2)}, u32[]{:S(2)}) %collective-permute-start.13) | collective-permute-done | bytes 98336 | tf_op jit(solution)/shard_map/ppermute | solution.py:459
  57.9 4.5 %correlate.1 = (f32[7,7,2,8,128]{4,3,2,1,0:T(8,128)S(1)}, f32[7,7,2,8,128]{4,3,2,1,0:T(8,128)S(1)}) custom-call(f32[2,32,192]{2,1,0:T(8,128)S(1)} %get-tuple-element.40.refs_0_, f32[2,32,192]{2,1,0:T(8,128)S(1)} %collective-permute-done.10.refs_1_, f32[2,32,192]{2,1,0:T(8,128)S(1)} %collective-permute-done.11.refs_2_, ...), custom_call_target="tpu_custom_call" | custom-call | flops 3699376128 | bytes 802816 | tf_op jit(solution)/shard_map/correlate/pallas_call | solution.py:413
  62.4 0.1 collective-permute-start.16
  62.5 0.8 reshape.53
  63.3 0.9 %collective-permute-done.16 = f32[7,7,2,8,128]{4,3,2,1,0:T(8,128)S(1)} collective-permute-done((f32[7,7,2,8,128]{4,3,2,1,0:T(8,128)S(1)}, f32[7,7,2,8,128]{4,3,2,1,0:T(8,128)S(1)}, u32[]{:S(2)}, u32[]{:S(2)}) %collective-permute-start.16) | collective-permute-done | bytes 401440 | tf_op jit(solution)/shard_map/ppermute | solution.py:459
  64.2 0.1 add.22
  64.3 0.1 collective-permute-start.17
  64.4 2.1 %collective-permute-start.18 = (f32[3,7,2,8,128]{4,3,2,1,0:T(8,128)S(1)}, f32[3,7,2,8,128]{4,3,2,1,0:T(8,128)S(1)}, u32[]{:S(2)}, u32[]{:S(2)}) collective-permute-start(f32[3,7,2,8,128]{4,3,2,1,0:T(8,128)S(1)} %slice.47), channel_id=1, source_target_pairs={{0,2},{1,3},{2,0},{3,1},{4,6},{5,7},{6,4},{7,5},{8,10},{9,11},{10,... | collective-permute-start | bytes 516104 | tf_op jit(solution)/shard_map/ppermute | solution.py:466
  66.5 6.3 %collective-permute-done.17 = f32[4,7,2,8,128]{4,3,2,1,0:T(8,128)S(1)} collective-permute-done((f32[4,7,2,8,128]{4,3,2,1,0:T(8,128)S(1)}, f32[4,7,2,8,128]{4,3,2,1,0:T(8,128)S(1)}, u32[]{:S(2)}, u32[]{:S(2)}) %collective-permute-start.17) | collective-permute-done | bytes 229408 | tf_op jit(solution)/shard_map/ppermute | solution.py:466
  72.8 0.1 collective-permute-start.19
  72.9 2.8 %collective-permute-done.18 = f32[3,7,2,8,128]{4,3,2,1,0:T(8,128)S(1)} collective-permute-done((f32[3,7,2,8,128]{4,3,2,1,0:T(8,128)S(1)}, f32[3,7,2,8,128]{4,3,2,1,0:T(8,128)S(1)}, u32[]{:S(2)}, u32[]{:S(2)}) %collective-permute-start.18) | collective-permute-done | bytes 172064 | tf_op jit(solution)/shard_map/ppermute | solution.py:466
  75.7 0.1 collective-permute-start.20
  75.8 0.0 collective-permute-done.19
  75.8 1.4 %collective-permute-done.20 = f32[3,7,2,8,128]{4,3,2,1,0:T(8,128)S(1)} collective-permute-done((f32[3,7,2,8,128]{4,3,2,1,0:T(8,128)S(1)}, f32[3,7,2,8,128]{4,3,2,1,0:T(8,128)S(1)}, u32[]{:S(2)}, u32[]{:S(2)}) %collective-permute-start.20) | collective-permute-done | bytes 172064 | tf_op jit(solution)/shard_map/ppermute | solution.py:459
  77.2 0.1 fusion.6
  77.3 1.0 %pad_maximum_fusion = f32[7,7,2,16,128]{4,3,2,1,0:T(8,128)} fusion(f32[7,7,2,8,128]{4,3,2,1,0:T(8,128)S(1)} %get-tuple-element.57, f32[7,7,2,8,128]{4,3,2,1,0:T(8,128)S(1)} %get-tuple-element.56), kind=kLoop, calls=%fused_computation | loop fusion | flops 200704 | bytes 1605632 | tf_op jit(solution)/shard_map/concatenate | solution.py:543
  (27 shorter events, 0.5 us)
Async XLA Ops:
  0.6 20.4 %copy-start.2 = (f32[2,128,128]{2,1,0:T(8,128)S(1)}, f32[2,128,128]{2,1,0:T(8,128)}, u32[]{:S(2)}) copy-start(f32[2,128,128]{2,1,0:T(8,128)} %inverse_ref.3) | copy-start | bytes 393220
  1.7 5.8 %collective-permute-start.3 = (f32[2,96,128]{2,1,0:T(8,128)S(1)}, f32[2,96,128]{2,1,0:T(8,128)S(1)}, u32[]{:S(2)}, u32[]{:S(2)}) collective-permute-start(f32[2,96,128]{2,1,0:T(8,128)S(1)} %bitcast.44), channel_id=1, source_target_pairs={{0,4},{4,0},{8,12},{12,8},{16,20},{20,16},{24,28},{28,24},{1,5},{5... | collective-permute-start | bytes 294920 | tf_op jit(solution)/shard_map/ppermute | solution.py:459
  4.7 2.8 %collective-permute-start.2 = (f32[2,96,128]{2,1,0:T(8,128)S(1)}, f32[2,96,128]{2,1,0:T(8,128)S(1)}, u32[]{:S(2)}, u32[]{:S(2)}) collective-permute-start(f32[2,96,128]{2,1,0:T(8,128)S(1)} %bitcast.43), channel_id=1, source_target_pairs={{4,8},{8,4},{12,16},{16,12},{20,24},{24,20},{5,9},{9,5},{13,17},{1... | collective-permute-start | bytes 294920 | tf_op jit(solution)/shard_map/ppermute | solution.py:459
  5.4 0.9 %copy-start = (f32[12,16,2,128]{3,2,1,0:T(2,128)S(1)}, f32[12,16,2,128]{3,2,1,0:T(2,128)}, u32[]{:S(2)}) copy-start(f32[12,16,2,128]{3,2,1,0:T(2,128)} %param.5) | copy-start | bytes 589828
  6.3 14.7 %copy-start.1 = (f32[7,7,2,128,128]{4,3,2,1,0:T(8,128)S(1)}, f32[7,7,2,128,128]{4,3,2,1,0:T(8,128)}, u32[]{:S(2)}) copy-start(f32[7,7,2,128,128]{4,3,2,1,0:T(8,128)} %blocks_ref.1) | copy-start | bytes 19267588
  6.4 5.0 %collective-permute-start.1 = (f32[2,36,128]{2,0,1:T(2,128)S(1)}, f32[2,36,128]{2,0,1:T(2,128)S(1)}, u32[]{:S(2)}, u32[]{:S(2)}) collective-permute-start(f32[2,36,128]{2,0,1:T(2,128)S(1)} %bitcast.46), channel_id=1, source_target_pairs={{0,1},{1,0},{2,3},{3,2},{4,5},{5,4},{6,7},{7,6},{8,9},{9,8},{10,11... | collective-permute-start | bytes 110600 | tf_op jit(solution)/shard_map/ppermute | solution.py:459
  6.5 4.9 %collective-permute-start = (f32[2,36,128]{2,0,1:T(2,128)S(1)}, f32[2,36,128]{2,0,1:T(2,128)S(1)}, u32[]{:S(2)}, u32[]{:S(2)}) collective-permute-start(f32[2,36,128]{2,0,1:T(2,128)S(1)} %bitcast.48), channel_id=1, source_target_pairs={{1,2},{2,1},{5,6},{6,5},{9,10},{10,9},{13,14},{14,13},{17,18},{18,... | collective-permute-start | bytes 110600 | tf_op jit(solution)/shard_map/ppermute | solution.py:459
  7.8 10.3 %collective-permute-start.4 = (f32[2,144,128]{2,0,1:T(2,128)S(1)}, f32[2,144,128]{2,0,1:T(2,128)S(1)}, u32[]{:S(2)}, u32[]{:S(2)}) collective-permute-start(f32[2,144,128]{2,0,1:T(2,128)S(1)} %bitcast.40), channel_id=1, source_target_pairs={{0,1},{1,0},{2,3},{3,2},{4,5},{5,4},{6,7},{7,6},{8,9},{9,8},{10,11... | collective-permute-start | bytes 442376 | tf_op jit(solution)/shard_map/ppermute | solution.py:459
  10.7 7.4 %collective-permute-start.6 = (f32[2,144,128]{2,0,1:T(2,128)S(1)}, f32[2,144,128]{2,0,1:T(2,128)S(1)}, u32[]{:S(2)}, u32[]{:S(2)}) collective-permute-start(f32[2,144,128]{2,0,1:T(2,128)S(1)} %bitcast.37), channel_id=1, source_target_pairs={{1,2},{2,1},{5,6},{6,5},{9,10},{10,9},{13,14},{14,13},{17,18},{18,... | collective-permute-start | bytes 442376 | tf_op jit(solution)/shard_map/ppermute | solution.py:459
  11.7 22.2 %collective-permute-start.9 = (f32[2,264,128]{2,1,0:T(8,128)S(1)}, f32[2,264,128]{2,1,0:T(8,128)S(1)}, u32[]{:S(2)}, u32[]{:S(2)}) collective-permute-start(f32[2,264,128]{2,1,0:T(8,128)S(1)} %copy.22.refs_0_), channel_id=1, source_target_pairs={{0,24},{4,28},{8,0},{12,4},{16,8},{20,12},{24,16},{28,20},{1,25},{... | collective-permute-start | bytes 811016 | tf_op jit(solution)/shard_map/ppermute | solution.py:466
  17.2 16.8 %collective-permute-start.8 = (f32[2,264,128]{2,1,0:T(8,128)S(1)}, f32[2,264,128]{2,1,0:T(8,128)S(1)}, u32[]{:S(2)}, u32[]{:S(2)}) collective-permute-start(f32[2,264,128]{2,1,0:T(8,128)S(1)} %copy.22.refs_0_), channel_id=1, source_target_pairs={{0,8},{4,12},{8,16},{12,20},{16,24},{20,28},{24,0},{28,4},{1,9},{5... | collective-permute-start | bytes 811016 | tf_op jit(solution)/shard_map/ppermute | solution.py:466
  17.2 16.8 %collective-permute-start.7 = (f32[2,264,128]{2,1,0:T(8,128)S(1)}, f32[2,264,128]{2,1,0:T(8,128)S(1)}, u32[]{:S(2)}, u32[]{:S(2)}) collective-permute-start(f32[2,264,128]{2,1,0:T(8,128)S(1)} %copy.22.refs_0_), channel_id=1, source_target_pairs={{0,4},{4,0},{8,12},{12,8},{16,20},{20,16},{24,28},{28,24},{1,5},{5... | collective-permute-start | bytes 811016 | tf_op jit(solution)/shard_map/ppermute | solution.py:459
  18.2 22.0 %collective-permute-start.5 = (f32[2,264,128]{2,1,0:T(8,128)S(1)}, f32[2,264,128]{2,1,0:T(8,128)S(1)}, u32[]{:S(2)}, u32[]{:S(2)}) collective-permute-start(f32[2,264,128]{2,1,0:T(8,128)S(1)} %copy.16), channel_id=1, source_target_pairs={{0,16},{4,20},{8,24},{12,28},{16,0},{20,4},{24,8},{28,12},{1,17},{... | collective-permute-start | bytes 811016 | tf_op jit(solution)/shard_map/ppermute | solution.py:466
  34.1 18.7 %collective-permute-start.15 = (f32[2,2,264,128]{3,2,1,0:T(8,128)S(1)}, f32[2,2,264,128]{3,2,1,0:T(8,128)S(1)}, u32[]{:S(2)}, u32[]{:S(2)}) collective-permute-start(f32[2,2,264,128]{3,2,1,0:T(8,128)S(1)} %pad_maximum_fusion.1), channel_id=1, source_target_pairs={{0,4},{4,0},{8,12},{12,8},{16,20},{20,16},{24,28},{28,24},{1,5},{5... | collective-permute-start | bytes 1622024 | tf_op jit(solution)/shard_map/ppermute | solution.py:459
  40.2 14.8 %collective-permute-start.14 = (f32[1,2,264,128]{3,2,1,0:T(8,128)S(1)}, f32[1,2,264,128]{3,2,1,0:T(8,128)S(1)}, u32[]{:S(2)}, u32[]{:S(2)}) collective-permute-start(f32[1,2,264,128]{3,2,1,0:T(8,128)S(1)} %bitcast.26), channel_id=1, source_target_pairs={{0,4},{4,0},{8,12},{12,8},{16,20},{20,16},{24,28},{28,24},{1,5},{5... | collective-permute-start | bytes 811016 | tf_op jit(solution)/shard_map/ppermute | solution.py:459
  43.1 6.3 %collective-permute-start.10 = (f32[2,32,192]{2,1,0:T(8,128)S(1)}, f32[2,32,192]{2,1,0:T(8,128)S(1)}, u32[]{:S(2)}, u32[]{:S(2)}) collective-permute-start(f32[2,32,192]{2,1,0:T(8,128)S(1)} %get-tuple-element.41), channel_id=1, source_target_pairs={{0,8},{4,12},{8,16},{12,20},{16,24},{20,28},{24,0},{28,4},{1,9},{5... | collective-permute-start | bytes 147464 | tf_op jit(solution)/shard_map/ppermute | solution.py:466
  43.1 8.7 %collective-permute-start.11 = (f32[2,32,192]{2,1,0:T(8,128)S(1)}, f32[2,32,192]{2,1,0:T(8,128)S(1)}, u32[]{:S(2)}, u32[]{:S(2)}) collective-permute-start(f32[2,32,192]{2,1,0:T(8,128)S(1)} %get-tuple-element.42), channel_id=1, source_target_pairs={{0,16},{4,20},{8,24},{12,28},{16,0},{20,4},{24,8},{28,12},{1,17},{... | collective-permute-start | bytes 147464 | tf_op jit(solution)/shard_map/ppermute | solution.py:466
  45.1 6.6 %collective-permute-start.12 = (f32[2,32,192]{2,1,0:T(8,128)S(1)}, f32[2,32,192]{2,1,0:T(8,128)S(1)}, u32[]{:S(2)}, u32[]{:S(2)}) collective-permute-start(f32[2,32,192]{2,1,0:T(8,128)S(1)} %get-tuple-element.43), channel_id=1, source_target_pairs={{0,24},{4,28},{8,0},{12,4},{16,8},{20,12},{24,16},{28,20},{1,25},{... | collective-permute-start | bytes 147464 | tf_op jit(solution)/shard_map/ppermute | solution.py:466
  51.8 6.1 %collective-permute-start.13 = (f32[4,32,192]{2,1,0:T(8,128)S(1)}, f32[4,32,192]{2,1,0:T(8,128)S(1)}, u32[]{:S(2)}, u32[]{:S(2)}) collective-permute-start(f32[4,32,192]{2,1,0:T(8,128)S(1)} %pad_maximum_fusion.5), channel_id=1, source_target_pairs={{0,4},{4,0},{8,12},{12,8},{16,20},{20,16},{24,28},{28,24},{1,5},{5... | collective-permute-start | bytes 294920 | tf_op jit(solution)/shard_map/ppermute | solution.py:459
  62.4 1.8 %collective-permute-start.16 = (f32[7,7,2,8,128]{4,3,2,1,0:T(8,128)S(1)}, f32[7,7,2,8,128]{4,3,2,1,0:T(8,128)S(1)}, u32[]{:S(2)}, u32[]{:S(2)}) collective-permute-start(f32[7,7,2,8,128]{4,3,2,1,0:T(8,128)S(1)} %get-tuple-element.52), channel_id=1, source_target_pairs={{0,1},{1,0},{2,3},{3,2},{4,5},{5,4},{6,7},{7,6},{8,9},{9,8},{10,11... | collective-permute-start | bytes 1204232 | tf_op jit(solution)/shard_map/ppermute | solution.py:459
  64.3 8.5 %collective-permute-start.17 = (f32[4,7,2,8,128]{4,3,2,1,0:T(8,128)S(1)}, f32[4,7,2,8,128]{4,3,2,1,0:T(8,128)S(1)}, u32[]{:S(2)}, u32[]{:S(2)}) collective-permute-start(f32[4,7,2,8,128]{4,3,2,1,0:T(8,128)S(1)} %slice.46), channel_id=1, source_target_pairs={{0,2},{1,3},{2,0},{3,1},{4,6},{5,7},{6,4},{7,5},{8,10},{9,11},{10,... | collective-permute-start | bytes 688136 | tf_op jit(solution)/shard_map/ppermute | solution.py:466
  64.4 11.3 %collective-permute-start.18 = (f32[3,7,2,8,128]{4,3,2,1,0:T(8,128)S(1)}, f32[3,7,2,8,128]{4,3,2,1,0:T(8,128)S(1)}, u32[]{:S(2)}, u32[]{:S(2)}) collective-permute-start(f32[3,7,2,8,128]{4,3,2,1,0:T(8,128)S(1)} %slice.47), channel_id=1, source_target_pairs={{0,2},{1,3},{2,0},{3,1},{4,6},{5,7},{6,4},{7,5},{8,10},{9,11},{10,... | collective-permute-start | bytes 516104 | tf_op jit(solution)/shard_map/ppermute | solution.py:466
  72.8 3.0 %collective-permute-start.19 = (f32[4,7,2,8,128]{4,3,2,1,0:T(8,128)S(1)}, f32[4,7,2,8,128]{4,3,2,1,0:T(8,128)S(1)}, u32[]{:S(2)}, u32[]{:S(2)}) collective-permute-start(f32[4,7,2,8,128]{4,3,2,1,0:T(8,128)S(1)} %slice_add_fusion.1), channel_id=1, source_target_pairs={{0,1},{1,0},{2,3},{3,2},{4,5},{5,4},{6,7},{7,6},{8,9},{9,8},{10,11... | collective-permute-start | bytes 688136 | tf_op jit(solution)/shard_map/ppermute | solution.py:459
  75.7 1.5 %collective-permute-start.20 = (f32[3,7,2,8,128]{4,3,2,1,0:T(8,128)S(1)}, f32[3,7,2,8,128]{4,3,2,1,0:T(8,128)S(1)}, u32[]{:S(2)}, u32[]{:S(2)}) collective-permute-start(f32[3,7,2,8,128]{4,3,2,1,0:T(8,128)S(1)} %slice_add_fusion), channel_id=1, source_target_pairs={{0,1},{1,0},{2,3},{3,2},{4,5},{5,4},{6,7},{7,6},{8,9},{9,8},{10,11... | collective-permute-start | bytes 516104 | tf_op jit(solution)/shard_map/ppermute | solution.py:459

commit v14 on v13

--- a/solution.py
+++ b/solution.py
@@ -128,8 +128,7 @@
 
     acc[...] = jnp.zeros_like(acc)
 
-    @pl.loop(0, span)
-    def _(a):
+    def one_lag(a):
         for b in range(span):
             real_high, real_low = split(blocks_ref[a, b, 0])
             imag_high, imag_low = split(blocks_ref[a, b, 1])
@@ -137,7 +136,14 @@
             store_block(w_low, (a, b), real_low, imag_low)
 
         at = pl.ds(pl.multiple_of((a // 2) * 2 * pitch, 2 * pitch), mid_rows * pitch)
-        acc[...] += products(x_high[a % 2, at, :], x_low[a % 2, at, :], w_high[a], w_low[a])
+        return products(x_high[a % 2, at, :], x_low[a % 2, at, :], w_high[a], w_low[a])
+
+    @pl.loop(0, span // 2)
+    def _(pair):
+        acc[...] += one_lag(2 * pair) + one_lag(2 * pair + 1)
+
+    if span % 2:
+        acc[...] += one_lag(span - 1)
 
     step_rows = largest_divisor(mid_rows, 18)
 

time: 78.4 us -> 77.8 us (level)
  transfers between devices with their start and end apart: 21 -> 21, of which waited for: 9 -> 9; matrix products, arithmetic and copies ran while one was open for 2% -> 2% of each run, Pallas kernels for 27% -> 26%
where the time goes in v14:
time: 77.8 us; the launch traced here: 77.7 us
  starting transfers between devices  27 us (35%)
  Pallas kernels  24.8 us (32%)
  waiting for transfers between devices  20 us (26%)
  local copies, waits for them, and re-layouts  3.3 us (4%)
  other arithmetic  1.52 us (2%)
  between operations  1.07 us (1%)
    ppermute x8, waiting for transfers between devices, shifted(): lax.ppermute(value, axis, [(i, (i + shift) % peers) for i in range(peers)])  15.2 us
    ppermute x8, starting transfers between devices, shifted(): lax.ppermute(value, axis, [(i, (i + shift) % peers) for i in range(peers)])  14.1 us
    ppermute x13, starting transfers between devices, swap(): return lax.ppermute(value, axis, pairs)  12.8 us
    pallas_call x1, Pallas kernels, first_sweep(): pl.pallas_call(functools.partial(first_sweep_kernel, (rows, cols, span, p...  12.4 us
    pallas_call x1, Pallas kernels, second_sweep(): pl.pallas_call(functools.partial(second_sweep_kernel, (rows, cols, span,...  5.34 us
    ppermute x13, waiting for transfers between devices, swap(): return lax.ppermute(value, axis, pairs)  4.78 us
    pallas_call x1, Pallas kernels, correlate(): pl.pallas_call(functools.partial(correlate_kernel, (rows, cols, span, pee...  4.51 us
    pallas_call x2, Pallas kernels, spread(): pl.pallas_call(functools.partial(spread_kernel, (rows, cols, span, peers)...  2.57 us
  transfers between devices with their start and end apart: 21, of which 9 were waited for; matrix products, arithmetic and copies ran while one was open for 2% of the time, Pallas kernels for 26%

profile of v14, /device:TPU:0, one launch (start us, length us, event | category | flops | bytes accessed | tf_op | source)
XLA Modules:
  0.0 77.7 jit_solution(1415434642756761957)
XLA Ops:
  0.6 0.0 copy-start.2
  0.7 1.0 %copy.31 = f32[12,16,2,128]{3,1,0,2:T(8,128)S(1)} copy(f32[12,16,2,128]{3,2,1,0:T(2,128)} %param.4) | data formatting | bytes 393216 | tf_op args[0]
  1.7 3.0 %collective-permute-start.3 = (f32[2,96,128]{2,1,0:T(8,128)S(1)}, f32[2,96,128]{2,1,0:T(8,128)S(1)}, u32[]{:S(2)}, u32[]{:S(2)}) collective-permute-start(f32[2,96,128]{2,1,0:T(8,128)S(1)} %bitcast.44), channel_id=1, source_target_pairs={{0,4},{4,0},{8,12},{12,8},{16,20},{20,16},{24,28},{28,24},{1,5},{5... | collective-permute-start | bytes 294920 | tf_op jit(solution)/shard_map/ppermute | solution.py:465
  4.7 0.7 collective-permute-start.2
  5.4 0.0 copy-start
  5.4 0.9 %copy-done = f32[12,16,2,128]{3,2,1,0:T(2,128)S(1)} copy-done((f32[12,16,2,128]{3,2,1,0:T(2,128)S(1)}, f32[12,16,2,128]{3,2,1,0:T(2,128)}, u32[]{:S(2)}) %copy-start) | copy-done | bytes 196632
  6.3 0.0 copy-start.1
  6.4 0.1 collective-permute-start.1
  6.5 0.8 %collective-permute-start = (f32[2,36,128]{2,0,1:T(2,128)S(1)}, f32[2,36,128]{2,0,1:T(2,128)S(1)}, u32[]{:S(2)}, u32[]{:S(2)}) collective-permute-start(f32[2,36,128]{2,0,1:T(2,128)S(1)} %bitcast.48), channel_id=1, source_target_pairs={{1,2},{2,1},{5,6},{6,5},{9,10},{10,9},{13,14},{14,13},{17,18},{18,... | collective-permute-start | bytes 110600 | tf_op jit(solution)/shard_map/ppermute | solution.py:465
  7.3 0.2 collective-permute-done.3
  7.5 0.0 collective-permute-done.2
  7.6 0.1 copy.17
  7.7 0.1 copy.15
  7.8 2.9 %collective-permute-start.4 = (f32[2,144,128]{2,0,1:T(2,128)S(1)}, f32[2,144,128]{2,0,1:T(2,128)S(1)}, u32[]{:S(2)}, u32[]{:S(2)}) collective-permute-start(f32[2,144,128]{2,0,1:T(2,128)S(1)} %bitcast.40), channel_id=1, source_target_pairs={{0,1},{1,0},{2,3},{3,2},{4,5},{5,4},{6,7},{7,6},{8,9},{9,8},{10,11... | collective-permute-start | bytes 442376 | tf_op jit(solution)/shard_map/ppermute | solution.py:465
  10.7 0.7 collective-permute-start.6
  11.4 0.0 collective-permute-done.1
  11.4 0.0 collective-permute-done
  11.5 0.2 copy.14
  11.7 5.5 %collective-permute-start.9 = (f32[2,264,128]{2,1,0:T(8,128)S(1)}, f32[2,264,128]{2,1,0:T(8,128)S(1)}, u32[]{:S(2)}, u32[]{:S(2)}) collective-permute-start(f32[2,264,128]{2,1,0:T(8,128)S(1)} %copy.22.refs_0_), channel_id=1, source_target_pairs={{0,24},{4,28},{8,0},{12,4},{16,8},{20,12},{24,16},{28,20},{1,25},{... | collective-permute-start | bytes 811016 | tf_op jit(solution)/shard_map/ppermute | solution.py:472
  17.2 0.0 collective-permute-start.8
  17.2 0.9 %collective-permute-start.7 = (f32[2,264,128]{2,1,0:T(8,128)S(1)}, f32[2,264,128]{2,1,0:T(8,128)S(1)}, u32[]{:S(2)}, u32[]{:S(2)}) collective-permute-start(f32[2,264,128]{2,1,0:T(8,128)S(1)} %copy.22.refs_0_), channel_id=1, source_target_pairs={{0,4},{4,0},{8,12},{12,8},{16,20},{20,16},{24,28},{28,24},{1,5},{5... | collective-permute-start | bytes 811016 | tf_op jit(solution)/shard_map/ppermute | solution.py:465
  18.1 0.0 collective-permute-done.4
  18.1 0.0 collective-permute-done.6
  18.2 2.7 %collective-permute-start.5 = (f32[2,264,128]{2,1,0:T(8,128)S(1)}, f32[2,264,128]{2,1,0:T(8,128)S(1)}, u32[]{:S(2)}, u32[]{:S(2)}) collective-permute-start(f32[2,264,128]{2,1,0:T(8,128)S(1)} %copy.16), channel_id=1, source_target_pairs={{0,16},{4,20},{8,24},{12,28},{16,0},{20,4},{24,8},{28,12},{1,17},{... | collective-permute-start | bytes 811016 | tf_op jit(solution)/shard_map/ppermute | solution.py:472
  20.8 0.1 select_maximum_fusion.source_ref
  21.0 0.0 copy-done.2
  21.0 0.0 copy-done.1
  21.0 12.4 %first_sweep.1 = (f32[18,24,256]{2,1,0:T(8,128)S(1)}, f32[12,16,256]{2,1,0:T(8,128)S(1)}, bf16[7,7,256,256]{3,2,1,0:T(8,128)(2,1)S(1)}, bf16[7,7,256,256]{3,2,1,0:T(8,128)(2,1)S(1)}) custom-call(f32[2,24,32,128]{3,2,1,0:T(8,128)S(1)} %select_maximum_fusion.source_ref, f32[2,128,128]{2,1,0:T(8,128)S(1)} %copy-done.2, f32[7,7,2,128,128]{4,3,2,1,0:T(8,128)S(1)} %copy-done.1), custom_call_target="tpu_custom_call" | custom-call | flops 8323596288 | bytes 19267584 | tf_op jit(solution)/shard_map/first_sweep/pallas_call | solution.py:172
  33.4 0.0 collective-permute-done.9.refs_3_
  33.4 0.0 collective-permute-done.8.refs_1_
  33.5 0.0 collective-permute-done.7.refs_4_
  33.5 0.1 collective-permute-start.15
  33.6 5.3 %second_sweep.1 = (f32[12,16,256]{2,1,0:T(8,128)S(1)}, f32[2,32,192]{2,1,0:T(8,128)S(1)}, f32[2,32,192]{2,1,0:T(8,128)S(1)}, f32[2,32,192]{2,1,0:T(8,128)S(1)}, f32[2,32,192]{2,1,0:T(8,128)S(1)}) custom-call(f32[18,24,256]{2,1,0:T(8,128)S(1)} %get-tuple-element.32.second_ref, f32[12,16,256]{2,1,0:T(8,128)S(1)} %get-tuple-element.33.source_ref, ...), custom_call_target="tpu_custom_call" | custom-call | flops 3699376128 | bytes 12845056 | tf_op jit(solution)/shard_map/second_sweep/pallas_call | solution.py:270
  38.9 1.2 %collective-permute-done.5.refs_2_ = f32[2,264,128]{2,1,0:T(8,128)S(1)} collective-permute-done((f32[2,264,128]{2,1,0:T(8,128)S(1)}, f32[2,264,128]{2,1,0:T(8,128)S(1)}, u32[]{:S(2)}, u32[]{:S(2)}) %collective-permute-start.5) | collective-permute-done | bytes 270368 | tf_op jit(solution)/shard_map/ppermute | solution.py:472
  40.2 2.9 %collective-permute-start.14 = (f32[1,2,264,128]{3,2,1,0:T(8,128)S(1)}, f32[1,2,264,128]{3,2,1,0:T(8,128)S(1)}, u32[]{:S(2)}, u32[]{:S(2)}) collective-permute-start(f32[1,2,264,128]{3,2,1,0:T(8,128)S(1)} %bitcast.26), channel_id=1, source_target_pairs={{0,4},{4,0},{8,12},{12,8},{16,20},{20,16},{24,28},{28,24},{1,5},{5... | collective-permute-start | bytes 811016 | tf_op jit(solution)/shard_map/ppermute | solution.py:465
  43.1 0.0 collective-permute-start.10
  43.1 2.1 %collective-permute-start.11 = (f32[2,32,192]{2,1,0:T(8,128)S(1)}, f32[2,32,192]{2,1,0:T(8,128)S(1)}, u32[]{:S(2)}, u32[]{:S(2)}) collective-permute-start(f32[2,32,192]{2,1,0:T(8,128)S(1)} %get-tuple-element.42), channel_id=1, source_target_pairs={{0,16},{4,20},{8,24},{12,28},{16,0},{20,4},{24,8},{28,12},{1,17},{... | collective-permute-start | bytes 147464 | tf_op jit(solution)/shard_map/ppermute | solution.py:472
  45.1 1.8 %collective-permute-start.12 = (f32[2,32,192]{2,1,0:T(8,128)S(1)}, f32[2,32,192]{2,1,0:T(8,128)S(1)}, u32[]{:S(2)}, u32[]{:S(2)}) collective-permute-start(f32[2,32,192]{2,1,0:T(8,128)S(1)} %get-tuple-element.43), channel_id=1, source_target_pairs={{0,24},{4,28},{8,0},{12,4},{16,8},{20,12},{24,16},{28,20},{1,25},{... | collective-permute-start | bytes 147464 | tf_op jit(solution)/shard_map/ppermute | solution.py:472
  46.9 2.4 %collective-permute-done.10.refs_1_ = f32[2,32,192]{2,1,0:T(8,128)S(1)} collective-permute-done((f32[2,32,192]{2,1,0:T(8,128)S(1)}, f32[2,32,192]{2,1,0:T(8,128)S(1)}, u32[]{:S(2)}, u32[]{:S(2)}) %collective-permute-start.10) | collective-permute-done | bytes 49184 | tf_op jit(solution)/shard_map/ppermute | solution.py:472
  49.3 2.4 %collective-permute-done.11.refs_2_ = f32[2,32,192]{2,1,0:T(8,128)S(1)} collective-permute-done((f32[2,32,192]{2,1,0:T(8,128)S(1)}, f32[2,32,192]{2,1,0:T(8,128)S(1)}, u32[]{:S(2)}, u32[]{:S(2)}) %collective-permute-start.11) | collective-permute-done | bytes 49184 | tf_op jit(solution)/shard_map/ppermute | solution.py:472
  51.7 0.0 collective-permute-done.12.refs_3_
  51.8 0.7 collective-permute-start.13
  52.5 0.0 collective-permute-done.15.refs_5_
  52.5 2.2 %spread.2 = (bf16[7,1536,256]{2,1,0:T(8,128)(2,1)S(1)}, bf16[7,1536,256]{2,1,0:T(8,128)(2,1)S(1)}) custom-call(f32[2,264,128]{2,1,0:T(8,128)S(1)} %copy.22.refs_0_, f32[2,264,128]{2,1,0:T(8,128)S(1)} %collective-permute-done.8.refs_1_, f32[2,264,128]{2,1,0:T(8,128)S(1)} %collective-permute-done.5.refs_2_, f32[2,264,128]{2,1,0:T(8,128)S(1)} %collective-permute-done.9.refs_3_, ...), custom_call_target="tpu_custom_call" | custom-call | bytes 1892352 | tf_op jit(solution)/shard_map/spread/pallas_call | solution.py:338
  54.7 0.0 collective-permute-done.14.refs_0_
  54.7 0.3 spread.3
  55.1 2.3 %collective-permute-done.13.refs_4_ = f32[4,32,192]{2,1,0:T(8,128)S(1)} collective-permute-done((f32[4,32,192]{2,1,0:T(8,128)S(1)}, f32[4,32,192]{2,1,0:T(8,128)S(1)}, u32[]{:S(2)}, u32[]{:S(2)}) %collective-permute-start.13) | collective-permute-done | bytes 98336 | tf_op jit(solution)/shard_map/ppermute | solution.py:465
  57.3 4.5 %correlate.1 = (f32[7,7,2,8,128]{4,3,2,1,0:T(8,128)S(1)}, f32[7,7,2,8,128]{4,3,2,1,0:T(8,128)S(1)}) custom-call(f32[2,32,192]{2,1,0:T(8,128)S(1)} %get-tuple-element.40.refs_0_, f32[2,32,192]{2,1,0:T(8,128)S(1)} %collective-permute-done.10.refs_1_, f32[2,32,192]{2,1,0:T(8,128)S(1)} %collective-permute-done.11.refs_2_, ...), custom_call_target="tpu_custom_call" | custom-call | flops 3699376128 | bytes 802816 | tf_op jit(solution)/shard_map/correlate/pallas_call | solution.py:419
  61.8 0.1 collective-permute-start.16
  61.9 0.8 reshape.53
  62.7 0.9 %collective-permute-done.16 = f32[7,7,2,8,128]{4,3,2,1,0:T(8,128)S(1)} collective-permute-done((f32[7,7,2,8,128]{4,3,2,1,0:T(8,128)S(1)}, f32[7,7,2,8,128]{4,3,2,1,0:T(8,128)S(1)}, u32[]{:S(2)}, u32[]{:S(2)}) %collective-permute-start.16) | collective-permute-done | bytes 401440 | tf_op jit(solution)/shard_map/ppermute | solution.py:465
  63.6 0.1 add.22
  63.7 0.5 collective-permute-start.17
  64.3 1.6 %collective-permute-start.18 = (f32[3,7,2,8,128]{4,3,2,1,0:T(8,128)S(1)}, f32[3,7,2,8,128]{4,3,2,1,0:T(8,128)S(1)}, u32[]{:S(2)}, u32[]{:S(2)}) collective-permute-start(f32[3,7,2,8,128]{4,3,2,1,0:T(8,128)S(1)} %slice.47), channel_id=1, source_target_pairs={{0,2},{1,3},{2,0},{3,1},{4,6},{5,7},{6,4},{7,5},{8,10},{9,11},{10,... | collective-permute-start | bytes 516104 | tf_op jit(solution)/shard_map/ppermute | solution.py:472
  65.9 6.3 %collective-permute-done.17 = f32[4,7,2,8,128]{4,3,2,1,0:T(8,128)S(1)} collective-permute-done((f32[4,7,2,8,128]{4,3,2,1,0:T(8,128)S(1)}, f32[4,7,2,8,128]{4,3,2,1,0:T(8,128)S(1)}, u32[]{:S(2)}, u32[]{:S(2)}) %collective-permute-start.17) | collective-permute-done | bytes 229408 | tf_op jit(solution)/shard_map/ppermute | solution.py:472
  72.3 0.1 collective-permute-start.19
  72.3 2.8 %collective-permute-done.18 = f32[3,7,2,8,128]{4,3,2,1,0:T(8,128)S(1)} collective-permute-done((f32[3,7,2,8,128]{4,3,2,1,0:T(8,128)S(1)}, f32[3,7,2,8,128]{4,3,2,1,0:T(8,128)S(1)}, u32[]{:S(2)}, u32[]{:S(2)}) %collective-permute-start.18) | collective-permute-done | bytes 172064 | tf_op jit(solution)/shard_map/ppermute | solution.py:472
  75.1 0.1 collective-permute-start.20
  75.2 0.0 collective-permute-done.19
  75.3 1.4 %collective-permute-done.20 = f32[3,7,2,8,128]{4,3,2,1,0:T(8,128)S(1)} collective-permute-done((f32[3,7,2,8,128]{4,3,2,1,0:T(8,128)S(1)}, f32[3,7,2,8,128]{4,3,2,1,0:T(8,128)S(1)}, u32[]{:S(2)}, u32[]{:S(2)}) %collective-permute-start.20) | collective-permute-done | bytes 172064 | tf_op jit(solution)/shard_map/ppermute | solution.py:465
  76.6 0.1 fusion.6
  76.7 1.0 %pad_maximum_fusion = f32[7,7,2,16,128]{4,3,2,1,0:T(8,128)} fusion(f32[7,7,2,8,128]{4,3,2,1,0:T(8,128)S(1)} %get-tuple-element.57, f32[7,7,2,8,128]{4,3,2,1,0:T(8,128)S(1)} %get-tuple-element.56), kind=kLoop, calls=%fused_computation | loop fusion | flops 200704 | bytes 1605632 | tf_op jit(solution)/shard_map/concatenate | solution.py:549
  (27 shorter events, 0.5 us)
Async XLA Ops:
  0.6 20.4 %copy-start.2 = (f32[2,128,128]{2,1,0:T(8,128)S(1)}, f32[2,128,128]{2,1,0:T(8,128)}, u32[]{:S(2)}) copy-start(f32[2,128,128]{2,1,0:T(8,128)} %inverse_ref.3) | copy-start | bytes 393220
  1.7 5.8 %collective-permute-start.3 = (f32[2,96,128]{2,1,0:T(8,128)S(1)}, f32[2,96,128]{2,1,0:T(8,128)S(1)}, u32[]{:S(2)}, u32[]{:S(2)}) collective-permute-start(f32[2,96,128]{2,1,0:T(8,128)S(1)} %bitcast.44), channel_id=1, source_target_pairs={{0,4},{4,0},{8,12},{12,8},{16,20},{20,16},{24,28},{28,24},{1,5},{5... | collective-permute-start | bytes 294920 | tf_op jit(solution)/shard_map/ppermute | solution.py:465
  4.7 2.8 %collective-permute-start.2 = (f32[2,96,128]{2,1,0:T(8,128)S(1)}, f32[2,96,128]{2,1,0:T(8,128)S(1)}, u32[]{:S(2)}, u32[]{:S(2)}) collective-permute-start(f32[2,96,128]{2,1,0:T(8,128)S(1)} %bitcast.43), channel_id=1, source_target_pairs={{4,8},{8,4},{12,16},{16,12},{20,24},{24,20},{5,9},{9,5},{13,17},{1... | collective-permute-start | bytes 294920 | tf_op jit(solution)/shard_map/ppermute | solution.py:465
  5.4 0.9 %copy-start = (f32[12,16,2,128]{3,2,1,0:T(2,128)S(1)}, f32[12,16,2,128]{3,2,1,0:T(2,128)}, u32[]{:S(2)}) copy-start(f32[12,16,2,128]{3,2,1,0:T(2,128)} %param.5) | copy-start | bytes 589828
  6.3 14.7 %copy-start.1 = (f32[7,7,2,128,128]{4,3,2,1,0:T(8,128)S(1)}, f32[7,7,2,128,128]{4,3,2,1,0:T(8,128)}, u32[]{:S(2)}) copy-start(f32[7,7,2,128,128]{4,3,2,1,0:T(8,128)} %blocks_ref.1) | copy-start | bytes 19267588
  6.4 5.0 %collective-permute-start.1 = (f32[2,36,128]{2,0,1:T(2,128)S(1)}, f32[2,36,128]{2,0,1:T(2,128)S(1)}, u32[]{:S(2)}, u32[]{:S(2)}) collective-permute-start(f32[2,36,128]{2,0,1:T(2,128)S(1)} %bitcast.46), channel_id=1, source_target_pairs={{0,1},{1,0},{2,3},{3,2},{4,5},{5,4},{6,7},{7,6},{8,9},{9,8},{10,11... | collective-permute-start | bytes 110600 | tf_op jit(solution)/shard_map/ppermute | solution.py:465
  6.5 4.9 %collective-permute-start = (f32[2,36,128]{2,0,1:T(2,128)S(1)}, f32[2,36,128]{2,0,1:T(2,128)S(1)}, u32[]{:S(2)}, u32[]{:S(2)}) collective-permute-start(f32[2,36,128]{2,0,1:T(2,128)S(1)} %bitcast.48), channel_id=1, source_target_pairs={{1,2},{2,1},{5,6},{6,5},{9,10},{10,9},{13,14},{14,13},{17,18},{18,... | collective-permute-start | bytes 110600 | tf_op jit(solution)/shard_map/ppermute | solution.py:465
  7.8 10.3 %collective-permute-start.4 = (f32[2,144,128]{2,0,1:T(2,128)S(1)}, f32[2,144,128]{2,0,1:T(2,128)S(1)}, u32[]{:S(2)}, u32[]{:S(2)}) collective-permute-start(f32[2,144,128]{2,0,1:T(2,128)S(1)} %bitcast.40), channel_id=1, source_target_pairs={{0,1},{1,0},{2,3},{3,2},{4,5},{5,4},{6,7},{7,6},{8,9},{9,8},{10,11... | collective-permute-start | bytes 442376 | tf_op jit(solution)/shard_map/ppermute | solution.py:465
  10.7 7.4 %collective-permute-start.6 = (f32[2,144,128]{2,0,1:T(2,128)S(1)}, f32[2,144,128]{2,0,1:T(2,128)S(1)}, u32[]{:S(2)}, u32[]{:S(2)}) collective-permute-start(f32[2,144,128]{2,0,1:T(2,128)S(1)} %bitcast.37), channel_id=1, source_target_pairs={{1,2},{2,1},{5,6},{6,5},{9,10},{10,9},{13,14},{14,13},{17,18},{18,... | collective-permute-start | bytes 442376 | tf_op jit(solution)/shard_map/ppermute | solution.py:465
  11.7 21.7 %collective-permute-start.9 = (f32[2,264,128]{2,1,0:T(8,128)S(1)}, f32[2,264,128]{2,1,0:T(8,128)S(1)}, u32[]{:S(2)}, u32[]{:S(2)}) collective-permute-start(f32[2,264,128]{2,1,0:T(8,128)S(1)} %copy.22.refs_0_), channel_id=1, source_target_pairs={{0,24},{4,28},{8,0},{12,4},{16,8},{20,12},{24,16},{28,20},{1,25},{... | collective-permute-start | bytes 811016 | tf_op jit(solution)/shard_map/ppermute | solution.py:472
  17.2 16.2 %collective-permute-start.8 = (f32[2,264,128]{2,1,0:T(8,128)S(1)}, f32[2,264,128]{2,1,0:T(8,128)S(1)}, u32[]{:S(2)}, u32[]{:S(2)}) collective-permute-start(f32[2,264,128]{2,1,0:T(8,128)S(1)} %copy.22.refs_0_), channel_id=1, source_target_pairs={{0,8},{4,12},{8,16},{12,20},{16,24},{20,28},{24,0},{28,4},{1,9},{5... | collective-permute-start | bytes 811016 | tf_op jit(solution)/shard_map/ppermute | solution.py:472
  17.2 16.3 %collective-permute-start.7 = (f32[2,264,128]{2,1,0:T(8,128)S(1)}, f32[2,264,128]{2,1,0:T(8,128)S(1)}, u32[]{:S(2)}, u32[]{:S(2)}) collective-permute-start(f32[2,264,128]{2,1,0:T(8,128)S(1)} %copy.22.refs_0_), channel_id=1, source_target_pairs={{0,4},{4,0},{8,12},{12,8},{16,20},{20,16},{24,28},{28,24},{1,5},{5... | collective-permute-start | bytes 811016 | tf_op jit(solution)/shard_map/ppermute | solution.py:465
  18.2 22.0 %collective-permute-start.5 = (f32[2,264,128]{2,1,0:T(8,128)S(1)}, f32[2,264,128]{2,1,0:T(8,128)S(1)}, u32[]{:S(2)}, u32[]{:S(2)}) collective-permute-start(f32[2,264,128]{2,1,0:T(8,128)S(1)} %copy.16), channel_id=1, source_target_pairs={{0,16},{4,20},{8,24},{12,28},{16,0},{20,4},{24,8},{28,12},{1,17},{... | collective-permute-start | bytes 811016 | tf_op jit(solution)/shard_map/ppermute | solution.py:472
  33.5 19.0 %collective-permute-start.15 = (f32[2,2,264,128]{3,2,1,0:T(8,128)S(1)}, f32[2,2,264,128]{3,2,1,0:T(8,128)S(1)}, u32[]{:S(2)}, u32[]{:S(2)}) collective-permute-start(f32[2,2,264,128]{3,2,1,0:T(8,128)S(1)} %pad_maximum_fusion.1), channel_id=1, source_target_pairs={{0,4},{4,0},{8,12},{12,8},{16,20},{20,16},{24,28},{28,24},{1,5},{5... | collective-permute-start | bytes 1622024 | tf_op jit(solution)/shard_map/ppermute | solution.py:465
  40.2 14.6 %collective-permute-start.14 = (f32[1,2,264,128]{3,2,1,0:T(8,128)S(1)}, f32[1,2,264,128]{3,2,1,0:T(8,128)S(1)}, u32[]{:S(2)}, u32[]{:S(2)}) collective-permute-start(f32[1,2,264,128]{3,2,1,0:T(8,128)S(1)} %bitcast.26), channel_id=1, source_target_pairs={{0,4},{4,0},{8,12},{12,8},{16,20},{20,16},{24,28},{28,24},{1,5},{5... | collective-permute-start | bytes 811016 | tf_op jit(solution)/shard_map/ppermute | solution.py:465
  43.1 6.3 %collective-permute-start.10 = (f32[2,32,192]{2,1,0:T(8,128)S(1)}, f32[2,32,192]{2,1,0:T(8,128)S(1)}, u32[]{:S(2)}, u32[]{:S(2)}) collective-permute-start(f32[2,32,192]{2,1,0:T(8,128)S(1)} %get-tuple-element.41), channel_id=1, source_target_pairs={{0,8},{4,12},{8,16},{12,20},{16,24},{20,28},{24,0},{28,4},{1,9},{5... | collective-permute-start | bytes 147464 | tf_op jit(solution)/shard_map/ppermute | solution.py:472
  43.1 8.7 %collective-permute-start.11 = (f32[2,32,192]{2,1,0:T(8,128)S(1)}, f32[2,32,192]{2,1,0:T(8,128)S(1)}, u32[]{:S(2)}, u32[]{:S(2)}) collective-permute-start(f32[2,32,192]{2,1,0:T(8,128)S(1)} %get-tuple-element.42), channel_id=1, source_target_pairs={{0,16},{4,20},{8,24},{12,28},{16,0},{20,4},{24,8},{28,12},{1,17},{... | collective-permute-start | bytes 147464 | tf_op jit(solution)/shard_map/ppermute | solution.py:472
  45.1 6.6 %collective-permute-start.12 = (f32[2,32,192]{2,1,0:T(8,128)S(1)}, f32[2,32,192]{2,1,0:T(8,128)S(1)}, u32[]{:S(2)}, u32[]{:S(2)}) collective-permute-start(f32[2,32,192]{2,1,0:T(8,128)S(1)} %get-tuple-element.43), channel_id=1, source_target_pairs={{0,24},{4,28},{8,0},{12,4},{16,8},{20,12},{24,16},{28,20},{1,25},{... | collective-permute-start | bytes 147464 | tf_op jit(solution)/shard_map/ppermute | solution.py:472
  51.8 5.5 %collective-permute-start.13 = (f32[4,32,192]{2,1,0:T(8,128)S(1)}, f32[4,32,192]{2,1,0:T(8,128)S(1)}, u32[]{:S(2)}, u32[]{:S(2)}) collective-permute-start(f32[4,32,192]{2,1,0:T(8,128)S(1)} %pad_maximum_fusion.5), channel_id=1, source_target_pairs={{0,4},{4,0},{8,12},{12,8},{16,20},{20,16},{24,28},{28,24},{1,5},{5... | collective-permute-start | bytes 294920 | tf_op jit(solution)/shard_map/ppermute | solution.py:465
  61.8 1.8 %collective-permute-start.16 = (f32[7,7,2,8,128]{4,3,2,1,0:T(8,128)S(1)}, f32[7,7,2,8,128]{4,3,2,1,0:T(8,128)S(1)}, u32[]{:S(2)}, u32[]{:S(2)}) collective-permute-start(f32[7,7,2,8,128]{4,3,2,1,0:T(8,128)S(1)} %get-tuple-element.52), channel_id=1, source_target_pairs={{0,1},{1,0},{2,3},{3,2},{4,5},{5,4},{6,7},{7,6},{8,9},{9,8},{10,11... | collective-permute-start | bytes 1204232 | tf_op jit(solution)/shard_map/ppermute | solution.py:465
  63.7 8.5 %collective-permute-start.17 = (f32[4,7,2,8,128]{4,3,2,1,0:T(8,128)S(1)}, f32[4,7,2,8,128]{4,3,2,1,0:T(8,128)S(1)}, u32[]{:S(2)}, u32[]{:S(2)}) collective-permute-start(f32[4,7,2,8,128]{4,3,2,1,0:T(8,128)S(1)} %slice.46), channel_id=1, source_target_pairs={{0,2},{1,3},{2,0},{3,1},{4,6},{5,7},{6,4},{7,5},{8,10},{9,11},{10,... | collective-permute-start | bytes 688136 | tf_op jit(solution)/shard_map/ppermute | solution.py:472
  64.3 10.8 %collective-permute-start.18 = (f32[3,7,2,8,128]{4,3,2,1,0:T(8,128)S(1)}, f32[3,7,2,8,128]{4,3,2,1,0:T(8,128)S(1)}, u32[]{:S(2)}, u32[]{:S(2)}) collective-permute-start(f32[3,7,2,8,128]{4,3,2,1,0:T(8,128)S(1)} %slice.47), channel_id=1, source_target_pairs={{0,2},{1,3},{2,0},{3,1},{4,6},{5,7},{6,4},{7,5},{8,10},{9,11},{10,... | collective-permute-start | bytes 516104 | tf_op jit(solution)/shard_map/ppermute | solution.py:472
  72.3 3.0 %collective-permute-start.19 = (f32[4,7,2,8,128]{4,3,2,1,0:T(8,128)S(1)}, f32[4,7,2,8,128]{4,3,2,1,0:T(8,128)S(1)}, u32[]{:S(2)}, u32[]{:S(2)}) collective-permute-start(f32[4,7,2,8,128]{4,3,2,1,0:T(8,128)S(1)} %slice_add_fusion.1), channel_id=1, source_target_pairs={{0,1},{1,0},{2,3},{3,2},{4,5},{5,4},{6,7},{7,6},{8,9},{9,8},{10,11... | collective-permute-start | bytes 688136 | tf_op jit(solution)/shard_map/ppermute | solution.py:465
  75.1 1.5 %collective-permute-start.20 = (f32[3,7,2,8,128]{4,3,2,1,0:T(8,128)S(1)}, f32[3,7,2,8,128]{4,3,2,1,0:T(8,128)S(1)}, u32[]{:S(2)}, u32[]{:S(2)}) collective-permute-start(f32[3,7,2,8,128]{4,3,2,1,0:T(8,128)S(1)} %slice_add_fusion), channel_id=1, source_target_pairs={{0,1},{1,0},{2,3},{3,2},{4,5},{5,4},{6,7},{7,6},{8,9},{9,8},{10,11... | collective-permute-start | bytes 516104 | tf_op jit(solution)/shard_map/ppermute | solution.py:465

commit v15 on v14

--- a/solution.py
+++ b/solution.py
@@ -116,13 +116,16 @@
 
     first[full_rows] = jnp.zeros((wide, lanes), f32)
 
-    @pl.loop(0, full_rows // 2)
+    step_rows = 2 * largest_divisor(full_rows // 2, 3)
+
+    @pl.loop(0, full_rows // step_rows)
     def _(s):
         for odd in range(2):
             for b in range(span):
-                value = first[pl.ds(2 * s + odd, 2), pl.ds(b, pitch), :]
-                high, low = split(value.reshape(2 * pitch, lanes))
-                to = pl.ds(pl.multiple_of(s * 2 * pitch, 2 * pitch), 2 * pitch)
+                value = first[pl.ds(s * step_rows + odd, step_rows), pl.ds(b, pitch), :]
+                count = step_rows * pitch
+                high, low = split(value.reshape(count, lanes))
+                to = pl.ds(pl.multiple_of(s * count, 2 * pitch), count)
                 x_high[odd, to, b * lanes : (b + 1) * lanes] = high
                 x_low[odd, to, b * lanes : (b + 1) * lanes] = low
 
@@ -236,12 +239,7 @@
         at = pl.ds(pl.multiple_of(a * cols, cols), own)
         return products(x_high[at, :], x_low[at, :], w_high[a], w_low[a])
 
-    @pl.loop(0, span // 2)
-    def _(pair):
-        acc[...] += one_lag(2 * pair) + one_lag(2 * pair + 1)
-
-    if span % 2:
-        acc[...] += one_lag(span - 1)
+    acc[...] = functools.reduce(lambda left, right: left + right, map(one_lag, range(span)))
 
     centre = second_ref[reach : reach + rows, pl.ds(reach, cols), :].reshape(own, lanes)
     source = source_ref[...].reshape(own, lanes)

time: 77.8 us -> 77.8 us (level)
  transfers between devices with their start and end apart: 21 -> 21, of which waited for: 9 -> 9; matrix products, arithmetic and copies ran while one was open for 2% -> 2% of each run, Pallas kernels for 26% -> 25%
where the time goes in v15:
time: 77.8 us; the launch traced here: 77.6 us
  starting transfers between devices  26.9 us (35%)
  Pallas kernels  24.3 us (31%)
  waiting for transfers between devices  20.6 us (26%)
  local copies, waits for them, and re-layouts  3.3 us (4%)
  other arithmetic  1.52 us (2%)
  between operations  1.08 us (1%)
    ppermute x8, waiting for transfers between devices, shifted(): lax.ppermute(value, axis, [(i, (i + shift) % peers) for i in range(peers)])  15.5 us
    ppermute x8, starting transfers between devices, shifted(): lax.ppermute(value, axis, [(i, (i + shift) % peers) for i in range(peers)])  14.1 us
    ppermute x13, starting transfers between devices, swap(): return lax.ppermute(value, axis, pairs)  12.8 us
    pallas_call x1, Pallas kernels, first_sweep(): pl.pallas_call(functools.partial(first_sweep_kernel, (rows, cols, span, p...  12.4 us
    ppermute x13, waiting for transfers between devices, swap(): return lax.ppermute(value, axis, pairs)  5.08 us
    pallas_call x1, Pallas kernels, second_sweep(): pl.pallas_call(functools.partial(second_sweep_kernel, (rows, cols, span,...  4.79 us
    pallas_call x1, Pallas kernels, correlate(): pl.pallas_call(functools.partial(correlate_kernel, (rows, cols, span, pee...  4.51 us
    pallas_call x2, Pallas kernels, spread(): pl.pallas_call(functools.partial(spread_kernel, (rows, cols, span, peers)...  2.57 us
  transfers between devices with their start and end apart: 21, of which 9 were waited for; matrix products, arithmetic and copies ran while one was open for 2% of the time, Pallas kernels for 25%

profile of v15, /device:TPU:0, one launch (start us, length us, event | category | flops | bytes accessed | tf_op | source)
XLA Modules:
  0.0 77.6 jit_solution(10290078583954423795)
XLA Ops:
  0.6 0.0 copy-start.2
  0.7 1.0 %copy.31 = f32[12,16,2,128]{3,1,0,2:T(8,128)S(1)} copy(f32[12,16,2,128]{3,2,1,0:T(2,128)} %param.4) | data formatting | bytes 393216 | tf_op args[0]
  1.7 3.0 %collective-permute-start.3 = (f32[2,96,128]{2,1,0:T(8,128)S(1)}, f32[2,96,128]{2,1,0:T(8,128)S(1)}, u32[]{:S(2)}, u32[]{:S(2)}) collective-permute-start(f32[2,96,128]{2,1,0:T(8,128)S(1)} %bitcast.44), channel_id=1, source_target_pairs={{0,4},{4,0},{8,12},{12,8},{16,20},{20,16},{24,28},{28,24},{1,5},{5... | collective-permute-start | bytes 294920 | tf_op jit(solution)/shard_map/ppermute | solution.py:463
  4.7 0.7 collective-permute-start.2
  5.4 0.0 copy-start
  5.4 0.9 %copy-done = f32[12,16,2,128]{3,2,1,0:T(2,128)S(1)} copy-done((f32[12,16,2,128]{3,2,1,0:T(2,128)S(1)}, f32[12,16,2,128]{3,2,1,0:T(2,128)}, u32[]{:S(2)}) %copy-start) | copy-done | bytes 196632
  6.3 0.0 copy-start.1
  6.4 0.1 collective-permute-start.1
  6.5 0.8 %collective-permute-start = (f32[2,36,128]{2,0,1:T(2,128)S(1)}, f32[2,36,128]{2,0,1:T(2,128)S(1)}, u32[]{:S(2)}, u32[]{:S(2)}) collective-permute-start(f32[2,36,128]{2,0,1:T(2,128)S(1)} %bitcast.48), channel_id=1, source_target_pairs={{1,2},{2,1},{5,6},{6,5},{9,10},{10,9},{13,14},{14,13},{17,18},{18,... | collective-permute-start | bytes 110600 | tf_op jit(solution)/shard_map/ppermute | solution.py:463
  7.3 0.2 collective-permute-done.3
  7.5 0.0 collective-permute-done.2
  7.6 0.1 copy.17
  7.7 0.1 copy.15
  7.8 2.9 %collective-permute-start.4 = (f32[2,144,128]{2,0,1:T(2,128)S(1)}, f32[2,144,128]{2,0,1:T(2,128)S(1)}, u32[]{:S(2)}, u32[]{:S(2)}) collective-permute-start(f32[2,144,128]{2,0,1:T(2,128)S(1)} %bitcast.40), channel_id=1, source_target_pairs={{0,1},{1,0},{2,3},{3,2},{4,5},{5,4},{6,7},{7,6},{8,9},{9,8},{10,11... | collective-permute-start | bytes 442376 | tf_op jit(solution)/shard_map/ppermute | solution.py:463
  10.7 0.7 collective-permute-start.6
  11.4 0.0 collective-permute-done.1
  11.4 0.0 collective-permute-done
  11.5 0.2 copy.14
  11.7 5.5 %collective-permute-start.9 = (f32[2,264,128]{2,1,0:T(8,128)S(1)}, f32[2,264,128]{2,1,0:T(8,128)S(1)}, u32[]{:S(2)}, u32[]{:S(2)}) collective-permute-start(f32[2,264,128]{2,1,0:T(8,128)S(1)} %copy.22.refs_0_), channel_id=1, source_target_pairs={{0,24},{4,28},{8,0},{12,4},{16,8},{20,12},{24,16},{28,20},{1,25},{... | collective-permute-start | bytes 811016 | tf_op jit(solution)/shard_map/ppermute | solution.py:470
  17.2 0.0 collective-permute-start.8
  17.2 0.9 %collective-permute-start.7 = (f32[2,264,128]{2,1,0:T(8,128)S(1)}, f32[2,264,128]{2,1,0:T(8,128)S(1)}, u32[]{:S(2)}, u32[]{:S(2)}) collective-permute-start(f32[2,264,128]{2,1,0:T(8,128)S(1)} %copy.22.refs_0_), channel_id=1, source_target_pairs={{0,4},{4,0},{8,12},{12,8},{16,20},{20,16},{24,28},{28,24},{1,5},{5... | collective-permute-start | bytes 811016 | tf_op jit(solution)/shard_map/ppermute | solution.py:463
  18.1 0.0 collective-permute-done.4
  18.1 0.0 collective-permute-done.6
  18.2 2.7 %collective-permute-start.5 = (f32[2,264,128]{2,1,0:T(8,128)S(1)}, f32[2,264,128]{2,1,0:T(8,128)S(1)}, u32[]{:S(2)}, u32[]{:S(2)}) collective-permute-start(f32[2,264,128]{2,1,0:T(8,128)S(1)} %copy.16), channel_id=1, source_target_pairs={{0,16},{4,20},{8,24},{12,28},{16,0},{20,4},{24,8},{28,12},{1,17},{... | collective-permute-start | bytes 811016 | tf_op jit(solution)/shard_map/ppermute | solution.py:470
  20.8 0.1 select_maximum_fusion.source_ref
  21.0 0.0 copy-done.2
  21.0 0.0 copy-done.1
  21.0 12.4 %first_sweep.1 = (f32[18,24,256]{2,1,0:T(8,128)S(1)}, f32[12,16,256]{2,1,0:T(8,128)S(1)}, bf16[7,7,256,256]{3,2,1,0:T(8,128)(2,1)S(1)}, bf16[7,7,256,256]{3,2,1,0:T(8,128)(2,1)S(1)}) custom-call(f32[2,24,32,128]{3,2,1,0:T(8,128)S(1)} %select_maximum_fusion.source_ref, f32[2,128,128]{2,1,0:T(8,128)S(1)} %copy-done.2, f32[7,7,2,128,128]{4,3,2,1,0:T(8,128)S(1)} %copy-done.1), custom_call_target="tpu_custom_call" | custom-call | flops 8323596288 | bytes 19267584 | tf_op jit(solution)/shard_map/first_sweep/pallas_call | solution.py:175
  33.4 0.0 collective-permute-done.9.refs_3_
  33.4 0.0 collective-permute-done.8.refs_1_
  33.5 0.0 collective-permute-done.7.refs_4_
  33.5 0.1 collective-permute-start.15
  33.6 4.8 %second_sweep.1 = (f32[12,16,256]{2,1,0:T(8,128)S(1)}, f32[2,32,192]{2,1,0:T(8,128)S(1)}, f32[2,32,192]{2,1,0:T(8,128)S(1)}, f32[2,32,192]{2,1,0:T(8,128)S(1)}, f32[2,32,192]{2,1,0:T(8,128)S(1)}) custom-call(f32[18,24,256]{2,1,0:T(8,128)S(1)} %get-tuple-element.32.second_ref, f32[12,16,256]{2,1,0:T(8,128)S(1)} %get-tuple-element.33.source_ref, ...), custom_call_target="tpu_custom_call" | custom-call | flops 3699376128 | bytes 12845056 | tf_op jit(solution)/shard_map/second_sweep/pallas_call | solution.py:268
  38.4 1.8 %collective-permute-done.5.refs_2_ = f32[2,264,128]{2,1,0:T(8,128)S(1)} collective-permute-done((f32[2,264,128]{2,1,0:T(8,128)S(1)}, f32[2,264,128]{2,1,0:T(8,128)S(1)}, u32[]{:S(2)}, u32[]{:S(2)}) %collective-permute-start.5) | collective-permute-done | bytes 270368 | tf_op jit(solution)/shard_map/ppermute | solution.py:470
  40.2 2.9 %collective-permute-start.14 = (f32[1,2,264,128]{3,2,1,0:T(8,128)S(1)}, f32[1,2,264,128]{3,2,1,0:T(8,128)S(1)}, u32[]{:S(2)}, u32[]{:S(2)}) collective-permute-start(f32[1,2,264,128]{3,2,1,0:T(8,128)S(1)} %bitcast.26), channel_id=1, source_target_pairs={{0,4},{4,0},{8,12},{12,8},{16,20},{20,16},{24,28},{28,24},{1,5},{5... | collective-permute-start | bytes 811016 | tf_op jit(solution)/shard_map/ppermute | solution.py:463
  43.1 0.0 collective-permute-start.10
  43.1 2.1 %collective-permute-start.11 = (f32[2,32,192]{2,1,0:T(8,128)S(1)}, f32[2,32,192]{2,1,0:T(8,128)S(1)}, u32[]{:S(2)}, u32[]{:S(2)}) collective-permute-start(f32[2,32,192]{2,1,0:T(8,128)S(1)} %get-tuple-element.42), channel_id=1, source_target_pairs={{0,16},{4,20},{8,24},{12,28},{16,0},{20,4},{24,8},{28,12},{1,17},{... | collective-permute-start | bytes 147464 | tf_op jit(solution)/shard_map/ppermute | solution.py:470
  45.1 1.8 %collective-permute-start.12 = (f32[2,32,192]{2,1,0:T(8,128)S(1)}, f32[2,32,192]{2,1,0:T(8,128)S(1)}, u32[]{:S(2)}, u32[]{:S(2)}) collective-permute-start(f32[2,32,192]{2,1,0:T(8,128)S(1)} %get-tuple-element.43), channel_id=1, source_target_pairs={{0,24},{4,28},{8,0},{12,4},{16,8},{20,12},{24,16},{28,20},{1,25},{... | collective-permute-start | bytes 147464 | tf_op jit(solution)/shard_map/ppermute | solution.py:470
  46.9 2.6 %collective-permute-done.10.refs_1_ = f32[2,32,192]{2,1,0:T(8,128)S(1)} collective-permute-done((f32[2,32,192]{2,1,0:T(8,128)S(1)}, f32[2,32,192]{2,1,0:T(8,128)S(1)}, u32[]{:S(2)}, u32[]{:S(2)}) %collective-permute-start.10) | collective-permute-done | bytes 49184 | tf_op jit(solution)/shard_map/ppermute | solution.py:470
  49.5 1.9 %collective-permute-done.11.refs_2_ = f32[2,32,192]{2,1,0:T(8,128)S(1)} collective-permute-done((f32[2,32,192]{2,1,0:T(8,128)S(1)}, f32[2,32,192]{2,1,0:T(8,128)S(1)}, u32[]{:S(2)}, u32[]{:S(2)}) %collective-permute-start.11) | collective-permute-done | bytes 49184 | tf_op jit(solution)/shard_map/ppermute | solution.py:470
  51.5 0.0 collective-permute-done.12.refs_3_
  51.5 0.6 collective-permute-start.13
  52.2 0.0 collective-permute-done.15.refs_5_
  52.2 2.2 %spread.2 = (bf16[7,1536,256]{2,1,0:T(8,128)(2,1)S(1)}, bf16[7,1536,256]{2,1,0:T(8,128)(2,1)S(1)}) custom-call(f32[2,264,128]{2,1,0:T(8,128)S(1)} %copy.22.refs_0_, f32[2,264,128]{2,1,0:T(8,128)S(1)} %collective-permute-done.8.refs_1_, f32[2,264,128]{2,1,0:T(8,128)S(1)} %collective-permute-done.5.refs_2_, f32[2,264,128]{2,1,0:T(8,128)S(1)} %collective-permute-done.9.refs_3_, ...), custom_call_target="tpu_custom_call" | custom-call | bytes 1892352 | tf_op jit(solution)/shard_map/spread/pallas_call | solution.py:336
  54.4 0.0 collective-permute-done.14.refs_0_
  54.4 0.3 spread.3
  54.8 2.5 %collective-permute-done.13.refs_4_ = f32[4,32,192]{2,1,0:T(8,128)S(1)} collective-permute-done((f32[4,32,192]{2,1,0:T(8,128)S(1)}, f32[4,32,192]{2,1,0:T(8,128)S(1)}, u32[]{:S(2)}, u32[]{:S(2)}) %collective-permute-start.13) | collective-permute-done | bytes 98336 | tf_op jit(solution)/shard_map/ppermute | solution.py:463
  57.3 4.5 %correlate.1 = (f32[7,7,2,8,128]{4,3,2,1,0:T(8,128)S(1)}, f32[7,7,2,8,128]{4,3,2,1,0:T(8,128)S(1)}) custom-call(f32[2,32,192]{2,1,0:T(8,128)S(1)} %get-tuple-element.40.refs_0_, f32[2,32,192]{2,1,0:T(8,128)S(1)} %collective-permute-done.10.refs_1_, f32[2,32,192]{2,1,0:T(8,128)S(1)} %collective-permute-done.11.refs_2_, ...), custom_call_target="tpu_custom_call" | custom-call | flops 3699376128 | bytes 802816 | tf_op jit(solution)/shard_map/correlate/pallas_call | solution.py:417
  61.8 0.1 collective-permute-start.16
  61.9 0.8 reshape.53
  62.7 0.9 %collective-permute-done.16 = f32[7,7,2,8,128]{4,3,2,1,0:T(8,128)S(1)} collective-permute-done((f32[7,7,2,8,128]{4,3,2,1,0:T(8,128)S(1)}, f32[7,7,2,8,128]{4,3,2,1,0:T(8,128)S(1)}, u32[]{:S(2)}, u32[]{:S(2)}) %collective-permute-start.16) | collective-permute-done | bytes 401440 | tf_op jit(solution)/shard_map/ppermute | solution.py:463
  63.6 0.1 add.22
  63.7 0.1 collective-permute-start.17
  63.8 2.1 %collective-permute-start.18 = (f32[3,7,2,8,128]{4,3,2,1,0:T(8,128)S(1)}, f32[3,7,2,8,128]{4,3,2,1,0:T(8,128)S(1)}, u32[]{:S(2)}, u32[]{:S(2)}) collective-permute-start(f32[3,7,2,8,128]{4,3,2,1,0:T(8,128)S(1)} %slice.47), channel_id=1, source_target_pairs={{0,2},{1,3},{2,0},{3,1},{4,6},{5,7},{6,4},{7,5},{8,10},{9,11},{10,... | collective-permute-start | bytes 516104 | tf_op jit(solution)/shard_map/ppermute | solution.py:470
  65.9 6.3 %collective-permute-done.17 = f32[4,7,2,8,128]{4,3,2,1,0:T(8,128)S(1)} collective-permute-done((f32[4,7,2,8,128]{4,3,2,1,0:T(8,128)S(1)}, f32[4,7,2,8,128]{4,3,2,1,0:T(8,128)S(1)}, u32[]{:S(2)}, u32[]{:S(2)}) %collective-permute-start.17) | collective-permute-done | bytes 229408 | tf_op jit(solution)/shard_map/ppermute | solution.py:470
  72.2 0.1 collective-permute-start.19
  72.3 2.8 %collective-permute-done.18 = f32[3,7,2,8,128]{4,3,2,1,0:T(8,128)S(1)} collective-permute-done((f32[3,7,2,8,128]{4,3,2,1,0:T(8,128)S(1)}, f32[3,7,2,8,128]{4,3,2,1,0:T(8,128)S(1)}, u32[]{:S(2)}, u32[]{:S(2)}) %collective-permute-start.18) | collective-permute-done | bytes 172064 | tf_op jit(solution)/shard_map/ppermute | solution.py:470
  75.1 0.1 collective-permute-start.20
  75.2 0.0 collective-permute-done.19
  75.2 1.4 %collective-permute-done.20 = f32[3,7,2,8,128]{4,3,2,1,0:T(8,128)S(1)} collective-permute-done((f32[3,7,2,8,128]{4,3,2,1,0:T(8,128)S(1)}, f32[3,7,2,8,128]{4,3,2,1,0:T(8,128)S(1)}, u32[]{:S(2)}, u32[]{:S(2)}) %collective-permute-start.20) | collective-permute-done | bytes 172064 | tf_op jit(solution)/shard_map/ppermute | solution.py:463
  76.6 0.1 fusion.6
  76.7 1.0 %pad_maximum_fusion = f32[7,7,2,16,128]{4,3,2,1,0:T(8,128)} fusion(f32[7,7,2,8,128]{4,3,2,1,0:T(8,128)S(1)} %get-tuple-element.57, f32[7,7,2,8,128]{4,3,2,1,0:T(8,128)S(1)} %get-tuple-element.56), kind=kLoop, calls=%fused_computation | loop fusion | flops 200704 | bytes 1605632 | tf_op jit(solution)/shard_map/concatenate | solution.py:547
  (27 shorter events, 0.5 us)
Async XLA Ops:
  0.6 20.4 %copy-start.2 = (f32[2,128,128]{2,1,0:T(8,128)S(1)}, f32[2,128,128]{2,1,0:T(8,128)}, u32[]{:S(2)}) copy-start(f32[2,128,128]{2,1,0:T(8,128)} %inverse_ref.3) | copy-start | bytes 393220
  1.7 5.8 %collective-permute-start.3 = (f32[2,96,128]{2,1,0:T(8,128)S(1)}, f32[2,96,128]{2,1,0:T(8,128)S(1)}, u32[]{:S(2)}, u32[]{:S(2)}) collective-permute-start(f32[2,96,128]{2,1,0:T(8,128)S(1)} %bitcast.44), channel_id=1, source_target_pairs={{0,4},{4,0},{8,12},{12,8},{16,20},{20,16},{24,28},{28,24},{1,5},{5... | collective-permute-start | bytes 294920 | tf_op jit(solution)/shard_map/ppermute | solution.py:463
  4.7 2.8 %collective-permute-start.2 = (f32[2,96,128]{2,1,0:T(8,128)S(1)}, f32[2,96,128]{2,1,0:T(8,128)S(1)}, u32[]{:S(2)}, u32[]{:S(2)}) collective-permute-start(f32[2,96,128]{2,1,0:T(8,128)S(1)} %bitcast.43), channel_id=1, source_target_pairs={{4,8},{8,4},{12,16},{16,12},{20,24},{24,20},{5,9},{9,5},{13,17},{1... | collective-permute-start | bytes 294920 | tf_op jit(solution)/shard_map/ppermute | solution.py:463
  5.4 0.9 %copy-start = (f32[12,16,2,128]{3,2,1,0:T(2,128)S(1)}, f32[12,16,2,128]{3,2,1,0:T(2,128)}, u32[]{:S(2)}) copy-start(f32[12,16,2,128]{3,2,1,0:T(2,128)} %param.5) | copy-start | bytes 589828
  6.3 14.7 %copy-start.1 = (f32[7,7,2,128,128]{4,3,2,1,0:T(8,128)S(1)}, f32[7,7,2,128,128]{4,3,2,1,0:T(8,128)}, u32[]{:S(2)}) copy-start(f32[7,7,2,128,128]{4,3,2,1,0:T(8,128)} %blocks_ref.1) | copy-start | bytes 19267588
  6.4 5.0 %collective-permute-start.1 = (f32[2,36,128]{2,0,1:T(2,128)S(1)}, f32[2,36,128]{2,0,1:T(2,128)S(1)}, u32[]{:S(2)}, u32[]{:S(2)}) collective-permute-start(f32[2,36,128]{2,0,1:T(2,128)S(1)} %bitcast.46), channel_id=1, source_target_pairs={{0,1},{1,0},{2,3},{3,2},{4,5},{5,4},{6,7},{7,6},{8,9},{9,8},{10,11... | collective-permute-start | bytes 110600 | tf_op jit(solution)/shard_map/ppermute | solution.py:463
  6.5 4.9 %collective-permute-start = (f32[2,36,128]{2,0,1:T(2,128)S(1)}, f32[2,36,128]{2,0,1:T(2,128)S(1)}, u32[]{:S(2)}, u32[]{:S(2)}) collective-permute-start(f32[2,36,128]{2,0,1:T(2,128)S(1)} %bitcast.48), channel_id=1, source_target_pairs={{1,2},{2,1},{5,6},{6,5},{9,10},{10,9},{13,14},{14,13},{17,18},{18,... | collective-permute-start | bytes 110600 | tf_op jit(solution)/shard_map/ppermute | solution.py:463
  7.8 10.3 %collective-permute-start.4 = (f32[2,144,128]{2,0,1:T(2,128)S(1)}, f32[2,144,128]{2,0,1:T(2,128)S(1)}, u32[]{:S(2)}, u32[]{:S(2)}) collective-permute-start(f32[2,144,128]{2,0,1:T(2,128)S(1)} %bitcast.40), channel_id=1, source_target_pairs={{0,1},{1,0},{2,3},{3,2},{4,5},{5,4},{6,7},{7,6},{8,9},{9,8},{10,11... | collective-permute-start | bytes 442376 | tf_op jit(solution)/shard_map/ppermute | solution.py:463
  10.7 7.4 %collective-permute-start.6 = (f32[2,144,128]{2,0,1:T(2,128)S(1)}, f32[2,144,128]{2,0,1:T(2,128)S(1)}, u32[]{:S(2)}, u32[]{:S(2)}) collective-permute-start(f32[2,144,128]{2,0,1:T(2,128)S(1)} %bitcast.37), channel_id=1, source_target_pairs={{1,2},{2,1},{5,6},{6,5},{9,10},{10,9},{13,14},{14,13},{17,18},{18,... | collective-permute-start | bytes 442376 | tf_op jit(solution)/shard_map/ppermute | solution.py:463
  11.7 21.7 %collective-permute-start.9 = (f32[2,264,128]{2,1,0:T(8,128)S(1)}, f32[2,264,128]{2,1,0:T(8,128)S(1)}, u32[]{:S(2)}, u32[]{:S(2)}) collective-permute-start(f32[2,264,128]{2,1,0:T(8,128)S(1)} %copy.22.refs_0_), channel_id=1, source_target_pairs={{0,24},{4,28},{8,0},{12,4},{16,8},{20,12},{24,16},{28,20},{1,25},{... | collective-permute-start | bytes 811016 | tf_op jit(solution)/shard_map/ppermute | solution.py:470
  17.2 16.2 %collective-permute-start.8 = (f32[2,264,128]{2,1,0:T(8,128)S(1)}, f32[2,264,128]{2,1,0:T(8,128)S(1)}, u32[]{:S(2)}, u32[]{:S(2)}) collective-permute-start(f32[2,264,128]{2,1,0:T(8,128)S(1)} %copy.22.refs_0_), channel_id=1, source_target_pairs={{0,8},{4,12},{8,16},{12,20},{16,24},{20,28},{24,0},{28,4},{1,9},{5... | collective-permute-start | bytes 811016 | tf_op jit(solution)/shard_map/ppermute | solution.py:470
  17.2 16.3 %collective-permute-start.7 = (f32[2,264,128]{2,1,0:T(8,128)S(1)}, f32[2,264,128]{2,1,0:T(8,128)S(1)}, u32[]{:S(2)}, u32[]{:S(2)}) collective-permute-start(f32[2,264,128]{2,1,0:T(8,128)S(1)} %copy.22.refs_0_), channel_id=1, source_target_pairs={{0,4},{4,0},{8,12},{12,8},{16,20},{20,16},{24,28},{28,24},{1,5},{5... | collective-permute-start | bytes 811016 | tf_op jit(solution)/shard_map/ppermute | solution.py:463
  18.2 22.0 %collective-permute-start.5 = (f32[2,264,128]{2,1,0:T(8,128)S(1)}, f32[2,264,128]{2,1,0:T(8,128)S(1)}, u32[]{:S(2)}, u32[]{:S(2)}) collective-permute-start(f32[2,264,128]{2,1,0:T(8,128)S(1)} %copy.16), channel_id=1, source_target_pairs={{0,16},{4,20},{8,24},{12,28},{16,0},{20,4},{24,8},{28,12},{1,17},{... | collective-permute-start | bytes 811016 | tf_op jit(solution)/shard_map/ppermute | solution.py:470
  33.5 18.7 %collective-permute-start.15 = (f32[2,2,264,128]{3,2,1,0:T(8,128)S(1)}, f32[2,2,264,128]{3,2,1,0:T(8,128)S(1)}, u32[]{:S(2)}, u32[]{:S(2)}) collective-permute-start(f32[2,2,264,128]{3,2,1,0:T(8,128)S(1)} %pad_maximum_fusion.1), channel_id=1, source_target_pairs={{0,4},{4,0},{8,12},{12,8},{16,20},{20,16},{24,28},{28,24},{1,5},{5... | collective-permute-start | bytes 1622024 | tf_op jit(solution)/shard_map/ppermute | solution.py:463
  40.2 14.2 %collective-permute-start.14 = (f32[1,2,264,128]{3,2,1,0:T(8,128)S(1)}, f32[1,2,264,128]{3,2,1,0:T(8,128)S(1)}, u32[]{:S(2)}, u32[]{:S(2)}) collective-permute-start(f32[1,2,264,128]{3,2,1,0:T(8,128)S(1)} %bitcast.26), channel_id=1, source_target_pairs={{0,4},{4,0},{8,12},{12,8},{16,20},{20,16},{24,28},{28,24},{1,5},{5... | collective-permute-start | bytes 811016 | tf_op jit(solution)/shard_map/ppermute | solution.py:463
  43.1 6.5 %collective-permute-start.10 = (f32[2,32,192]{2,1,0:T(8,128)S(1)}, f32[2,32,192]{2,1,0:T(8,128)S(1)}, u32[]{:S(2)}, u32[]{:S(2)}) collective-permute-start(f32[2,32,192]{2,1,0:T(8,128)S(1)} %get-tuple-element.41), channel_id=1, source_target_pairs={{0,8},{4,12},{8,16},{12,20},{16,24},{20,28},{24,0},{28,4},{1,9},{5... | collective-permute-start | bytes 147464 | tf_op jit(solution)/shard_map/ppermute | solution.py:470
  43.1 8.4 %collective-permute-start.11 = (f32[2,32,192]{2,1,0:T(8,128)S(1)}, f32[2,32,192]{2,1,0:T(8,128)S(1)}, u32[]{:S(2)}, u32[]{:S(2)}) collective-permute-start(f32[2,32,192]{2,1,0:T(8,128)S(1)} %get-tuple-element.42), channel_id=1, source_target_pairs={{0,16},{4,20},{8,24},{12,28},{16,0},{20,4},{24,8},{28,12},{1,17},{... | collective-permute-start | bytes 147464 | tf_op jit(solution)/shard_map/ppermute | solution.py:470
  45.1 6.4 %collective-permute-start.12 = (f32[2,32,192]{2,1,0:T(8,128)S(1)}, f32[2,32,192]{2,1,0:T(8,128)S(1)}, u32[]{:S(2)}, u32[]{:S(2)}) collective-permute-start(f32[2,32,192]{2,1,0:T(8,128)S(1)} %get-tuple-element.43), channel_id=1, source_target_pairs={{0,24},{4,28},{8,0},{12,4},{16,8},{20,12},{24,16},{28,20},{1,25},{... | collective-permute-start | bytes 147464 | tf_op jit(solution)/shard_map/ppermute | solution.py:470
  51.5 5.8 %collective-permute-start.13 = (f32[4,32,192]{2,1,0:T(8,128)S(1)}, f32[4,32,192]{2,1,0:T(8,128)S(1)}, u32[]{:S(2)}, u32[]{:S(2)}) collective-permute-start(f32[4,32,192]{2,1,0:T(8,128)S(1)} %pad_maximum_fusion.5), channel_id=1, source_target_pairs={{0,4},{4,0},{8,12},{12,8},{16,20},{20,16},{24,28},{28,24},{1,5},{5... | collective-permute-start | bytes 294920 | tf_op jit(solution)/shard_map/ppermute | solution.py:463
  61.8 1.8 %collective-permute-start.16 = (f32[7,7,2,8,128]{4,3,2,1,0:T(8,128)S(1)}, f32[7,7,2,8,128]{4,3,2,1,0:T(8,128)S(1)}, u32[]{:S(2)}, u32[]{:S(2)}) collective-permute-start(f32[7,7,2,8,128]{4,3,2,1,0:T(8,128)S(1)} %get-tuple-element.52), channel_id=1, source_target_pairs={{0,1},{1,0},{2,3},{3,2},{4,5},{5,4},{6,7},{7,6},{8,9},{9,8},{10,11... | collective-permute-start | bytes 1204232 | tf_op jit(solution)/shard_map/ppermute | solution.py:463
  63.7 8.5 %collective-permute-start.17 = (f32[4,7,2,8,128]{4,3,2,1,0:T(8,128)S(1)}, f32[4,7,2,8,128]{4,3,2,1,0:T(8,128)S(1)}, u32[]{:S(2)}, u32[]{:S(2)}) collective-permute-start(f32[4,7,2,8,128]{4,3,2,1,0:T(8,128)S(1)} %slice.46), channel_id=1, source_target_pairs={{0,2},{1,3},{2,0},{3,1},{4,6},{5,7},{6,4},{7,5},{8,10},{9,11},{10,... | collective-permute-start | bytes 688136 | tf_op jit(solution)/shard_map/ppermute | solution.py:470
  63.8 11.3 %collective-permute-start.18 = (f32[3,7,2,8,128]{4,3,2,1,0:T(8,128)S(1)}, f32[3,7,2,8,128]{4,3,2,1,0:T(8,128)S(1)}, u32[]{:S(2)}, u32[]{:S(2)}) collective-permute-start(f32[3,7,2,8,128]{4,3,2,1,0:T(8,128)S(1)} %slice.47), channel_id=1, source_target_pairs={{0,2},{1,3},{2,0},{3,1},{4,6},{5,7},{6,4},{7,5},{8,10},{9,11},{10,... | collective-permute-start | bytes 516104 | tf_op jit(solution)/shard_map/ppermute | solution.py:470
  72.2 3.0 %collective-permute-start.19 = (f32[4,7,2,8,128]{4,3,2,1,0:T(8,128)S(1)}, f32[4,7,2,8,128]{4,3,2,1,0:T(8,128)S(1)}, u32[]{:S(2)}, u32[]{:S(2)}) collective-permute-start(f32[4,7,2,8,128]{4,3,2,1,0:T(8,128)S(1)} %slice_add_fusion.1), channel_id=1, source_target_pairs={{0,1},{1,0},{2,3},{3,2},{4,5},{5,4},{6,7},{7,6},{8,9},{9,8},{10,11... | collective-permute-start | bytes 688136 | tf_op jit(solution)/shard_map/ppermute | solution.py:463
  75.1 1.5 %collective-permute-start.20 = (f32[3,7,2,8,128]{4,3,2,1,0:T(8,128)S(1)}, f32[3,7,2,8,128]{4,3,2,1,0:T(8,128)S(1)}, u32[]{:S(2)}, u32[]{:S(2)}) collective-permute-start(f32[3,7,2,8,128]{4,3,2,1,0:T(8,128)S(1)} %slice_add_fusion), channel_id=1, source_target_pairs={{0,1},{1,0},{2,3},{3,2},{4,5},{5,4},{6,7},{7,6},{8,9},{9,8},{10,11... | collective-permute-start | bytes 516104 | tf_op jit(solution)/shard_map/ppermute | solution.py:463

commit v16 on v15

--- a/solution.py
+++ b/solution.py
@@ -537,7 +537,7 @@
         mine, other = correlate(shares, twin_shares, s_high, s_low, lags, rows, cols, factor)
         mine = mine + swap(other, "col", 0)
         mine, adjoint = lax.optimization_barrier((mine, adjoint))
-        for piece in (mine[: span // 2 + 1], mine[span // 2 + 1 :]):
+        for piece in (mine[: span - 2], mine[span - 2 :]):
             total = piece
             for k in range(2, lax.axis_size("col"), 2):
                 total = total + shifted(piece, "col", k)

time: 77.8 us -> 77.7 us (level)
  no operation moved by 1% of the time
where the time goes in v16:
time: 77.7 us; the launch traced here: 77.6 us
  starting transfers between devices  26.9 us (35%)
  Pallas kernels  24.3 us (31%)
  waiting for transfers between devices  20.5 us (26%)
  local copies, waits for them, and re-layouts  3.3 us (4%)
  other arithmetic  1.54 us (2%)
  between operations  1.07 us (1%)
    ppermute x8, waiting for transfers between devices, shifted(): lax.ppermute(value, axis, [(i, (i + shift) % peers) for i in range(peers)])  15.5 us
    ppermute x8, starting transfers between devices, shifted(): lax.ppermute(value, axis, [(i, (i + shift) % peers) for i in range(peers)])  14.1 us
    ppermute x13, starting transfers between devices, swap(): return lax.ppermute(value, axis, pairs)  12.8 us
    pallas_call x1, Pallas kernels, first_sweep(): pl.pallas_call(functools.partial(first_sweep_kernel, (rows, cols, span, p...  12.4 us
    ppermute x13, waiting for transfers between devices, swap(): return lax.ppermute(value, axis, pairs)  4.99 us
    pallas_call x1, Pallas kernels, second_sweep(): pl.pallas_call(functools.partial(second_sweep_kernel, (rows, cols, span,...  4.79 us
    pallas_call x1, Pallas kernels, correlate(): pl.pallas_call(functools.partial(correlate_kernel, (rows, cols, span, pee...  4.51 us
    pallas_call x2, Pallas kernels, spread(): pl.pallas_call(functools.partial(spread_kernel, (rows, cols, span, peers)...  2.57 us
  transfers between devices with their start and end apart: 21, of which 9 were waited for; matrix products, arithmetic and copies ran while one was open for 2% of the time, Pallas kernels for 25%

profile of v16, /device:TPU:0, one launch (start us, length us, event | category | flops | bytes accessed | tf_op | source)
XLA Modules:
  0.0 77.6 jit_solution(5250055697150895852)
XLA Ops:
  0.6 0.0 copy-start.2
  0.7 1.0 %copy.31 = f32[12,16,2,128]{3,1,0,2:T(8,128)S(1)} copy(f32[12,16,2,128]{3,2,1,0:T(2,128)} %param.4) | data formatting | bytes 393216 | tf_op args[0]
  1.7 3.0 %collective-permute-start.3 = (f32[2,96,128]{2,1,0:T(8,128)S(1)}, f32[2,96,128]{2,1,0:T(8,128)S(1)}, u32[]{:S(2)}, u32[]{:S(2)}) collective-permute-start(f32[2,96,128]{2,1,0:T(8,128)S(1)} %bitcast.44), channel_id=1, source_target_pairs={{0,4},{4,0},{8,12},{12,8},{16,20},{20,16},{24,28},{28,24},{1,5},{5... | collective-permute-start | bytes 294920 | tf_op jit(solution)/shard_map/ppermute | solution.py:463
  4.7 0.7 collective-permute-start.2
  5.4 0.0 copy-start
  5.4 0.9 %copy-done = f32[12,16,2,128]{3,2,1,0:T(2,128)S(1)} copy-done((f32[12,16,2,128]{3,2,1,0:T(2,128)S(1)}, f32[12,16,2,128]{3,2,1,0:T(2,128)}, u32[]{:S(2)}) %copy-start) | copy-done | bytes 196632
  6.3 0.0 copy-start.1
  6.4 0.1 collective-permute-start.1
  6.5 0.8 %collective-permute-start = (f32[2,36,128]{2,0,1:T(2,128)S(1)}, f32[2,36,128]{2,0,1:T(2,128)S(1)}, u32[]{:S(2)}, u32[]{:S(2)}) collective-permute-start(f32[2,36,128]{2,0,1:T(2,128)S(1)} %bitcast.48), channel_id=1, source_target_pairs={{1,2},{2,1},{5,6},{6,5},{9,10},{10,9},{13,14},{14,13},{17,18},{18,... | collective-permute-start | bytes 110600 | tf_op jit(solution)/shard_map/ppermute | solution.py:463
  7.3 0.2 collective-permute-done.3
  7.5 0.0 collective-permute-done.2
  7.6 0.1 copy.17
  7.7 0.1 copy.15
  7.8 2.9 %collective-permute-start.4 = (f32[2,144,128]{2,0,1:T(2,128)S(1)}, f32[2,144,128]{2,0,1:T(2,128)S(1)}, u32[]{:S(2)}, u32[]{:S(2)}) collective-permute-start(f32[2,144,128]{2,0,1:T(2,128)S(1)} %bitcast.40), channel_id=1, source_target_pairs={{0,1},{1,0},{2,3},{3,2},{4,5},{5,4},{6,7},{7,6},{8,9},{9,8},{10,11... | collective-permute-start | bytes 442376 | tf_op jit(solution)/shard_map/ppermute | solution.py:463
  10.7 0.7 collective-permute-start.6
  11.4 0.0 collective-permute-done.1
  11.4 0.0 collective-permute-done
  11.5 0.2 copy.14
  11.7 5.5 %collective-permute-start.9 = (f32[2,264,128]{2,1,0:T(8,128)S(1)}, f32[2,264,128]{2,1,0:T(8,128)S(1)}, u32[]{:S(2)}, u32[]{:S(2)}) collective-permute-start(f32[2,264,128]{2,1,0:T(8,128)S(1)} %copy.22.refs_0_), channel_id=1, source_target_pairs={{0,24},{4,28},{8,0},{12,4},{16,8},{20,12},{24,16},{28,20},{1,25},{... | collective-permute-start | bytes 811016 | tf_op jit(solution)/shard_map/ppermute | solution.py:470
  17.2 0.0 collective-permute-start.8
  17.2 0.9 %collective-permute-start.7 = (f32[2,264,128]{2,1,0:T(8,128)S(1)}, f32[2,264,128]{2,1,0:T(8,128)S(1)}, u32[]{:S(2)}, u32[]{:S(2)}) collective-permute-start(f32[2,264,128]{2,1,0:T(8,128)S(1)} %copy.22.refs_0_), channel_id=1, source_target_pairs={{0,4},{4,0},{8,12},{12,8},{16,20},{20,16},{24,28},{28,24},{1,5},{5... | collective-permute-start | bytes 811016 | tf_op jit(solution)/shard_map/ppermute | solution.py:463
  18.1 0.0 collective-permute-done.4
  18.1 0.0 collective-permute-done.6
  18.2 2.7 %collective-permute-start.5 = (f32[2,264,128]{2,1,0:T(8,128)S(1)}, f32[2,264,128]{2,1,0:T(8,128)S(1)}, u32[]{:S(2)}, u32[]{:S(2)}) collective-permute-start(f32[2,264,128]{2,1,0:T(8,128)S(1)} %copy.16), channel_id=1, source_target_pairs={{0,16},{4,20},{8,24},{12,28},{16,0},{20,4},{24,8},{28,12},{1,17},{... | collective-permute-start | bytes 811016 | tf_op jit(solution)/shard_map/ppermute | solution.py:470
  20.8 0.1 select_maximum_fusion.source_ref
  21.0 0.0 copy-done.2
  21.0 0.0 copy-done.1
  21.0 12.4 %first_sweep.1 = (f32[18,24,256]{2,1,0:T(8,128)S(1)}, f32[12,16,256]{2,1,0:T(8,128)S(1)}, bf16[7,7,256,256]{3,2,1,0:T(8,128)(2,1)S(1)}, bf16[7,7,256,256]{3,2,1,0:T(8,128)(2,1)S(1)}) custom-call(f32[2,24,32,128]{3,2,1,0:T(8,128)S(1)} %select_maximum_fusion.source_ref, f32[2,128,128]{2,1,0:T(8,128)S(1)} %copy-done.2, f32[7,7,2,128,128]{4,3,2,1,0:T(8,128)S(1)} %copy-done.1), custom_call_target="tpu_custom_call" | custom-call | flops 8323596288 | bytes 19267584 | tf_op jit(solution)/shard_map/first_sweep/pallas_call | solution.py:175
  33.4 0.0 collective-permute-done.9.refs_3_
  33.4 0.0 collective-permute-done.8.refs_1_
  33.5 0.0 collective-permute-done.7.refs_4_
  33.5 0.1 collective-permute-start.15
  33.6 4.8 %second_sweep.1 = (f32[12,16,256]{2,1,0:T(8,128)S(1)}, f32[2,32,192]{2,1,0:T(8,128)S(1)}, f32[2,32,192]{2,1,0:T(8,128)S(1)}, f32[2,32,192]{2,1,0:T(8,128)S(1)}, f32[2,32,192]{2,1,0:T(8,128)S(1)}) custom-call(f32[18,24,256]{2,1,0:T(8,128)S(1)} %get-tuple-element.32.second_ref, f32[12,16,256]{2,1,0:T(8,128)S(1)} %get-tuple-element.33.source_ref, ...), custom_call_target="tpu_custom_call" | custom-call | flops 3699376128 | bytes 12845056 | tf_op jit(solution)/shard_map/second_sweep/pallas_call | solution.py:268
  38.4 1.8 %collective-permute-done.5.refs_2_ = f32[2,264,128]{2,1,0:T(8,128)S(1)} collective-permute-done((f32[2,264,128]{2,1,0:T(8,128)S(1)}, f32[2,264,128]{2,1,0:T(8,128)S(1)}, u32[]{:S(2)}, u32[]{:S(2)}) %collective-permute-start.5) | collective-permute-done | bytes 270368 | tf_op jit(solution)/shard_map/ppermute | solution.py:470
  40.2 2.9 %collective-permute-start.14 = (f32[1,2,264,128]{3,2,1,0:T(8,128)S(1)}, f32[1,2,264,128]{3,2,1,0:T(8,128)S(1)}, u32[]{:S(2)}, u32[]{:S(2)}) collective-permute-start(f32[1,2,264,128]{3,2,1,0:T(8,128)S(1)} %bitcast.26), channel_id=1, source_target_pairs={{0,4},{4,0},{8,12},{12,8},{16,20},{20,16},{24,28},{28,24},{1,5},{5... | collective-permute-start | bytes 811016 | tf_op jit(solution)/shard_map/ppermute | solution.py:463
  43.1 0.0 collective-permute-start.10
  43.1 2.1 %collective-permute-start.11 = (f32[2,32,192]{2,1,0:T(8,128)S(1)}, f32[2,32,192]{2,1,0:T(8,128)S(1)}, u32[]{:S(2)}, u32[]{:S(2)}) collective-permute-start(f32[2,32,192]{2,1,0:T(8,128)S(1)} %get-tuple-element.42), channel_id=1, source_target_pairs={{0,16},{4,20},{8,24},{12,28},{16,0},{20,4},{24,8},{28,12},{1,17},{... | collective-permute-start | bytes 147464 | tf_op jit(solution)/shard_map/ppermute | solution.py:470
  45.1 1.8 %collective-permute-start.12 = (f32[2,32,192]{2,1,0:T(8,128)S(1)}, f32[2,32,192]{2,1,0:T(8,128)S(1)}, u32[]{:S(2)}, u32[]{:S(2)}) collective-permute-start(f32[2,32,192]{2,1,0:T(8,128)S(1)} %get-tuple-element.43), channel_id=1, source_target_pairs={{0,24},{4,28},{8,0},{12,4},{16,8},{20,12},{24,16},{28,20},{1,25},{... | collective-permute-start | bytes 147464 | tf_op jit(solution)/shard_map/ppermute | solution.py:470
  46.9 2.6 %collective-permute-done.10.refs_1_ = f32[2,32,192]{2,1,0:T(8,128)S(1)} collective-permute-done((f32[2,32,192]{2,1,0:T(8,128)S(1)}, f32[2,32,192]{2,1,0:T(8,128)S(1)}, u32[]{:S(2)}, u32[]{:S(2)}) %collective-permute-start.10) | collective-permute-done | bytes 49184 | tf_op jit(solution)/shard_map/ppermute | solution.py:470
  49.5 1.9 %collective-permute-done.11.refs_2_ = f32[2,32,192]{2,1,0:T(8,128)S(1)} collective-permute-done((f32[2,32,192]{2,1,0:T(8,128)S(1)}, f32[2,32,192]{2,1,0:T(8,128)S(1)}, u32[]{:S(2)}, u32[]{:S(2)}) %collective-permute-start.11) | collective-permute-done | bytes 49184 | tf_op jit(solution)/shard_map/ppermute | solution.py:470
  51.5 0.0 collective-permute-done.12.refs_3_
  51.5 0.6 collective-permute-start.13
  52.2 0.0 collective-permute-done.15.refs_5_
  52.2 2.2 %spread.2 = (bf16[7,1536,256]{2,1,0:T(8,128)(2,1)S(1)}, bf16[7,1536,256]{2,1,0:T(8,128)(2,1)S(1)}) custom-call(f32[2,264,128]{2,1,0:T(8,128)S(1)} %copy.22.refs_0_, f32[2,264,128]{2,1,0:T(8,128)S(1)} %collective-permute-done.8.refs_1_, f32[2,264,128]{2,1,0:T(8,128)S(1)} %collective-permute-done.5.refs_2_, f32[2,264,128]{2,1,0:T(8,128)S(1)} %collective-permute-done.9.refs_3_, ...), custom_call_target="tpu_custom_call" | custom-call | bytes 1892352 | tf_op jit(solution)/shard_map/spread/pallas_call | solution.py:336
  54.4 0.0 collective-permute-done.14.refs_0_
  54.4 0.3 spread.3
  54.8 2.5 %collective-permute-done.13.refs_4_ = f32[4,32,192]{2,1,0:T(8,128)S(1)} collective-permute-done((f32[4,32,192]{2,1,0:T(8,128)S(1)}, f32[4,32,192]{2,1,0:T(8,128)S(1)}, u32[]{:S(2)}, u32[]{:S(2)}) %collective-permute-start.13) | collective-permute-done | bytes 98336 | tf_op jit(solution)/shard_map/ppermute | solution.py:463
  57.3 4.5 %correlate.1 = (f32[7,7,2,8,128]{4,3,2,1,0:T(8,128)S(1)}, f32[7,7,2,8,128]{4,3,2,1,0:T(8,128)S(1)}) custom-call(f32[2,32,192]{2,1,0:T(8,128)S(1)} %get-tuple-element.40.refs_0_, f32[2,32,192]{2,1,0:T(8,128)S(1)} %collective-permute-done.10.refs_1_, f32[2,32,192]{2,1,0:T(8,128)S(1)} %collective-permute-done.11.refs_2_, ...), custom_call_target="tpu_custom_call" | custom-call | flops 3699376128 | bytes 802816 | tf_op jit(solution)/shard_map/correlate/pallas_call | solution.py:417
  61.8 0.1 collective-permute-start.16
  61.9 0.8 reshape.53
  62.7 0.9 %collective-permute-done.16 = f32[7,7,2,8,128]{4,3,2,1,0:T(8,128)S(1)} collective-permute-done((f32[7,7,2,8,128]{4,3,2,1,0:T(8,128)S(1)}, f32[7,7,2,8,128]{4,3,2,1,0:T(8,128)S(1)}, u32[]{:S(2)}, u32[]{:S(2)}) %collective-permute-start.16) | collective-permute-done | bytes 401440 | tf_op jit(solution)/shard_map/ppermute | solution.py:463
  63.6 0.1 add.22
  63.7 0.1 collective-permute-start.17
  63.8 2.1 %collective-permute-start.18 = (f32[2,7,2,8,128]{4,3,2,1,0:T(8,128)S(1)}, f32[2,7,2,8,128]{4,3,2,1,0:T(8,128)S(1)}, u32[]{:S(2)}, u32[]{:S(2)}) collective-permute-start(f32[2,7,2,8,128]{4,3,2,1,0:T(8,128)S(1)} %slice.47), channel_id=1, source_target_pairs={{0,2},{1,3},{2,0},{3,1},{4,6},{5,7},{6,4},{7,5},{8,10},{9,11},{10,... | collective-permute-start | bytes 344072 | tf_op jit(solution)/shard_map/ppermute | solution.py:470
  65.9 7.6 %collective-permute-done.17 = f32[5,7,2,8,128]{4,3,2,1,0:T(8,128)S(1)} collective-permute-done((f32[5,7,2,8,128]{4,3,2,1,0:T(8,128)S(1)}, f32[5,7,2,8,128]{4,3,2,1,0:T(8,128)S(1)}, u32[]{:S(2)}, u32[]{:S(2)}) %collective-permute-start.17) | collective-permute-done | bytes 286752 | tf_op jit(solution)/shard_map/ppermute | solution.py:470
  73.4 0.1 slice_add_fusion.1
  73.5 0.1 collective-permute-start.19
  73.6 1.5 %collective-permute-done.18 = f32[2,7,2,8,128]{4,3,2,1,0:T(8,128)S(1)} collective-permute-done((f32[2,7,2,8,128]{4,3,2,1,0:T(8,128)S(1)}, f32[2,7,2,8,128]{4,3,2,1,0:T(8,128)S(1)}, u32[]{:S(2)}, u32[]{:S(2)}) %collective-permute-start.18) | collective-permute-done | bytes 114720 | tf_op jit(solution)/shard_map/ppermute | solution.py:470
  75.1 0.1 collective-permute-start.20
  75.2 0.0 collective-permute-done.19
  75.2 1.3 %collective-permute-done.20 = f32[2,7,2,8,128]{4,3,2,1,0:T(8,128)S(1)} collective-permute-done((f32[2,7,2,8,128]{4,3,2,1,0:T(8,128)S(1)}, f32[2,7,2,8,128]{4,3,2,1,0:T(8,128)S(1)}, u32[]{:S(2)}, u32[]{:S(2)}) %collective-permute-start.20) | collective-permute-done | bytes 114720 | tf_op jit(solution)/shard_map/ppermute | solution.py:463
  76.5 0.1 fusion.6
  76.6 1.0 %pad_maximum_fusion = f32[7,7,2,16,128]{4,3,2,1,0:T(8,128)} fusion(f32[7,7,2,8,128]{4,3,2,1,0:T(8,128)S(1)} %get-tuple-element.57, f32[7,7,2,8,128]{4,3,2,1,0:T(8,128)S(1)} %get-tuple-element.56), kind=kLoop, calls=%fused_computation | loop fusion | flops 200704 | bytes 1605632 | tf_op jit(solution)/shard_map/concatenate | solution.py:547
  (26 shorter events, 0.5 us)
Async XLA Ops:
  0.6 20.4 %copy-start.2 = (f32[2,128,128]{2,1,0:T(8,128)S(1)}, f32[2,128,128]{2,1,0:T(8,128)}, u32[]{:S(2)}) copy-start(f32[2,128,128]{2,1,0:T(8,128)} %inverse_ref.3) | copy-start | bytes 393220
  1.7 5.8 %collective-permute-start.3 = (f32[2,96,128]{2,1,0:T(8,128)S(1)}, f32[2,96,128]{2,1,0:T(8,128)S(1)}, u32[]{:S(2)}, u32[]{:S(2)}) collective-permute-start(f32[2,96,128]{2,1,0:T(8,128)S(1)} %bitcast.44), channel_id=1, source_target_pairs={{0,4},{4,0},{8,12},{12,8},{16,20},{20,16},{24,28},{28,24},{1,5},{5... | collective-permute-start | bytes 294920 | tf_op jit(solution)/shard_map/ppermute | solution.py:463
  4.7 2.8 %collective-permute-start.2 = (f32[2,96,128]{2,1,0:T(8,128)S(1)}, f32[2,96,128]{2,1,0:T(8,128)S(1)}, u32[]{:S(2)}, u32[]{:S(2)}) collective-permute-start(f32[2,96,128]{2,1,0:T(8,128)S(1)} %bitcast.43), channel_id=1, source_target_pairs={{4,8},{8,4},{12,16},{16,12},{20,24},{24,20},{5,9},{9,5},{13,17},{1... | collective-permute-start | bytes 294920 | tf_op jit(solution)/shard_map/ppermute | solution.py:463
  5.4 0.9 %copy-start = (f32[12,16,2,128]{3,2,1,0:T(2,128)S(1)}, f32[12,16,2,128]{3,2,1,0:T(2,128)}, u32[]{:S(2)}) copy-start(f32[12,16,2,128]{3,2,1,0:T(2,128)} %param.5) | copy-start | bytes 589828
  6.3 14.7 %copy-start.1 = (f32[7,7,2,128,128]{4,3,2,1,0:T(8,128)S(1)}, f32[7,7,2,128,128]{4,3,2,1,0:T(8,128)}, u32[]{:S(2)}) copy-start(f32[7,7,2,128,128]{4,3,2,1,0:T(8,128)} %blocks_ref.1) | copy-start | bytes 19267588
  6.4 5.0 %collective-permute-start.1 = (f32[2,36,128]{2,0,1:T(2,128)S(1)}, f32[2,36,128]{2,0,1:T(2,128)S(1)}, u32[]{:S(2)}, u32[]{:S(2)}) collective-permute-start(f32[2,36,128]{2,0,1:T(2,128)S(1)} %bitcast.46), channel_id=1, source_target_pairs={{0,1},{1,0},{2,3},{3,2},{4,5},{5,4},{6,7},{7,6},{8,9},{9,8},{10,11... | collective-permute-start | bytes 110600 | tf_op jit(solution)/shard_map/ppermute | solution.py:463
  6.5 4.9 %collective-permute-start = (f32[2,36,128]{2,0,1:T(2,128)S(1)}, f32[2,36,128]{2,0,1:T(2,128)S(1)}, u32[]{:S(2)}, u32[]{:S(2)}) collective-permute-start(f32[2,36,128]{2,0,1:T(2,128)S(1)} %bitcast.48), channel_id=1, source_target_pairs={{1,2},{2,1},{5,6},{6,5},{9,10},{10,9},{13,14},{14,13},{17,18},{18,... | collective-permute-start | bytes 110600 | tf_op jit(solution)/shard_map/ppermute | solution.py:463
  7.8 10.3 %collective-permute-start.4 = (f32[2,144,128]{2,0,1:T(2,128)S(1)}, f32[2,144,128]{2,0,1:T(2,128)S(1)}, u32[]{:S(2)}, u32[]{:S(2)}) collective-permute-start(f32[2,144,128]{2,0,1:T(2,128)S(1)} %bitcast.40), channel_id=1, source_target_pairs={{0,1},{1,0},{2,3},{3,2},{4,5},{5,4},{6,7},{7,6},{8,9},{9,8},{10,11... | collective-permute-start | bytes 442376 | tf_op jit(solution)/shard_map/ppermute | solution.py:463
  10.7 7.4 %collective-permute-start.6 = (f32[2,144,128]{2,0,1:T(2,128)S(1)}, f32[2,144,128]{2,0,1:T(2,128)S(1)}, u32[]{:S(2)}, u32[]{:S(2)}) collective-permute-start(f32[2,144,128]{2,0,1:T(2,128)S(1)} %bitcast.37), channel_id=1, source_target_pairs={{1,2},{2,1},{5,6},{6,5},{9,10},{10,9},{13,14},{14,13},{17,18},{18,... | collective-permute-start | bytes 442376 | tf_op jit(solution)/shard_map/ppermute | solution.py:463
  11.7 21.7 %collective-permute-start.9 = (f32[2,264,128]{2,1,0:T(8,128)S(1)}, f32[2,264,128]{2,1,0:T(8,128)S(1)}, u32[]{:S(2)}, u32[]{:S(2)}) collective-permute-start(f32[2,264,128]{2,1,0:T(8,128)S(1)} %copy.22.refs_0_), channel_id=1, source_target_pairs={{0,24},{4,28},{8,0},{12,4},{16,8},{20,12},{24,16},{28,20},{1,25},{... | collective-permute-start | bytes 811016 | tf_op jit(solution)/shard_map/ppermute | solution.py:470
  17.2 16.2 %collective-permute-start.8 = (f32[2,264,128]{2,1,0:T(8,128)S(1)}, f32[2,264,128]{2,1,0:T(8,128)S(1)}, u32[]{:S(2)}, u32[]{:S(2)}) collective-permute-start(f32[2,264,128]{2,1,0:T(8,128)S(1)} %copy.22.refs_0_), channel_id=1, source_target_pairs={{0,8},{4,12},{8,16},{12,20},{16,24},{20,28},{24,0},{28,4},{1,9},{5... | collective-permute-start | bytes 811016 | tf_op jit(solution)/shard_map/ppermute | solution.py:470
  17.2 16.3 %collective-permute-start.7 = (f32[2,264,128]{2,1,0:T(8,128)S(1)}, f32[2,264,128]{2,1,0:T(8,128)S(1)}, u32[]{:S(2)}, u32[]{:S(2)}) collective-permute-start(f32[2,264,128]{2,1,0:T(8,128)S(1)} %copy.22.refs_0_), channel_id=1, source_target_pairs={{0,4},{4,0},{8,12},{12,8},{16,20},{20,16},{24,28},{28,24},{1,5},{5... | collective-permute-start | bytes 811016 | tf_op jit(solution)/shard_map/ppermute | solution.py:463
  18.2 22.0 %collective-permute-start.5 = (f32[2,264,128]{2,1,0:T(8,128)S(1)}, f32[2,264,128]{2,1,0:T(8,128)S(1)}, u32[]{:S(2)}, u32[]{:S(2)}) collective-permute-start(f32[2,264,128]{2,1,0:T(8,128)S(1)} %copy.16), channel_id=1, source_target_pairs={{0,16},{4,20},{8,24},{12,28},{16,0},{20,4},{24,8},{28,12},{1,17},{... | collective-permute-start | bytes 811016 | tf_op jit(solution)/shard_map/ppermute | solution.py:470
  33.5 18.7 %collective-permute-start.15 = (f32[2,2,264,128]{3,2,1,0:T(8,128)S(1)}, f32[2,2,264,128]{3,2,1,0:T(8,128)S(1)}, u32[]{:S(2)}, u32[]{:S(2)}) collective-permute-start(f32[2,2,264,128]{3,2,1,0:T(8,128)S(1)} %pad_maximum_fusion.1), channel_id=1, source_target_pairs={{0,4},{4,0},{8,12},{12,8},{16,20},{20,16},{24,28},{28,24},{1,5},{5... | collective-permute-start | bytes 1622024 | tf_op jit(solution)/shard_map/ppermute | solution.py:463
  40.2 14.2 %collective-permute-start.14 = (f32[1,2,264,128]{3,2,1,0:T(8,128)S(1)}, f32[1,2,264,128]{3,2,1,0:T(8,128)S(1)}, u32[]{:S(2)}, u32[]{:S(2)}) collective-permute-start(f32[1,2,264,128]{3,2,1,0:T(8,128)S(1)} %bitcast.26), channel_id=1, source_target_pairs={{0,4},{4,0},{8,12},{12,8},{16,20},{20,16},{24,28},{28,24},{1,5},{5... | collective-permute-start | bytes 811016 | tf_op jit(solution)/shard_map/ppermute | solution.py:463
  43.1 6.5 %collective-permute-start.10 = (f32[2,32,192]{2,1,0:T(8,128)S(1)}, f32[2,32,192]{2,1,0:T(8,128)S(1)}, u32[]{:S(2)}, u32[]{:S(2)}) collective-permute-start(f32[2,32,192]{2,1,0:T(8,128)S(1)} %get-tuple-element.41), channel_id=1, source_target_pairs={{0,8},{4,12},{8,16},{12,20},{16,24},{20,28},{24,0},{28,4},{1,9},{5... | collective-permute-start | bytes 147464 | tf_op jit(solution)/shard_map/ppermute | solution.py:470
  43.1 8.4 %collective-permute-start.11 = (f32[2,32,192]{2,1,0:T(8,128)S(1)}, f32[2,32,192]{2,1,0:T(8,128)S(1)}, u32[]{:S(2)}, u32[]{:S(2)}) collective-permute-start(f32[2,32,192]{2,1,0:T(8,128)S(1)} %get-tuple-element.42), channel_id=1, source_target_pairs={{0,16},{4,20},{8,24},{12,28},{16,0},{20,4},{24,8},{28,12},{1,17},{... | collective-permute-start | bytes 147464 | tf_op jit(solution)/shard_map/ppermute | solution.py:470
  45.1 6.4 %collective-permute-start.12 = (f32[2,32,192]{2,1,0:T(8,128)S(1)}, f32[2,32,192]{2,1,0:T(8,128)S(1)}, u32[]{:S(2)}, u32[]{:S(2)}) collective-permute-start(f32[2,32,192]{2,1,0:T(8,128)S(1)} %get-tuple-element.43), channel_id=1, source_target_pairs={{0,24},{4,28},{8,0},{12,4},{16,8},{20,12},{24,16},{28,20},{1,25},{... | collective-permute-start | bytes 147464 | tf_op jit(solution)/shard_map/ppermute | solution.py:470
  51.5 5.8 %collective-permute-start.13 = (f32[4,32,192]{2,1,0:T(8,128)S(1)}, f32[4,32,192]{2,1,0:T(8,128)S(1)}, u32[]{:S(2)}, u32[]{:S(2)}) collective-permute-start(f32[4,32,192]{2,1,0:T(8,128)S(1)} %pad_maximum_fusion.5), channel_id=1, source_target_pairs={{0,4},{4,0},{8,12},{12,8},{16,20},{20,16},{24,28},{28,24},{1,5},{5... | collective-permute-start | bytes 294920 | tf_op jit(solution)/shard_map/ppermute | solution.py:463
  61.8 1.8 %collective-permute-start.16 = (f32[7,7,2,8,128]{4,3,2,1,0:T(8,128)S(1)}, f32[7,7,2,8,128]{4,3,2,1,0:T(8,128)S(1)}, u32[]{:S(2)}, u32[]{:S(2)}) collective-permute-start(f32[7,7,2,8,128]{4,3,2,1,0:T(8,128)S(1)} %get-tuple-element.52), channel_id=1, source_target_pairs={{0,1},{1,0},{2,3},{3,2},{4,5},{5,4},{6,7},{7,6},{8,9},{9,8},{10,11... | collective-permute-start | bytes 1204232 | tf_op jit(solution)/shard_map/ppermute | solution.py:463
  63.7 9.7 %collective-permute-start.17 = (f32[5,7,2,8,128]{4,3,2,1,0:T(8,128)S(1)}, f32[5,7,2,8,128]{4,3,2,1,0:T(8,128)S(1)}, u32[]{:S(2)}, u32[]{:S(2)}) collective-permute-start(f32[5,7,2,8,128]{4,3,2,1,0:T(8,128)S(1)} %slice.46), channel_id=1, source_target_pairs={{0,2},{1,3},{2,0},{3,1},{4,6},{5,7},{6,4},{7,5},{8,10},{9,11},{10,... | collective-permute-start | bytes 860168 | tf_op jit(solution)/shard_map/ppermute | solution.py:470
  63.8 11.3 %collective-permute-start.18 = (f32[2,7,2,8,128]{4,3,2,1,0:T(8,128)S(1)}, f32[2,7,2,8,128]{4,3,2,1,0:T(8,128)S(1)}, u32[]{:S(2)}, u32[]{:S(2)}) collective-permute-start(f32[2,7,2,8,128]{4,3,2,1,0:T(8,128)S(1)} %slice.47), channel_id=1, source_target_pairs={{0,2},{1,3},{2,0},{3,1},{4,6},{5,7},{6,4},{7,5},{8,10},{9,11},{10,... | collective-permute-start | bytes 344072 | tf_op jit(solution)/shard_map/ppermute | solution.py:470
  73.5 1.7 %collective-permute-start.19 = (f32[5,7,2,8,128]{4,3,2,1,0:T(8,128)S(1)}, f32[5,7,2,8,128]{4,3,2,1,0:T(8,128)S(1)}, u32[]{:S(2)}, u32[]{:S(2)}) collective-permute-start(f32[5,7,2,8,128]{4,3,2,1,0:T(8,128)S(1)} %slice_add_fusion.1), channel_id=1, source_target_pairs={{0,1},{1,0},{2,3},{3,2},{4,5},{5,4},{6,7},{7,6},{8,9},{9,8},{10,11... | collective-permute-start | bytes 860168 | tf_op jit(solution)/shard_map/ppermute | solution.py:463
  75.1 1.4 %collective-permute-start.20 = (f32[2,7,2,8,128]{4,3,2,1,0:T(8,128)S(1)}, f32[2,7,2,8,128]{4,3,2,1,0:T(8,128)S(1)}, u32[]{:S(2)}, u32[]{:S(2)}) collective-permute-start(f32[2,7,2,8,128]{4,3,2,1,0:T(8,128)S(1)} %slice_add_fusion), channel_id=1, source_target_pairs={{0,1},{1,0},{2,3},{3,2},{4,5},{5,4},{6,7},{7,6},{8,9},{9,8},{10,11... | collective-permute-start | bytes 344072 | tf_op jit(solution)/shard_map/ppermute | solution.py:463
